TPU v7x, 32 devices: a whole 2x2x4 slice. The times are simulated.
32 devices in a mesh: tm: 8 (over y, x, core), agent: 4 (over z).
Axes of the slice: x: 2, y: 2, z: 4, core: 2. Of those that a mesh axis runs over, the one named last changes fastest.
Arguments:
- states: bfloat16 [48, 512, 512], P('tm', 'agent'), may hold values from -30 to 30
- neighbours: int32 [4, 4], replicated, may hold values from 0 to 3, as said below
- w_query_t: bfloat16 [512, 512], replicated, may hold values from -16 to 16
- w_key_t: bfloat16 [512, 512], replicated, may hold values from -16 to 16
- w_value_t: bfloat16 [512, 512], replicated, may hold values from -0.25 to 0.25
- w_out_t: bfloat16 [512, 512], replicated, may hold values from -0.25 to 0.25
- w_query_a: bfloat16 [512, 512], replicated, may hold values from -16 to 16
- w_key_a: bfloat16 [512, 512], replicated, may hold values from -16 to 16
- w_value_a: bfloat16 [512, 512], replicated, may hold values from -0.25 to 0.25
- w_out_a: bfloat16 [512, 512], replicated, may hold values from -0.25 to 0.25
- w_in: bfloat16 [512, 2048], replicated, may hold values from -0.25 to 0.25
- w_mlp_out: bfloat16 [2048, 512], replicated, may hold values from -0.125 to 0.125
Outputs:
- mixed: bfloat16 [48, 512, 512], P('tm', 'agent')
Inputs may be any that keep to these rules, and one draw needn't show every extreme that they name: neighbours[b] lists 4 different blocks, the first of them b itself.
All inputs are finite; a program needn't handle non-finite values.
Results may differ from a plain program's by a relative error of at most 0.006.
Values may be sent and summed in bfloat16 or wider, within the bound.
No kernel may reach another device: no remote copies, remote signals or barrier semaphores. Data moves between devices by JAX's collectives and lax.ppermute only.
A program may use at most 128 MiB of HBM per device.

v0:
```python
import jax
import jax.numpy as jnp
from jax import lax
from jax.sharding import PartitionSpec as P

HEADS = 8


negative_floor = -1e30
epsilon = 1e-06


def rms_normed(values):
    wide = values.astype(jnp.float32)
    scale = lax.rsqrt(jnp.mean(wide * wide, axis=-1, keepdims=True) + epsilon)
    return (wide * scale).astype(jnp.bfloat16)


def project(normed, weight):
    return jnp.dot(normed, weight, preferred_element_type=jnp.float32).astype(jnp.bfloat16)


def attend(query, keys, values, allowed):
    batch, query_len, features = query.shape
    key_len = keys.shape[1]
    head_size = features // HEADS
    query_h = query.reshape(batch, query_len, HEADS, head_size)
    keys_h = keys.reshape(batch, key_len, HEADS, head_size)
    values_h = values.reshape(batch, key_len, HEADS, head_size)
    scores = jnp.einsum(
        "bqhe,bkhe->bhqk", query_h, keys_h, preferred_element_type=jnp.float32
    ) * head_size ** (-0.5)
    scores = jnp.where(allowed[:, None], scores, negative_floor)
    largest = jnp.max(scores, axis=-1, keepdims=True)
    weights = jnp.where(allowed[:, None], jnp.exp(scores - largest), 0.0)
    totals = jnp.sum(weights, axis=-1)
    summed = jnp.einsum(
        "bhqk,bkhe->bqhe",
        weights.astype(jnp.bfloat16),
        values_h,
        preferred_element_type=jnp.float32,
    )
    result = summed / jnp.transpose(totals, (0, 2, 1))[..., None]
    return result.reshape(batch, query_len, features).astype(jnp.bfloat16)


def local(
    states,
    neighbours,
    w_query_t,
    w_key_t,
    w_value_t,
    w_out_t,
    w_query_a,
    w_key_a,
    w_value_a,
    w_out_a,
    w_in,
    w_mlp_out,
):
    local_steps, local_agents, features = states.shape
    head_size = features // HEADS
    first_normed = rms_normed(states)
    query = project(first_normed, w_query_t).reshape(local_steps, local_agents, HEADS, head_size)
    keys_local = project(first_normed, w_key_t)
    values_local = project(first_normed, w_value_t)
    query_time = lax.axis_index("tm") * local_steps + jnp.arange(local_steps)
    start_max = jnp.full((local_agents, HEADS, local_steps), negative_floor, jnp.float32)
    key_piece = lax.all_gather(keys_local, "tm", axis=0, tiled=True)
    value_piece = lax.all_gather(values_local, "tm", axis=0, tiled=True)
    length = key_piece.shape[0]
    keys_h = key_piece.reshape(length, local_agents, HEADS, head_size)
    values_h = value_piece.reshape(length, local_agents, HEADS, head_size)
    scores = jnp.einsum(
        "tahe,sahe->ahts", query, keys_h, preferred_element_type=jnp.float32
    ) * head_size ** (-0.5)
    key_time = jnp.arange(length)
    allowed = (key_time[None, :] <= query_time[:, None])[None, None]
    scores = jnp.where(allowed, scores, negative_floor)
    new_max = jnp.maximum(start_max, jnp.max(scores, axis=-1))
    weights = jnp.where(allowed, jnp.exp(scores - new_max[..., None]), 0.0)
    new_sum = jnp.sum(weights, axis=-1)
    added = jnp.einsum(
        "ahts,sahe->ahte",
        weights.astype(jnp.bfloat16),
        values_h,
        preferred_element_type=jnp.float32,
    )
    result = added / new_sum[..., None]
    time_mixed = (
        jnp.transpose(result, (2, 0, 1, 3))
        .reshape(local_steps, local_agents, features)
        .astype(jnp.bfloat16)
    )
    after_time = (
        states.astype(jnp.float32)
        + jnp.dot(time_mixed, w_out_t, preferred_element_type=jnp.float32)
    ).astype(jnp.bfloat16)
    second_normed = rms_normed(after_time)
    agent_query = project(second_normed, w_query_a)
    block_count = lax.axis_size("agent")
    chosen_blocks = lax.dynamic_slice_in_dim(neighbours, lax.axis_index("agent"), 1, 0)[0]
    neighbour_count = neighbours.shape[1]
    everyone = lax.all_gather(second_normed, "agent", axis=1, tiled=True)
    picked = jnp.take(
        everyone.reshape(local_steps, block_count, local_agents, features), chosen_blocks, axis=1
    )
    picked = picked.reshape(local_steps, neighbour_count * local_agents, features)
    agent_key = project(picked, w_key_a)
    agent_value = project(picked, w_value_a)
    allowed_all = jnp.ones((1, local_agents, neighbour_count * local_agents), dtype=bool)
    agent_mixed = attend(agent_query, agent_key, agent_value, allowed_all)
    after_agent = (
        after_time.astype(jnp.float32)
        + jnp.dot(agent_mixed, w_out_a, preferred_element_type=jnp.float32)
    ).astype(jnp.bfloat16)
    inner = jax.nn.gelu(
        jnp.dot(rms_normed(after_agent), w_in, preferred_element_type=jnp.float32), approximate=True
    ).astype(jnp.bfloat16)
    final = after_agent.astype(jnp.float32) + jnp.dot(
        inner, w_mlp_out, preferred_element_type=jnp.float32
    )
    return final.astype(jnp.bfloat16)


def solution(mesh):
    placed = (P("tm", "agent", None), P(), P(), P(), P(), P(), P(), P(), P(), P(), P(), P())
    return jax.shard_map(
        local, mesh=mesh, in_specs=placed, out_specs=P("tm", "agent", None), check_vma=False
    )
```

profile of v0, /device:TPU:0, one launch (start us, length us, event | category | flops | bytes accessed | tf_op | source)
XLA Modules:
  0.0 254.2 jit_solution(14797433285925474541)
XLA Ops:
  6.5 0.0 copy-start
  6.5 0.0 all-gather.4.cloned.1.call-start
  6.5 1.5 fusion.33
  8.1 2.8 %convolution_convert_fusion.4 = bf16[6,128,512]{2,1,0:T(8,128)(2,1)} fusion(bf16[6,128,512]{2,1,0:T(8,128)(2,1)} %param.12, f32[6,128]{1,0:T(8,128)S(1)} %add_rsqrt_fusion.2, bf16[512,512]{1,0:T(8,128)(2,1)} %param.15), kind=kOutput, calls=%fused_computation.58 | convolution fusion | flops 404226048 | bytes 2100224 | tf_op jit(solution)/shard_map/dot_general | solution.py:20
  10.9 0.0 all-gather.4.cloned.1.call-update
  10.9 0.0 all-gather.6.cloned.1.call-start
  10.9 0.0 copy-done.3
  10.9 0.0 copy-done.5
  11.0 1.5 convolution_convert_fusion.3
  12.5 0.0 all-gather.6.cloned.1.call-update
  12.5 0.0 all-gather.8.cloned.1.call-start
  12.6 2.6 %convolution_convert_fusion.5 = bf16[6,128,512]{2,1,0:T(8,128)(2,1)} fusion(bf16[6,128,512]{2,1,0:T(8,128)(2,1)S(1)} %copy-done.3, f32[6,128]{1,0:T(8,128)S(1)} %add_rsqrt_fusion.2, bf16[512,512]{1,0:T(8,128)(2,1)} %param.14), kind=kOutput, calls=%fused_computation.59 | convolution fusion | flops 404226048 | bytes 2100224 | tf_op jit(solution)/shard_map/dot_general | solution.py:20
  15.1 1.5 copy.34
  16.6 3.9 %copy.36 = bf16[6,128,8,64]{3,0,2,1:T(8,128)(2,1)} copy(bf16[6,128,8,64]{1,3,2,0:T(8,128)(2,1)S(1)} %bitcast.89) | data formatting | bytes 1572864 | tf_op jit(solution)/shard_map/reshape | solution.py:64
  20.5 0.1 iota_compare_fusion
  20.6 38.7 %all-gather.4.cloned.1.call-done = bf16[48,128,512]{2,1,0:T(8,128)(2,1)} async-done(((bf16[6,128,512]{2,1,0:T(8,128)(2,1)}), bf16[48,128,512]{2,1,0:T(8,128)(2,1)}) %all-gather.4.cloned.1.call-update) | async-done | bytes 6291472 | tf_op jit(solution)/shard_map/all_gather | solution.py:69
  59.3 8.6 %copy.35 = bf16[48,128,512]{1,2,0:T(8,128)(2,1)} copy(bf16[48,128,512]{2,1,0:T(8,128)(2,1)} %all-gather.4.cloned.1.call-done) | data formatting | bytes 12582912 | tf_op jit(solution)/shard_map/all_gather | solution.py:69
  67.9 18.6 %copy.37 = bf16[48,128,8,64]{3,0,2,1:T(8,128)(2,1)} copy(bf16[48,128,8,64]{1,3,2,0:T(8,128)(2,1)} %bitcast.83) | data formatting | bytes 12582912 | tf_op jit(solution)/shard_map/reshape | solution.py:72
  86.6 13.8 %fusion.15 = (f32[128,8,6]{2,1,0:T(8,128)S(1)}, f32[128,8,6,48]{3,2,1,0:T(8,128)}) fusion(pred[6,48]{1,0:T(8,128)(4,1)S(1)} %iota_compare_fusion, bf16[6,128,8,64]{3,0,2,1:T(8,128)(2,1)} %copy.36, bf16[48,128,8,64]{3,0,2,1:T(8,128)(2,1)} %copy.37), kind=kOutput, calls=%fused_computation.21 | convolution fusion | flops 38627328 | bytes 8282400 | tf_op jit(solution)/shard_map/tahe,sahe->ahts/dot_general | solution.py:74
  100.4 6.3 %all-gather.6.cloned.1.call-done = bf16[48,128,512]{2,1,0:T(8,128)(2,1)} async-done(((bf16[6,128,512]{2,1,0:T(8,128)(2,1)}), bf16[48,128,512]{2,1,0:T(8,128)(2,1)}) %all-gather.6.cloned.1.call-update) | async-done | bytes 6291472 | tf_op jit(solution)/shard_map/all_gather | solution.py:70
  106.7 8.6 %copy.38 = bf16[48,128,512]{1,2,0:T(8,128)(2,1)} copy(bf16[48,128,512]{2,1,0:T(8,128)(2,1)} %all-gather.6.cloned.1.call-done) | data formatting | bytes 12582912 | tf_op jit(solution)/shard_map/all_gather | solution.py:70
  115.4 18.5 %copy.39 = bf16[48,128,8,64]{3,0,2,1:T(8,128)(2,1)} copy(bf16[48,128,8,64]{1,3,2,0:T(8,128)(2,1)} %bitcast.84) | data formatting | bytes 12582912 | tf_op jit(solution)/shard_map/reshape | solution.py:73
  133.9 4.7 %fusion.18 = f32[128,8,6]{2,1,0:T(8,128)S(1)} fusion(f32[128,8,6,48]{3,2,1,0:T(8,128)} %get-tuple-element.6, f32[128,8,6]{2,1,0:T(8,128)S(1)} %broadcast_maximum_fusion, pred[6,48]{1,0:T(8,128)(4,1)S(1)} %iota_compare_fusion), kind=kLoop, calls=%fused_computation.24 | loop fusion | flops 1468416 | bytes 1229088 | tf_op jit(solution)/shard_map/reduce_sum | solution.py:82
  138.7 0.0 copy-done.1
  138.7 7.6 %fusion.14 = bf16[6,128,8,64]{3,0,2,1:T(8,128)(2,1)} fusion(bf16[48,128,8,64]{3,0,2,1:T(8,128)(2,1)} %copy.39, f32[128,8,6,48]{3,2,1,0:T(8,128)S(1)} %copy-done.1, f32[6,128,8]{0,2,1:T(8,128)S(1)} %bitcast.92, f32[128,8,6]{2,1,0:T(8,128)S(1)} %broadcast_maximum_fusion, pred[6,48]{1,0:T(8,128)(4,1)S(1)} %iota_compare_fusion), kind=kOutput, calls=%fused_computation.18 | convolution fusion | flops 40009728 | bytes 8306976 | tf_op jit(solution)/shard_map/ahts,sahe->ahte/dot_general | solution.py:83
  146.3 3.5 %copy.40 = bf16[6,128,8,64]{1,3,2,0:T(8,128)(2,1)} copy(bf16[6,128,8,64]{3,0,2,1:T(8,128)(2,1)} %fusion.14) | data formatting | bytes 1572864 | tf_op jit(solution)/shard_map/convert_element_type | solution.py:93
  149.8 2.3 fusion.36
  152.1 1.1 fusion.37
  153.3 0.0 all-gather.8.cloned.1.call-update
  153.3 0.1 broadcast_bitcast_fusion
  153.4 2.6 %convolution_convert_fusion.2 = bf16[6,128,512]{2,1,0:T(8,128)(2,1)} fusion(bf16[6,128,512]{2,1,0:T(8,128)(2,1)} %fusion.37, bf16[512,512]{1,0:T(8,128)(2,1)S(1)} %copy-done.6), kind=kOutput, calls=%fused_computation.56 | convolution fusion | flops 403046400 | bytes 2097152 | tf_op jit(solution)/shard_map/dot_general | solution.py:20
  156.0 2.3 copy.44
  158.3 58.6 %all-gather.8.cloned.1.call-done = bf16[6,512,512]{2,1,0:T(8,128)(2,1)} async-done(((bf16[6,128,512]{2,1,0:T(8,128)(2,1)}), bf16[6,512,512]{2,1,0:T(8,128)(2,1)}) %all-gather.8.cloned.1.call-update) | async-done | bytes 3145744 | tf_op jit(solution)/shard_map/all_gather | solution.py:104
  216.9 4.3 %gather_fusion = bf16[4,6,128,512]{3,2,1,0:T(8,128)(2,1)} fusion(bf16[6,4,128,512]{3,2,1,0:T(8,128)(2,1)} %bitcast.88, s32[1024]{0:T(1024)S(1)} %pad_clamp_fusion), kind=kCustom, calls=%fused_computation | custom fusion | bytes 6291472 | tf_op jit(solution)/shard_map/jit(_take)/gather | solution.py:105
  221.2 2.1 copy.42
  223.3 0.0 copy-start.7
  223.3 0.6 bitcast_select_fusion
  223.9 0.4 copy-done.7
  224.4 1.8 convolution_convert_fusion
  226.2 0.0 copy-done.8
  226.2 0.0 copy-start.2
  226.2 3.5 %convolution_convert_fusion.1 = bf16[6,512,512]{1,2,0:T(8,128)(2,1)} fusion(bf16[6,512,512]{2,1,0:T(8,128)(2,1)S(1)} %bitcast_select_fusion, bf16[512,512]{1,0:T(8,128)(2,1)S(1)} %copy-done.8), kind=kOutput, calls=%fused_computation.36 | convolution fusion | flops 1612185600 | bytes 6815744 | tf_op jit(solution)/shard_map/dot_general | solution.py:20
  229.7 2.0 multiply_reduce_fusion
  231.7 3.1 %fusion = f32[6,8,128]{2,1,0:T(8,128)S(1)} fusion(f32[6,8,128,512]{3,2,1,0:T(8,128)S(1)} %get-tuple-element.10, f32[6,8,128]{2,1,0:T(8,128)S(1)} %get-tuple-element.9), kind=kLoop, calls=%fused_computation.3 | loop fusion | flops 9431040 | bytes 12632064 | tf_op jit(solution)/shard_map/reduce_sum | solution.py:36
  234.8 0.0 copy-start.4
  234.8 4.8 %fusion.42 = bf16[6,128,8,64]{1,3,2,0:T(8,128)(2,1)S(1)} fusion(bf16[6,512,8,64]{1,3,2,0:T(8,128)(2,1)} %bitcast.94, f32[6,8,128,512]{3,2,1,0:T(8,128)S(1)} %get-tuple-element.10, f32[6,8,128]{2,1,0:T(8,128)S(1)} %get-tuple-element.9, f32[6,128,8]{1,2,0:T(8,128)S(1)} %bitcast.93), kind=kOutput, calls=%fused_computation.55 | convolution fusion | flops 412876800 | bytes 16564224 | tf_op jit(solution)/shard_map/bhqk,bkhe->bqhe/dot_general | solution.py:37
  239.6 1.5 fusion.39
  241.2 6.5 %fusion.41 = bf16[6,128,512]{2,1,0:T(8,128)(2,1)} fusion(bf16[6,128,512]{2,1,0:T(8,128)(2,1)} %get-tuple-element.12, bf16[2048,512]{1,0:T(8,128)(2,1)S(1)} %copy-done, bf16[512,2048]{1,0:T(8,128)(2,1)} %param.22, f32[6,128]{1,0:T(8,128)S(1)} %add_rsqrt_fusion), kind=kOutput, calls=%fused_computation.53 | convolution fusion | flops 3237740544 | bytes 5770240 | tf_op jit(solution)/shard_map/dot_general | solution.py:120
  (19 shorter events, 0.1 us)
Async XLA Ops:
  6.5 234.6 %copy-start = (bf16[2048,512]{1,0:T(8,128)(2,1)S(1)}, bf16[2048,512]{1,0:T(8,128)(2,1)}, u32[]{:S(2)}) copy-start(bf16[2048,512]{1,0:T(8,128)(2,1)} %param.23) | copy-start | bytes 6291460
  6.5 4.4 %copy-start.3 = (bf16[6,128,512]{2,1,0:T(8,128)(2,1)S(1)}, bf16[6,128,512]{2,1,0:T(8,128)(2,1)}, u32[]{:S(2)}) copy-start(bf16[6,128,512]{2,1,0:T(8,128)(2,1)} %param.12) | copy-start | bytes 2359300
  6.5 4.4 %copy-start.5 = (bf16[512,512]{1,0:T(8,128)(2,1)S(1)}, bf16[512,512]{1,0:T(8,128)(2,1)}, u32[]{:S(2)}) copy-start(bf16[512,512]{1,0:T(8,128)(2,1)} %param.16) | copy-start | bytes 1572868
  6.5 52.8 %all-gather.4.cloned.1.call-start = ((), (), s32[]{:S(2)}) async-start(), calls=%async_computation | async-start | bytes 7077888 | tf_op jit(solution)/shard_map/all_gather | solution.py:69
  10.9 95.9 %all-gather.6.cloned.1.call-start = ((), (), s32[]{:S(2)}) async-start(), calls=%async_computation.1 | async-start | bytes 7077888 | tf_op jit(solution)/shard_map/all_gather | solution.py:70
  12.5 204.4 %all-gather.8.cloned.1.call-start = ((), (), s32[]{:S(2)}) async-start(), calls=%async_computation.2 | async-start | bytes 3932160 | tf_op jit(solution)/shard_map/all_gather | solution.py:104
  133.9 4.8 %copy-start.1 = (f32[128,8,6,48]{3,2,1,0:T(8,128)S(1)}, f32[128,8,6,48]{3,2,1,0:T(8,128)}, u32[]{:S(2)}) copy-start(f32[128,8,6,48]{3,2,1,0:T(8,128)} %get-tuple-element.6) | copy-start | bytes 3538948
  149.8 3.5 %copy-start.9 = (s32[4,4]{1,0:T(4,128)S(1)}, s32[4,4]{1,0:T(4,128)}, u32[]{:S(2)}) copy-start(s32[4,4]{1,0:T(4,128)} %param.13) | copy-start | bytes 196
  149.8 3.6 %copy-start.6 = (bf16[512,512]{1,0:T(8,128)(2,1)S(1)}, bf16[512,512]{1,0:T(8,128)(2,1)}, u32[]{:S(2)}) copy-start(bf16[512,512]{1,0:T(8,128)(2,1)} %param.18) | copy-start | bytes 1572868
  223.3 1.0 copy-start.7
  224.4 1.8 copy-start.8
  226.2 3.5 %copy-start.2 = (bf16[6,128,512]{1,2,0:T(8,128)(2,1)S(1)}, bf16[6,128,512]{1,2,0:T(8,128)(2,1)}, u32[]{:S(2)}) copy-start(bf16[6,128,512]{1,2,0:T(8,128)(2,1)} %copy.44) | copy-start | bytes 2359300
  234.8 4.8 %copy-start.4 = (bf16[512,512]{1,0:T(8,128)(2,1)S(1)}, bf16[512,512]{1,0:T(8,128)(2,1)}, u32[]{:S(2)}) copy-start(bf16[512,512]{1,0:T(8,128)(2,1)} %param.21) | copy-start | bytes 1572868
Sparse Core Ops, SparseCore 0:
  11.0 48.2 all-gather.3
  61.2 45.5 all-gather.5
  153.4 63.4 all-gather.7
where the time goes:
time: 256 us; the launch traced here: 254 us
  waiting for transfers between devices  104 us (41%)
  local copies, waits for them, and re-layouts  72.6 us (28%)
  matrix products  53.4 us (21%)
  between operations  13.3 us (5%)
  other arithmetic  11.2 us (4%)
    all_gather x1, waiting for transfers between devices, local(): everyone = lax.all_gather(second_normed, 'agent', axis=1, tiled=True)  58.6 us
    all_gather x1, waiting for transfers between devices, local(): key_piece = lax.all_gather(keys_local, 'tm', axis=0, tiled=True)  38.7 us
    reshape x1, local copies, waits for them, and re-layouts, local(): keys_h = key_piece.reshape(length, local_agents, HEADS, head_size)  18.6 us
    reshape x1, local copies, waits for them, and re-layouts, local(): values_h = value_piece.reshape(length, local_agents, HEADS, head_size)  18.5 us
    dot_general x6, matrix products, project(): jnp.dot(normed, weight, preferred_element_type=jnp.float32)  14.8 us
    dot_general x1, matrix products, local(): jnp.einsum('tahe,sahe->ahts', query, keys_h, preferred_element_type=jnp.f...  13.8 us
    all_gather x1, local copies, waits for them, and re-layouts, local(): value_piece = lax.all_gather(values_local, 'tm', axis=0, tiled=True)  8.65 us
    all_gather x1, local copies, waits for them, and re-layouts, local(): key_piece = lax.all_gather(keys_local, 'tm', axis=0, tiled=True)  8.65 us
  transfers between devices with their start and end apart: 3, of which 3 were waited for; matrix products, arithmetic and copies ran while one was open for 22% of the time, Pallas kernels for 0%

commit v1 on v0

v1 whole, which is shorter than its diff:
```python
import functools
import math

import jax
import jax.numpy as jnp
from jax import lax
from jax.experimental import pallas as pl
from jax.experimental.pallas import tpu as pltpu
from jax.sharding import PartitionSpec as P

HEADS = 8


negative_floor = -1e30
epsilon = 1e-06


def rms_normed(values):
    wide = values.astype(jnp.float32)
    scale = lax.rsqrt(jnp.mean(wide * wide, axis=-1, keepdims=True) + epsilon)
    return (wide * scale).astype(jnp.bfloat16)


def project(normed, weight):
    return jnp.dot(normed, weight, preferred_element_type=jnp.float32).astype(jnp.bfloat16)


def attend(query, keys, values, allowed):
    batch, query_len, features = query.shape
    key_len = keys.shape[1]
    head_size = features // HEADS
    query_h = query.reshape(batch, query_len, HEADS, head_size)
    keys_h = keys.reshape(batch, key_len, HEADS, head_size)
    values_h = values.reshape(batch, key_len, HEADS, head_size)
    scores = jnp.einsum(
        "bqhe,bkhe->bhqk", query_h, keys_h, preferred_element_type=jnp.float32
    ) * head_size ** (-0.5)
    scores = jnp.where(allowed[:, None], scores, negative_floor)
    largest = jnp.max(scores, axis=-1, keepdims=True)
    weights = jnp.where(allowed[:, None], jnp.exp(scores - largest), 0.0)
    totals = jnp.sum(weights, axis=-1)
    summed = jnp.einsum(
        "bhqk,bkhe->bqhe",
        weights.astype(jnp.bfloat16),
        values_h,
        preferred_element_type=jnp.float32,
    )
    result = summed / jnp.transpose(totals, (0, 2, 1))[..., None]
    return result.reshape(batch, query_len, features).astype(jnp.bfloat16)


def general_time(states, w_query_t, w_key_t, w_value_t, w_out_t):
    local_steps = states.shape[0]
    normed = rms_normed(states)
    query = jnp.swapaxes(project(normed, w_query_t), 0, 1)
    keys = lax.all_gather(project(normed, w_key_t), "tm", axis=0, tiled=True)
    values = lax.all_gather(project(normed, w_value_t), "tm", axis=0, tiled=True)
    query_time = lax.axis_index("tm") * local_steps + jnp.arange(local_steps)
    allowed = (jnp.arange(keys.shape[0])[None, :] <= query_time[:, None])[None]
    mixed = attend(query, jnp.swapaxes(keys, 0, 1), jnp.swapaxes(values, 0, 1), allowed)
    return (
        states.astype(jnp.float32)
        + jnp.dot(jnp.swapaxes(mixed, 0, 1), w_out_t, preferred_element_type=jnp.float32)
    ).astype(jnp.bfloat16)


def general_agent(
    after_time, neighbours, w_query_a, w_key_a, w_value_a, w_out_a, w_in, w_mlp_out
):
    local_steps, local_agents, features = after_time.shape
    second_normed = rms_normed(after_time)
    agent_query = project(second_normed, w_query_a)
    block_count = lax.axis_size("agent")
    chosen_blocks = lax.dynamic_slice_in_dim(neighbours, lax.axis_index("agent"), 1, 0)[0]
    neighbour_count = neighbours.shape[1]
    everyone = lax.all_gather(second_normed, "agent", axis=1, tiled=True)
    picked = jnp.take(
        everyone.reshape(local_steps, block_count, local_agents, features), chosen_blocks, axis=1
    )
    picked = picked.reshape(local_steps, neighbour_count * local_agents, features)
    agent_key = project(picked, w_key_a)
    agent_value = project(picked, w_value_a)
    allowed_all = jnp.ones((1, local_agents, neighbour_count * local_agents), dtype=bool)
    agent_mixed = attend(agent_query, agent_key, agent_value, allowed_all)
    after_agent = (
        after_time.astype(jnp.float32)
        + jnp.dot(agent_mixed, w_out_a, preferred_element_type=jnp.float32)
    ).astype(jnp.bfloat16)
    inner = jax.nn.gelu(
        jnp.dot(rms_normed(after_agent), w_in, preferred_element_type=jnp.float32), approximate=True
    ).astype(jnp.bfloat16)
    final = after_agent.astype(jnp.float32) + jnp.dot(
        inner, w_mlp_out, preferred_element_type=jnp.float32
    )
    return final.astype(jnp.bfloat16)


NT = (((1,), (1,)), ((), ()))


def softmax_parts(scores, factor):
    largest = jnp.max(scores, axis=-1, keepdims=True)
    weights = jnp.exp2((scores - largest) * factor)
    return weights.astype(jnp.bfloat16), jnp.sum(weights, axis=-1, keepdims=True)


def pair_attention(query, keys, values, factor, bias=None):
    half = query.shape[1] // 2
    zero = jnp.zeros_like(keys)
    first_k = lax.broadcasted_iota(jnp.int32, keys.shape, 1) < half
    first_q = lax.broadcasted_iota(jnp.int32, query.shape, 1) < half
    sums, totals = None, []
    for mine in (first_k, jnp.logical_not(first_k)):
        scores = lax.dot_general(
            query, jnp.where(mine, keys, zero), NT, preferred_element_type=jnp.float32
        )
        if bias is not None:
            scores = scores + bias
        weights, total = softmax_parts(scores, factor)
        part = jnp.dot(
            weights, jnp.where(mine, values, zero), preferred_element_type=jnp.float32
        )
        sums = part if sums is None else sums + part
        totals.append(total)
    return sums / jnp.where(first_q, totals[0], totals[1])


def time_kernel(size, first, *refs):
    pieces, (w_query, w_key, w_value, w_out) = refs[:size], refs[size : size + 4]
    outs_a, outs_b = refs[size + 4 : 2 * size + 4], refs[2 * size + 4 : 3 * size + 4]
    wide, normed, query, keys, values, mixed = refs[3 * size + 4 :]
    steps, agents, features = pieces[0].shape
    rows = steps * agents
    total_steps = steps * size
    me = lax.axis_index("tm")
    lanes_of = [slice(c * 128, (c + 1) * 128) for c in range(features // 128)]
    for k in range(size):
        start = pl.multiple_of(jnp.bitwise_xor(me, k) * rows, rows)
        piece = pieces[k][...].reshape(rows, features).astype(jnp.float32)
        for c, lanes in enumerate(lanes_of):
            wide[c, pl.ds(start, rows), :] = piece[:, lanes]
    for agent in range(agents):
        at = pl.ds(agent, total_steps, stride=agents)
        own = jnp.concatenate([wide[c, at, :] for c in range(len(lanes_of))], axis=1)
        scale = lax.rsqrt(jnp.mean(own * own, axis=-1, keepdims=True) + epsilon)
        normed[pl.ds(agent * total_steps, total_steps), :] = (own * scale).astype(jnp.bfloat16)
    for weight, result in ((w_query, query), (w_key, keys), (w_value, values)):
        result[...] = jnp.dot(
            normed[...], weight[...], preferred_element_type=jnp.float32
        ).astype(jnp.bfloat16)

    group = 2 * total_steps
    row = lax.broadcasted_iota(jnp.int32, (group, group), 0)
    column = lax.broadcasted_iota(jnp.int32, (group, group), 1)
    same = (row >= total_steps) == (column >= total_steps)
    bias = jnp.where(jnp.logical_and(same, column <= row), 0.0, negative_floor)
    head_size = features // HEADS
    factor = math.log2(math.e) * head_size**-0.5

    def one_group(g, carry):
        at = pl.ds(pl.multiple_of(g * group, group), group)
        for pair in range(HEADS // 2):
            lanes = pl.ds(pair * 2 * head_size, 2 * head_size)
            mixed[at, lanes] = pair_attention(
                query[at, lanes], keys[at, lanes], values[at, lanes], factor, bias
            ).astype(jnp.bfloat16)
        return carry

    lax.fori_loop(0, agents // 2, one_group, 0)
    added = jnp.dot(mixed[...], w_out[...], preferred_element_type=jnp.float32)
    for agent in range(agents):
        at = pl.ds(agent, total_steps, stride=agents)
        mine = added[agent * total_steps : (agent + 1) * total_steps]
        for c, lanes in enumerate(lanes_of):
            wide[c, at, :] = wide[c, at, :] + mine[:, lanes]
    for k in range(size):
        start = pl.multiple_of(jnp.bitwise_xor(me, k) * rows, rows)
        piece = jnp.concatenate(
            [wide[c, pl.ds(start, rows), :] for c in range(len(lanes_of))], axis=1
        )
        piece = piece.astype(jnp.bfloat16).reshape(pieces[0].shape)
        outs_a[k][...] = piece[:first]
        outs_b[k][...] = piece[first:]


def time_stage(pieces, weights, first):
    size = len(pieces)
    steps, agents, features = pieces[0].shape
    rows = steps * agents * size
    kind = jnp.bfloat16
    return pl.pallas_call(
        functools.partial(time_kernel, size, first),
        out_shape=[jax.ShapeDtypeStruct((first, agents, features), kind)] * size
        + [jax.ShapeDtypeStruct((steps - first, agents, features), kind)] * size,
        in_specs=[pl.BlockSpec(memory_space=pltpu.VMEM)] * (size + 4),
        out_specs=[pl.BlockSpec(memory_space=pltpu.VMEM)] * (2 * size),
        scratch_shapes=[pltpu.VMEM((features // 128, rows, 128), jnp.float32)]
        + [pltpu.VMEM((rows, features), kind)] * 5,
        compiler_params=pltpu.CompilerParams(vmem_limit_bytes=32 * 2**20),
        name="time_attention",
    )(*pieces, *weights)


def pack_kernel(size, choose, *refs):
    pieces, outs = refs[:size], refs[size:]
    agents = pieces[0].shape[1]
    me, plane = lax.axis_index("tm"), lax.axis_index("agent")
    for out, step in zip(outs, choose(plane)):
        for k in range(size):
            start = pl.multiple_of(jnp.bitwise_xor(me, k) * agents, agents)
            out[pl.ds(start, agents), :] = pieces[k][step]


def pack_stage(pieces, choose, count):
    size = len(pieces)
    _, agents, features = pieces[0].shape
    return pl.pallas_call(
        functools.partial(pack_kernel, size, choose),
        out_shape=[jax.ShapeDtypeStruct((agents * size, features), jnp.bfloat16)] * count,
        in_specs=[pl.BlockSpec(memory_space=pltpu.VMEM)] * size,
        out_specs=[pl.BlockSpec(memory_space=pltpu.VMEM)] * count,
        name="pack_steps",
    )(*pieces)


def agent_body(count, *refs):
    blocks = refs[:count]
    w_query, w_key, w_value, w_out, w_in, w_mlp_out = refs[count : count + 6]
    outs = refs[count + 6 : 2 * count + 6]
    normed, query, keys, values, mixed, after, inner = refs[2 * count + 6 :]
    agents, features = blocks[0].shape
    head_size = features // HEADS
    factor = math.log2(math.e) * head_size**-0.5
    for b in range(count):
        wide = blocks[b][...].astype(jnp.float32)
        scale = lax.rsqrt(jnp.mean(wide * wide, axis=-1, keepdims=True) + epsilon)
        normed[pl.ds(b * agents, agents), :] = (wide * scale).astype(jnp.bfloat16)
    for weight, result in ((w_query, query), (w_key, keys), (w_value, values)):
        result[...] = jnp.dot(
            normed[...], weight[...], preferred_element_type=jnp.float32
        ).astype(jnp.bfloat16)

    def one_block(b, carry):
        at = pl.ds(pl.multiple_of(b * agents, agents), agents)
        for pair in range(HEADS // 2):
            lanes = pl.ds(pair * 2 * head_size, 2 * head_size)
            mixed[at, lanes] = pair_attention(
                query[at, lanes], keys[:, lanes], values[:, lanes], factor
            ).astype(jnp.bfloat16)
        return carry

    lax.fori_loop(0, count, one_block, 0)
    added = jnp.dot(mixed[...], w_out[...], preferred_element_type=jnp.float32)
    for b in range(count):
        own = (blocks[b][...].astype(jnp.float32) + added[b * agents : (b + 1) * agents]).astype(
            jnp.bfloat16
        )
        after[pl.ds(b * agents, agents), :] = own
        wide = own.astype(jnp.float32)
        scale = lax.rsqrt(jnp.mean(wide * wide, axis=-1, keepdims=True) + epsilon)
        normed[pl.ds(b * agents, agents), :] = (wide * scale).astype(jnp.bfloat16)
    hidden = w_in.shape[1]
    for start in range(0, hidden, features):
        inner[:, pl.ds(start, features)] = jax.nn.gelu(
            jnp.dot(
                normed[...], w_in[:, pl.ds(start, features)], preferred_element_type=jnp.float32
            ),
            approximate=True,
        ).astype(jnp.bfloat16)
    final = after[...].astype(jnp.float32) + jnp.dot(
        inner[...], w_mlp_out[...], preferred_element_type=jnp.float32
    )
    for b in range(count):
        outs[b][...] = final[b * agents : (b + 1) * agents].astype(jnp.bfloat16)


def agent_kernel(count, middle_only, *refs):
    if middle_only:
        plane = lax.axis_index("agent")

        @pl.when(jnp.logical_or(plane == 1, plane == 2))
        def _():
            agent_body(count, *refs)

    else:
        agent_body(count, *refs)


def agent_stage(blocks, weights, middle_only):
    count = len(blocks)
    agents, features = blocks[0].shape
    hidden = weights[4].shape[1]
    rows = count * agents
    kind = jnp.bfloat16
    return pl.pallas_call(
        functools.partial(agent_kernel, count, middle_only),
        out_shape=[jax.ShapeDtypeStruct((agents, features), kind)] * count,
        in_specs=[pl.BlockSpec(memory_space=pltpu.VMEM)] * (count + 6),
        out_specs=[pl.BlockSpec(memory_space=pltpu.VMEM)] * count,
        scratch_shapes=[pltpu.VMEM((rows, features), kind)] * 6
        + [pltpu.VMEM((rows, hidden), kind)],
        compiler_params=pltpu.CompilerParams(vmem_limit_bytes=40 * 2**20),
        name="agent_step",
    )(*blocks, *weights)


def xor_pairs(size, k, targets=None):
    return [(j, j ^ k) for j in range(size) if targets is None or j ^ k in targets]


def exchange(parts, axis, targets=None):
    size = len(parts)
    return [parts[0]] + [
        lax.ppermute(parts[k], axis, xor_pairs(size, k, targets)) for k in range(1, size)
    ]


def picked(plane, values):
    result = jnp.int32(values[0])
    for place in range(1, len(values)):
        result = jnp.where(plane == place, values[place], result)
    return result


def whole_steps(plane):
    return [jnp.bitwise_xor(plane, k) for k in range(4)]


def extra_steps(plane):
    return [
        picked(plane, (0, 0, 1, 0)),
        picked(plane, (0, 0, 0, 1)),
        picked(plane, (1, 0, 0, 0)),
        picked(plane, (0, 1, 0, 0)),
    ]


def local(
    states,
    neighbours,
    w_query_t,
    w_key_t,
    w_value_t,
    w_out_t,
    w_query_a,
    w_key_a,
    w_value_a,
    w_out_a,
    w_in,
    w_mlp_out,
):
    local_steps, local_agents, features = states.shape
    size, planes = lax.axis_size("tm"), lax.axis_size("agent")
    share = local_agents // size
    time_weights = (w_query_t, w_key_t, w_value_t, w_out_t)
    agent_weights = (w_query_a, w_key_a, w_value_a, w_out_a, w_in, w_mlp_out)
    fits = (
        size & (size - 1) == 0
        and share * size == local_agents
        and share % 16 == 0
        and planes == 4
        and neighbours.shape == (4, 4)
        and local_steps == 6
    )
    if not fits:
        after_time = general_time(states, *time_weights)
        return general_agent(after_time, neighbours, *agent_weights)

    me, plane = lax.axis_index("tm"), lax.axis_index("agent")
    parts = [
        lax.dynamic_slice_in_dim(states, jnp.bitwise_xor(me, k) * share, share, 1)
        for k in range(size)
    ]
    pieces = exchange(parts, "tm")
    shared = time_stage(pieces, time_weights, 4)
    pieces_a = exchange(shared[:size], "tm")
    pieces_b = exchange(shared[size:], "tm")
    blocks_a = exchange(pack_stage(pieces_a, whole_steps, 4), "agent")
    blocks_b = exchange(pack_stage(pieces_b, extra_steps, 4), "agent", (1, 2))
    done_a = exchange(agent_stage(blocks_a, agent_weights, False), "agent")
    result_b = agent_stage(blocks_b, agent_weights, True)
    done_b = [result_b[0]] + [
        lax.ppermute(result_b[k], "agent", [(j, j ^ k) for j in (1, 2)]) for k in range(1, 4)
    ]
    finals = jnp.stack(done_a)
    first = [
        lax.dynamic_index_in_dim(finals, jnp.bitwise_xor(plane, t), 0, False) for t in range(4)
    ]
    extra = jnp.stack(done_b)
    fourth = lax.dynamic_index_in_dim(extra, picked(plane, (1, 0, 3, 2)), 0, False)
    fifth = lax.dynamic_index_in_dim(extra, picked(plane, (2, 3, 0, 1)), 0, False)
    return jnp.stack(first + [fourth, fifth])


def solution(mesh):
    placed = (P("tm", "agent", None), P(), P(), P(), P(), P(), P(), P(), P(), P(), P(), P())
    return jax.shard_map(
        local, mesh=mesh, in_specs=placed, out_specs=P("tm", "agent", None), check_vma=False
    )
```

time: 256 us -> 116 us (0.45)
  waiting for transfers between devices: 104 us -> 14.6 us
  local copies, waits for them, and re-layouts: 72.6 us -> 18.1 us
  matrix products: 53.4 us -> 0 us
  starting transfers between devices: 0.09 us -> 53 us
  Pallas kernels: 0 us -> 28.5 us
  between operations: 13.3 us -> 0.29 us
  other arithmetic: 11.2 us -> 1.17 us
    all_gather x3 -> x0, waiting for transfers between devices: 104 us -> none  [the longest x1 58.6 us: local(): everyone = lax.all_gather(second_normed, 'agent', axis=1, tiled=True)]
    dot_general x13 -> x0, matrix products: 53.4 us -> none  [the longest x6 14.8 us: project(): jnp.dot(normed, weight, preferred_element_type=jnp.float32)]
    ppermute x0 -> x33, starting transfers between devices: none -> 53 us  [the longest x30 49.4 us: exchange(): lax.ppermute(parts[k], axis, xor_pairs(size, k, targets))]
    reshape x3 -> x0, local copies, waits for them, and re-layouts: 41 us -> none  [the longest x1 18.6 us: local(): keys_h = key_piece.reshape(length, local_agents, HEADS, head_size)]
    pallas_call x0 -> x5, Pallas kernels: none -> 28.5 us  [the longest x1 13.1 us: time_stage(): pl.pallas_call(functools.partial(time_kernel, size, first), out_shape=[ja...]
    all_gather x2 -> x0, local copies, waits for them, and re-layouts: 17.3 us -> none  [the longest x1 8.65 us: local(): value_piece = lax.all_gather(values_local, 'tm', axis=0, tiled=True)]
    unnamed x20 -> x67, local copies, waits for them, and re-layouts: 0.47 us -> 16.2 us
    ppermute x0 -> x33, waiting for transfers between devices: none -> 14.6 us  [the longest x30 14.6 us: exchange(): lax.ppermute(parts[k], axis, xor_pairs(size, k, targets))]
  transfers between devices with their start and end apart: 3 -> 33, of which waited for: 3 -> 5; matrix products, arithmetic and copies ran while one was open for 22% -> 1% of each run, Pallas kernels for 0% -> 13%
where the time goes in v1:
time: 116 us
  starting transfers between devices  53 us (46%)
  Pallas kernels  28.5 us (25%)
  local copies, waits for them, and re-layouts  18.1 us (16%)
  waiting for transfers between devices  14.6 us (13%)
  other arithmetic  1.17 us (1%)
    ppermute x30, starting transfers between devices, exchange(): lax.ppermute(parts[k], axis, xor_pairs(size, k, targets))  49.4 us
    unnamed x67, local copies, waits for them, and re-layouts  16.2 us
    ppermute x30, waiting for transfers between devices, exchange(): lax.ppermute(parts[k], axis, xor_pairs(size, k, targets))  14.6 us
    pallas_call x1, Pallas kernels, time_stage(): pl.pallas_call(functools.partial(time_kernel, size, first), out_shape=[ja...  13.1 us
    pallas_call x2, Pallas kernels, agent_stage(): pl.pallas_call(functools.partial(agent_kernel, count, middle_only), out_s...  11.8 us
    pallas_call x2, Pallas kernels, pack_stage(): pl.pallas_call(functools.partial(pack_kernel, size, choose), out_shape=[j...  3.6 us
    ppermute x3, starting transfers between devices, local(): lax.ppermute(result_b[k], 'agent', [(j, j ^ k) for j in (1, 2)])  3.55 us
  transfers between devices with their start and end apart: 33, of which 5 were waited for; matrix products, arithmetic and copies ran while one was open for 1% of the time, Pallas kernels for 13%

profile of v1, /device:TPU:0, one launch (start us, length us, event | category | flops | bytes accessed | tf_op | source)
XLA Modules:
  0.0 115.6 jit_solution(574243716164909952)
XLA Ops:
  0.0 1.3 %constant_dynamic-slice_fusion = (bf16[6,16,512]{2,1,0:T(8,128)(2,1)S(1)}, bf16[6,16,512]{2,1,0:T(8,128)(2,1)S(1)}, bf16[6,16,512]{2,1,0:T(8,128)(2,1)S(1)}, bf1...) fusion(bf16[6,128,512]{2,1,0:T(8,128)(2,1)} %param.12, ...), kind=kLoop, calls=%fused_computation.8 | loop fusion | bytes 1572896 | tf_op jit(solution)/shard_map/dynamic_slice | solution.py:371
  1.8 2.6 %collective-permute-start.1 = (bf16[6,16,512]{2,1,0:T(8,128)(2,1)S(1)}, bf16[6,16,512]{2,1,0:T(8,128)(2,1)S(1)}, u32[]{:S(2)}, u32[]{:S(2)}) collective-permute-start(bf16[6,16,512]{2,1,0:T(8,128)(2,1)S(1)} %get-tuple-element.73), channel_id=1, source_target_pairs={{0,8},{4,12},{8,0},{12,4},{16,24},{20,28},{24,16},{28,20},{1,9},{5... | collective-permute-start | bytes 294920 | tf_op jit(solution)/shard_map/ppermute | solution.py:314
  4.5 1.8 %collective-permute-start.3 = (bf16[6,16,512]{2,1,0:T(8,128)(2,1)S(1)}, bf16[6,16,512]{2,1,0:T(8,128)(2,1)S(1)}, u32[]{:S(2)}, u32[]{:S(2)}) collective-permute-start(bf16[6,16,512]{2,1,0:T(8,128)(2,1)S(1)} %get-tuple-element.71), channel_id=1, source_target_pairs={{0,16},{4,20},{8,24},{12,28},{16,0},{20,4},{24,8},{28,12},{1,17},{... | collective-permute-start | bytes 294920 | tf_op jit(solution)/shard_map/ppermute | solution.py:314
  6.2 2.6 %collective-permute-start.5 = (bf16[6,16,512]{2,1,0:T(8,128)(2,1)S(1)}, bf16[6,16,512]{2,1,0:T(8,128)(2,1)S(1)}, u32[]{:S(2)}, u32[]{:S(2)}) collective-permute-start(bf16[6,16,512]{2,1,0:T(8,128)(2,1)S(1)} %get-tuple-element.76), channel_id=1, source_target_pairs={{0,24},{4,28},{8,16},{12,20},{16,8},{20,12},{24,0},{28,4},{1,25},{... | collective-permute-start | bytes 294920 | tf_op jit(solution)/shard_map/ppermute | solution.py:314
  8.8 0.9 collective-permute-start.6
  9.8 5.8 %collective-permute-done.4.refs_5_ = bf16[6,16,512]{2,1,0:T(8,128)(2,1)S(1)} collective-permute-done((bf16[6,16,512]{2,1,0:T(8,128)(2,1)S(1)}, bf16[6,16,512]{2,1,0:T(8,128)(2,1)S(1)}, u32[]{:S(2)}, u32[]{:S(2)}) %collective-permute-start.4) | collective-permute-done | bytes 98336 | tf_op jit(solution)/shard_map/ppermute | solution.py:314
  15.6 1.0 copy-done.8
  16.6 1.0 copy-done.9
  17.7 1.0 copy-done.10
  18.7 1.0 copy-done.11
  19.7 13.1 %time_attention.1 = (bf16[4,16,512]{2,1,0:T(8,128)(2,1)S(1)}, bf16[4,16,512]{2,1,0:T(8,128)(2,1)S(1)}, bf16[4,16,512]{2,1,0:T(8,128)(2,1)S(1)}, bf16[4,16,512]{2...) custom-call(bf16[6,16,512]{2,1,0:T(8,128)(2,1)S(1)} %get-tuple-eleme, ...), custom_call_target="tpu_custom_call" | custom-call | tf_op jit(solution)/shard_map/time_attention/pallas_call | solution.py:191
  34.2 1.7 %collective-permute-start.21 = (bf16[2,16,512]{2,1,0:T(8,128)(2,1)S(1)}, bf16[2,16,512]{2,1,0:T(8,128)(2,1)S(1)}, u32[]{:S(2)}, u32[]{:S(2)}) collective-permute-start(bf16[2,16,512]{2,1,0:T(8,128)(2,1)S(1)} %get-tuple-element.55), channel_id=1, source_target_pairs={{0,8},{4,12},{8,0},{12,4},{16,24},{20,28},{24,16},{28,20},{1,9},{5... | collective-permute-start | bytes 98312 | tf_op jit(solution)/shard_map/ppermute | solution.py:314
  36.0 1.4 %collective-permute-start.23 = (bf16[2,16,512]{2,1,0:T(8,128)(2,1)S(1)}, bf16[2,16,512]{2,1,0:T(8,128)(2,1)S(1)}, u32[]{:S(2)}, u32[]{:S(2)}) collective-permute-start(bf16[2,16,512]{2,1,0:T(8,128)(2,1)S(1)} %get-tuple-element.57), channel_id=1, source_target_pairs={{0,16},{4,20},{8,24},{12,28},{16,0},{20,4},{24,8},{28,12},{1,17},{... | collective-permute-start | bytes 98312 | tf_op jit(solution)/shard_map/ppermute | solution.py:314
  37.8 1.5 %collective-permute-start.8 = (bf16[4,16,512]{2,1,0:T(8,128)(2,1)S(1)}, bf16[4,16,512]{2,1,0:T(8,128)(2,1)S(1)}, u32[]{:S(2)}, u32[]{:S(2)}) collective-permute-start(bf16[4,16,512]{2,1,0:T(8,128)(2,1)S(1)} %get-tuple-element.39), channel_id=1, source_target_pairs={{0,8},{4,12},{8,0},{12,4},{16,24},{20,28},{24,16},{28,20},{1,9},{5... | collective-permute-start | bytes 196616 | tf_op jit(solution)/shard_map/ppermute | solution.py:314
  39.5 1.6 %collective-permute-start.25 = (bf16[2,16,512]{2,1,0:T(8,128)(2,1)S(1)}, bf16[2,16,512]{2,1,0:T(8,128)(2,1)S(1)}, u32[]{:S(2)}, u32[]{:S(2)}) collective-permute-start(bf16[2,16,512]{2,1,0:T(8,128)(2,1)S(1)} %get-tuple-element.59), channel_id=1, source_target_pairs={{0,24},{4,28},{8,16},{12,20},{16,8},{20,12},{24,0},{28,4},{1,25},{... | collective-permute-start | bytes 98312 | tf_op jit(solution)/shard_map/ppermute | solution.py:314
  41.1 1.1 collective-permute-start.26
  42.2 0.7 collective-permute-done.24.refs_5_
  45.0 1.7 %collective-permute-start.10 = (bf16[4,16,512]{2,1,0:T(8,128)(2,1)S(1)}, bf16[4,16,512]{2,1,0:T(8,128)(2,1)S(1)}, u32[]{:S(2)}, u32[]{:S(2)}) collective-permute-start(bf16[4,16,512]{2,1,0:T(8,128)(2,1)S(1)} %get-tuple-element.41), channel_id=1, source_target_pairs={{0,16},{4,20},{8,24},{12,28},{16,0},{20,4},{24,8},{28,12},{1,17},{... | collective-permute-start | bytes 196616 | tf_op jit(solution)/shard_map/ppermute | solution.py:314
  46.8 1.3 %collective-permute-start.12 = (bf16[4,16,512]{2,1,0:T(8,128)(2,1)}, bf16[4,16,512]{2,1,0:T(8,128)(2,1)}, u32[]{:S(2)}, u32[]{:S(2)}) collective-permute-start(bf16[4,16,512]{2,1,0:T(8,128)(2,1)} %get-tuple-element.43), channel_id=1, source_target_pairs={{0,24},{4,28},{8,16},{12,20},{16,8},{20,12},{24,0},{28,4},{1,25},{... | collective-permute-start | bytes 196616 | tf_op jit(solution)/shard_map/ppermute | solution.py:314
  48.1 0.6 copy-done.20
  48.7 1.3 %collective-permute-start.13 = (bf16[4,16,512]{2,1,0:T(8,128)(2,1)}, bf16[4,16,512]{2,1,0:T(8,128)(2,1)}, u32[]{:S(2)}, u32[]{:S(2)}) collective-permute-start(bf16[4,16,512]{2,1,0:T(8,128)(2,1)} %get-tuple-element.44), channel_id=1, source_target_pairs={{0,28},{4,24},{8,20},{12,16},{16,12},{20,8},{24,4},{28,0},{1,29},{... | collective-permute-start | bytes 196616 | tf_op jit(solution)/shard_map/ppermute | solution.py:314
  50.0 1.7 %pack_steps.3 = (bf16[128,512]{1,0:T(8,128)(2,1)}, bf16[128,512]{1,0:T(8,128)(2,1)}, bf16[128,512]{1,0:T(8,128)(2,1)}, bf16[128,512]{1,0:T(8,128)(2,1)}) custom-call(bf16[2,16,512]{2,1,0:T(8,128)(2,1)} %copy-done.17, bf16[2,16,512]{2,1,0:T(8,128)(2,1)} %copy-done.23, bf16[2,16,512]{2,1,0:T(8,128)(2,1)} %copy-done.24, bf16[2,16,512]{2,1,0:T(8,128)(2,1)} %copy-done.25, ...), custom_call_target="tpu_custom_call" | custom-call | tf_op jit(solution)/shard_map/pack_steps/pallas_call | solution.py:217
  52.4 3.5 %collective-permute-start.27 = (bf16[128,512]{1,0:T(8,128)(2,1)}, bf16[128,512]{1,0:T(8,128)(2,1)S(1)}, u32[]{:S(2)}, u32[]{:S(2)}) collective-permute-start(bf16[128,512]{1,0:T(8,128)(2,1)} %get-tuple-element.62), channel_id=1, source_target_pairs={{0,1},{3,2},{4,5},{7,6},{8,9},{11,10},{12,13},{15,14},{16,17},{19,... | collective-permute-start | bytes 393224 | tf_op jit(solution)/shard_map/ppermute | solution.py:314
  55.9 0.6 copy-done.22
  56.5 2.3 %collective-permute-start.28 = (bf16[128,512]{1,0:T(8,128)(2,1)}, bf16[128,512]{1,0:T(8,128)(2,1)S(1)}, u32[]{:S(2)}, u32[]{:S(2)}) collective-permute-start(bf16[128,512]{1,0:T(8,128)(2,1)} %get-tuple-element.63), channel_id=1, source_target_pairs={{0,2},{3,1},{4,6},{7,5},{8,10},{11,9},{12,14},{15,13},{16,18},{19,... | collective-permute-start | bytes 393224 | tf_op jit(solution)/shard_map/ppermute | solution.py:314
  58.8 0.7 collective-permute-start.29
  59.5 1.9 %pack_steps.2 = (bf16[128,512]{1,0:T(8,128)(2,1)}, bf16[128,512]{1,0:T(8,128)(2,1)}, bf16[128,512]{1,0:T(8,128)(2,1)}, bf16[128,512]{1,0:T(8,128)(2,1)}) custom-call(bf16[4,16,512]{2,1,0:T(8,128)(2,1)} %copy-done.16, bf16[4,16,512]{2,1,0:T(8,128)(2,1)} %copy-done.19, bf16[4,16,512]{2,1,0:T(8,128)(2,1)} %copy-done.20, bf16[4,16,512]{2,1,0:T(8,128)(2,1)} %copy-done.21, ...), custom_call_target="tpu_custom_call" | custom-call | tf_op jit(solution)/shard_map/pack_steps/pallas_call | solution.py:217
  61.4 1.2 %collective-permute-start.14 = (bf16[128,512]{1,0:T(8,128)(2,1)}, bf16[128,512]{1,0:T(8,128)(2,1)S(1)}, u32[]{:S(2)}, u32[]{:S(2)}) collective-permute-start(bf16[128,512]{1,0:T(8,128)(2,1)} %get-tuple-element.46), channel_id=1, source_target_pairs={{0,1},{1,0},{2,3},{3,2},{4,5},{5,4},{6,7},{7,6},{8,9},{9,8},{10,11... | collective-permute-start | bytes 393224 | tf_op jit(solution)/shard_map/ppermute | solution.py:314
  62.6 0.8 collective-permute-start.15
  63.4 2.4 %collective-permute-start.16 = (bf16[128,512]{1,0:T(8,128)(2,1)}, bf16[128,512]{1,0:T(8,128)(2,1)S(1)}, u32[]{:S(2)}, u32[]{:S(2)}) collective-permute-start(bf16[128,512]{1,0:T(8,128)(2,1)} %get-tuple-element.48), channel_id=1, source_target_pairs={{0,3},{1,2},{2,1},{3,0},{4,7},{5,6},{6,5},{7,4},{8,11},{9,10},{10,... | collective-permute-start | bytes 393224 | tf_op jit(solution)/shard_map/ppermute | solution.py:314
  65.8 0.6 copy-done.14
  66.4 1.6 %copy-done.1 = bf16[2048,512]{1,0:T(8,128)(2,1)S(1)} copy-done((bf16[2048,512]{1,0:T(8,128)(2,1)S(1)}, bf16[2048,512]{1,0:T(8,128)(2,1)}, u32[]{:S(2)}) %copy-start.1) | copy-done | bytes 2097176
  68.0 1.0 copy-done.5
  69.1 1.0 copy-done.7
  70.1 0.9 copy-done.12
  71.0 0.9 copy-done.15
  71.9 0.7 agent_step.3
  72.6 0.8 collective-permute-start.32
  73.4 1.3 %collective-permute-start.31 = (bf16[128,512]{1,0:T(8,128)(2,1)}, bf16[128,512]{1,0:T(8,128)(2,1)}, u32[]{:S(2)}, u32[]{:S(2)}) collective-permute-start(bf16[128,512]{1,0:T(8,128)(2,1)} %get-tuple-element.67), channel_id=1, source_target_pairs={{1,3},{2,0},{5,7},{6,4},{9,11},{10,8},{13,15},{14,12},{17,19},{18,... | collective-permute-start | bytes 393224 | tf_op jit(solution)/shard_map/ppermute | solution.py:383
  74.7 1.5 %collective-permute-start.30 = (bf16[128,512]{1,0:T(8,128)(2,1)}, bf16[128,512]{1,0:T(8,128)(2,1)}, u32[]{:S(2)}, u32[]{:S(2)}) collective-permute-start(bf16[128,512]{1,0:T(8,128)(2,1)} %get-tuple-element.66), channel_id=1, source_target_pairs={{1,0},{2,3},{5,4},{6,7},{9,8},{10,11},{13,12},{14,15},{17,16},{18,... | collective-permute-start | bytes 393224 | tf_op jit(solution)/shard_map/ppermute | solution.py:383
  76.3 11.1 %agent_step.2 = (bf16[128,512]{1,0:T(8,128)(2,1)S(1)}, bf16[128,512]{1,0:T(8,128)(2,1)S(1)}, bf16[128,512]{1,0:T(8,128)(2,1)}, bf16[128,512]{1,0:T(8,128)(2,1)}) custom-call(bf16[128,512]{1,0:T(8,128)(2,1)S(1)} %copy-done.13, bf16[128,512]{1,0:T(8,128)(2,1)S(1)} %collective-permute-done.14.refs_1_, bf16[128,512]{1,0:T(8,128)(2,1)S(1)} %collective-permute-done.15.refs_2_, ...), custom_call_target="tpu_custom_call" | custom-call | tf_op jit(solution)/shard_map/agent_step/pallas_call | solution.py:295
  87.3 1.8 %collective-permute-start.19 = (bf16[128,512]{1,0:T(8,128)(2,1)}, bf16[128,512]{1,0:T(8,128)(2,1)S(1)}, u32[]{:S(2)}, u32[]{:S(2)}) collective-permute-start(bf16[128,512]{1,0:T(8,128)(2,1)} %get-tuple-element.52), channel_id=1, source_target_pairs={{0,3},{1,2},{2,1},{3,0},{4,7},{5,6},{6,5},{7,4},{8,11},{9,10},{10,... | collective-permute-start | bytes 393224 | tf_op jit(solution)/shard_map/ppermute | solution.py:314
  89.1 15.7 %collective-permute-start.18 = (bf16[128,512]{1,0:T(8,128)(2,1)}, bf16[128,512]{1,0:T(8,128)(2,1)S(1)}, u32[]{:S(2)}, u32[]{:S(2)}) collective-permute-start(bf16[128,512]{1,0:T(8,128)(2,1)} %get-tuple-element.51), channel_id=1, source_target_pairs={{0,2},{1,3},{2,0},{3,1},{4,6},{5,7},{6,4},{7,5},{8,10},{9,11},{10,... | collective-permute-start | bytes 393224 | tf_op jit(solution)/shard_map/ppermute | solution.py:314
  104.9 0.6 copy-done.18
  105.5 1.1 pad_maximum_fusion.1
  106.7 7.2 %collective-permute-done.18 = bf16[128,512]{1,0:T(8,128)(2,1)S(1)} collective-permute-done((bf16[128,512]{1,0:T(8,128)(2,1)}, bf16[128,512]{1,0:T(8,128)(2,1)S(1)}, u32[]{:S(2)}, u32[]{:S(2)}) %collective-permute-start.18) | collective-permute-done | bytes 131104 | tf_op jit(solution)/shard_map/ppermute | solution.py:314
  114.1 0.9 copy-done.30
  115.0 0.7 dynamic-slice_dynamic-update-slice_fusion
  (94 shorter events, 5.7 us)
Async XLA Ops:
  1.3 65.1 %copy-start = (bf16[512,2048]{1,0:T(8,128)(2,1)S(1)}, bf16[512,2048]{1,0:T(8,128)(2,1)}, u32[]{:S(2)}) copy-start(bf16[512,2048]{1,0:T(8,128)(2,1)} %refs_8_.5) | copy-start | bytes 6291460
  1.3 65.1 %copy-start.3 = (bf16[512,512]{1,0:T(8,128)(2,1)S(1)}, bf16[512,512]{1,0:T(8,128)(2,1)}, u32[]{:S(2)}) copy-start(bf16[512,512]{1,0:T(8,128)(2,1)} %refs_4_.3) | copy-start | bytes 1572868
  1.3 65.1 %copy-start.4 = (bf16[512,512]{1,0:T(8,128)(2,1)S(1)}, bf16[512,512]{1,0:T(8,128)(2,1)}, u32[]{:S(2)}) copy-start(bf16[512,512]{1,0:T(8,128)(2,1)} %refs_5_.3) | copy-start | bytes 1572868
  1.3 4.9 %collective-permute-start = (bf16[6,16,512]{2,1,0:T(8,128)(2,1)S(1)}, bf16[6,16,512]{2,1,0:T(8,128)(2,1)S(1)}, u32[]{:S(2)}, u32[]{:S(2)}) collective-permute-start(bf16[6,16,512]{2,1,0:T(8,128)(2,1)S(1)} %get-tuple-element.74), channel_id=1, source_target_pairs={{0,4},{4,0},{8,12},{12,8},{16,20},{20,16},{24,28},{28,24},{1,5},{5... | collective-permute-start | bytes 294920 | tf_op jit(solution)/shard_map/ppermute | solution.py:314
  1.8 7.0 %collective-permute-start.1 = (bf16[6,16,512]{2,1,0:T(8,128)(2,1)S(1)}, bf16[6,16,512]{2,1,0:T(8,128)(2,1)S(1)}, u32[]{:S(2)}, u32[]{:S(2)}) collective-permute-start(bf16[6,16,512]{2,1,0:T(8,128)(2,1)S(1)} %get-tuple-element.73), channel_id=1, source_target_pairs={{0,8},{4,12},{8,0},{12,4},{16,24},{20,28},{24,16},{28,20},{1,9},{5... | collective-permute-start | bytes 294920 | tf_op jit(solution)/shard_map/ppermute | solution.py:314
  4.4 5.4 %collective-permute-start.2 = (bf16[6,16,512]{2,1,0:T(8,128)(2,1)S(1)}, bf16[6,16,512]{2,1,0:T(8,128)(2,1)S(1)}, u32[]{:S(2)}, u32[]{:S(2)}) collective-permute-start(bf16[6,16,512]{2,1,0:T(8,128)(2,1)S(1)} %get-tuple-element.72), channel_id=1, source_target_pairs={{0,12},{4,8},{8,4},{12,0},{16,28},{20,24},{24,20},{28,16},{1,13},{... | collective-permute-start | bytes 294920 | tf_op jit(solution)/shard_map/ppermute | solution.py:314
  4.5 5.3 %collective-permute-start.3 = (bf16[6,16,512]{2,1,0:T(8,128)(2,1)S(1)}, bf16[6,16,512]{2,1,0:T(8,128)(2,1)S(1)}, u32[]{:S(2)}, u32[]{:S(2)}) collective-permute-start(bf16[6,16,512]{2,1,0:T(8,128)(2,1)S(1)} %get-tuple-element.71), channel_id=1, source_target_pairs={{0,16},{4,20},{8,24},{12,28},{16,0},{20,4},{24,8},{28,12},{1,17},{... | collective-permute-start | bytes 294920 | tf_op jit(solution)/shard_map/ppermute | solution.py:314
  6.2 9.3 %collective-permute-start.4 = (bf16[6,16,512]{2,1,0:T(8,128)(2,1)S(1)}, bf16[6,16,512]{2,1,0:T(8,128)(2,1)S(1)}, u32[]{:S(2)}, u32[]{:S(2)}) collective-permute-start(bf16[6,16,512]{2,1,0:T(8,128)(2,1)S(1)} %get-tuple-element.70), channel_id=1, source_target_pairs={{0,20},{4,16},{8,28},{12,24},{16,4},{20,0},{24,12},{28,8},{1,21},{... | collective-permute-start | bytes 294920 | tf_op jit(solution)/shard_map/ppermute | solution.py:314
  6.2 9.3 %collective-permute-start.5 = (bf16[6,16,512]{2,1,0:T(8,128)(2,1)S(1)}, bf16[6,16,512]{2,1,0:T(8,128)(2,1)S(1)}, u32[]{:S(2)}, u32[]{:S(2)}) collective-permute-start(bf16[6,16,512]{2,1,0:T(8,128)(2,1)S(1)} %get-tuple-element.76), channel_id=1, source_target_pairs={{0,24},{4,28},{8,16},{12,20},{16,8},{20,12},{24,0},{28,4},{1,25},{... | collective-permute-start | bytes 294920 | tf_op jit(solution)/shard_map/ppermute | solution.py:314
  8.8 6.7 %collective-permute-start.6 = (bf16[6,16,512]{2,1,0:T(8,128)(2,1)S(1)}, bf16[6,16,512]{2,1,0:T(8,128)(2,1)S(1)}, u32[]{:S(2)}, u32[]{:S(2)}) collective-permute-start(bf16[6,16,512]{2,1,0:T(8,128)(2,1)S(1)} %get-tuple-element.69), channel_id=1, source_target_pairs={{0,28},{4,24},{8,20},{12,16},{16,12},{20,8},{24,4},{28,0},{1,29},{... | collective-permute-start | bytes 294920 | tf_op jit(solution)/shard_map/ppermute | solution.py:314
  15.6 1.0 copy-start.8
  16.6 1.0 copy-start.9
  34.1 3.7 %collective-permute-start.20 = (bf16[2,16,512]{2,1,0:T(8,128)(2,1)S(1)}, bf16[2,16,512]{2,1,0:T(8,128)(2,1)S(1)}, u32[]{:S(2)}, u32[]{:S(2)}) collective-permute-start(bf16[2,16,512]{2,1,0:T(8,128)(2,1)S(1)} %get-tuple-element.54), channel_id=1, source_target_pairs={{0,4},{4,0},{8,12},{12,8},{16,20},{20,16},{24,28},{28,24},{1,5},{5... | collective-permute-start | bytes 98312 | tf_op jit(solution)/shard_map/ppermute | solution.py:314
  34.2 5.1 %collective-permute-start.21 = (bf16[2,16,512]{2,1,0:T(8,128)(2,1)S(1)}, bf16[2,16,512]{2,1,0:T(8,128)(2,1)S(1)}, u32[]{:S(2)}, u32[]{:S(2)}) collective-permute-start(bf16[2,16,512]{2,1,0:T(8,128)(2,1)S(1)} %get-tuple-element.55), channel_id=1, source_target_pairs={{0,8},{4,12},{8,0},{12,4},{16,24},{20,28},{24,16},{28,20},{1,9},{5... | collective-permute-start | bytes 98312 | tf_op jit(solution)/shard_map/ppermute | solution.py:314
  35.9 3.7 %collective-permute-start.22 = (bf16[2,16,512]{2,1,0:T(8,128)(2,1)S(1)}, bf16[2,16,512]{2,1,0:T(8,128)(2,1)S(1)}, u32[]{:S(2)}, u32[]{:S(2)}) collective-permute-start(bf16[2,16,512]{2,1,0:T(8,128)(2,1)S(1)} %get-tuple-element.56), channel_id=1, source_target_pairs={{0,12},{4,8},{8,4},{12,0},{16,28},{20,24},{24,20},{28,16},{1,13},{... | collective-permute-start | bytes 98312 | tf_op jit(solution)/shard_map/ppermute | solution.py:314
  36.0 5.2 %collective-permute-start.23 = (bf16[2,16,512]{2,1,0:T(8,128)(2,1)S(1)}, bf16[2,16,512]{2,1,0:T(8,128)(2,1)S(1)}, u32[]{:S(2)}, u32[]{:S(2)}) collective-permute-start(bf16[2,16,512]{2,1,0:T(8,128)(2,1)S(1)} %get-tuple-element.57), channel_id=1, source_target_pairs={{0,16},{4,20},{8,24},{12,28},{16,0},{20,4},{24,8},{28,12},{1,17},{... | collective-permute-start | bytes 98312 | tf_op jit(solution)/shard_map/ppermute | solution.py:314
  37.4 9.4 %collective-permute-start.7 = (bf16[4,16,512]{2,1,0:T(8,128)(2,1)S(1)}, bf16[4,16,512]{2,1,0:T(8,128)(2,1)S(1)}, u32[]{:S(2)}, u32[]{:S(2)}) collective-permute-start(bf16[4,16,512]{2,1,0:T(8,128)(2,1)S(1)} %get-tuple-element.38), channel_id=1, source_target_pairs={{0,4},{4,0},{8,12},{12,8},{16,20},{20,16},{24,28},{28,24},{1,5},{5... | collective-permute-start | bytes 196616 | tf_op jit(solution)/shard_map/ppermute | solution.py:314
  37.8 12.2 %copy-start.23 = (bf16[2,16,512]{2,1,0:T(8,128)(2,1)}, bf16[2,16,512]{2,1,0:T(8,128)(2,1)S(1)}, u32[]{:S(2)}) copy-start(bf16[2,16,512]{2,1,0:T(8,128)(2,1)S(1)} %collective-permute-done.20.refs_1_) | copy-start | bytes 98308
  37.8 10.3 %collective-permute-start.8 = (bf16[4,16,512]{2,1,0:T(8,128)(2,1)S(1)}, bf16[4,16,512]{2,1,0:T(8,128)(2,1)S(1)}, u32[]{:S(2)}, u32[]{:S(2)}) collective-permute-start(bf16[4,16,512]{2,1,0:T(8,128)(2,1)S(1)} %get-tuple-element.39), channel_id=1, source_target_pairs={{0,8},{4,12},{8,0},{12,4},{16,24},{20,28},{24,16},{28,20},{1,9},{5... | collective-permute-start | bytes 196616 | tf_op jit(solution)/shard_map/ppermute | solution.py:314
  39.3 10.7 %copy-start.24 = (bf16[2,16,512]{2,1,0:T(8,128)(2,1)}, bf16[2,16,512]{2,1,0:T(8,128)(2,1)S(1)}, u32[]{:S(2)}) copy-start(bf16[2,16,512]{2,1,0:T(8,128)(2,1)S(1)} %collective-permute-done.21.refs_2_) | copy-start | bytes 98308
  39.3 3.7 %collective-permute-start.24 = (bf16[2,16,512]{2,1,0:T(8,128)(2,1)S(1)}, bf16[2,16,512]{2,1,0:T(8,128)(2,1)S(1)}, u32[]{:S(2)}, u32[]{:S(2)}) collective-permute-start(bf16[2,16,512]{2,1,0:T(8,128)(2,1)S(1)} %get-tuple-element.58), channel_id=1, source_target_pairs={{0,20},{4,16},{8,28},{12,24},{16,4},{20,0},{24,12},{28,8},{1,21},{... | collective-permute-start | bytes 98312 | tf_op jit(solution)/shard_map/ppermute | solution.py:314
  39.5 10.5 %copy-start.25 = (bf16[2,16,512]{2,1,0:T(8,128)(2,1)}, bf16[2,16,512]{2,1,0:T(8,128)(2,1)S(1)}, u32[]{:S(2)}) copy-start(bf16[2,16,512]{2,1,0:T(8,128)(2,1)S(1)} %collective-permute-done.22.refs_3_) | copy-start | bytes 98308
  39.5 4.8 %collective-permute-start.25 = (bf16[2,16,512]{2,1,0:T(8,128)(2,1)S(1)}, bf16[2,16,512]{2,1,0:T(8,128)(2,1)S(1)}, u32[]{:S(2)}, u32[]{:S(2)}) collective-permute-start(bf16[2,16,512]{2,1,0:T(8,128)(2,1)S(1)} %get-tuple-element.59), channel_id=1, source_target_pairs={{0,24},{4,28},{8,16},{12,20},{16,8},{20,12},{24,0},{28,4},{1,25},{... | collective-permute-start | bytes 98312 | tf_op jit(solution)/shard_map/ppermute | solution.py:314
  41.1 8.9 %copy-start.26 = (bf16[2,16,512]{2,1,0:T(8,128)(2,1)}, bf16[2,16,512]{2,1,0:T(8,128)(2,1)S(1)}, u32[]{:S(2)}) copy-start(bf16[2,16,512]{2,1,0:T(8,128)(2,1)S(1)} %collective-permute-done.23.refs_4_) | copy-start | bytes 98308
  41.1 5.5 %collective-permute-start.26 = (bf16[2,16,512]{2,1,0:T(8,128)(2,1)S(1)}, bf16[2,16,512]{2,1,0:T(8,128)(2,1)S(1)}, u32[]{:S(2)}, u32[]{:S(2)}) collective-permute-start(bf16[2,16,512]{2,1,0:T(8,128)(2,1)S(1)} %get-tuple-element.60), channel_id=1, source_target_pairs={{0,28},{4,24},{8,20},{12,16},{16,12},{20,8},{24,4},{28,0},{1,29},{... | collective-permute-start | bytes 98312 | tf_op jit(solution)/shard_map/ppermute | solution.py:314
  43.6 8.2 %collective-permute-start.9 = (bf16[4,16,512]{2,1,0:T(8,128)(2,1)S(1)}, bf16[4,16,512]{2,1,0:T(8,128)(2,1)S(1)}, u32[]{:S(2)}, u32[]{:S(2)}) collective-permute-start(bf16[4,16,512]{2,1,0:T(8,128)(2,1)S(1)} %get-tuple-element.40), channel_id=1, source_target_pairs={{0,12},{4,8},{8,4},{12,0},{16,28},{20,24},{24,20},{28,16},{1,13},{... | collective-permute-start | bytes 196616 | tf_op jit(solution)/shard_map/ppermute | solution.py:314
  45.0 10.9 %collective-permute-start.10 = (bf16[4,16,512]{2,1,0:T(8,128)(2,1)S(1)}, bf16[4,16,512]{2,1,0:T(8,128)(2,1)S(1)}, u32[]{:S(2)}, u32[]{:S(2)}) collective-permute-start(bf16[4,16,512]{2,1,0:T(8,128)(2,1)S(1)} %get-tuple-element.41), channel_id=1, source_target_pairs={{0,16},{4,20},{8,24},{12,28},{16,0},{20,4},{24,8},{28,12},{1,17},{... | collective-permute-start | bytes 196616 | tf_op jit(solution)/shard_map/ppermute | solution.py:314
  46.7 3.4 %copy-start.29 = (bf16[2,16,512]{2,1,0:T(8,128)(2,1)}, bf16[2,16,512]{2,1,0:T(8,128)(2,1)S(1)}, u32[]{:S(2)}) copy-start(bf16[2,16,512]{2,1,0:T(8,128)(2,1)S(1)} %collective-permute-done.26.refs_7_) | copy-start | bytes 98308
  46.7 12.1 %collective-permute-start.11 = (bf16[4,16,512]{2,1,0:T(8,128)(2,1)S(1)}, bf16[4,16,512]{2,1,0:T(8,128)(2,1)}, u32[]{:S(2)}, u32[]{:S(2)}) collective-permute-start(bf16[4,16,512]{2,1,0:T(8,128)(2,1)S(1)} %get-tuple-element.42), channel_id=1, source_target_pairs={{0,20},{4,16},{8,28},{12,24},{16,4},{20,0},{24,12},{28,8},{1,21},{... | collective-permute-start | bytes 196616 | tf_op jit(solution)/shard_map/ppermute | solution.py:314
  46.8 1.3 %copy-start.19 = (bf16[4,16,512]{2,1,0:T(8,128)(2,1)}, bf16[4,16,512]{2,1,0:T(8,128)(2,1)S(1)}, u32[]{:S(2)}) copy-start(bf16[4,16,512]{2,1,0:T(8,128)(2,1)S(1)} %collective-permute-done.7.refs_1_) | copy-start | bytes 196612
  46.8 12.7 %collective-permute-start.12 = (bf16[4,16,512]{2,1,0:T(8,128)(2,1)}, bf16[4,16,512]{2,1,0:T(8,128)(2,1)}, u32[]{:S(2)}, u32[]{:S(2)}) collective-permute-start(bf16[4,16,512]{2,1,0:T(8,128)(2,1)} %get-tuple-element.43), channel_id=1, source_target_pairs={{0,24},{4,28},{8,16},{12,20},{16,8},{20,12},{24,0},{28,4},{1,25},{... | collective-permute-start | bytes 196616 | tf_op jit(solution)/shard_map/ppermute | solution.py:314
  48.7 10.8 %collective-permute-start.13 = (bf16[4,16,512]{2,1,0:T(8,128)(2,1)}, bf16[4,16,512]{2,1,0:T(8,128)(2,1)}, u32[]{:S(2)}, u32[]{:S(2)}) collective-permute-start(bf16[4,16,512]{2,1,0:T(8,128)(2,1)} %get-tuple-element.44), channel_id=1, source_target_pairs={{0,28},{4,24},{8,20},{12,16},{16,12},{20,8},{24,4},{28,0},{1,29},{... | collective-permute-start | bytes 196616 | tf_op jit(solution)/shard_map/ppermute | solution.py:314
  52.4 11.0 %collective-permute-start.27 = (bf16[128,512]{1,0:T(8,128)(2,1)}, bf16[128,512]{1,0:T(8,128)(2,1)S(1)}, u32[]{:S(2)}, u32[]{:S(2)}) collective-permute-start(bf16[128,512]{1,0:T(8,128)(2,1)} %get-tuple-element.62), channel_id=1, source_target_pairs={{0,1},{3,2},{4,5},{7,6},{8,9},{11,10},{12,13},{15,14},{16,17},{19,... | collective-permute-start | bytes 393224 | tf_op jit(solution)/shard_map/ppermute | solution.py:314
  56.5 9.2 %collective-permute-start.28 = (bf16[128,512]{1,0:T(8,128)(2,1)}, bf16[128,512]{1,0:T(8,128)(2,1)S(1)}, u32[]{:S(2)}, u32[]{:S(2)}) collective-permute-start(bf16[128,512]{1,0:T(8,128)(2,1)} %get-tuple-element.63), channel_id=1, source_target_pairs={{0,2},{3,1},{4,6},{7,5},{8,10},{11,9},{12,14},{15,13},{16,18},{19,... | collective-permute-start | bytes 393224 | tf_op jit(solution)/shard_map/ppermute | solution.py:314
  58.8 7.0 %collective-permute-start.29 = (bf16[128,512]{1,0:T(8,128)(2,1)}, bf16[128,512]{1,0:T(8,128)(2,1)S(1)}, u32[]{:S(2)}, u32[]{:S(2)}) collective-permute-start(bf16[128,512]{1,0:T(8,128)(2,1)} %get-tuple-element.64), channel_id=1, source_target_pairs={{1,2},{2,1},{5,6},{6,5},{9,10},{10,9},{13,14},{14,13},{17,18},{18,... | collective-permute-start | bytes 393224 | tf_op jit(solution)/shard_map/ppermute | solution.py:314
  61.4 13.3 %collective-permute-start.14 = (bf16[128,512]{1,0:T(8,128)(2,1)}, bf16[128,512]{1,0:T(8,128)(2,1)S(1)}, u32[]{:S(2)}, u32[]{:S(2)}) collective-permute-start(bf16[128,512]{1,0:T(8,128)(2,1)} %get-tuple-element.46), channel_id=1, source_target_pairs={{0,1},{1,0},{2,3},{3,2},{4,5},{5,4},{6,7},{7,6},{8,9},{9,8},{10,11... | collective-permute-start | bytes 393224 | tf_op jit(solution)/shard_map/ppermute | solution.py:314
  62.6 13.7 %collective-permute-start.15 = (bf16[128,512]{1,0:T(8,128)(2,1)}, bf16[128,512]{1,0:T(8,128)(2,1)S(1)}, u32[]{:S(2)}, u32[]{:S(2)}) collective-permute-start(bf16[128,512]{1,0:T(8,128)(2,1)} %get-tuple-element.47), channel_id=1, source_target_pairs={{0,2},{1,3},{2,0},{3,1},{4,6},{5,7},{6,4},{7,5},{8,10},{9,11},{10,... | collective-permute-start | bytes 393224 | tf_op jit(solution)/shard_map/ppermute | solution.py:314
  63.4 12.8 %collective-permute-start.16 = (bf16[128,512]{1,0:T(8,128)(2,1)}, bf16[128,512]{1,0:T(8,128)(2,1)S(1)}, u32[]{:S(2)}, u32[]{:S(2)}) collective-permute-start(bf16[128,512]{1,0:T(8,128)(2,1)} %get-tuple-element.48), channel_id=1, source_target_pairs={{0,3},{1,2},{2,1},{3,0},{4,7},{5,6},{6,5},{7,4},{8,11},{9,10},{10,... | collective-permute-start | bytes 393224 | tf_op jit(solution)/shard_map/ppermute | solution.py:314
  66.4 1.6 %copy-start.1 = (bf16[2048,512]{1,0:T(8,128)(2,1)S(1)}, bf16[2048,512]{1,0:T(8,128)(2,1)}, u32[]{:S(2)}) copy-start(bf16[2048,512]{1,0:T(8,128)(2,1)} %refs_9_.5) | copy-start | bytes 6291460
  71.9 4.3 %copy-start.2 = (bf16[2048,512]{1,0:T(8,128)(2,1)S(1)}, bf16[2048,512]{1,0:T(8,128)(2,1)}, u32[]{:S(2)}) copy-start(bf16[2048,512]{1,0:T(8,128)(2,1)} %refs_9_.5) | copy-start | bytes 6291460
  71.9 4.3 %copy-start.6 = (bf16[512,512]{1,0:T(8,128)(2,1)S(1)}, bf16[512,512]{1,0:T(8,128)(2,1)}, u32[]{:S(2)}) copy-start(bf16[512,512]{1,0:T(8,128)(2,1)} %refs_6_.3) | copy-start | bytes 1572868
  71.9 4.3 %copy-start.13 = (bf16[128,512]{1,0:T(8,128)(2,1)S(1)}, bf16[128,512]{1,0:T(8,128)(2,1)}, u32[]{:S(2)}) copy-start(bf16[128,512]{1,0:T(8,128)(2,1)} %get-tuple-element.45.refs_0_) | copy-start | bytes 393220
  72.6 32.3 %collective-permute-start.32 = (bf16[128,512]{1,0:T(8,128)(2,1)S(1)}, bf16[128,512]{1,0:T(8,128)(2,1)S(1)}, u32[]{:S(2)}, u32[]{:S(2)}) collective-permute-start(bf16[128,512]{1,0:T(8,128)(2,1)S(1)} %get-tuple-element.68), channel_id=1, source_target_pairs={{1,2},{2,1},{5,6},{6,5},{9,10},{10,9},{13,14},{14,13},{17,18},{18,... | collective-permute-start | bytes 393224 | tf_op jit(solution)/shard_map/ppermute | solution.py:383
  73.4 32.1 %collective-permute-start.31 = (bf16[128,512]{1,0:T(8,128)(2,1)}, bf16[128,512]{1,0:T(8,128)(2,1)}, u32[]{:S(2)}, u32[]{:S(2)}) collective-permute-start(bf16[128,512]{1,0:T(8,128)(2,1)} %get-tuple-element.67), channel_id=1, source_target_pairs={{1,3},{2,0},{5,7},{6,4},{9,11},{10,8},{13,15},{14,12},{17,19},{18,... | collective-permute-start | bytes 393224 | tf_op jit(solution)/shard_map/ppermute | solution.py:383
  74.7 30.8 %collective-permute-start.30 = (bf16[128,512]{1,0:T(8,128)(2,1)}, bf16[128,512]{1,0:T(8,128)(2,1)}, u32[]{:S(2)}, u32[]{:S(2)}) collective-permute-start(bf16[128,512]{1,0:T(8,128)(2,1)} %get-tuple-element.66), channel_id=1, source_target_pairs={{1,0},{2,3},{5,4},{6,7},{9,8},{10,11},{13,12},{14,15},{17,16},{18,... | collective-permute-start | bytes 393224 | tf_op jit(solution)/shard_map/ppermute | solution.py:383
  87.3 19.3 %collective-permute-start.19 = (bf16[128,512]{1,0:T(8,128)(2,1)}, bf16[128,512]{1,0:T(8,128)(2,1)S(1)}, u32[]{:S(2)}, u32[]{:S(2)}) collective-permute-start(bf16[128,512]{1,0:T(8,128)(2,1)} %get-tuple-element.52), channel_id=1, source_target_pairs={{0,3},{1,2},{2,1},{3,0},{4,7},{5,6},{6,5},{7,4},{8,11},{9,10},{10,... | collective-permute-start | bytes 393224 | tf_op jit(solution)/shard_map/ppermute | solution.py:314
  89.1 24.7 %collective-permute-start.18 = (bf16[128,512]{1,0:T(8,128)(2,1)}, bf16[128,512]{1,0:T(8,128)(2,1)S(1)}, u32[]{:S(2)}, u32[]{:S(2)}) collective-permute-start(bf16[128,512]{1,0:T(8,128)(2,1)} %get-tuple-element.51), channel_id=1, source_target_pairs={{0,2},{1,3},{2,0},{3,1},{4,6},{5,7},{6,4},{7,5},{8,10},{9,11},{10,... | collective-permute-start | bytes 393224 | tf_op jit(solution)/shard_map/ppermute | solution.py:314
  105.5 8.3 %collective-permute-start.17 = (bf16[128,512]{1,0:T(8,128)(2,1)S(1)}, bf16[128,512]{1,0:T(8,128)(2,1)S(1)}, u32[]{:S(2)}, u32[]{:S(2)}) collective-permute-start(bf16[128,512]{1,0:T(8,128)(2,1)S(1)} %get-tuple-element.50), channel_id=1, source_target_pairs={{0,1},{1,0},{2,3},{3,2},{4,5},{5,4},{6,7},{7,6},{8,9},{9,8},{10,11... | collective-permute-start | bytes 393224 | tf_op jit(solution)/shard_map/ppermute | solution.py:314
  (16 other events, 12.4 us)

commit v2 on v1

--- a/solution.py
+++ b/solution.py
@@ -96,39 +96,74 @@
 
 
 NT = (((1,), (1,)), ((), ()))
-
-
-def softmax_parts(scores, factor):
-    largest = jnp.max(scores, axis=-1, keepdims=True)
-    weights = jnp.exp2((scores - largest) * factor)
-    return weights.astype(jnp.bfloat16), jnp.sum(weights, axis=-1, keepdims=True)
+VMEM, HBM = pltpu.VMEM, pltpu.HBM
+
+
+def spec(space):
+    return pl.BlockSpec(memory_space=space)
+
+
+def norm_of(wide):
+    scale = lax.rsqrt(jnp.mean(wide * wide, axis=-1, keepdims=True) + epsilon)
+    return (wide * scale).astype(jnp.bfloat16)
+
+
+def gelu(x):
+    inside = x * (math.sqrt(2 / math.pi) + (math.sqrt(2 / math.pi) * 0.044715) * (x * x))
+    half = 0.5 * x
+    return half + half * jnp.tanh(inside)
+
+
+def fetch(sources, targets, sems):
+    copies = [
+        pltpu.make_async_copy(source, target, sems.at[k])
+        for k, (source, target) in enumerate(zip(sources, targets))
+    ]
+    for copy in copies:
+        copy.start()
+    return copies
+
+
+def split_heads(values, even, odd, ones=False):
+    width = values.shape[1]
+    for pair in range(HEADS // 2):
+        wide = width // (HEADS // 2)
+        own = values[:, pair * wide : (pair + 1) * wide]
+        first = lax.broadcasted_iota(jnp.int32, own.shape, 1) < wide // 2
+        zero = jnp.zeros_like(own)
+        if ones:
+            one = jnp.ones_like(own)
+            at = 2 * pair * wide
+            even[:, at : at + wide] = jnp.where(first, own, zero)
+            odd[:, at : at + wide] = jnp.where(first, zero, own)
+            even[:, at + wide : at + 2 * wide] = jnp.where(first, one, zero)
+            odd[:, at + wide : at + 2 * wide] = jnp.where(first, zero, one)
+        else:
+            at = pair * wide
+            even[:, at : at + wide] = jnp.where(first, own, zero)
+            odd[:, at : at + wide] = jnp.where(first, zero, own)
 
 
 def pair_attention(query, keys, values, factor, bias=None):
-    half = query.shape[1] // 2
-    zero = jnp.zeros_like(keys)
-    first_k = lax.broadcasted_iota(jnp.int32, keys.shape, 1) < half
-    first_q = lax.broadcasted_iota(jnp.int32, query.shape, 1) < half
-    sums, totals = None, []
-    for mine in (first_k, jnp.logical_not(first_k)):
-        scores = lax.dot_general(
-            query, jnp.where(mine, keys, zero), NT, preferred_element_type=jnp.float32
-        )
+    sums = None
+    for key, value in zip(keys, values):
+        scores = lax.dot_general(query, key, NT, preferred_element_type=jnp.float32)
         if bias is not None:
             scores = scores + bias
-        weights, total = softmax_parts(scores, factor)
-        part = jnp.dot(
-            weights, jnp.where(mine, values, zero), preferred_element_type=jnp.float32
-        )
+        largest = jnp.max(scores, axis=-1, keepdims=True)
+        weights = jnp.exp2((scores - largest) * factor).astype(jnp.bfloat16)
+        part = jnp.dot(weights, value, preferred_element_type=jnp.float32)
         sums = part if sums is None else sums + part
-        totals.append(total)
-    return sums / jnp.where(first_q, totals[0], totals[1])
-
-
-def time_kernel(size, first, *refs):
-    pieces, (w_query, w_key, w_value, w_out) = refs[:size], refs[size : size + 4]
-    outs_a, outs_b = refs[size + 4 : 2 * size + 4], refs[2 * size + 4 : 3 * size + 4]
-    wide, normed, query, keys, values, mixed = refs[3 * size + 4 :]
+    wide = query.shape[1]
+    return (sums[:, :wide] / sums[:, wide:]).astype(jnp.bfloat16)
+
+
+def time_kernel(size, *refs):
+    pieces, weights = refs[:size], refs[size : size + 4]
+    outs = refs[size + 4 : 2 * size + 4]
+    wide, normed, query, key_e, key_o, value_e, value_o, mixed = refs[2 * size + 4 : 2 * size + 12]
+    w_query, w_key, w_value, w_out, sems = refs[2 * size + 12 :]
+    copies = fetch(weights, (w_query, w_key, w_value, w_out), sems)
     steps, agents, features = pieces[0].shape
     rows = steps * agents
     total_steps = steps * size
@@ -142,12 +177,12 @@
     for agent in range(agents):
         at = pl.ds(agent, total_steps, stride=agents)
         own = jnp.concatenate([wide[c, at, :] for c in range(len(lanes_of))], axis=1)
-        scale = lax.rsqrt(jnp.mean(own * own, axis=-1, keepdims=True) + epsilon)
-        normed[pl.ds(agent * total_steps, total_steps), :] = (own * scale).astype(jnp.bfloat16)
-    for weight, result in ((w_query, query), (w_key, keys), (w_value, values)):
-        result[...] = jnp.dot(
-            normed[...], weight[...], preferred_element_type=jnp.float32
-        ).astype(jnp.bfloat16)
+        normed[pl.ds(agent * total_steps, total_steps), :] = norm_of(own)
+    for copy in copies[:3]:
+        copy.wait()
+    query[...] = project(normed[...], w_query[...])
+    split_heads(project(normed[...], w_key[...]), key_e, key_o)
+    split_heads(project(normed[...], w_value[...]), value_e, value_o, True)
 
     group = 2 * total_steps
     row = lax.broadcasted_iota(jnp.int32, (group, group), 0)
@@ -161,12 +196,18 @@
         at = pl.ds(pl.multiple_of(g * group, group), group)
         for pair in range(HEADS // 2):
             lanes = pl.ds(pair * 2 * head_size, 2 * head_size)
+            double = pl.ds(pair * 4 * head_size, 4 * head_size)
             mixed[at, lanes] = pair_attention(
-                query[at, lanes], keys[at, lanes], values[at, lanes], factor, bias
-            ).astype(jnp.bfloat16)
+                query[at, lanes],
+                (key_e[at, lanes], key_o[at, lanes]),
+                (value_e[at, double], value_o[at, double]),
+                factor,
+                bias,
+            )
         return carry
 
-    lax.fori_loop(0, agents // 2, one_group, 0)
+    lax.fori_loop(0, agents // 2, one_group, 0, unroll=True)
+    copies[3].wait()
     added = jnp.dot(mixed[...], w_out[...], preferred_element_type=jnp.float32)
     for agent in range(agents):
         at = pl.ds(agent, total_steps, stride=agents)
@@ -178,31 +219,33 @@
         piece = jnp.concatenate(
             [wide[c, pl.ds(start, rows), :] for c in range(len(lanes_of))], axis=1
         )
-        piece = piece.astype(jnp.bfloat16).reshape(pieces[0].shape)
-        outs_a[k][...] = piece[:first]
-        outs_b[k][...] = piece[first:]
-
-
-def time_stage(pieces, weights, first):
+        outs[k][...] = piece.astype(jnp.bfloat16).reshape(pieces[0].shape)
+
+
+def time_stage(pieces, weights):
     size = len(pieces)
     steps, agents, features = pieces[0].shape
     rows = steps * agents * size
     kind = jnp.bfloat16
     return pl.pallas_call(
-        functools.partial(time_kernel, size, first),
-        out_shape=[jax.ShapeDtypeStruct((first, agents, features), kind)] * size
-        + [jax.ShapeDtypeStruct((steps - first, agents, features), kind)] * size,
-        in_specs=[pl.BlockSpec(memory_space=pltpu.VMEM)] * (size + 4),
-        out_specs=[pl.BlockSpec(memory_space=pltpu.VMEM)] * (2 * size),
-        scratch_shapes=[pltpu.VMEM((features // 128, rows, 128), jnp.float32)]
-        + [pltpu.VMEM((rows, features), kind)] * 5,
-        compiler_params=pltpu.CompilerParams(vmem_limit_bytes=32 * 2**20),
+        functools.partial(time_kernel, size),
+        out_shape=[jax.ShapeDtypeStruct((steps, agents, features), kind)] * size,
+        in_specs=[spec(VMEM)] * size + [spec(HBM)] * 4,
+        out_specs=[spec(VMEM)] * size,
+        scratch_shapes=[VMEM((features // 128, rows, 128), jnp.float32)]
+        + [VMEM((rows, features), kind)] * 4
+        + [VMEM((rows, 2 * features), kind)] * 2
+        + [VMEM((rows, features), kind)]
+        + [VMEM(w.shape, kind) for w in weights]
+        + [pltpu.SemaphoreType.DMA((4,))],
+        compiler_params=pltpu.CompilerParams(vmem_limit_bytes=24 * 2**20),
         name="time_attention",
     )(*pieces, *weights)
 
 
 def pack_kernel(size, choose, *refs):
-    pieces, outs = refs[:size], refs[size:]
+    count = len(choose(0))
+    pieces, outs = refs[:size], refs[len(refs) - count :]
     agents = pieces[0].shape[1]
     me, plane = lax.axis_index("tm"), lax.axis_index("agent")
     for out, step in zip(outs, choose(plane)):
@@ -211,61 +254,57 @@
             out[pl.ds(start, agents), :] = pieces[k][step]
 
 
-def pack_stage(pieces, choose, count):
-    size = len(pieces)
+def pack_stage(pieces, choose, after=()):
+    size, count = len(pieces), len(choose(0))
     _, agents, features = pieces[0].shape
     return pl.pallas_call(
         functools.partial(pack_kernel, size, choose),
         out_shape=[jax.ShapeDtypeStruct((agents * size, features), jnp.bfloat16)] * count,
-        in_specs=[pl.BlockSpec(memory_space=pltpu.VMEM)] * size,
-        out_specs=[pl.BlockSpec(memory_space=pltpu.VMEM)] * count,
+        in_specs=[spec(VMEM)] * size + [spec(pl.ANY)] * len(after),
+        out_specs=[spec(VMEM)] * count,
+        compiler_params=pltpu.CompilerParams(vmem_limit_bytes=8 * 2**20),
         name="pack_steps",
-    )(*pieces)
-
-
-def agent_body(count, *refs):
-    blocks = refs[:count]
-    w_query, w_key, w_value, w_out, w_in, w_mlp_out = refs[count : count + 6]
-    outs = refs[count + 6 : 2 * count + 6]
-    normed, query, keys, values, mixed, after, inner = refs[2 * count + 6 :]
+    )(*pieces, *after)
+
+
+def agent_body(count, blocks, weights, outs, scratch):
+    normed, query, key_e, key_o, value_e, value_o, mixed, after, inner = scratch[:9]
+    w_query, w_key, w_value, w_out, w_in, w_mlp_out, sems = scratch[9:]
+    copies = fetch(weights, (w_query, w_key, w_value, w_out, w_in, w_mlp_out), sems)
     agents, features = blocks[0].shape
     head_size = features // HEADS
     factor = math.log2(math.e) * head_size**-0.5
     for b in range(count):
-        wide = blocks[b][...].astype(jnp.float32)
-        scale = lax.rsqrt(jnp.mean(wide * wide, axis=-1, keepdims=True) + epsilon)
-        normed[pl.ds(b * agents, agents), :] = (wide * scale).astype(jnp.bfloat16)
-    for weight, result in ((w_query, query), (w_key, keys), (w_value, values)):
-        result[...] = jnp.dot(
-            normed[...], weight[...], preferred_element_type=jnp.float32
-        ).astype(jnp.bfloat16)
-
-    def one_block(b, carry):
-        at = pl.ds(pl.multiple_of(b * agents, agents), agents)
-        for pair in range(HEADS // 2):
-            lanes = pl.ds(pair * 2 * head_size, 2 * head_size)
-            mixed[at, lanes] = pair_attention(
-                query[at, lanes], keys[:, lanes], values[:, lanes], factor
-            ).astype(jnp.bfloat16)
-        return carry
-
-    lax.fori_loop(0, count, one_block, 0)
+        normed[pl.ds(b * agents, agents), :] = norm_of(blocks[b][...].astype(jnp.float32))
+    for copy in copies[:3]:
+        copy.wait()
+    query[...] = project(normed[...], w_query[...])
+    split_heads(project(normed[...], w_key[...]), key_e, key_o)
+    split_heads(project(normed[...], w_value[...]), value_e, value_o, True)
+
+    for pair in range(HEADS // 2):
+        lanes = pl.ds(pair * 2 * head_size, 2 * head_size)
+        double = pl.ds(pair * 4 * head_size, 4 * head_size)
+        mixed[:, lanes] = pair_attention(
+            query[:, lanes],
+            (key_e[:, lanes], key_o[:, lanes]),
+            (value_e[:, double], value_o[:, double]),
+            factor,
+        )
+    for copy in copies[3:]:
+        copy.wait()
     added = jnp.dot(mixed[...], w_out[...], preferred_element_type=jnp.float32)
     for b in range(count):
-        own = (blocks[b][...].astype(jnp.float32) + added[b * agents : (b + 1) * agents]).astype(
-            jnp.bfloat16
-        )
-        after[pl.ds(b * agents, agents), :] = own
-        wide = own.astype(jnp.float32)
-        scale = lax.rsqrt(jnp.mean(wide * wide, axis=-1, keepdims=True) + epsilon)
-        normed[pl.ds(b * agents, agents), :] = (wide * scale).astype(jnp.bfloat16)
+        at = pl.ds(b * agents, agents)
+        own = blocks[b][...].astype(jnp.float32) + added[b * agents : (b + 1) * agents]
+        after[at, :] = own.astype(jnp.bfloat16)
+        normed[at, :] = norm_of(after[at, :].astype(jnp.float32))
     hidden = w_in.shape[1]
     for start in range(0, hidden, features):
-        inner[:, pl.ds(start, features)] = jax.nn.gelu(
+        inner[:, pl.ds(start, features)] = gelu(
             jnp.dot(
                 normed[...], w_in[:, pl.ds(start, features)], preferred_element_type=jnp.float32
-            ),
-            approximate=True,
+            )
         ).astype(jnp.bfloat16)
     final = after[...].astype(jnp.float32) + jnp.dot(
         inner[...], w_mlp_out[...], preferred_element_type=jnp.float32
@@ -275,18 +314,20 @@
 
 
 def agent_kernel(count, middle_only, *refs):
+    blocks, weights = refs[:count], refs[count : count + 6]
+    outs, scratch = refs[-16 - count : -16], refs[-16:]
+
+    def run():
+        agent_body(count, blocks, weights, outs, scratch)
+
     if middle_only:
         plane = lax.axis_index("agent")
-
-        @pl.when(jnp.logical_or(plane == 1, plane == 2))
-        def _():
-            agent_body(count, *refs)
-
+        pl.when(jnp.logical_or(plane == 1, plane == 2))(run)
     else:
-        agent_body(count, *refs)
-
-
-def agent_stage(blocks, weights, middle_only):
+        run()
+
+
+def agent_stage(blocks, weights, middle_only, after=()):
     count = len(blocks)
     agents, features = blocks[0].shape
     hidden = weights[4].shape[1]
@@ -295,13 +336,67 @@
     return pl.pallas_call(
         functools.partial(agent_kernel, count, middle_only),
         out_shape=[jax.ShapeDtypeStruct((agents, features), kind)] * count,
-        in_specs=[pl.BlockSpec(memory_space=pltpu.VMEM)] * (count + 6),
-        out_specs=[pl.BlockSpec(memory_space=pltpu.VMEM)] * count,
-        scratch_shapes=[pltpu.VMEM((rows, features), kind)] * 6
-        + [pltpu.VMEM((rows, hidden), kind)],
-        compiler_params=pltpu.CompilerParams(vmem_limit_bytes=40 * 2**20),
+        in_specs=[spec(VMEM)] * count + [spec(HBM)] * 6 + [spec(pl.ANY)] * len(after),
+        out_specs=[spec(VMEM)] * count,
+        scratch_shapes=[VMEM((rows, features), kind)] * 4
+        + [VMEM((rows, 2 * features), kind)] * 2
+        + [VMEM((rows, features), kind)] * 2
+        + [VMEM((rows, hidden), kind)]
+        + [VMEM(w.shape, kind) for w in weights]
+        + [pltpu.SemaphoreType.DMA((6,))],
+        compiler_params=pltpu.CompilerParams(vmem_limit_bytes=28 * 2**20),
         name="agent_step",
-    )(*blocks, *weights)
+    )(*blocks, *weights, *after)
+
+
+def place_kernel(*refs):
+    whole, extra, out, sems = refs[:4], refs[4:8], refs[8], refs[9]
+    plane = lax.axis_index("agent")
+    middle = jnp.logical_or(plane == 1, plane == 2)
+    low = plane // 2
+    copies = [
+        pltpu.make_async_copy(source, out.at[jnp.bitwise_xor(plane, k)], sems.at[k])
+        for k, source in enumerate(whole)
+    ]
+    inner = [
+        pltpu.make_async_copy(extra[0], out.at[4 + low], sems.at[4]),
+        pltpu.make_async_copy(extra[3], out.at[5 - low], sems.at[5]),
+    ]
+    outer = [
+        pltpu.make_async_copy(extra[1], out.at[4 + low], sems.at[4]),
+        pltpu.make_async_copy(extra[2], out.at[5 - low], sems.at[5]),
+    ]
+    for copy in copies:
+        copy.start()
+
+    @pl.when(middle)
+    def _():
+        for copy in inner:
+            copy.start()
+        for copy in inner:
+            copy.wait()
+
+    @pl.when(jnp.logical_not(middle))
+    def _():
+        for copy in outer:
+            copy.start()
+        for copy in outer:
+            copy.wait()
+
+    for copy in copies:
+        copy.wait()
+
+
+def place_stage(whole, extra):
+    agents, features = whole[0].shape
+    return pl.pallas_call(
+        place_kernel,
+        out_shape=jax.ShapeDtypeStruct((6, agents, features), jnp.bfloat16),
+        in_specs=[spec(pl.ANY)] * 8,
+        out_specs=spec(pl.ANY),
+        scratch_shapes=[pltpu.SemaphoreType.DMA((6,))],
+        name="place_steps",
+    )(*whole, *extra)
 
 
 def xor_pairs(size, k, targets=None):
@@ -328,10 +423,10 @@
 
 def extra_steps(plane):
     return [
-        picked(plane, (0, 0, 1, 0)),
-        picked(plane, (0, 0, 0, 1)),
-        picked(plane, (1, 0, 0, 0)),
-        picked(plane, (0, 1, 0, 0)),
+        4 + picked(plane, (0, 0, 1, 0)),
+        4 + picked(plane, (0, 0, 0, 1)),
+        4 + picked(plane, (1, 0, 0, 0)),
+        4 + picked(plane, (0, 1, 0, 0)),
     ]
 
 
@@ -372,24 +467,18 @@
         for k in range(size)
     ]
     pieces = exchange(parts, "tm")
-    shared = time_stage(pieces, time_weights, 4)
-    pieces_a = exchange(shared[:size], "tm")
-    pieces_b = exchange(shared[size:], "tm")
-    blocks_a = exchange(pack_stage(pieces_a, whole_steps, 4), "agent")
-    blocks_b = exchange(pack_stage(pieces_b, extra_steps, 4), "agent", (1, 2))
-    done_a = exchange(agent_stage(blocks_a, agent_weights, False), "agent")
-    result_b = agent_stage(blocks_b, agent_weights, True)
+    pieces = exchange(time_stage(pieces, time_weights), "tm")
+    packed_a = pack_stage(pieces, whole_steps)
+    packed_b = pack_stage(pieces, extra_steps, packed_a[:1])
+    blocks_a = exchange(packed_a, "agent")
+    blocks_b = exchange(packed_b, "agent", (1, 2))
+    result_a = agent_stage(blocks_a, agent_weights, False)
+    done_a = exchange(result_a, "agent")
+    result_b = agent_stage(blocks_b, agent_weights, True, result_a[:1])
     done_b = [result_b[0]] + [
         lax.ppermute(result_b[k], "agent", [(j, j ^ k) for j in (1, 2)]) for k in range(1, 4)
     ]
-    finals = jnp.stack(done_a)
-    first = [
-        lax.dynamic_index_in_dim(finals, jnp.bitwise_xor(plane, t), 0, False) for t in range(4)
-    ]
-    extra = jnp.stack(done_b)
-    fourth = lax.dynamic_index_in_dim(extra, picked(plane, (1, 0, 3, 2)), 0, False)
-    fifth = lax.dynamic_index_in_dim(extra, picked(plane, (2, 3, 0, 1)), 0, False)
-    return jnp.stack(first + [fourth, fifth])
+    return place_stage(done_a, done_b)
 
 
 def solution(mesh):

time: 116 us -> 115 us (level)
  starting transfers between devices: 53 us -> 38.5 us
  waiting for transfers between devices: 14.6 us -> 28.5 us
  Pallas kernels: 28.5 us -> 39.5 us
  local copies, waits for them, and re-layouts: 18.1 us -> 7.92 us
  other arithmetic: 1.17 us -> 0 us
    pallas_call x1 -> x2, Pallas kernels: 13.1 us -> 31.6 us  [the longest x1 25 us: place_stage(): pl.pallas_call(place_kernel, out_shape=jax.ShapeDtypeStruct((6, agents, f...]
    ppermute x30 -> x23, starting transfers between devices: 49.4 us -> 35.2 us  [exchange(): lax.ppermute(parts[k], axis, xor_pairs(size, k, targets))]
    unnamed x67 -> x36, local copies, waits for them, and re-layouts: 16.2 us -> 6.54 us
    ppermute x3, waiting for transfers between devices: 0.01 us -> 7.64 us  [local(): lax.ppermute(result_b[k], 'agent', [(j, j ^ k) for j in (1, 2)])]
    ppermute x30 -> x23, waiting for transfers between devices: 14.6 us -> 20.9 us  [exchange(): lax.ppermute(parts[k], axis, xor_pairs(size, k, targets))]
    pallas_call x2, Pallas kernels: 11.8 us -> 7.81 us  [agent_stage(): pl.pallas_call(functools.partial(agent_kernel, count, middle_only), out_s...]
    pallas_call x2, Pallas kernels: 3.6 us -> 0.11 us  [pack_stage(): pl.pallas_call(functools.partial(pack_kernel, size, choose), out_shape=[j...]
    another operation x2 -> x0, other arithmetic: 1.17 us -> none  [the longest x1 1.1 us: local(): extra = jnp.stack(done_b)]
  transfers between devices with their start and end apart: 33 -> 26, of which waited for: 5 -> 11; matrix products, arithmetic and copies ran while one was open for 1% -> 0% of each run, Pallas kernels for 13% -> 7%
where the time goes in v2:
time: 115 us
  Pallas kernels  39.5 us (34%)
  starting transfers between devices  38.5 us (33%)
  waiting for transfers between devices  28.5 us (25%)
  local copies, waits for them, and re-layouts  7.92 us (7%)
    ppermute x23, starting transfers between devices, exchange(): lax.ppermute(parts[k], axis, xor_pairs(size, k, targets))  35.2 us
    pallas_call x1, Pallas kernels, place_stage(): pl.pallas_call(place_kernel, out_shape=jax.ShapeDtypeStruct((6, agents, f...  25 us
    ppermute x23, waiting for transfers between devices, exchange(): lax.ppermute(parts[k], axis, xor_pairs(size, k, targets))  20.9 us
    pallas_call x2, Pallas kernels, agent_stage(): pl.pallas_call(functools.partial(agent_kernel, count, middle_only), out_s...  7.81 us
    ppermute x3, waiting for transfers between devices, local(): lax.ppermute(result_b[k], 'agent', [(j, j ^ k) for j in (1, 2)])  7.64 us
    pallas_call x1, Pallas kernels, time_stage(): pl.pallas_call(functools.partial(time_kernel, size), out_shape=[jax.Shape...  6.61 us
    unnamed x36, local copies, waits for them, and re-layouts  6.54 us
    ppermute x3, starting transfers between devices, local(): lax.ppermute(result_b[k], 'agent', [(j, j ^ k) for j in (1, 2)])  3.24 us
  transfers between devices with their start and end apart: 26, of which 11 were waited for; matrix products, arithmetic and copies ran while one was open for 0% of the time, Pallas kernels for 7%

profile of v2, /device:TPU:0, one launch (start us, length us, event | category | flops | bytes accessed | tf_op | source)
XLA Modules:
  0.0 114.9 jit_solution(15434706734367785783)
XLA Ops:
  0.0 1.4 %constant_dynamic-slice_fusion = (bf16[6,16,512]{2,1,0:T(8,128)(2,1)S(1)}, bf16[6,16,512]{2,1,0:T(8,128)(2,1)S(1)}, bf16[6,16,512]{2,1,0:T(8,128)(2,1)S(1)}, bf1...) fusion(bf16[6,128,512]{2,1,0:T(8,128)(2,1)} %param.12, ...), kind=kLoop, calls=%fused_computation | loop fusion | bytes 1572896 | tf_op jit(solution)/shard_map/dynamic_slice | solution.py:466
  1.4 3.4 %collective-permute-start.6 = (bf16[6,16,512]{2,1,0:T(8,128)(2,1)S(1)}, bf16[6,16,512]{2,1,0:T(8,128)(2,1)S(1)}, u32[]{:S(2)}, u32[]{:S(2)}) collective-permute-start(bf16[6,16,512]{2,1,0:T(8,128)(2,1)S(1)} %get-tuple-element.53), channel_id=1, source_target_pairs={{0,28},{4,24},{8,20},{12,16},{16,12},{20,8},{24,4},{28,0},{1,29},{... | collective-permute-start | bytes 294920 | tf_op jit(solution)/shard_map/ppermute | solution.py:409
  4.8 0.8 collective-permute-start.4
  5.6 1.5 %collective-permute-start.3 = (bf16[6,16,512]{2,1,0:T(8,128)(2,1)S(1)}, bf16[6,16,512]{2,1,0:T(8,128)(2,1)S(1)}, u32[]{:S(2)}, u32[]{:S(2)}) collective-permute-start(bf16[6,16,512]{2,1,0:T(8,128)(2,1)S(1)} %get-tuple-element.55), channel_id=1, source_target_pairs={{0,16},{4,20},{8,24},{12,28},{16,0},{20,4},{24,8},{28,12},{1,17},{... | collective-permute-start | bytes 294920 | tf_op jit(solution)/shard_map/ppermute | solution.py:409
  7.1 1.2 %collective-permute-start.1 = (bf16[6,16,512]{2,1,0:T(8,128)(2,1)S(1)}, bf16[6,16,512]{2,1,0:T(8,128)(2,1)S(1)}, u32[]{:S(2)}, u32[]{:S(2)}) collective-permute-start(bf16[6,16,512]{2,1,0:T(8,128)(2,1)S(1)} %get-tuple-element.57), channel_id=1, source_target_pairs={{0,8},{4,12},{8,0},{12,4},{16,24},{20,28},{24,16},{28,20},{1,9},{5... | collective-permute-start | bytes 294920 | tf_op jit(solution)/shard_map/ppermute | solution.py:409
  8.3 0.7 collective-permute-start
  9.0 1.1 %collective-permute-done.4.refs_5_ = bf16[6,16,512]{2,1,0:T(8,128)(2,1)S(1)} collective-permute-done((bf16[6,16,512]{2,1,0:T(8,128)(2,1)S(1)}, bf16[6,16,512]{2,1,0:T(8,128)(2,1)S(1)}, u32[]{:S(2)}, u32[]{:S(2)}) %collective-permute-start.4) | collective-permute-done | bytes 98336 | tf_op jit(solution)/shard_map/ppermute | solution.py:409
  10.1 2.5 %collective-permute-start.5 = (bf16[6,16,512]{2,1,0:T(8,128)(2,1)S(1)}, bf16[6,16,512]{2,1,0:T(8,128)(2,1)S(1)}, u32[]{:S(2)}, u32[]{:S(2)}) collective-permute-start(bf16[6,16,512]{2,1,0:T(8,128)(2,1)S(1)} %get-tuple-element.60), channel_id=1, source_target_pairs={{0,24},{4,28},{8,16},{12,20},{16,8},{20,12},{24,0},{28,4},{1,25},{... | collective-permute-start | bytes 294920 | tf_op jit(solution)/shard_map/ppermute | solution.py:409
  12.6 1.1 collective-permute-done.1.refs_2_
  13.8 2.7 %collective-permute-done.5.refs_6_ = bf16[6,16,512]{2,1,0:T(8,128)(2,1)S(1)} collective-permute-done((bf16[6,16,512]{2,1,0:T(8,128)(2,1)S(1)}, bf16[6,16,512]{2,1,0:T(8,128)(2,1)S(1)}, u32[]{:S(2)}, u32[]{:S(2)}) %collective-permute-start.5) | collective-permute-done | bytes 98336 | tf_op jit(solution)/shard_map/ppermute | solution.py:409
  16.5 1.0 copy-done.7
  17.5 1.0 copy-done.8
  18.5 1.0 copy-done.9
  19.6 1.0 copy-done.10
  20.6 6.6 %time_attention.1 = (bf16[6,16,512]{2,1,0:T(8,128)(2,1)S(1)}, bf16[6,16,512]{2,1,0:T(8,128)(2,1)S(1)}, bf16[6,16,512]{2,1,0:T(8,128)(2,1)S(1)}, bf16[6,16,512]{2...) custom-call(bf16[6,16,512]{2,1,0:T(8,128)(2,1)S(1)} %get-tuple-eleme, ...), custom_call_target="tpu_custom_call" | custom-call | tf_op jit(solution)/shard_map/time_attention/pallas_call | solution.py:230
  27.2 0.1 collective-permute-start.7
  27.3 1.9 %collective-permute-start.8 = (bf16[6,16,512]{2,1,0:T(8,128)(2,1)S(1)}, bf16[6,16,512]{2,1,0:T(8,128)(2,1)S(1)}, u32[]{:S(2)}, u32[]{:S(2)}) collective-permute-start(bf16[6,16,512]{2,1,0:T(8,128)(2,1)S(1)} %get-tuple-element.31), channel_id=1, source_target_pairs={{0,8},{4,12},{8,0},{12,4},{16,24},{20,28},{24,16},{28,20},{1,9},{5... | collective-permute-start | bytes 294920 | tf_op jit(solution)/shard_map/ppermute | solution.py:409
  29.3 0.1 collective-permute-start.9
  29.3 1.8 %collective-permute-start.10 = (bf16[6,16,512]{2,1,0:T(8,128)(2,1)S(1)}, bf16[6,16,512]{2,1,0:T(8,128)(2,1)S(1)}, u32[]{:S(2)}, u32[]{:S(2)}) collective-permute-start(bf16[6,16,512]{2,1,0:T(8,128)(2,1)S(1)} %get-tuple-element.33), channel_id=1, source_target_pairs={{0,16},{4,20},{8,24},{12,28},{16,0},{20,4},{24,8},{28,12},{1,17},{... | collective-permute-start | bytes 294920 | tf_op jit(solution)/shard_map/ppermute | solution.py:409
  31.1 1.7 %collective-permute-start.12 = (bf16[6,16,512]{2,1,0:T(8,128)(2,1)S(1)}, bf16[6,16,512]{2,1,0:T(8,128)(2,1)S(1)}, u32[]{:S(2)}, u32[]{:S(2)}) collective-permute-start(bf16[6,16,512]{2,1,0:T(8,128)(2,1)S(1)} %get-tuple-element.35), channel_id=1, source_target_pairs={{0,24},{4,28},{8,16},{12,20},{16,8},{20,12},{24,0},{28,4},{1,25},{... | collective-permute-start | bytes 294920 | tf_op jit(solution)/shard_map/ppermute | solution.py:409
  32.8 0.2 collective-permute-done.8.refs_2_
  33.0 0.7 collective-permute-start.13
  33.7 0.8 collective-permute-done.9.refs_3_
  34.5 0.2 collective-permute-done.10.refs_4_
  34.6 5.8 %collective-permute-done.11.refs_5_ = bf16[6,16,512]{2,1,0:T(8,128)(2,1)S(1)} collective-permute-done((bf16[6,16,512]{2,1,0:T(8,128)(2,1)S(1)}, bf16[6,16,512]{2,1,0:T(8,128)(2,1)S(1)}, u32[]{:S(2)}, u32[]{:S(2)}) %collective-permute-start.11) | collective-permute-done | bytes 98336 | tf_op jit(solution)/shard_map/ppermute | solution.py:409
  40.4 0.1 pack_steps.2
  40.5 1.6 %collective-permute-start.14 = (bf16[128,512]{1,0:T(8,128)(2,1)S(1)}, bf16[128,512]{1,0:T(8,128)(2,1)S(1)}, u32[]{:S(2)}, u32[]{:S(2)}) collective-permute-start(bf16[128,512]{1,0:T(8,128)(2,1)S(1)} %get-tuple-element.38), channel_id=1, source_target_pairs={{0,1},{1,0},{2,3},{3,2},{4,5},{5,4},{6,7},{7,6},{8,9},{9,8},{10,11... | collective-permute-start | bytes 393224 | tf_op jit(solution)/shard_map/ppermute | solution.py:409
  42.1 2.6 %collective-permute-start.15 = (bf16[128,512]{1,0:T(8,128)(2,1)S(1)}, bf16[128,512]{1,0:T(8,128)(2,1)S(1)}, u32[]{:S(2)}, u32[]{:S(2)}) collective-permute-start(bf16[128,512]{1,0:T(8,128)(2,1)S(1)} %get-tuple-element.39), channel_id=1, source_target_pairs={{0,2},{1,3},{2,0},{3,1},{4,6},{5,7},{6,4},{7,5},{8,10},{9,11},{10,... | collective-permute-start | bytes 393224 | tf_op jit(solution)/shard_map/ppermute | solution.py:409
  44.7 0.2 collective-permute-start.16
  45.0 2.6 %collective-permute-start.20 = (bf16[128,512]{1,0:T(8,128)(2,1)S(1)}, bf16[128,512]{1,0:T(8,128)(2,1)S(1)}, u32[]{:S(2)}, u32[]{:S(2)}) collective-permute-start(bf16[128,512]{1,0:T(8,128)(2,1)S(1)} %get-tuple-element.46), channel_id=1, source_target_pairs={{0,1},{3,2},{4,5},{7,6},{8,9},{11,10},{12,13},{15,14},{16,17},{19,... | collective-permute-start | bytes 393224 | tf_op jit(solution)/shard_map/ppermute | solution.py:409
  47.6 2.3 %collective-permute-start.21 = (bf16[128,512]{1,0:T(8,128)(2,1)S(1)}, bf16[128,512]{1,0:T(8,128)(2,1)S(1)}, u32[]{:S(2)}, u32[]{:S(2)}) collective-permute-start(bf16[128,512]{1,0:T(8,128)(2,1)S(1)} %get-tuple-element.47), channel_id=1, source_target_pairs={{0,2},{3,1},{4,6},{7,5},{8,10},{11,9},{12,14},{15,13},{16,18},{19,... | collective-permute-start | bytes 393224 | tf_op jit(solution)/shard_map/ppermute | solution.py:409
  49.9 0.8 collective-permute-start.22
  50.7 4.3 %collective-permute-done.15.refs_2_ = bf16[128,512]{1,0:T(8,128)(2,1)S(1)} collective-permute-done((bf16[128,512]{1,0:T(8,128)(2,1)S(1)}, bf16[128,512]{1,0:T(8,128)(2,1)S(1)}, u32[]{:S(2)}, u32[]{:S(2)}) %collective-permute-start.15) | collective-permute-done | bytes 131104 | tf_op jit(solution)/shard_map/ppermute | solution.py:409
  55.1 1.0 copy-done.5
  56.1 7.8 %agent_step.2 = (bf16[128,512]{1,0:T(8,128)(2,1)S(1)}, bf16[128,512]{1,0:T(8,128)(2,1)S(1)}, bf16[128,512]{1,0:T(8,128)(2,1)S(1)}, bf16[128,512]{1,0:T(8,128)(2,1)S(1)}) custom-call(bf16[128,512]{1,0:T(8,128)(2,1)S(1)} %get-tuple-element.37.refs_0_.refs_8_, bf16[128,512]{1,0:T(8,128)(2,1)S(1)} %collective-permute-done.14.refs_1_, ...), custom_call_target="tpu_custom_call" | custom-call | tf_op jit(solution)/shard_map/agent_step/pallas_call | solution.py:336
  63.9 6.2 %collective-permute-start.17 = (bf16[128,512]{1,0:T(8,128)(2,1)S(1)}, bf16[128,512]{1,0:T(8,128)(2,1)S(1)}, u32[]{:S(2)}, u32[]{:S(2)}) collective-permute-start(bf16[128,512]{1,0:T(8,128)(2,1)S(1)} %get-tuple-element.42), channel_id=1, source_target_pairs={{0,1},{1,0},{2,3},{3,2},{4,5},{5,4},{6,7},{7,6},{8,9},{9,8},{10,11... | collective-permute-start | bytes 393224 | tf_op jit(solution)/shard_map/ppermute | solution.py:409
  70.1 1.1 collective-permute-start.18
  71.2 1.4 %collective-permute-start.19 = (bf16[128,512]{1,0:T(8,128)(2,1)S(1)}, bf16[128,512]{1,0:T(8,128)(2,1)S(1)}, u32[]{:S(2)}, u32[]{:S(2)}) collective-permute-start(bf16[128,512]{1,0:T(8,128)(2,1)S(1)} %get-tuple-element.44), channel_id=1, source_target_pairs={{0,3},{1,2},{2,1},{3,0},{4,7},{5,6},{6,5},{7,4},{8,11},{9,10},{10,... | collective-permute-start | bytes 393224 | tf_op jit(solution)/shard_map/ppermute | solution.py:409
  72.6 0.1 agent_step.3
  72.7 0.6 copy-done.11
  73.3 1.3 %collective-permute-start.23 = (bf16[128,512]{1,0:T(8,128)(2,1)S(1)}, bf16[128,512]{1,0:T(8,128)(2,1)S(1)}, u32[]{:S(2)}, u32[]{:S(2)}) collective-permute-start(bf16[128,512]{1,0:T(8,128)(2,1)S(1)} %get-tuple-element.50), channel_id=1, source_target_pairs={{1,0},{2,3},{5,4},{6,7},{9,8},{10,11},{13,12},{14,15},{17,16},{18,... | collective-permute-start | bytes 393224 | tf_op jit(solution)/shard_map/ppermute | solution.py:479
  74.6 1.3 %collective-permute-start.24 = (bf16[128,512]{1,0:T(8,128)(2,1)S(1)}, bf16[128,512]{1,0:T(8,128)(2,1)S(1)}, u32[]{:S(2)}, u32[]{:S(2)}) collective-permute-start(bf16[128,512]{1,0:T(8,128)(2,1)S(1)} %get-tuple-element.51), channel_id=1, source_target_pairs={{1,3},{2,0},{5,7},{6,4},{9,11},{10,8},{13,15},{14,12},{17,19},{18,... | collective-permute-start | bytes 393224 | tf_op jit(solution)/shard_map/ppermute | solution.py:479
  76.0 0.7 collective-permute-start.25
  76.6 4.7 %collective-permute-done.18.refs_2_ = bf16[128,512]{1,0:T(8,128)(2,1)S(1)} collective-permute-done((bf16[128,512]{1,0:T(8,128)(2,1)S(1)}, bf16[128,512]{1,0:T(8,128)(2,1)S(1)}, u32[]{:S(2)}, u32[]{:S(2)}) %collective-permute-start.18) | collective-permute-done | bytes 131104 | tf_op jit(solution)/shard_map/ppermute | solution.py:409
  81.4 5.5 %collective-permute-done.23.refs_5_ = bf16[128,512]{1,0:T(8,128)(2,1)S(1)} collective-permute-done((bf16[128,512]{1,0:T(8,128)(2,1)S(1)}, bf16[128,512]{1,0:T(8,128)(2,1)S(1)}, u32[]{:S(2)}, u32[]{:S(2)}) %collective-permute-start.23) | collective-permute-done | bytes 131104 | tf_op jit(solution)/shard_map/ppermute | solution.py:479
  86.8 2.2 %collective-permute-done.24.refs_6_ = bf16[128,512]{1,0:T(8,128)(2,1)S(1)} collective-permute-done((bf16[128,512]{1,0:T(8,128)(2,1)S(1)}, bf16[128,512]{1,0:T(8,128)(2,1)S(1)}, u32[]{:S(2)}, u32[]{:S(2)}) %collective-permute-start.24) | collective-permute-done | bytes 131104 | tf_op jit(solution)/shard_map/ppermute | solution.py:479
  89.0 0.6 copy-done.16
  89.7 25.0 %place_steps.1 = bf16[6,128,512]{2,1,0:T(8,128)(2,1)} custom-call(bf16[128,512]{1,0:T(8,128)(2,1)} %copy-done.6, bf16[128,512]{1,0:T(8,128)(2,1)} %copy-done.12, bf16[128,512]{1,0:T(8,128)(2,1)} %copy-done.13, bf16[128,512]{1,0:T(8,128)(2,1)} %copy-done.14, bf16[128,512]{1,0:T(8,128)(2,1)} %copy-done.11, bf16[128,512]{1,0:T(8,128)(2,1)} %copy-done.15, ...), custom_call_target="tpu_custom_call" | custom-call | tf_op jit(solution)/shard_map/place_steps/pallas_call | solution.py:392
  (47 shorter events, 0.2 us)
Async XLA Ops:
  0.0 55.0 %copy-start.2 = (bf16[512,512]{1,0:T(8,128)(2,1)S(1)}, bf16[512,512]{1,0:T(8,128)(2,1)}, u32[]{:S(2)}) copy-start(bf16[512,512]{1,0:T(8,128)(2,1)} %refs_4_.3) | copy-start | bytes 1572868
  0.0 55.0 %copy-start.3 = (bf16[512,512]{1,0:T(8,128)(2,1)S(1)}, bf16[512,512]{1,0:T(8,128)(2,1)}, u32[]{:S(2)}) copy-start(bf16[512,512]{1,0:T(8,128)(2,1)} %refs_5_.3) | copy-start | bytes 1572868
  0.0 55.0 %copy-start.4 = (bf16[512,512]{1,0:T(8,128)(2,1)S(1)}, bf16[512,512]{1,0:T(8,128)(2,1)}, u32[]{:S(2)}) copy-start(bf16[512,512]{1,0:T(8,128)(2,1)} %refs_6_.3) | copy-start | bytes 1572868
  1.4 6.9 %collective-permute-start.6 = (bf16[6,16,512]{2,1,0:T(8,128)(2,1)S(1)}, bf16[6,16,512]{2,1,0:T(8,128)(2,1)S(1)}, u32[]{:S(2)}, u32[]{:S(2)}) collective-permute-start(bf16[6,16,512]{2,1,0:T(8,128)(2,1)S(1)} %get-tuple-element.53), channel_id=1, source_target_pairs={{0,28},{4,24},{8,20},{12,16},{16,12},{20,8},{24,4},{28,0},{1,29},{... | collective-permute-start | bytes 294920 | tf_op jit(solution)/shard_map/ppermute | solution.py:409
  4.8 5.3 %collective-permute-start.4 = (bf16[6,16,512]{2,1,0:T(8,128)(2,1)S(1)}, bf16[6,16,512]{2,1,0:T(8,128)(2,1)S(1)}, u32[]{:S(2)}, u32[]{:S(2)}) collective-permute-start(bf16[6,16,512]{2,1,0:T(8,128)(2,1)S(1)} %get-tuple-element.54), channel_id=1, source_target_pairs={{0,20},{4,16},{8,28},{12,24},{16,4},{20,0},{24,12},{28,8},{1,21},{... | collective-permute-start | bytes 294920 | tf_op jit(solution)/shard_map/ppermute | solution.py:409
  5.6 7.0 %collective-permute-start.3 = (bf16[6,16,512]{2,1,0:T(8,128)(2,1)S(1)}, bf16[6,16,512]{2,1,0:T(8,128)(2,1)S(1)}, u32[]{:S(2)}, u32[]{:S(2)}) collective-permute-start(bf16[6,16,512]{2,1,0:T(8,128)(2,1)S(1)} %get-tuple-element.55), channel_id=1, source_target_pairs={{0,16},{4,20},{8,24},{12,28},{16,0},{20,4},{24,8},{28,12},{1,17},{... | collective-permute-start | bytes 294920 | tf_op jit(solution)/shard_map/ppermute | solution.py:409
  7.1 5.5 %collective-permute-start.2 = (bf16[6,16,512]{2,1,0:T(8,128)(2,1)S(1)}, bf16[6,16,512]{2,1,0:T(8,128)(2,1)S(1)}, u32[]{:S(2)}, u32[]{:S(2)}) collective-permute-start(bf16[6,16,512]{2,1,0:T(8,128)(2,1)S(1)} %get-tuple-element.56), channel_id=1, source_target_pairs={{0,12},{4,8},{8,4},{12,0},{16,28},{20,24},{24,20},{28,16},{1,13},{... | collective-permute-start | bytes 294920 | tf_op jit(solution)/shard_map/ppermute | solution.py:409
  7.1 6.7 %collective-permute-start.1 = (bf16[6,16,512]{2,1,0:T(8,128)(2,1)S(1)}, bf16[6,16,512]{2,1,0:T(8,128)(2,1)S(1)}, u32[]{:S(2)}, u32[]{:S(2)}) collective-permute-start(bf16[6,16,512]{2,1,0:T(8,128)(2,1)S(1)} %get-tuple-element.57), channel_id=1, source_target_pairs={{0,8},{4,12},{8,0},{12,4},{16,24},{20,28},{24,16},{28,20},{1,9},{5... | collective-permute-start | bytes 294920 | tf_op jit(solution)/shard_map/ppermute | solution.py:409
  8.3 5.5 %collective-permute-start = (bf16[6,16,512]{2,1,0:T(8,128)(2,1)S(1)}, bf16[6,16,512]{2,1,0:T(8,128)(2,1)S(1)}, u32[]{:S(2)}, u32[]{:S(2)}) collective-permute-start(bf16[6,16,512]{2,1,0:T(8,128)(2,1)S(1)} %get-tuple-element.58), channel_id=1, source_target_pairs={{0,4},{4,0},{8,12},{12,8},{16,20},{20,16},{24,28},{28,24},{1,5},{5... | collective-permute-start | bytes 294920 | tf_op jit(solution)/shard_map/ppermute | solution.py:409
  10.1 6.3 %collective-permute-start.5 = (bf16[6,16,512]{2,1,0:T(8,128)(2,1)S(1)}, bf16[6,16,512]{2,1,0:T(8,128)(2,1)S(1)}, u32[]{:S(2)}, u32[]{:S(2)}) collective-permute-start(bf16[6,16,512]{2,1,0:T(8,128)(2,1)S(1)} %get-tuple-element.60), channel_id=1, source_target_pairs={{0,24},{4,28},{8,16},{12,20},{16,8},{20,12},{24,0},{28,4},{1,25},{... | collective-permute-start | bytes 294920 | tf_op jit(solution)/shard_map/ppermute | solution.py:409
  16.5 1.0 copy-start.7
  17.5 1.0 copy-start.8
  18.5 1.0 copy-start.9
  19.6 1.0 copy-start.10
  20.6 34.4 %copy-start = (bf16[512,2048]{1,0:T(8,128)(2,1)S(1)}, bf16[512,2048]{1,0:T(8,128)(2,1)}, u32[]{:S(2)}) copy-start(bf16[512,2048]{1,0:T(8,128)(2,1)} %refs_8_.5) | copy-start | bytes 6291460
  20.6 34.4 %copy-start.1 = (bf16[2048,512]{1,0:T(8,128)(2,1)S(1)}, bf16[2048,512]{1,0:T(8,128)(2,1)}, u32[]{:S(2)}) copy-start(bf16[2048,512]{1,0:T(8,128)(2,1)} %refs_9_.5) | copy-start | bytes 6291460
  27.2 3.8 %collective-permute-start.7 = (bf16[6,16,512]{2,1,0:T(8,128)(2,1)S(1)}, bf16[6,16,512]{2,1,0:T(8,128)(2,1)S(1)}, u32[]{:S(2)}, u32[]{:S(2)}) collective-permute-start(bf16[6,16,512]{2,1,0:T(8,128)(2,1)S(1)} %get-tuple-element.30), channel_id=1, source_target_pairs={{0,4},{4,0},{8,12},{12,8},{16,20},{20,16},{24,28},{28,24},{1,5},{5... | collective-permute-start | bytes 294920 | tf_op jit(solution)/shard_map/ppermute | solution.py:409
  27.3 5.6 %collective-permute-start.8 = (bf16[6,16,512]{2,1,0:T(8,128)(2,1)S(1)}, bf16[6,16,512]{2,1,0:T(8,128)(2,1)S(1)}, u32[]{:S(2)}, u32[]{:S(2)}) collective-permute-start(bf16[6,16,512]{2,1,0:T(8,128)(2,1)S(1)} %get-tuple-element.31), channel_id=1, source_target_pairs={{0,8},{4,12},{8,0},{12,4},{16,24},{20,28},{24,16},{28,20},{1,9},{5... | collective-permute-start | bytes 294920 | tf_op jit(solution)/shard_map/ppermute | solution.py:409
  29.3 5.2 %collective-permute-start.9 = (bf16[6,16,512]{2,1,0:T(8,128)(2,1)S(1)}, bf16[6,16,512]{2,1,0:T(8,128)(2,1)S(1)}, u32[]{:S(2)}, u32[]{:S(2)}) collective-permute-start(bf16[6,16,512]{2,1,0:T(8,128)(2,1)S(1)} %get-tuple-element.32), channel_id=1, source_target_pairs={{0,12},{4,8},{8,4},{12,0},{16,28},{20,24},{24,20},{28,16},{1,13},{... | collective-permute-start | bytes 294920 | tf_op jit(solution)/shard_map/ppermute | solution.py:409
  29.3 5.3 %collective-permute-start.10 = (bf16[6,16,512]{2,1,0:T(8,128)(2,1)S(1)}, bf16[6,16,512]{2,1,0:T(8,128)(2,1)S(1)}, u32[]{:S(2)}, u32[]{:S(2)}) collective-permute-start(bf16[6,16,512]{2,1,0:T(8,128)(2,1)S(1)} %get-tuple-element.33), channel_id=1, source_target_pairs={{0,16},{4,20},{8,24},{12,28},{16,0},{20,4},{24,8},{28,12},{1,17},{... | collective-permute-start | bytes 294920 | tf_op jit(solution)/shard_map/ppermute | solution.py:409
  31.1 9.3 %collective-permute-start.11 = (bf16[6,16,512]{2,1,0:T(8,128)(2,1)S(1)}, bf16[6,16,512]{2,1,0:T(8,128)(2,1)S(1)}, u32[]{:S(2)}, u32[]{:S(2)}) collective-permute-start(bf16[6,16,512]{2,1,0:T(8,128)(2,1)S(1)} %get-tuple-element.34), channel_id=1, source_target_pairs={{0,20},{4,16},{8,28},{12,24},{16,4},{20,0},{24,12},{28,8},{1,21},{... | collective-permute-start | bytes 294920 | tf_op jit(solution)/shard_map/ppermute | solution.py:409
  31.1 9.3 %collective-permute-start.12 = (bf16[6,16,512]{2,1,0:T(8,128)(2,1)S(1)}, bf16[6,16,512]{2,1,0:T(8,128)(2,1)S(1)}, u32[]{:S(2)}, u32[]{:S(2)}) collective-permute-start(bf16[6,16,512]{2,1,0:T(8,128)(2,1)S(1)} %get-tuple-element.35), channel_id=1, source_target_pairs={{0,24},{4,28},{8,16},{12,20},{16,8},{20,12},{24,0},{28,4},{1,25},{... | collective-permute-start | bytes 294920 | tf_op jit(solution)/shard_map/ppermute | solution.py:409
  33.0 7.4 %collective-permute-start.13 = (bf16[6,16,512]{2,1,0:T(8,128)(2,1)S(1)}, bf16[6,16,512]{2,1,0:T(8,128)(2,1)S(1)}, u32[]{:S(2)}, u32[]{:S(2)}) collective-permute-start(bf16[6,16,512]{2,1,0:T(8,128)(2,1)S(1)} %get-tuple-element.36), channel_id=1, source_target_pairs={{0,28},{4,24},{8,20},{12,16},{16,12},{20,8},{24,4},{28,0},{1,29},{... | collective-permute-start | bytes 294920 | tf_op jit(solution)/shard_map/ppermute | solution.py:409
  40.5 9.4 %collective-permute-start.14 = (bf16[128,512]{1,0:T(8,128)(2,1)S(1)}, bf16[128,512]{1,0:T(8,128)(2,1)S(1)}, u32[]{:S(2)}, u32[]{:S(2)}) collective-permute-start(bf16[128,512]{1,0:T(8,128)(2,1)S(1)} %get-tuple-element.38), channel_id=1, source_target_pairs={{0,1},{1,0},{2,3},{3,2},{4,5},{5,4},{6,7},{7,6},{8,9},{9,8},{10,11... | collective-permute-start | bytes 393224 | tf_op jit(solution)/shard_map/ppermute | solution.py:409
  42.1 12.9 %collective-permute-start.15 = (bf16[128,512]{1,0:T(8,128)(2,1)S(1)}, bf16[128,512]{1,0:T(8,128)(2,1)S(1)}, u32[]{:S(2)}, u32[]{:S(2)}) collective-permute-start(bf16[128,512]{1,0:T(8,128)(2,1)S(1)} %get-tuple-element.39), channel_id=1, source_target_pairs={{0,2},{1,3},{2,0},{3,1},{4,6},{5,7},{6,4},{7,5},{8,10},{9,11},{10,... | collective-permute-start | bytes 393224 | tf_op jit(solution)/shard_map/ppermute | solution.py:409
  44.7 10.3 %collective-permute-start.16 = (bf16[128,512]{1,0:T(8,128)(2,1)S(1)}, bf16[128,512]{1,0:T(8,128)(2,1)S(1)}, u32[]{:S(2)}, u32[]{:S(2)}) collective-permute-start(bf16[128,512]{1,0:T(8,128)(2,1)S(1)} %get-tuple-element.40), channel_id=1, source_target_pairs={{0,3},{1,2},{2,1},{3,0},{4,7},{5,6},{6,5},{7,4},{8,11},{9,10},{10,... | collective-permute-start | bytes 393224 | tf_op jit(solution)/shard_map/ppermute | solution.py:409
  45.0 26.2 %collective-permute-start.20 = (bf16[128,512]{1,0:T(8,128)(2,1)S(1)}, bf16[128,512]{1,0:T(8,128)(2,1)S(1)}, u32[]{:S(2)}, u32[]{:S(2)}) collective-permute-start(bf16[128,512]{1,0:T(8,128)(2,1)S(1)} %get-tuple-element.46), channel_id=1, source_target_pairs={{0,1},{3,2},{4,5},{7,6},{8,9},{11,10},{12,13},{15,14},{16,17},{19,... | collective-permute-start | bytes 393224 | tf_op jit(solution)/shard_map/ppermute | solution.py:409
  47.6 25.0 %collective-permute-start.21 = (bf16[128,512]{1,0:T(8,128)(2,1)S(1)}, bf16[128,512]{1,0:T(8,128)(2,1)S(1)}, u32[]{:S(2)}, u32[]{:S(2)}) collective-permute-start(bf16[128,512]{1,0:T(8,128)(2,1)S(1)} %get-tuple-element.47), channel_id=1, source_target_pairs={{0,2},{3,1},{4,6},{7,5},{8,10},{11,9},{12,14},{15,13},{16,18},{19,... | collective-permute-start | bytes 393224 | tf_op jit(solution)/shard_map/ppermute | solution.py:409
  49.9 22.7 %collective-permute-start.22 = (bf16[128,512]{1,0:T(8,128)(2,1)S(1)}, bf16[128,512]{1,0:T(8,128)(2,1)S(1)}, u32[]{:S(2)}, u32[]{:S(2)}) collective-permute-start(bf16[128,512]{1,0:T(8,128)(2,1)S(1)} %get-tuple-element.48), channel_id=1, source_target_pairs={{1,2},{2,1},{5,6},{6,5},{9,10},{10,9},{13,14},{14,13},{17,18},{18,... | collective-permute-start | bytes 393224 | tf_op jit(solution)/shard_map/ppermute | solution.py:409
  55.1 1.0 copy-start.5
  63.9 8.8 %copy-start.6 = (bf16[128,512]{1,0:T(8,128)(2,1)}, bf16[128,512]{1,0:T(8,128)(2,1)S(1)}, u32[]{:S(2)}) copy-start(bf16[128,512]{1,0:T(8,128)(2,1)S(1)} %get-tuple-element.41.refs_10_.refs_0_) | copy-start | bytes 393220
  63.9 12.0 %collective-permute-start.17 = (bf16[128,512]{1,0:T(8,128)(2,1)S(1)}, bf16[128,512]{1,0:T(8,128)(2,1)S(1)}, u32[]{:S(2)}, u32[]{:S(2)}) collective-permute-start(bf16[128,512]{1,0:T(8,128)(2,1)S(1)} %get-tuple-element.42), channel_id=1, source_target_pairs={{0,1},{1,0},{2,3},{3,2},{4,5},{5,4},{6,7},{7,6},{8,9},{9,8},{10,11... | collective-permute-start | bytes 393224 | tf_op jit(solution)/shard_map/ppermute | solution.py:409
  70.1 11.2 %collective-permute-start.18 = (bf16[128,512]{1,0:T(8,128)(2,1)S(1)}, bf16[128,512]{1,0:T(8,128)(2,1)S(1)}, u32[]{:S(2)}, u32[]{:S(2)}) collective-permute-start(bf16[128,512]{1,0:T(8,128)(2,1)S(1)} %get-tuple-element.43), channel_id=1, source_target_pairs={{0,2},{1,3},{2,0},{3,1},{4,6},{5,7},{6,4},{7,5},{8,10},{9,11},{10,... | collective-permute-start | bytes 393224 | tf_op jit(solution)/shard_map/ppermute | solution.py:409
  71.2 10.1 %collective-permute-start.19 = (bf16[128,512]{1,0:T(8,128)(2,1)S(1)}, bf16[128,512]{1,0:T(8,128)(2,1)S(1)}, u32[]{:S(2)}, u32[]{:S(2)}) collective-permute-start(bf16[128,512]{1,0:T(8,128)(2,1)S(1)} %get-tuple-element.44), channel_id=1, source_target_pairs={{0,3},{1,2},{2,1},{3,0},{4,7},{5,6},{6,5},{7,4},{8,11},{9,10},{10,... | collective-permute-start | bytes 393224 | tf_op jit(solution)/shard_map/ppermute | solution.py:409
  72.7 0.7 copy-start.11
  73.3 13.5 %collective-permute-start.23 = (bf16[128,512]{1,0:T(8,128)(2,1)S(1)}, bf16[128,512]{1,0:T(8,128)(2,1)S(1)}, u32[]{:S(2)}, u32[]{:S(2)}) collective-permute-start(bf16[128,512]{1,0:T(8,128)(2,1)S(1)} %get-tuple-element.50), channel_id=1, source_target_pairs={{1,0},{2,3},{5,4},{6,7},{9,8},{10,11},{13,12},{14,15},{17,16},{18,... | collective-permute-start | bytes 393224 | tf_op jit(solution)/shard_map/ppermute | solution.py:479
  74.6 14.4 %collective-permute-start.24 = (bf16[128,512]{1,0:T(8,128)(2,1)S(1)}, bf16[128,512]{1,0:T(8,128)(2,1)S(1)}, u32[]{:S(2)}, u32[]{:S(2)}) collective-permute-start(bf16[128,512]{1,0:T(8,128)(2,1)S(1)} %get-tuple-element.51), channel_id=1, source_target_pairs={{1,3},{2,0},{5,7},{6,4},{9,11},{10,8},{13,15},{14,12},{17,19},{18,... | collective-permute-start | bytes 393224 | tf_op jit(solution)/shard_map/ppermute | solution.py:479
  75.9 13.1 %copy-start.12 = (bf16[128,512]{1,0:T(8,128)(2,1)}, bf16[128,512]{1,0:T(8,128)(2,1)S(1)}, u32[]{:S(2)}) copy-start(bf16[128,512]{1,0:T(8,128)(2,1)S(1)} %collective-permute-done.17.refs_1_) | copy-start | bytes 393220
  76.0 13.1 %collective-permute-start.25 = (bf16[128,512]{1,0:T(8,128)(2,1)S(1)}, bf16[128,512]{1,0:T(8,128)(2,1)S(1)}, u32[]{:S(2)}, u32[]{:S(2)}) collective-permute-start(bf16[128,512]{1,0:T(8,128)(2,1)S(1)} %get-tuple-element.52), channel_id=1, source_target_pairs={{1,2},{2,1},{5,6},{6,5},{9,10},{10,9},{13,14},{14,13},{17,18},{18,... | collective-permute-start | bytes 393224 | tf_op jit(solution)/shard_map/ppermute | solution.py:479
  81.4 7.7 %copy-start.13 = (bf16[128,512]{1,0:T(8,128)(2,1)}, bf16[128,512]{1,0:T(8,128)(2,1)S(1)}, u32[]{:S(2)}) copy-start(bf16[128,512]{1,0:T(8,128)(2,1)S(1)} %collective-permute-done.18.refs_2_) | copy-start | bytes 393220
  81.4 7.7 %copy-start.14 = (bf16[128,512]{1,0:T(8,128)(2,1)}, bf16[128,512]{1,0:T(8,128)(2,1)S(1)}, u32[]{:S(2)}) copy-start(bf16[128,512]{1,0:T(8,128)(2,1)S(1)} %collective-permute-done.19.refs_3_) | copy-start | bytes 393220
  86.8 2.2 %copy-start.15 = (bf16[128,512]{1,0:T(8,128)(2,1)}, bf16[128,512]{1,0:T(8,128)(2,1)S(1)}, u32[]{:S(2)}) copy-start(bf16[128,512]{1,0:T(8,128)(2,1)S(1)} %collective-permute-done.23.refs_5_) | copy-start | bytes 393220
  89.0 0.7 copy-start.16
  89.0 0.7 copy-start.17

commit v3 on v2

--- a/solution.py
+++ b/solution.py
@@ -112,6 +112,10 @@
     inside = x * (math.sqrt(2 / math.pi) + (math.sqrt(2 / math.pi) * 0.044715) * (x * x))
     half = 0.5 * x
     return half + half * jnp.tanh(inside)
+
+
+def in_hbm(weights):
+    return [pltpu.with_memory_space_constraint(w, HBM) for w in weights]
 
 
 def fetch(sources, targets, sems):
@@ -178,10 +182,11 @@
         at = pl.ds(agent, total_steps, stride=agents)
         own = jnp.concatenate([wide[c, at, :] for c in range(len(lanes_of))], axis=1)
         normed[pl.ds(agent * total_steps, total_steps), :] = norm_of(own)
-    for copy in copies[:3]:
-        copy.wait()
+    copies[0].wait()
     query[...] = project(normed[...], w_query[...])
+    copies[1].wait()
     split_heads(project(normed[...], w_key[...]), key_e, key_o)
+    copies[2].wait()
     split_heads(project(normed[...], w_value[...]), value_e, value_o, True)
 
     group = 2 * total_steps
@@ -240,7 +245,7 @@
         + [pltpu.SemaphoreType.DMA((4,))],
         compiler_params=pltpu.CompilerParams(vmem_limit_bytes=24 * 2**20),
         name="time_attention",
-    )(*pieces, *weights)
+    )(*pieces, *in_hbm(weights))
 
 
 def pack_kernel(size, choose, *refs):
@@ -268,16 +273,14 @@
 
 
 def agent_body(count, blocks, weights, outs, scratch):
-    normed, query, key_e, key_o, value_e, value_o, mixed, after, inner = scratch[:9]
-    w_query, w_key, w_value, w_out, w_in, w_mlp_out, sems = scratch[9:]
-    copies = fetch(weights, (w_query, w_key, w_value, w_out, w_in, w_mlp_out), sems)
+    normed, query, key_e, key_o, value_e, value_o, mixed, after, inner, w_out, sems = scratch
+    w_query, w_key, w_value, far_out, w_in, w_mlp_out = weights
+    copies = fetch((far_out,), (w_out,), sems)
     agents, features = blocks[0].shape
     head_size = features // HEADS
     factor = math.log2(math.e) * head_size**-0.5
     for b in range(count):
         normed[pl.ds(b * agents, agents), :] = norm_of(blocks[b][...].astype(jnp.float32))
-    for copy in copies[:3]:
-        copy.wait()
     query[...] = project(normed[...], w_query[...])
     split_heads(project(normed[...], w_key[...]), key_e, key_o)
     split_heads(project(normed[...], w_value[...]), value_e, value_o, True)
@@ -291,8 +294,7 @@
             (value_e[:, double], value_o[:, double]),
             factor,
         )
-    for copy in copies[3:]:
-        copy.wait()
+    copies[0].wait()
     added = jnp.dot(mixed[...], w_out[...], preferred_element_type=jnp.float32)
     for b in range(count):
         at = pl.ds(b * agents, agents)
@@ -315,7 +317,7 @@
 
 def agent_kernel(count, middle_only, *refs):
     blocks, weights = refs[:count], refs[count : count + 6]
-    outs, scratch = refs[-16 - count : -16], refs[-16:]
+    outs, scratch = refs[-11 - count : -11], refs[-11:]
 
     def run():
         agent_body(count, blocks, weights, outs, scratch)
@@ -336,17 +338,19 @@
     return pl.pallas_call(
         functools.partial(agent_kernel, count, middle_only),
         out_shape=[jax.ShapeDtypeStruct((agents, features), kind)] * count,
-        in_specs=[spec(VMEM)] * count + [spec(HBM)] * 6 + [spec(pl.ANY)] * len(after),
+        in_specs=[spec(VMEM)] * (count + 3)
+        + [spec(HBM)]
+        + [spec(VMEM)] * 2
+        + [spec(pl.ANY)] * len(after),
         out_specs=[spec(VMEM)] * count,
         scratch_shapes=[VMEM((rows, features), kind)] * 4
         + [VMEM((rows, 2 * features), kind)] * 2
         + [VMEM((rows, features), kind)] * 2
         + [VMEM((rows, hidden), kind)]
-        + [VMEM(w.shape, kind) for w in weights]
-        + [pltpu.SemaphoreType.DMA((6,))],
-        compiler_params=pltpu.CompilerParams(vmem_limit_bytes=28 * 2**20),
+        + [VMEM(weights[3].shape, kind), pltpu.SemaphoreType.DMA((1,))],
+        compiler_params=pltpu.CompilerParams(vmem_limit_bytes=20 * 2**20),
         name="agent_step",
-    )(*blocks, *weights, *after)
+    )(*blocks, *weights[:3], *in_hbm(weights[3:4]), *weights[4:], *after)
 
 
 def place_kernel(*refs):
@@ -392,8 +396,8 @@
     return pl.pallas_call(
         place_kernel,
         out_shape=jax.ShapeDtypeStruct((6, agents, features), jnp.bfloat16),
-        in_specs=[spec(pl.ANY)] * 8,
-        out_specs=spec(pl.ANY),
+        in_specs=[spec(VMEM)] * 8,
+        out_specs=spec(HBM),
         scratch_shapes=[pltpu.SemaphoreType.DMA((6,))],
         name="place_steps",
     )(*whole, *extra)
@@ -408,6 +412,10 @@
     return [parts[0]] + [
         lax.ppermute(parts[k], axis, xor_pairs(size, k, targets)) for k in range(1, size)
     ]
+
+
+def together(parts):
+    return lax.optimization_barrier(tuple(parts))
 
 
 def picked(plane, values):
@@ -466,12 +474,10 @@
         lax.dynamic_slice_in_dim(states, jnp.bitwise_xor(me, k) * share, share, 1)
         for k in range(size)
     ]
-    pieces = exchange(parts, "tm")
-    pieces = exchange(time_stage(pieces, time_weights), "tm")
-    packed_a = pack_stage(pieces, whole_steps)
-    packed_b = pack_stage(pieces, extra_steps, packed_a[:1])
-    blocks_a = exchange(packed_a, "agent")
-    blocks_b = exchange(packed_b, "agent", (1, 2))
+    pieces = together(exchange(parts, "tm"))
+    pieces = together(exchange(time_stage(pieces, time_weights), "tm"))
+    blocks_a = exchange(pack_stage(pieces, whole_steps), "agent")
+    blocks_b = exchange(pack_stage(pieces, extra_steps, blocks_a[2:3]), "agent", (1, 2))
     result_a = agent_stage(blocks_a, agent_weights, False)
     done_a = exchange(result_a, "agent")
     result_b = agent_stage(blocks_b, agent_weights, True, result_a[:1])

time: 115 us -> 83.8 us (0.73)
  Pallas kernels: 39.5 us -> 16.7 us
  local copies, waits for them, and re-layouts: 7.92 us -> 2.72 us
  starting transfers between devices: 38.5 us -> 33.7 us
  waiting for transfers between devices: 28.5 us -> 29.9 us
    pallas_call x1, Pallas kernels: 25 us -> 2.21 us  [place_stage(): pl.pallas_call(place_kernel, out_shape=jax.ShapeDtypeStruct((6, agents, f...]
    unnamed x36 -> x26, local copies, waits for them, and re-layouts: 6.54 us -> 1.34 us
    ppermute x23, starting transfers between devices: 35.2 us -> 30.5 us  [exchange(): lax.ppermute(parts[k], axis, xor_pairs(size, k, targets))]
    ppermute x23, waiting for transfers between devices: 20.9 us -> 22.6 us  [exchange(): lax.ppermute(parts[k], axis, xor_pairs(size, k, targets))]
  transfers between devices with their start and end apart: 26 -> 26, of which waited for: 11 -> 11; matrix products, arithmetic and copies ran while one was open for 0% -> 0% of each run, Pallas kernels for 7% -> 9%
where the time goes in v3:
time: 83.8 us; the launch traced here: 83.5 us
  starting transfers between devices  33.7 us (40%)
  waiting for transfers between devices  29.9 us (36%)
  Pallas kernels  16.7 us (20%)
  local copies, waits for them, and re-layouts  2.72 us (3%)
    ppermute x23, starting transfers between devices, exchange(): lax.ppermute(parts[k], axis, xor_pairs(size, k, targets))  30.5 us
    ppermute x23, waiting for transfers between devices, exchange(): lax.ppermute(parts[k], axis, xor_pairs(size, k, targets))  22.6 us
    ppermute x3, waiting for transfers between devices, local(): lax.ppermute(result_b[k], 'agent', [(j, j ^ k) for j in (1, 2)])  7.34 us
    pallas_call x2, Pallas kernels, agent_stage(): pl.pallas_call(functools.partial(agent_kernel, count, middle_only), out_s...  7.19 us
    pallas_call x1, Pallas kernels, time_stage(): pl.pallas_call(functools.partial(time_kernel, size), out_shape=[jax.Shape...  7.17 us
    ppermute x3, starting transfers between devices, local(): lax.ppermute(result_b[k], 'agent', [(j, j ^ k) for j in (1, 2)])  3.24 us
    pallas_call x1, Pallas kernels, place_stage(): pl.pallas_call(place_kernel, out_shape=jax.ShapeDtypeStruct((6, agents, f...  2.21 us
  transfers between devices with their start and end apart: 26, of which 11 were waited for; matrix products, arithmetic and copies ran while one was open for 0% of the time, Pallas kernels for 9%

profile of v3, /device:TPU:0, one launch (start us, length us, event | category | flops | bytes accessed | tf_op | source)
XLA Modules:
  0.0 83.5 jit_solution(10620086830989996223)
XLA Ops:
  0.0 1.4 %constant_dynamic-slice_fusion = (bf16[6,16,512]{2,1,0:T(8,128)(2,1)S(1)}, bf16[6,16,512]{2,1,0:T(8,128)(2,1)S(1)}, bf16[6,16,512]{2,1,0:T(8,128)(2,1)S(1)}, bf1...) fusion(bf16[6,128,512]{2,1,0:T(8,128)(2,1)} %param.12, ...), kind=kLoop, calls=%fused_computation | loop fusion | bytes 1572896 | tf_op jit(solution)/shard_map/dynamic_slice | solution.py:474
  1.4 3.4 %collective-permute-start.6 = (bf16[6,16,512]{2,1,0:T(8,128)(2,1)S(1)}, bf16[6,16,512]{2,1,0:T(8,128)(2,1)S(1)}, u32[]{:S(2)}, u32[]{:S(2)}) collective-permute-start(bf16[6,16,512]{2,1,0:T(8,128)(2,1)S(1)} %get-tuple-element.85), channel_id=1, source_target_pairs={{0,28},{4,24},{8,20},{12,16},{16,12},{20,8},{24,4},{28,0},{1,29},{... | collective-permute-start | bytes 294920 | tf_op jit(solution)/shard_map/ppermute | solution.py:413
  4.8 0.8 collective-permute-start.4
  5.6 1.5 %collective-permute-start.3 = (bf16[6,16,512]{2,1,0:T(8,128)(2,1)S(1)}, bf16[6,16,512]{2,1,0:T(8,128)(2,1)S(1)}, u32[]{:S(2)}, u32[]{:S(2)}) collective-permute-start(bf16[6,16,512]{2,1,0:T(8,128)(2,1)S(1)} %get-tuple-element.87), channel_id=1, source_target_pairs={{0,16},{4,20},{8,24},{12,28},{16,0},{20,4},{24,8},{28,12},{1,17},{... | collective-permute-start | bytes 294920 | tf_op jit(solution)/shard_map/ppermute | solution.py:413
  7.1 1.2 %collective-permute-start.1 = (bf16[6,16,512]{2,1,0:T(8,128)(2,1)S(1)}, bf16[6,16,512]{2,1,0:T(8,128)(2,1)S(1)}, u32[]{:S(2)}, u32[]{:S(2)}) collective-permute-start(bf16[6,16,512]{2,1,0:T(8,128)(2,1)S(1)} %get-tuple-element.89), channel_id=1, source_target_pairs={{0,8},{4,12},{8,0},{12,4},{16,24},{20,28},{24,16},{28,20},{1,9},{5... | collective-permute-start | bytes 294920 | tf_op jit(solution)/shard_map/ppermute | solution.py:413
  8.3 0.7 collective-permute-start
  9.0 1.1 %collective-permute-done.4.refs_5_ = bf16[6,16,512]{2,1,0:T(8,128)(2,1)S(1)} collective-permute-done((bf16[6,16,512]{2,1,0:T(8,128)(2,1)S(1)}, bf16[6,16,512]{2,1,0:T(8,128)(2,1)S(1)}, u32[]{:S(2)}, u32[]{:S(2)}) %collective-permute-start.4) | collective-permute-done | bytes 98336 | tf_op jit(solution)/shard_map/ppermute | solution.py:413
  10.1 2.5 %collective-permute-start.5 = (bf16[6,16,512]{2,1,0:T(8,128)(2,1)S(1)}, bf16[6,16,512]{2,1,0:T(8,128)(2,1)S(1)}, u32[]{:S(2)}, u32[]{:S(2)}) collective-permute-start(bf16[6,16,512]{2,1,0:T(8,128)(2,1)S(1)} %get-tuple-element.92), channel_id=1, source_target_pairs={{0,24},{4,28},{8,16},{12,20},{16,8},{20,12},{24,0},{28,4},{1,25},{... | collective-permute-start | bytes 294920 | tf_op jit(solution)/shard_map/ppermute | solution.py:413
  12.6 0.0 collective-permute-done.3.refs_4_
  12.6 0.0 collective-permute-done.2.refs_3_
  12.6 1.1 %collective-permute-done.1.refs_2_ = bf16[6,16,512]{2,1,0:T(8,128)(2,1)S(1)} collective-permute-done((bf16[6,16,512]{2,1,0:T(8,128)(2,1)S(1)}, bf16[6,16,512]{2,1,0:T(8,128)(2,1)S(1)}, u32[]{:S(2)}, u32[]{:S(2)}) %collective-permute-start.1) | collective-permute-done | bytes 98336 | tf_op jit(solution)/shard_map/ppermute | solution.py:413
  13.8 0.0 collective-permute-done.refs_1_
  13.8 2.7 %collective-permute-done.5.refs_6_ = bf16[6,16,512]{2,1,0:T(8,128)(2,1)S(1)} collective-permute-done((bf16[6,16,512]{2,1,0:T(8,128)(2,1)S(1)}, bf16[6,16,512]{2,1,0:T(8,128)(2,1)S(1)}, u32[]{:S(2)}, u32[]{:S(2)}) %collective-permute-start.5) | collective-permute-done | bytes 98336 | tf_op jit(solution)/shard_map/ppermute | solution.py:413
  16.5 7.2 %time_attention.1 = (bf16[6,16,512]{2,1,0:T(8,128)(2,1)S(1)}, bf16[6,16,512]{2,1,0:T(8,128)(2,1)S(1)}, bf16[6,16,512]{2,1,0:T(8,128)(2,1)S(1)}, bf16[6,16,512]{2...) custom-call(bf16[6,16,512]{2,1,0:T(8,128)(2,1)S(1)} %get-tuple-eleme, ...), custom_call_target="tpu_custom_call" | custom-call | tf_op jit(solution)/shard_map/time_attention/pallas_call | solution.py:235
  23.6 0.1 collective-permute-start.7
  23.7 1.9 %collective-permute-start.8 = (bf16[6,16,512]{2,1,0:T(8,128)(2,1)S(1)}, bf16[6,16,512]{2,1,0:T(8,128)(2,1)S(1)}, u32[]{:S(2)}, u32[]{:S(2)}) collective-permute-start(bf16[6,16,512]{2,1,0:T(8,128)(2,1)S(1)} %get-tuple-element.55), channel_id=1, source_target_pairs={{0,8},{4,12},{8,0},{12,4},{16,24},{20,28},{24,16},{28,20},{1,9},{5... | collective-permute-start | bytes 294920 | tf_op jit(solution)/shard_map/ppermute | solution.py:413
  25.6 0.1 collective-permute-start.9
  25.7 1.8 %collective-permute-start.10 = (bf16[6,16,512]{2,1,0:T(8,128)(2,1)S(1)}, bf16[6,16,512]{2,1,0:T(8,128)(2,1)S(1)}, u32[]{:S(2)}, u32[]{:S(2)}) collective-permute-start(bf16[6,16,512]{2,1,0:T(8,128)(2,1)S(1)} %get-tuple-element.57), channel_id=1, source_target_pairs={{0,16},{4,20},{8,24},{12,28},{16,0},{20,4},{24,8},{28,12},{1,17},{... | collective-permute-start | bytes 294920 | tf_op jit(solution)/shard_map/ppermute | solution.py:413
  27.5 0.0 collective-permute-start.11
  27.5 0.0 collective-permute-done.7.refs_1_
  27.5 1.7 %collective-permute-start.12 = (bf16[6,16,512]{2,1,0:T(8,128)(2,1)S(1)}, bf16[6,16,512]{2,1,0:T(8,128)(2,1)S(1)}, u32[]{:S(2)}, u32[]{:S(2)}) collective-permute-start(bf16[6,16,512]{2,1,0:T(8,128)(2,1)S(1)} %get-tuple-element.59), channel_id=1, source_target_pairs={{0,24},{4,28},{8,16},{12,20},{16,8},{20,12},{24,0},{28,4},{1,25},{... | collective-permute-start | bytes 294920 | tf_op jit(solution)/shard_map/ppermute | solution.py:413
  29.2 0.2 collective-permute-done.8.refs_2_
  29.4 0.7 collective-permute-start.13
  30.1 0.8 collective-permute-done.9.refs_3_
  30.8 0.2 collective-permute-done.10.refs_4_
  31.0 5.8 %collective-permute-done.11.refs_5_ = bf16[6,16,512]{2,1,0:T(8,128)(2,1)S(1)} collective-permute-done((bf16[6,16,512]{2,1,0:T(8,128)(2,1)S(1)}, bf16[6,16,512]{2,1,0:T(8,128)(2,1)S(1)}, u32[]{:S(2)}, u32[]{:S(2)}) %collective-permute-start.11) | collective-permute-done | bytes 98336 | tf_op jit(solution)/shard_map/ppermute | solution.py:413
  36.8 0.1 pack_steps.2
  36.9 2.6 %collective-permute-start.15 = (bf16[128,512]{1,0:T(8,128)(2,1)S(1)}, bf16[128,512]{1,0:T(8,128)(2,1)S(1)}, u32[]{:S(2)}, u32[]{:S(2)}) collective-permute-start(bf16[128,512]{1,0:T(8,128)(2,1)S(1)} %get-tuple-element.71), channel_id=1, source_target_pairs={{0,2},{1,3},{2,0},{3,1},{4,6},{5,7},{6,4},{7,5},{8,10},{9,11},{10,... | collective-permute-start | bytes 393224 | tf_op jit(solution)/shard_map/ppermute | solution.py:413
  39.5 1.6 %collective-permute-start.14 = (bf16[128,512]{1,0:T(8,128)(2,1)S(1)}, bf16[128,512]{1,0:T(8,128)(2,1)S(1)}, u32[]{:S(2)}, u32[]{:S(2)}) collective-permute-start(bf16[128,512]{1,0:T(8,128)(2,1)S(1)} %get-tuple-element.70), channel_id=1, source_target_pairs={{0,1},{1,0},{2,3},{3,2},{4,5},{5,4},{6,7},{7,6},{8,9},{9,8},{10,11... | collective-permute-start | bytes 393224 | tf_op jit(solution)/shard_map/ppermute | solution.py:413
  41.1 0.2 collective-permute-start.16
  41.3 5.7 %collective-permute-done.15.refs_2_.refs_8_ = bf16[128,512]{1,0:T(8,128)(2,1)S(1)} collective-permute-done((bf16[128,512]{1,0:T(8,128)(2,1)S(1)}, bf16[128,512]{1,0:T(8,128)(2,1)S(1)}, u32[]{:S(2)}, u32[]{:S(2)}) %collective-permute-start.15) | collective-permute-done | bytes 131104 | tf_op jit(solution)/shard_map/ppermute | solution.py:413
  47.1 2.3 %collective-permute-start.20 = (bf16[128,512]{1,0:T(8,128)(2,1)S(1)}, bf16[128,512]{1,0:T(8,128)(2,1)S(1)}, u32[]{:S(2)}, u32[]{:S(2)}) collective-permute-start(bf16[128,512]{1,0:T(8,128)(2,1)S(1)} %get-tuple-element.78), channel_id=1, source_target_pairs={{0,1},{3,2},{4,5},{7,6},{8,9},{11,10},{12,13},{15,14},{16,17},{19,... | collective-permute-start | bytes 393224 | tf_op jit(solution)/shard_map/ppermute | solution.py:413
  49.4 1.3 %collective-permute-start.21 = (bf16[128,512]{1,0:T(8,128)(2,1)S(1)}, bf16[128,512]{1,0:T(8,128)(2,1)S(1)}, u32[]{:S(2)}, u32[]{:S(2)}) collective-permute-start(bf16[128,512]{1,0:T(8,128)(2,1)S(1)} %get-tuple-element.79), channel_id=1, source_target_pairs={{0,2},{3,1},{4,6},{7,5},{8,10},{11,9},{12,14},{15,13},{16,18},{19,... | collective-permute-start | bytes 393224 | tf_op jit(solution)/shard_map/ppermute | solution.py:413
  50.7 0.8 %collective-permute-start.22 = (bf16[128,512]{1,0:T(8,128)(2,1)S(1)}, bf16[128,512]{1,0:T(8,128)(2,1)S(1)}, u32[]{:S(2)}, u32[]{:S(2)}) collective-permute-start(bf16[128,512]{1,0:T(8,128)(2,1)S(1)} %get-tuple-element.80), channel_id=1, source_target_pairs={{1,2},{2,1},{5,6},{6,5},{9,10},{10,9},{13,14},{14,13},{17,18},{18,... | collective-permute-start | bytes 393224 | tf_op jit(solution)/shard_map/ppermute | solution.py:413
  51.6 7.2 %agent_step.2 = (bf16[128,512]{1,0:T(8,128)(2,1)S(1)}, bf16[128,512]{1,0:T(8,128)(2,1)S(1)}, bf16[128,512]{1,0:T(8,128)(2,1)S(1)}, bf16[128,512]{1,0:T(8,128)(2,1)S(1)}) custom-call(bf16[128,512]{1,0:T(8,128)(2,1)S(1)} %get-tuple-element.69.refs_0_, bf16[128,512]{1,0:T(8,128)(2,1)S(1)} %collective-permute-done.14.refs_1_, ...), custom_call_target="tpu_custom_call" | custom-call | tf_op jit(solution)/shard_map/agent_step/pallas_call | solution.py:338
  58.8 1.6 %collective-permute-start.17 = (bf16[128,512]{1,0:T(8,128)(2,1)S(1)}, bf16[128,512]{1,0:T(8,128)(2,1)S(1)}, u32[]{:S(2)}, u32[]{:S(2)}) collective-permute-start(bf16[128,512]{1,0:T(8,128)(2,1)S(1)} %get-tuple-element.74), channel_id=1, source_target_pairs={{0,1},{1,0},{2,3},{3,2},{4,5},{5,4},{6,7},{7,6},{8,9},{9,8},{10,11... | collective-permute-start | bytes 393224 | tf_op jit(solution)/shard_map/ppermute | solution.py:413
  60.4 2.3 %collective-permute-start.18 = (bf16[128,512]{1,0:T(8,128)(2,1)S(1)}, bf16[128,512]{1,0:T(8,128)(2,1)S(1)}, u32[]{:S(2)}, u32[]{:S(2)}) collective-permute-start(bf16[128,512]{1,0:T(8,128)(2,1)S(1)} %get-tuple-element.75), channel_id=1, source_target_pairs={{0,2},{1,3},{2,0},{3,1},{4,6},{5,7},{6,4},{7,5},{8,10},{9,11},{10,... | collective-permute-start | bytes 393224 | tf_op jit(solution)/shard_map/ppermute | solution.py:413
  62.7 1.4 %collective-permute-start.19 = (bf16[128,512]{1,0:T(8,128)(2,1)S(1)}, bf16[128,512]{1,0:T(8,128)(2,1)S(1)}, u32[]{:S(2)}, u32[]{:S(2)}) collective-permute-start(bf16[128,512]{1,0:T(8,128)(2,1)S(1)} %get-tuple-element.76), channel_id=1, source_target_pairs={{0,3},{1,2},{2,1},{3,0},{4,7},{5,6},{6,5},{7,4},{8,11},{9,10},{10,... | collective-permute-start | bytes 393224 | tf_op jit(solution)/shard_map/ppermute | solution.py:413
  64.1 0.6 copy-done.6
  64.8 1.3 %collective-permute-start.23 = (bf16[128,512]{1,0:T(8,128)(2,1)S(1)}, bf16[128,512]{1,0:T(8,128)(2,1)S(1)}, u32[]{:S(2)}, u32[]{:S(2)}) collective-permute-start(bf16[128,512]{1,0:T(8,128)(2,1)S(1)} %get-tuple-element.82), channel_id=1, source_target_pairs={{1,0},{2,3},{5,4},{6,7},{9,8},{10,11},{13,12},{14,15},{17,16},{18,... | collective-permute-start | bytes 393224 | tf_op jit(solution)/shard_map/ppermute | solution.py:485
  66.1 1.3 %collective-permute-start.24 = (bf16[128,512]{1,0:T(8,128)(2,1)S(1)}, bf16[128,512]{1,0:T(8,128)(2,1)S(1)}, u32[]{:S(2)}, u32[]{:S(2)}) collective-permute-start(bf16[128,512]{1,0:T(8,128)(2,1)S(1)} %get-tuple-element.83), channel_id=1, source_target_pairs={{1,3},{2,0},{5,7},{6,4},{9,11},{10,8},{13,15},{14,12},{17,19},{18,... | collective-permute-start | bytes 393224 | tf_op jit(solution)/shard_map/ppermute | solution.py:485
  67.4 0.7 collective-permute-start.25
  68.1 5.0 %collective-permute-done.19.refs_3_ = bf16[128,512]{1,0:T(8,128)(2,1)S(1)} collective-permute-done((bf16[128,512]{1,0:T(8,128)(2,1)S(1)}, bf16[128,512]{1,0:T(8,128)(2,1)S(1)}, u32[]{:S(2)}, u32[]{:S(2)}) %collective-permute-start.19) | collective-permute-done | bytes 131104 | tf_op jit(solution)/shard_map/ppermute | solution.py:413
  73.1 6.1 %collective-permute-done.23.refs_5_ = bf16[128,512]{1,0:T(8,128)(2,1)S(1)} collective-permute-done((bf16[128,512]{1,0:T(8,128)(2,1)S(1)}, bf16[128,512]{1,0:T(8,128)(2,1)S(1)}, u32[]{:S(2)}, u32[]{:S(2)}) %collective-permute-start.23) | collective-permute-done | bytes 131104 | tf_op jit(solution)/shard_map/ppermute | solution.py:485
  79.2 1.2 %collective-permute-done.24.refs_6_ = bf16[128,512]{1,0:T(8,128)(2,1)S(1)} collective-permute-done((bf16[128,512]{1,0:T(8,128)(2,1)S(1)}, bf16[128,512]{1,0:T(8,128)(2,1)S(1)}, u32[]{:S(2)}, u32[]{:S(2)}) %collective-permute-start.24) | collective-permute-done | bytes 131104 | tf_op jit(solution)/shard_map/ppermute | solution.py:485
  80.5 0.6 copy-done.11
  81.1 0.1 copy-done.12
  81.1 2.2 %place_steps.1 = bf16[6,128,512]{2,1,0:T(8,128)(2,1)} custom-call(bf16[128,512]{1,0:T(8,128)(2,1)} %copy-done.5, bf16[128,512]{1,0:T(8,128)(2,1)} %copy-done.7, bf16[128,512]{1,0:T(8,128)(2,1)} %copy-done.8, bf16[128,512]{1,0:T(8,128)(2,1)} %copy-done.9, bf16[128,512]{1,0:T(8,128)(2,1)} %copy-done.6, bf16[128,512]{1,0:T(8,128)(2,1)} %copy-done.10, ...), custom_call_target="tpu_custom_call" | custom-call | tf_op jit(solution)/shard_map/place_steps/pallas_call | solution.py:396
  (37 shorter events, 0.1 us)
Async XLA Ops:
  0.0 51.6 %copy-start.2 = (bf16[512,512]{1,0:T(8,128)(2,1)S(1)}, bf16[512,512]{1,0:T(8,128)(2,1)}, u32[]{:S(2)}) copy-start(bf16[512,512]{1,0:T(8,128)(2,1)} %refs_4_.3) | copy-start | bytes 1572868
  0.0 51.6 %copy-start.3 = (bf16[512,512]{1,0:T(8,128)(2,1)S(1)}, bf16[512,512]{1,0:T(8,128)(2,1)}, u32[]{:S(2)}) copy-start(bf16[512,512]{1,0:T(8,128)(2,1)} %refs_5_.3) | copy-start | bytes 1572868
  0.0 51.6 %copy-start.4 = (bf16[512,512]{1,0:T(8,128)(2,1)S(1)}, bf16[512,512]{1,0:T(8,128)(2,1)}, u32[]{:S(2)}) copy-start(bf16[512,512]{1,0:T(8,128)(2,1)} %refs_6_.3) | copy-start | bytes 1572868
  1.4 6.9 %collective-permute-start.6 = (bf16[6,16,512]{2,1,0:T(8,128)(2,1)S(1)}, bf16[6,16,512]{2,1,0:T(8,128)(2,1)S(1)}, u32[]{:S(2)}, u32[]{:S(2)}) collective-permute-start(bf16[6,16,512]{2,1,0:T(8,128)(2,1)S(1)} %get-tuple-element.85), channel_id=1, source_target_pairs={{0,28},{4,24},{8,20},{12,16},{16,12},{20,8},{24,4},{28,0},{1,29},{... | collective-permute-start | bytes 294920 | tf_op jit(solution)/shard_map/ppermute | solution.py:413
  4.8 5.3 %collective-permute-start.4 = (bf16[6,16,512]{2,1,0:T(8,128)(2,1)S(1)}, bf16[6,16,512]{2,1,0:T(8,128)(2,1)S(1)}, u32[]{:S(2)}, u32[]{:S(2)}) collective-permute-start(bf16[6,16,512]{2,1,0:T(8,128)(2,1)S(1)} %get-tuple-element.86), channel_id=1, source_target_pairs={{0,20},{4,16},{8,28},{12,24},{16,4},{20,0},{24,12},{28,8},{1,21},{... | collective-permute-start | bytes 294920 | tf_op jit(solution)/shard_map/ppermute | solution.py:413
  5.6 7.0 %collective-permute-start.3 = (bf16[6,16,512]{2,1,0:T(8,128)(2,1)S(1)}, bf16[6,16,512]{2,1,0:T(8,128)(2,1)S(1)}, u32[]{:S(2)}, u32[]{:S(2)}) collective-permute-start(bf16[6,16,512]{2,1,0:T(8,128)(2,1)S(1)} %get-tuple-element.87), channel_id=1, source_target_pairs={{0,16},{4,20},{8,24},{12,28},{16,0},{20,4},{24,8},{28,12},{1,17},{... | collective-permute-start | bytes 294920 | tf_op jit(solution)/shard_map/ppermute | solution.py:413
  7.1 5.5 %collective-permute-start.2 = (bf16[6,16,512]{2,1,0:T(8,128)(2,1)S(1)}, bf16[6,16,512]{2,1,0:T(8,128)(2,1)S(1)}, u32[]{:S(2)}, u32[]{:S(2)}) collective-permute-start(bf16[6,16,512]{2,1,0:T(8,128)(2,1)S(1)} %get-tuple-element.88), channel_id=1, source_target_pairs={{0,12},{4,8},{8,4},{12,0},{16,28},{20,24},{24,20},{28,16},{1,13},{... | collective-permute-start | bytes 294920 | tf_op jit(solution)/shard_map/ppermute | solution.py:413
  7.1 6.7 %collective-permute-start.1 = (bf16[6,16,512]{2,1,0:T(8,128)(2,1)S(1)}, bf16[6,16,512]{2,1,0:T(8,128)(2,1)S(1)}, u32[]{:S(2)}, u32[]{:S(2)}) collective-permute-start(bf16[6,16,512]{2,1,0:T(8,128)(2,1)S(1)} %get-tuple-element.89), channel_id=1, source_target_pairs={{0,8},{4,12},{8,0},{12,4},{16,24},{20,28},{24,16},{28,20},{1,9},{5... | collective-permute-start | bytes 294920 | tf_op jit(solution)/shard_map/ppermute | solution.py:413
  8.3 5.5 %collective-permute-start = (bf16[6,16,512]{2,1,0:T(8,128)(2,1)S(1)}, bf16[6,16,512]{2,1,0:T(8,128)(2,1)S(1)}, u32[]{:S(2)}, u32[]{:S(2)}) collective-permute-start(bf16[6,16,512]{2,1,0:T(8,128)(2,1)S(1)} %get-tuple-element.90), channel_id=1, source_target_pairs={{0,4},{4,0},{8,12},{12,8},{16,20},{20,16},{24,28},{28,24},{1,5},{5... | collective-permute-start | bytes 294920 | tf_op jit(solution)/shard_map/ppermute | solution.py:413
  10.1 6.3 %collective-permute-start.5 = (bf16[6,16,512]{2,1,0:T(8,128)(2,1)S(1)}, bf16[6,16,512]{2,1,0:T(8,128)(2,1)S(1)}, u32[]{:S(2)}, u32[]{:S(2)}) collective-permute-start(bf16[6,16,512]{2,1,0:T(8,128)(2,1)S(1)} %get-tuple-element.92), channel_id=1, source_target_pairs={{0,24},{4,28},{8,16},{12,20},{16,8},{20,12},{24,0},{28,4},{1,25},{... | collective-permute-start | bytes 294920 | tf_op jit(solution)/shard_map/ppermute | solution.py:413
  16.5 35.1 %copy-start = (bf16[512,2048]{1,0:T(8,128)(2,1)S(1)}, bf16[512,2048]{1,0:T(8,128)(2,1)}, u32[]{:S(2)}) copy-start(bf16[512,2048]{1,0:T(8,128)(2,1)} %refs_8_.5) | copy-start | bytes 6291460
  16.5 35.1 %copy-start.1 = (bf16[2048,512]{1,0:T(8,128)(2,1)S(1)}, bf16[2048,512]{1,0:T(8,128)(2,1)}, u32[]{:S(2)}) copy-start(bf16[2048,512]{1,0:T(8,128)(2,1)} %refs_9_.5) | copy-start | bytes 6291460
  23.6 3.8 %collective-permute-start.7 = (bf16[6,16,512]{2,1,0:T(8,128)(2,1)S(1)}, bf16[6,16,512]{2,1,0:T(8,128)(2,1)S(1)}, u32[]{:S(2)}, u32[]{:S(2)}) collective-permute-start(bf16[6,16,512]{2,1,0:T(8,128)(2,1)S(1)} %get-tuple-element.54), channel_id=1, source_target_pairs={{0,4},{4,0},{8,12},{12,8},{16,20},{20,16},{24,28},{28,24},{1,5},{5... | collective-permute-start | bytes 294920 | tf_op jit(solution)/shard_map/ppermute | solution.py:413
  23.7 5.7 %collective-permute-start.8 = (bf16[6,16,512]{2,1,0:T(8,128)(2,1)S(1)}, bf16[6,16,512]{2,1,0:T(8,128)(2,1)S(1)}, u32[]{:S(2)}, u32[]{:S(2)}) collective-permute-start(bf16[6,16,512]{2,1,0:T(8,128)(2,1)S(1)} %get-tuple-element.55), channel_id=1, source_target_pairs={{0,8},{4,12},{8,0},{12,4},{16,24},{20,28},{24,16},{28,20},{1,9},{5... | collective-permute-start | bytes 294920 | tf_op jit(solution)/shard_map/ppermute | solution.py:413
  25.6 5.2 %collective-permute-start.9 = (bf16[6,16,512]{2,1,0:T(8,128)(2,1)S(1)}, bf16[6,16,512]{2,1,0:T(8,128)(2,1)S(1)}, u32[]{:S(2)}, u32[]{:S(2)}) collective-permute-start(bf16[6,16,512]{2,1,0:T(8,128)(2,1)S(1)} %get-tuple-element.56), channel_id=1, source_target_pairs={{0,12},{4,8},{8,4},{12,0},{16,28},{20,24},{24,20},{28,16},{1,13},{... | collective-permute-start | bytes 294920 | tf_op jit(solution)/shard_map/ppermute | solution.py:413
  25.7 5.3 %collective-permute-start.10 = (bf16[6,16,512]{2,1,0:T(8,128)(2,1)S(1)}, bf16[6,16,512]{2,1,0:T(8,128)(2,1)S(1)}, u32[]{:S(2)}, u32[]{:S(2)}) collective-permute-start(bf16[6,16,512]{2,1,0:T(8,128)(2,1)S(1)} %get-tuple-element.57), channel_id=1, source_target_pairs={{0,16},{4,20},{8,24},{12,28},{16,0},{20,4},{24,8},{28,12},{1,17},{... | collective-permute-start | bytes 294920 | tf_op jit(solution)/shard_map/ppermute | solution.py:413
  27.5 9.3 %collective-permute-start.11 = (bf16[6,16,512]{2,1,0:T(8,128)(2,1)S(1)}, bf16[6,16,512]{2,1,0:T(8,128)(2,1)S(1)}, u32[]{:S(2)}, u32[]{:S(2)}) collective-permute-start(bf16[6,16,512]{2,1,0:T(8,128)(2,1)S(1)} %get-tuple-element.58), channel_id=1, source_target_pairs={{0,20},{4,16},{8,28},{12,24},{16,4},{20,0},{24,12},{28,8},{1,21},{... | collective-permute-start | bytes 294920 | tf_op jit(solution)/shard_map/ppermute | solution.py:413
  27.5 9.3 %collective-permute-start.12 = (bf16[6,16,512]{2,1,0:T(8,128)(2,1)S(1)}, bf16[6,16,512]{2,1,0:T(8,128)(2,1)S(1)}, u32[]{:S(2)}, u32[]{:S(2)}) collective-permute-start(bf16[6,16,512]{2,1,0:T(8,128)(2,1)S(1)} %get-tuple-element.59), channel_id=1, source_target_pairs={{0,24},{4,28},{8,16},{12,20},{16,8},{20,12},{24,0},{28,4},{1,25},{... | collective-permute-start | bytes 294920 | tf_op jit(solution)/shard_map/ppermute | solution.py:413
  29.4 7.4 %collective-permute-start.13 = (bf16[6,16,512]{2,1,0:T(8,128)(2,1)S(1)}, bf16[6,16,512]{2,1,0:T(8,128)(2,1)S(1)}, u32[]{:S(2)}, u32[]{:S(2)}) collective-permute-start(bf16[6,16,512]{2,1,0:T(8,128)(2,1)S(1)} %get-tuple-element.60), channel_id=1, source_target_pairs={{0,28},{4,24},{8,20},{12,16},{16,12},{20,8},{24,4},{28,0},{1,29},{... | collective-permute-start | bytes 294920 | tf_op jit(solution)/shard_map/ppermute | solution.py:413
  36.9 10.2 %collective-permute-start.15 = (bf16[128,512]{1,0:T(8,128)(2,1)S(1)}, bf16[128,512]{1,0:T(8,128)(2,1)S(1)}, u32[]{:S(2)}, u32[]{:S(2)}) collective-permute-start(bf16[128,512]{1,0:T(8,128)(2,1)S(1)} %get-tuple-element.71), channel_id=1, source_target_pairs={{0,2},{1,3},{2,0},{3,1},{4,6},{5,7},{6,4},{7,5},{8,10},{9,11},{10,... | collective-permute-start | bytes 393224 | tf_op jit(solution)/shard_map/ppermute | solution.py:413
  39.5 12.1 %collective-permute-start.14 = (bf16[128,512]{1,0:T(8,128)(2,1)S(1)}, bf16[128,512]{1,0:T(8,128)(2,1)S(1)}, u32[]{:S(2)}, u32[]{:S(2)}) collective-permute-start(bf16[128,512]{1,0:T(8,128)(2,1)S(1)} %get-tuple-element.70), channel_id=1, source_target_pairs={{0,1},{1,0},{2,3},{3,2},{4,5},{5,4},{6,7},{7,6},{8,9},{9,8},{10,11... | collective-permute-start | bytes 393224 | tf_op jit(solution)/shard_map/ppermute | solution.py:413
  41.1 10.5 %collective-permute-start.16 = (bf16[128,512]{1,0:T(8,128)(2,1)S(1)}, bf16[128,512]{1,0:T(8,128)(2,1)S(1)}, u32[]{:S(2)}, u32[]{:S(2)}) collective-permute-start(bf16[128,512]{1,0:T(8,128)(2,1)S(1)} %get-tuple-element.72), channel_id=1, source_target_pairs={{0,3},{1,2},{2,1},{3,0},{4,7},{5,6},{6,5},{7,4},{8,11},{9,10},{10,... | collective-permute-start | bytes 393224 | tf_op jit(solution)/shard_map/ppermute | solution.py:413
  47.1 15.6 %collective-permute-start.20 = (bf16[128,512]{1,0:T(8,128)(2,1)S(1)}, bf16[128,512]{1,0:T(8,128)(2,1)S(1)}, u32[]{:S(2)}, u32[]{:S(2)}) collective-permute-start(bf16[128,512]{1,0:T(8,128)(2,1)S(1)} %get-tuple-element.78), channel_id=1, source_target_pairs={{0,1},{3,2},{4,5},{7,6},{8,9},{11,10},{12,13},{15,14},{16,17},{19,... | collective-permute-start | bytes 393224 | tf_op jit(solution)/shard_map/ppermute | solution.py:413
  49.4 14.7 %collective-permute-start.21 = (bf16[128,512]{1,0:T(8,128)(2,1)S(1)}, bf16[128,512]{1,0:T(8,128)(2,1)S(1)}, u32[]{:S(2)}, u32[]{:S(2)}) collective-permute-start(bf16[128,512]{1,0:T(8,128)(2,1)S(1)} %get-tuple-element.79), channel_id=1, source_target_pairs={{0,2},{3,1},{4,6},{7,5},{8,10},{11,9},{12,14},{15,13},{16,18},{19,... | collective-permute-start | bytes 393224 | tf_op jit(solution)/shard_map/ppermute | solution.py:413
  50.7 13.4 %collective-permute-start.22 = (bf16[128,512]{1,0:T(8,128)(2,1)S(1)}, bf16[128,512]{1,0:T(8,128)(2,1)S(1)}, u32[]{:S(2)}, u32[]{:S(2)}) collective-permute-start(bf16[128,512]{1,0:T(8,128)(2,1)S(1)} %get-tuple-element.80), channel_id=1, source_target_pairs={{1,2},{2,1},{5,6},{6,5},{9,10},{10,9},{13,14},{14,13},{17,18},{18,... | collective-permute-start | bytes 393224 | tf_op jit(solution)/shard_map/ppermute | solution.py:413
  58.8 5.3 %copy-start.5 = (bf16[128,512]{1,0:T(8,128)(2,1)}, bf16[128,512]{1,0:T(8,128)(2,1)S(1)}, u32[]{:S(2)}) copy-start(bf16[128,512]{1,0:T(8,128)(2,1)S(1)} %get-tuple-element.73.refs_10_.refs_0_) | copy-start | bytes 393220
  58.8 8.6 %collective-permute-start.17 = (bf16[128,512]{1,0:T(8,128)(2,1)S(1)}, bf16[128,512]{1,0:T(8,128)(2,1)S(1)}, u32[]{:S(2)}, u32[]{:S(2)}) collective-permute-start(bf16[128,512]{1,0:T(8,128)(2,1)S(1)} %get-tuple-element.74), channel_id=1, source_target_pairs={{0,1},{1,0},{2,3},{3,2},{4,5},{5,4},{6,7},{7,6},{8,9},{9,8},{10,11... | collective-permute-start | bytes 393224 | tf_op jit(solution)/shard_map/ppermute | solution.py:413
  60.4 7.6 %collective-permute-start.18 = (bf16[128,512]{1,0:T(8,128)(2,1)S(1)}, bf16[128,512]{1,0:T(8,128)(2,1)S(1)}, u32[]{:S(2)}, u32[]{:S(2)}) collective-permute-start(bf16[128,512]{1,0:T(8,128)(2,1)S(1)} %get-tuple-element.75), channel_id=1, source_target_pairs={{0,2},{1,3},{2,0},{3,1},{4,6},{5,7},{6,4},{7,5},{8,10},{9,11},{10,... | collective-permute-start | bytes 393224 | tf_op jit(solution)/shard_map/ppermute | solution.py:413
  62.7 10.4 %collective-permute-start.19 = (bf16[128,512]{1,0:T(8,128)(2,1)S(1)}, bf16[128,512]{1,0:T(8,128)(2,1)S(1)}, u32[]{:S(2)}, u32[]{:S(2)}) collective-permute-start(bf16[128,512]{1,0:T(8,128)(2,1)S(1)} %get-tuple-element.76), channel_id=1, source_target_pairs={{0,3},{1,2},{2,1},{3,0},{4,7},{5,6},{6,5},{7,4},{8,11},{9,10},{10,... | collective-permute-start | bytes 393224 | tf_op jit(solution)/shard_map/ppermute | solution.py:413
  64.1 0.6 copy-start.6
  64.8 14.4 %collective-permute-start.23 = (bf16[128,512]{1,0:T(8,128)(2,1)S(1)}, bf16[128,512]{1,0:T(8,128)(2,1)S(1)}, u32[]{:S(2)}, u32[]{:S(2)}) collective-permute-start(bf16[128,512]{1,0:T(8,128)(2,1)S(1)} %get-tuple-element.82), channel_id=1, source_target_pairs={{1,0},{2,3},{5,4},{6,7},{9,8},{10,11},{13,12},{14,15},{17,16},{18,... | collective-permute-start | bytes 393224 | tf_op jit(solution)/shard_map/ppermute | solution.py:485
  66.1 14.4 %collective-permute-start.24 = (bf16[128,512]{1,0:T(8,128)(2,1)S(1)}, bf16[128,512]{1,0:T(8,128)(2,1)S(1)}, u32[]{:S(2)}, u32[]{:S(2)}) collective-permute-start(bf16[128,512]{1,0:T(8,128)(2,1)S(1)} %get-tuple-element.83), channel_id=1, source_target_pairs={{1,3},{2,0},{5,7},{6,4},{9,11},{10,8},{13,15},{14,12},{17,19},{18,... | collective-permute-start | bytes 393224 | tf_op jit(solution)/shard_map/ppermute | solution.py:485
  67.4 13.1 %copy-start.7 = (bf16[128,512]{1,0:T(8,128)(2,1)}, bf16[128,512]{1,0:T(8,128)(2,1)S(1)}, u32[]{:S(2)}) copy-start(bf16[128,512]{1,0:T(8,128)(2,1)S(1)} %collective-permute-done.17.refs_1_) | copy-start | bytes 393220
  67.4 13.0 %collective-permute-start.25 = (bf16[128,512]{1,0:T(8,128)(2,1)S(1)}, bf16[128,512]{1,0:T(8,128)(2,1)S(1)}, u32[]{:S(2)}, u32[]{:S(2)}) collective-permute-start(bf16[128,512]{1,0:T(8,128)(2,1)S(1)} %get-tuple-element.84), channel_id=1, source_target_pairs={{1,2},{2,1},{5,6},{6,5},{9,10},{10,9},{13,14},{14,13},{17,18},{18,... | collective-permute-start | bytes 393224 | tf_op jit(solution)/shard_map/ppermute | solution.py:485
  68.1 12.4 %copy-start.8 = (bf16[128,512]{1,0:T(8,128)(2,1)}, bf16[128,512]{1,0:T(8,128)(2,1)S(1)}, u32[]{:S(2)}) copy-start(bf16[128,512]{1,0:T(8,128)(2,1)S(1)} %collective-permute-done.18.refs_2_) | copy-start | bytes 393220
  73.1 7.4 %copy-start.9 = (bf16[128,512]{1,0:T(8,128)(2,1)}, bf16[128,512]{1,0:T(8,128)(2,1)S(1)}, u32[]{:S(2)}) copy-start(bf16[128,512]{1,0:T(8,128)(2,1)S(1)} %collective-permute-done.19.refs_3_) | copy-start | bytes 393220
  79.2 1.2 %copy-start.10 = (bf16[128,512]{1,0:T(8,128)(2,1)}, bf16[128,512]{1,0:T(8,128)(2,1)S(1)}, u32[]{:S(2)}) copy-start(bf16[128,512]{1,0:T(8,128)(2,1)S(1)} %collective-permute-done.23.refs_5_) | copy-start | bytes 393220
  80.4 0.6 copy-start.11
  80.4 0.7 copy-start.12

commit v4 on v3

--- a/solution.py
+++ b/solution.py
@@ -162,12 +162,40 @@
     return (sums[:, :wide] / sums[:, wide:]).astype(jnp.bfloat16)
 
 
+def share_kernel(size, *refs):
+    states, outs, sems = refs[0], refs[1 : size + 1], refs[size + 1]
+    agents = outs[0].shape[1]
+    me = lax.axis_index("tm")
+    copies = []
+    for k, out in enumerate(outs):
+        at = pl.ds(pl.multiple_of(jnp.bitwise_xor(me, k) * agents, agents), agents)
+        copies.append(pltpu.make_async_copy(states.at[:, at, :], out, sems.at[k]))
+    for copy in copies:
+        copy.start()
+    for copy in copies:
+        copy.wait()
+
+
+def share_stage(states, size):
+    steps, agents, features = states.shape
+    shape = jax.ShapeDtypeStruct((steps, agents // size, features), states.dtype)
+    return pl.pallas_call(
+        functools.partial(share_kernel, size),
+        out_shape=[shape] * size,
+        in_specs=[spec(HBM)],
+        out_specs=[spec(VMEM)] * size,
+        scratch_shapes=[pltpu.SemaphoreType.DMA((size,))],
+        compiler_params=pltpu.CompilerParams(vmem_limit_bytes=4 * 2**20),
+        cost_estimate=pl.CostEstimate(flops=2 * 10**10, bytes_accessed=10**7, transcendentals=0),
+        name="cut_shares",
+    )(*in_hbm([states]))
+
+
 def time_kernel(size, *refs):
     pieces, weights = refs[:size], refs[size : size + 4]
     outs = refs[size + 4 : 2 * size + 4]
     wide, normed, query, key_e, key_o, value_e, value_o, mixed = refs[2 * size + 4 : 2 * size + 12]
-    w_query, w_key, w_value, w_out, sems = refs[2 * size + 12 :]
-    copies = fetch(weights, (w_query, w_key, w_value, w_out), sems)
+    w_query, w_key, w_value, w_out = weights
     steps, agents, features = pieces[0].shape
     rows = steps * agents
     total_steps = steps * size
@@ -182,11 +210,8 @@
         at = pl.ds(agent, total_steps, stride=agents)
         own = jnp.concatenate([wide[c, at, :] for c in range(len(lanes_of))], axis=1)
         normed[pl.ds(agent * total_steps, total_steps), :] = norm_of(own)
-    copies[0].wait()
     query[...] = project(normed[...], w_query[...])
-    copies[1].wait()
     split_heads(project(normed[...], w_key[...]), key_e, key_o)
-    copies[2].wait()
     split_heads(project(normed[...], w_value[...]), value_e, value_o, True)
 
     group = 2 * total_steps
@@ -212,7 +237,6 @@
         return carry
 
     lax.fori_loop(0, agents // 2, one_group, 0, unroll=True)
-    copies[3].wait()
     added = jnp.dot(mixed[...], w_out[...], preferred_element_type=jnp.float32)
     for agent in range(agents):
         at = pl.ds(agent, total_steps, stride=agents)
@@ -235,17 +259,20 @@
     return pl.pallas_call(
         functools.partial(time_kernel, size),
         out_shape=[jax.ShapeDtypeStruct((steps, agents, features), kind)] * size,
-        in_specs=[spec(VMEM)] * size + [spec(HBM)] * 4,
+        in_specs=[spec(VMEM)] * (size + 4),
         out_specs=[spec(VMEM)] * size,
         scratch_shapes=[VMEM((features // 128, rows, 128), jnp.float32)]
         + [VMEM((rows, features), kind)] * 4
         + [VMEM((rows, 2 * features), kind)] * 2
-        + [VMEM((rows, features), kind)]
-        + [VMEM(w.shape, kind) for w in weights]
-        + [pltpu.SemaphoreType.DMA((4,))],
+        + [VMEM((rows, features), kind)],
         compiler_params=pltpu.CompilerParams(vmem_limit_bytes=24 * 2**20),
+        cost_estimate=pl.CostEstimate(
+            flops=8 * rows * features * features,
+            bytes_accessed=2 * (2 * rows + 4 * features) * features,
+            transcendentals=rows * HEADS * steps * size,
+        ),
         name="time_attention",
-    )(*pieces, *in_hbm(weights))
+    )(*pieces, *weights)
 
 
 def pack_kernel(size, choose, *refs):
@@ -284,7 +311,6 @@
     query[...] = project(normed[...], w_query[...])
     split_heads(project(normed[...], w_key[...]), key_e, key_o)
     split_heads(project(normed[...], w_value[...]), value_e, value_o, True)
-
     for pair in range(HEADS // 2):
         lanes = pl.ds(pair * 2 * head_size, 2 * head_size)
         double = pl.ds(pair * 4 * head_size, 4 * head_size)
@@ -348,70 +374,86 @@
         + [VMEM((rows, features), kind)] * 2
         + [VMEM((rows, hidden), kind)]
         + [VMEM(weights[3].shape, kind), pltpu.SemaphoreType.DMA((1,))],
-        compiler_params=pltpu.CompilerParams(vmem_limit_bytes=20 * 2**20),
+        compiler_params=pltpu.CompilerParams(vmem_limit_bytes=16 * 2**20),
+        cost_estimate=pl.CostEstimate(
+            flops=2 * rows * features * (4 * features + 2 * hidden + 2 * rows),
+            bytes_accessed=2 * rows * features * 8,
+            transcendentals=rows * (HEADS * rows + hidden),
+        ),
         name="agent_step",
     )(*blocks, *weights[:3], *in_hbm(weights[3:4]), *weights[4:], *after)
 
 
 def place_kernel(*refs):
-    whole, extra, out, sems = refs[:4], refs[4:8], refs[8], refs[9]
+    sources, out, sems = refs[:4], refs[4], refs[5]
+    plane = lax.axis_index("agent")
+    copies = [
+        pltpu.make_async_copy(source, out.at[jnp.bitwise_xor(plane, k)], sems.at[k])
+        for k, source in enumerate(sources)
+    ]
+    for copy in copies:
+        copy.start()
+    for copy in copies:
+        copy.wait()
+
+
+def place_extra_kernel(*refs):
+    sources, out, sems = refs[:4], refs[5], refs[6]
     plane = lax.axis_index("agent")
     middle = jnp.logical_or(plane == 1, plane == 2)
     low = plane // 2
-    copies = [
-        pltpu.make_async_copy(source, out.at[jnp.bitwise_xor(plane, k)], sems.at[k])
-        for k, source in enumerate(whole)
-    ]
-    inner = [
-        pltpu.make_async_copy(extra[0], out.at[4 + low], sems.at[4]),
-        pltpu.make_async_copy(extra[3], out.at[5 - low], sems.at[5]),
-    ]
-    outer = [
-        pltpu.make_async_copy(extra[1], out.at[4 + low], sems.at[4]),
-        pltpu.make_async_copy(extra[2], out.at[5 - low], sems.at[5]),
-    ]
-    for copy in copies:
-        copy.start()
-
-    @pl.when(middle)
-    def _():
-        for copy in inner:
+
+    def place(one, other):
+        copies = [
+            pltpu.make_async_copy(one, out.at[4 + low], sems.at[0]),
+            pltpu.make_async_copy(other, out.at[5 - low], sems.at[1]),
+        ]
+        for copy in copies:
             copy.start()
-        for copy in inner:
+        for copy in copies:
             copy.wait()
 
-    @pl.when(jnp.logical_not(middle))
-    def _():
-        for copy in outer:
-            copy.start()
-        for copy in outer:
-            copy.wait()
-
-    for copy in copies:
-        copy.wait()
+    pl.when(middle)(lambda: place(sources[0], sources[3]))
+    pl.when(jnp.logical_not(middle))(lambda: place(sources[1], sources[2]))
 
 
 def place_stage(whole, extra):
     agents, features = whole[0].shape
+    shape = jax.ShapeDtypeStruct((6, agents, features), jnp.bfloat16)
+    begun = pl.pallas_call(
+        place_kernel,
+        out_shape=shape,
+        in_specs=[spec(VMEM)] * 4,
+        out_specs=spec(HBM),
+        scratch_shapes=[pltpu.SemaphoreType.DMA((4,))],
+        compiler_params=pltpu.CompilerParams(vmem_limit_bytes=4 * 2**20),
+        name="place_steps",
+    )(*whole)
     return pl.pallas_call(
-        place_kernel,
-        out_shape=jax.ShapeDtypeStruct((6, agents, features), jnp.bfloat16),
-        in_specs=[spec(VMEM)] * 8,
+        place_extra_kernel,
+        out_shape=shape,
+        in_specs=[spec(VMEM)] * 4 + [spec(HBM)],
         out_specs=spec(HBM),
-        scratch_shapes=[pltpu.SemaphoreType.DMA((6,))],
-        name="place_steps",
-    )(*whole, *extra)
+        input_output_aliases={4: 0},
+        scratch_shapes=[pltpu.SemaphoreType.DMA((2,))],
+        compiler_params=pltpu.CompilerParams(vmem_limit_bytes=4 * 2**20),
+        name="place_extra",
+    )(*extra, begun)
 
 
 def xor_pairs(size, k, targets=None):
     return [(j, j ^ k) for j in range(size) if targets is None or j ^ k in targets]
 
 
-def exchange(parts, axis, targets=None):
+def exchange(parts, axis, targets=None, ordered=False):
     size = len(parts)
-    return [parts[0]] + [
-        lax.ppermute(parts[k], axis, xor_pairs(size, k, targets)) for k in range(1, size)
-    ]
+    moved = {}
+    for k in range(size - 1, 0, -1):
+        part = parts[k]
+        if ordered and k == 1:
+            part, moved[size - 1] = lax.optimization_barrier((part, moved[size - 1]))
+        moved[k] = lax.ppermute(part, axis, xor_pairs(size, k, targets))
+    return [parts[0]] + [moved[k] for k in range(1, size)]
 
 
 def together(parts):
@@ -469,20 +511,16 @@
         after_time = general_time(states, *time_weights)
         return general_agent(after_time, neighbours, *agent_weights)
 
-    me, plane = lax.axis_index("tm"), lax.axis_index("agent")
-    parts = [
-        lax.dynamic_slice_in_dim(states, jnp.bitwise_xor(me, k) * share, share, 1)
-        for k in range(size)
-    ]
-    pieces = together(exchange(parts, "tm"))
-    pieces = together(exchange(time_stage(pieces, time_weights), "tm"))
+    pieces = together(exchange(share_stage(states, size), "tm", ordered=True))
+    pieces = together(exchange(time_stage(pieces, time_weights), "tm", ordered=True))
     blocks_a = exchange(pack_stage(pieces, whole_steps), "agent")
     blocks_b = exchange(pack_stage(pieces, extra_steps, blocks_a[2:3]), "agent", (1, 2))
+
     result_a = agent_stage(blocks_a, agent_weights, False)
     done_a = exchange(result_a, "agent")
     result_b = agent_stage(blocks_b, agent_weights, True, result_a[:1])
     done_b = [result_b[0]] + [
-        lax.ppermute(result_b[k], "agent", [(j, j ^ k) for j in (1, 2)]) for k in range(1, 4)
+        lax.ppermute(result_b[k], "agent", [(j, j ^ k) for j in (1, 2)]) for k in (1, 2, 3)
     ]
     return place_stage(done_a, done_b)
 

time: 83.8 us -> 77.9 us (0.930)
  waiting for transfers between devices: 29.9 us -> 24.6 us
  local copies, waits for them, and re-layouts: 2.72 us -> 0.05 us
  starting transfers between devices: 33.7 us -> 36.3 us
    ppermute x23, waiting for transfers between devices: 22.6 us -> 18.6 us  [exchange(): moved[k] = lax.ppermute(part, axis, xor_pairs(size, k, targets))]
    ppermute x23, starting transfers between devices: 30.5 us -> 33 us  [exchange(): moved[k] = lax.ppermute(part, axis, xor_pairs(size, k, targets))]
    dynamic_slice x1 -> x0, local copies, waits for them, and re-layouts: 1.38 us -> none  [local(): lax.dynamic_slice_in_dim(states, jnp.bitwise_xor(me, k) * share, share, 1)]
    ppermute x3, waiting for transfers between devices: 7.34 us -> 6.05 us  [local(): lax.ppermute(result_b[k], 'agent', [(j, j ^ k) for j in (1, 2)])]
    unnamed x26 -> x18, local copies, waits for them, and re-layouts: 1.34 us -> 0.05 us
    pallas_call x1, Pallas kernels: 7.17 us -> 6.04 us  [time_stage(): pl.pallas_call(functools.partial(time_kernel, size), out_shape=[jax.Shape...]
    pallas_call x1 -> x3, Pallas kernels: 2.21 us -> 2.97 us  [the longest x1 1.43 us: share_stage(): pl.pallas_call(functools.partial(share_kernel, size), out_shape=[shape] *...]
  transfers between devices with their start and end apart: 26 -> 26, of which waited for: 11 -> 9; matrix products, arithmetic and copies ran while one was open for 0% -> 0% of each run, Pallas kernels for 9% -> 10%
where the time goes in v4:
time: 77.9 us; the launch traced here: 77.7 us
  starting transfers between devices  36.3 us (47%)
  waiting for transfers between devices  24.6 us (32%)
  Pallas kernels  16.3 us (21%)
    ppermute x23, starting transfers between devices, exchange(): moved[k] = lax.ppermute(part, axis, xor_pairs(size, k, targets))  33 us
    ppermute x23, waiting for transfers between devices, exchange(): moved[k] = lax.ppermute(part, axis, xor_pairs(size, k, targets))  18.6 us
    pallas_call x2, Pallas kernels, agent_stage(): pl.pallas_call(functools.partial(agent_kernel, count, middle_only), out_s...  7.19 us
    ppermute x3, waiting for transfers between devices, local(): lax.ppermute(result_b[k], 'agent', [(j, j ^ k) for j in (1, 2)])  6.05 us
    pallas_call x1, Pallas kernels, time_stage(): pl.pallas_call(functools.partial(time_kernel, size), out_shape=[jax.Shape...  6.04 us
    ppermute x3, starting transfers between devices, local(): lax.ppermute(result_b[k], 'agent', [(j, j ^ k) for j in (1, 2)])  3.24 us
  transfers between devices with their start and end apart: 26, of which 9 were waited for; matrix products, arithmetic and copies ran while one was open for 0% of the time, Pallas kernels for 10%

profile of v4, /device:TPU:0, one launch (start us, length us, event | category | flops | bytes accessed | tf_op | source)
XLA Modules:
  0.0 77.7 jit_solution(3515318290085252167)
XLA Ops:
  0.0 1.4 %cut_shares.1 = (bf16[6,16,512]{2,1,0:T(8,128)(2,1)S(1)}, bf16[6,16,512]{2,1,0:T(8,128)(2,1)S(1)}, bf16[6,16,512]{2,1,0:T(8,128)(2,1)S(1)}, bf16[6,16,512]{2,1,0...) custom-call(bf16[6,128,512]{2,1,0:T(8,128)(2,1)} %refs_0_.1), custom_call_target="tpu_custom_call" | custom-call | flops 20000000000 | bytes 10000000 | tf_op jit(solution)/shard_map/cut_shares/pallas_call | solution.py:182
  1.4 3.4 %collective-permute-start = (bf16[6,16,512]{2,1,0:T(8,128)(2,1)S(1)}, bf16[6,16,512]{2,1,0:T(8,128)(2,1)S(1)}, u32[]{:S(2)}, u32[]{:S(2)}) collective-permute-start(bf16[6,16,512]{2,1,0:T(8,128)(2,1)S(1)} %get-tuple-element.59), channel_id=1, source_target_pairs={{0,28},{4,24},{8,20},{12,16},{16,12},{20,8},{24,4},{28,0},{1,29},{... | collective-permute-start | bytes 294920 | tf_op jit(solution)/shard_map/ppermute | solution.py:455
  4.9 0.5 collective-permute-start.2
  5.4 1.5 %collective-permute-start.3 = (bf16[6,16,512]{2,1,0:T(8,128)(2,1)S(1)}, bf16[6,16,512]{2,1,0:T(8,128)(2,1)S(1)}, u32[]{:S(2)}, u32[]{:S(2)}) collective-permute-start(bf16[6,16,512]{2,1,0:T(8,128)(2,1)S(1)} %get-tuple-element.62), channel_id=1, source_target_pairs={{0,12},{4,8},{8,4},{12,0},{16,28},{20,24},{24,20},{28,16},{1,13},{... | collective-permute-start | bytes 294920 | tf_op jit(solution)/shard_map/ppermute | solution.py:455
  6.9 0.5 collective-permute-start.4
  7.4 0.9 %collective-permute-start.5 = (bf16[6,16,512]{2,1,0:T(8,128)(2,1)S(1)}, bf16[6,16,512]{2,1,0:T(8,128)(2,1)S(1)}, u32[]{:S(2)}, u32[]{:S(2)}) collective-permute-start(bf16[6,16,512]{2,1,0:T(8,128)(2,1)S(1)} %get-tuple-element.64), channel_id=1, source_target_pairs={{0,20},{4,16},{8,28},{12,24},{16,4},{20,0},{24,12},{28,8},{1,21},{... | collective-permute-start | bytes 294920 | tf_op jit(solution)/shard_map/ppermute | solution.py:455
  8.4 3.1 %collective-permute-start.6 = (bf16[6,16,512]{2,1,0:T(8,128)(2,1)S(1)}, bf16[6,16,512]{2,1,0:T(8,128)(2,1)S(1)}, u32[]{:S(2)}, u32[]{:S(2)}) collective-permute-start(bf16[6,16,512]{2,1,0:T(8,128)(2,1)S(1)} %get-tuple-element.65), channel_id=1, source_target_pairs={{0,24},{4,28},{8,16},{12,20},{16,8},{20,12},{24,0},{28,4},{1,25},{... | collective-permute-start | bytes 294920 | tf_op jit(solution)/shard_map/ppermute | solution.py:455
  11.5 0.0 collective-permute-done.2.refs_2_
  11.5 0.0 collective-permute-start.1
  11.5 1.7 %collective-permute-done.3.refs_3_ = bf16[6,16,512]{2,1,0:T(8,128)(2,1)S(1)} collective-permute-done((bf16[6,16,512]{2,1,0:T(8,128)(2,1)S(1)}, bf16[6,16,512]{2,1,0:T(8,128)(2,1)S(1)}, u32[]{:S(2)}, u32[]{:S(2)}) %collective-permute-start.3) | collective-permute-done | bytes 98336 | tf_op jit(solution)/shard_map/ppermute | solution.py:455
  13.2 0.0 collective-permute-done.4.refs_4_
  13.2 1.8 %collective-permute-done.5.refs_5_ = bf16[6,16,512]{2,1,0:T(8,128)(2,1)S(1)} collective-permute-done((bf16[6,16,512]{2,1,0:T(8,128)(2,1)S(1)}, bf16[6,16,512]{2,1,0:T(8,128)(2,1)S(1)}, u32[]{:S(2)}, u32[]{:S(2)}) %collective-permute-start.5) | collective-permute-done | bytes 98336 | tf_op jit(solution)/shard_map/ppermute | solution.py:455
  15.1 0.0 copy-start
  15.1 0.0 copy-start.1
  15.1 0.0 copy-start.6
  15.1 0.0 copy-start.7
  15.1 0.0 copy-start.8
  15.1 6.0 %time_attention.1 = (bf16[6,16,512]{2,1,0:T(8,128)(2,1)S(1)}, bf16[6,16,512]{2,1,0:T(8,128)(2,1)S(1)}, bf16[6,16,512]{2,1,0:T(8,128)(2,1)S(1)}, bf16[6,16,512]{2...) custom-call(bf16[6,16,512]{2,1,0:T(8,128)(2,1)S(1)} %get-tuple-eleme, ...), custom_call_target="tpu_custom_call" | custom-call | flops 1610612736 | bytes 3670016 | tf_op jit(solution)/shard_map/time_attention/pallas_call | solution.py:259
  21.2 2.1 %collective-permute-start.7 = (bf16[6,16,512]{2,1,0:T(8,128)(2,1)S(1)}, bf16[6,16,512]{2,1,0:T(8,128)(2,1)S(1)}, u32[]{:S(2)}, u32[]{:S(2)}) collective-permute-start(bf16[6,16,512]{2,1,0:T(8,128)(2,1)S(1)} %get-tuple-element.77), channel_id=1, source_target_pairs={{0,28},{4,24},{8,20},{12,16},{16,12},{20,8},{24,4},{28,0},{1,29},{... | collective-permute-start | bytes 294920 | tf_op jit(solution)/shard_map/ppermute | solution.py:455
  23.3 0.6 collective-permute-start.9
  23.9 1.6 %collective-permute-start.10 = (bf16[6,16,512]{2,1,0:T(8,128)(2,1)S(1)}, bf16[6,16,512]{2,1,0:T(8,128)(2,1)S(1)}, u32[]{:S(2)}, u32[]{:S(2)}) collective-permute-start(bf16[6,16,512]{2,1,0:T(8,128)(2,1)S(1)} %get-tuple-element.80), channel_id=1, source_target_pairs={{0,12},{4,8},{8,4},{12,0},{16,28},{20,24},{24,20},{28,16},{1,13},{... | collective-permute-start | bytes 294920 | tf_op jit(solution)/shard_map/ppermute | solution.py:455
  25.4 0.5 collective-permute-start.11
  25.9 0.8 %collective-permute-start.12 = (bf16[6,16,512]{2,1,0:T(8,128)(2,1)S(1)}, bf16[6,16,512]{2,1,0:T(8,128)(2,1)S(1)}, u32[]{:S(2)}, u32[]{:S(2)}) collective-permute-start(bf16[6,16,512]{2,1,0:T(8,128)(2,1)S(1)} %get-tuple-element.82), channel_id=1, source_target_pairs={{0,20},{4,16},{8,28},{12,24},{16,4},{20,0},{24,12},{28,8},{1,21},{... | collective-permute-start | bytes 294920 | tf_op jit(solution)/shard_map/ppermute | solution.py:455
  26.8 0.0 collective-permute-done.7.refs_7_
  26.8 3.2 %collective-permute-start.13 = (bf16[6,16,512]{2,1,0:T(8,128)(2,1)S(1)}, bf16[6,16,512]{2,1,0:T(8,128)(2,1)S(1)}, u32[]{:S(2)}, u32[]{:S(2)}) collective-permute-start(bf16[6,16,512]{2,1,0:T(8,128)(2,1)S(1)} %get-tuple-element.83), channel_id=1, source_target_pairs={{0,24},{4,28},{8,16},{12,20},{16,8},{20,12},{24,0},{28,4},{1,25},{... | collective-permute-start | bytes 294920 | tf_op jit(solution)/shard_map/ppermute | solution.py:455
  30.0 1.8 %collective-permute-done.10.refs_3_ = bf16[6,16,512]{2,1,0:T(8,128)(2,1)S(1)} collective-permute-done((bf16[6,16,512]{2,1,0:T(8,128)(2,1)S(1)}, bf16[6,16,512]{2,1,0:T(8,128)(2,1)S(1)}, u32[]{:S(2)}, u32[]{:S(2)}) %collective-permute-start.10) | collective-permute-done | bytes 98336 | tf_op jit(solution)/shard_map/ppermute | solution.py:455
  31.7 0.0 collective-permute-done.11.refs_4_
  31.7 2.0 %collective-permute-done.13.refs_6_ = bf16[6,16,512]{2,1,0:T(8,128)(2,1)S(1)} collective-permute-done((bf16[6,16,512]{2,1,0:T(8,128)(2,1)S(1)}, bf16[6,16,512]{2,1,0:T(8,128)(2,1)S(1)}, u32[]{:S(2)}, u32[]{:S(2)}) %collective-permute-start.13) | collective-permute-done | bytes 98336 | tf_op jit(solution)/shard_map/ppermute | solution.py:455
  33.7 0.1 pack_steps.2
  33.8 3.0 %collective-permute-start.14 = (bf16[128,512]{1,0:T(8,128)(2,1)S(1)}, bf16[128,512]{1,0:T(8,128)(2,1)S(1)}, u32[]{:S(2)}, u32[]{:S(2)}) collective-permute-start(bf16[128,512]{1,0:T(8,128)(2,1)S(1)} %get-tuple-element.93), channel_id=1, source_target_pairs={{0,2},{1,3},{2,0},{3,1},{4,6},{5,7},{6,4},{7,5},{8,10},{9,11},{10,... | collective-permute-start | bytes 393224 | tf_op jit(solution)/shard_map/ppermute | solution.py:455
  36.8 1.6 %collective-permute-start.18 = (bf16[128,512]{1,0:T(8,128)(2,1)S(1)}, bf16[128,512]{1,0:T(8,128)(2,1)S(1)}, u32[]{:S(2)}, u32[]{:S(2)}) collective-permute-start(bf16[128,512]{1,0:T(8,128)(2,1)S(1)} %get-tuple-element.99), channel_id=1, source_target_pairs={{0,1},{1,0},{2,3},{3,2},{4,5},{5,4},{6,7},{7,6},{8,9},{9,8},{10,11... | collective-permute-start | bytes 393224 | tf_op jit(solution)/shard_map/ppermute | solution.py:455
  38.3 5.7 %collective-permute-done.14.refs_8_.refs_2_ = bf16[128,512]{1,0:T(8,128)(2,1)S(1)} collective-permute-done((bf16[128,512]{1,0:T(8,128)(2,1)S(1)}, bf16[128,512]{1,0:T(8,128)(2,1)S(1)}, u32[]{:S(2)}, u32[]{:S(2)}) %collective-permute-start.14) | collective-permute-done | bytes 131104 | tf_op jit(solution)/shard_map/ppermute | solution.py:455
  44.1 2.6 %collective-permute-start.15 = (bf16[128,512]{1,0:T(8,128)(2,1)S(1)}, bf16[128,512]{1,0:T(8,128)(2,1)S(1)}, u32[]{:S(2)}, u32[]{:S(2)}) collective-permute-start(bf16[128,512]{1,0:T(8,128)(2,1)S(1)} %get-tuple-element.95), channel_id=1, source_target_pairs={{0,1},{3,2},{4,5},{7,6},{8,9},{11,10},{12,13},{15,14},{16,17},{19,... | collective-permute-start | bytes 393224 | tf_op jit(solution)/shard_map/ppermute | solution.py:455
  46.7 1.3 %collective-permute-start.16 = (bf16[128,512]{1,0:T(8,128)(2,1)S(1)}, bf16[128,512]{1,0:T(8,128)(2,1)S(1)}, u32[]{:S(2)}, u32[]{:S(2)}) collective-permute-start(bf16[128,512]{1,0:T(8,128)(2,1)S(1)} %get-tuple-element.96), channel_id=1, source_target_pairs={{0,2},{3,1},{4,6},{7,5},{8,10},{11,9},{12,14},{15,13},{16,18},{19,... | collective-permute-start | bytes 393224 | tf_op jit(solution)/shard_map/ppermute | solution.py:455
  48.0 0.8 %collective-permute-start.17 = (bf16[128,512]{1,0:T(8,128)(2,1)S(1)}, bf16[128,512]{1,0:T(8,128)(2,1)S(1)}, u32[]{:S(2)}, u32[]{:S(2)}) collective-permute-start(bf16[128,512]{1,0:T(8,128)(2,1)S(1)} %get-tuple-element.97), channel_id=1, source_target_pairs={{1,2},{2,1},{5,6},{6,5},{9,10},{10,9},{13,14},{14,13},{17,18},{18,... | collective-permute-start | bytes 393224 | tf_op jit(solution)/shard_map/ppermute | solution.py:455
  48.9 7.2 %agent_step.2 = (bf16[128,512]{1,0:T(8,128)(2,1)S(1)}, bf16[128,512]{1,0:T(8,128)(2,1)S(1)}, bf16[128,512]{1,0:T(8,128)(2,1)S(1)}, bf16[128,512]{1,0:T(8,128)(2,1)S(1)}) custom-call(bf16[128,512]{1,0:T(8,128)(2,1)S(1)} %get-tuple-element.98.refs_0_, bf16[128,512]{1,0:T(8,128)(2,1)S(1)} %collective-permute-done.18.refs_1_, ...), custom_call_target="tpu_custom_call" | custom-call | flops 3758096384 | bytes 4194304 | tf_op jit(solution)/shard_map/agent_step/pallas_call | solution.py:364
  56.1 1.2 %collective-permute-start.23 = (bf16[128,512]{1,0:T(8,128)(2,1)S(1)}, bf16[128,512]{1,0:T(8,128)(2,1)S(1)}, u32[]{:S(2)}, u32[]{:S(2)}) collective-permute-start(bf16[128,512]{1,0:T(8,128)(2,1)S(1)} %get-tuple-element.106), channel_id=1, source_target_pairs={{0,1},{1,0},{2,3},{3,2},{4,5},{5,4},{6,7},{7,6},{8,9},{9,8},{10,11... | collective-permute-start | bytes 393224 | tf_op jit(solution)/shard_map/ppermute | solution.py:455
  57.3 2.3 %collective-permute-start.24 = (bf16[128,512]{1,0:T(8,128)(2,1)S(1)}, bf16[128,512]{1,0:T(8,128)(2,1)S(1)}, u32[]{:S(2)}, u32[]{:S(2)}) collective-permute-start(bf16[128,512]{1,0:T(8,128)(2,1)S(1)} %get-tuple-element.107), channel_id=1, source_target_pairs={{0,2},{1,3},{2,0},{3,1},{4,6},{5,7},{6,4},{7,5},{8,10},{9,11},{10,... | collective-permute-start | bytes 393224 | tf_op jit(solution)/shard_map/ppermute | solution.py:455
  59.6 1.4 %collective-permute-start.25 = (bf16[128,512]{1,0:T(8,128)(2,1)S(1)}, bf16[128,512]{1,0:T(8,128)(2,1)S(1)}, u32[]{:S(2)}, u32[]{:S(2)}) collective-permute-start(bf16[128,512]{1,0:T(8,128)(2,1)S(1)} %get-tuple-element.108), channel_id=1, source_target_pairs={{0,3},{1,2},{2,1},{3,0},{4,7},{5,6},{6,5},{7,4},{8,11},{9,10},{10,... | collective-permute-start | bytes 393224 | tf_op jit(solution)/shard_map/ppermute | solution.py:455
  61.0 1.3 %collective-permute-start.20 = (bf16[128,512]{1,0:T(8,128)(2,1)S(1)}, bf16[128,512]{1,0:T(8,128)(2,1)S(1)}, u32[]{:S(2)}, u32[]{:S(2)}) collective-permute-start(bf16[128,512]{1,0:T(8,128)(2,1)S(1)} %get-tuple-element.103), channel_id=1, source_target_pairs={{1,0},{2,3},{5,4},{6,7},{9,8},{10,11},{13,12},{14,15},{17,16},{18,... | collective-permute-start | bytes 393224 | tf_op jit(solution)/shard_map/ppermute | solution.py:523
  62.3 1.3 %collective-permute-start.21 = (bf16[128,512]{1,0:T(8,128)(2,1)S(1)}, bf16[128,512]{1,0:T(8,128)(2,1)S(1)}, u32[]{:S(2)}, u32[]{:S(2)}) collective-permute-start(bf16[128,512]{1,0:T(8,128)(2,1)S(1)} %get-tuple-element.104), channel_id=1, source_target_pairs={{1,3},{2,0},{5,7},{6,4},{9,11},{10,8},{13,15},{14,12},{17,19},{18,... | collective-permute-start | bytes 393224 | tf_op jit(solution)/shard_map/ppermute | solution.py:523
  63.6 0.3 collective-permute-done.23.refs_1_
  63.9 0.7 collective-permute-start.22
  64.6 5.3 %collective-permute-done.25.refs_3_ = bf16[128,512]{1,0:T(8,128)(2,1)S(1)} collective-permute-done((bf16[128,512]{1,0:T(8,128)(2,1)S(1)}, bf16[128,512]{1,0:T(8,128)(2,1)S(1)}, u32[]{:S(2)}, u32[]{:S(2)}) %collective-permute-start.25) | collective-permute-done | bytes 131104 | tf_op jit(solution)/shard_map/ppermute | solution.py:455
  69.9 0.8 %place_steps.1.refs_4_ = bf16[6,128,512]{2,1,0:T(8,128)(2,1)} custom-call(bf16[128,512]{1,0:T(8,128)(2,1)S(1)} %get-tuple-element.101.refs_10_.refs_0_, bf16[128,512]{1,0:T(8,128)(2,1)S(1)} %collective-permute-done.23.refs_1_, bf16[128,512]{1,0:T(8,128)(2,1)S(1)} %collective-permute-done.24.refs_2_, bf16[128,512]{1,0:T(8,128)(2,1)S(1)} %collective-permute-done.25.refs_3_), custom_call_target="tpu_custom_call" | custom-call | tf_op jit(solution)/shard_map/place_steps/pallas_call | solution.py:423
  70.7 4.5 %collective-permute-done.20.refs_1_ = bf16[128,512]{1,0:T(8,128)(2,1)S(1)} collective-permute-done((bf16[128,512]{1,0:T(8,128)(2,1)S(1)}, bf16[128,512]{1,0:T(8,128)(2,1)S(1)}, u32[]{:S(2)}, u32[]{:S(2)}) %collective-permute-start.20) | collective-permute-done | bytes 131104 | tf_op jit(solution)/shard_map/ppermute | solution.py:523
  75.3 1.5 %collective-permute-done.21.refs_2_ = bf16[128,512]{1,0:T(8,128)(2,1)S(1)} collective-permute-done((bf16[128,512]{1,0:T(8,128)(2,1)S(1)}, bf16[128,512]{1,0:T(8,128)(2,1)S(1)}, u32[]{:S(2)}, u32[]{:S(2)}) %collective-permute-start.21) | collective-permute-done | bytes 131104 | tf_op jit(solution)/shard_map/ppermute | solution.py:523
  76.8 0.7 place_extra.1
  (30 shorter events, 0.1 us)
Async XLA Ops:
  0.0 15.1 %copy-start.5 = (bf16[512,512]{1,0:T(8,128)(2,1)S(1)}, bf16[512,512]{1,0:T(8,128)(2,1)}, u32[]{:S(2)}) copy-start(bf16[512,512]{1,0:T(8,128)(2,1)} %refs_11_.1) | copy-start | bytes 1572868
  0.0 15.1 %copy-start.4 = (bf16[512,512]{1,0:T(8,128)(2,1)S(1)}, bf16[512,512]{1,0:T(8,128)(2,1)}, u32[]{:S(2)}) copy-start(bf16[512,512]{1,0:T(8,128)(2,1)} %refs_10_.1) | copy-start | bytes 1572868
  0.0 15.1 %copy-start.3 = (bf16[512,512]{1,0:T(8,128)(2,1)S(1)}, bf16[512,512]{1,0:T(8,128)(2,1)}, u32[]{:S(2)}) copy-start(bf16[512,512]{1,0:T(8,128)(2,1)} %refs_9_.3) | copy-start | bytes 1572868
  0.0 15.1 %copy-start.2 = (bf16[512,512]{1,0:T(8,128)(2,1)S(1)}, bf16[512,512]{1,0:T(8,128)(2,1)}, u32[]{:S(2)}) copy-start(bf16[512,512]{1,0:T(8,128)(2,1)} %refs_8_.3) | copy-start | bytes 1572868
  1.4 6.9 %collective-permute-start = (bf16[6,16,512]{2,1,0:T(8,128)(2,1)S(1)}, bf16[6,16,512]{2,1,0:T(8,128)(2,1)S(1)}, u32[]{:S(2)}, u32[]{:S(2)}) collective-permute-start(bf16[6,16,512]{2,1,0:T(8,128)(2,1)S(1)} %get-tuple-element.59), channel_id=1, source_target_pairs={{0,28},{4,24},{8,20},{12,16},{16,12},{20,8},{24,4},{28,0},{1,29},{... | collective-permute-start | bytes 294920 | tf_op jit(solution)/shard_map/ppermute | solution.py:455
  4.9 6.6 %collective-permute-start.2 = (bf16[6,16,512]{2,1,0:T(8,128)(2,1)S(1)}, bf16[6,16,512]{2,1,0:T(8,128)(2,1)S(1)}, u32[]{:S(2)}, u32[]{:S(2)}) collective-permute-start(bf16[6,16,512]{2,1,0:T(8,128)(2,1)S(1)} %get-tuple-element.61), channel_id=1, source_target_pairs={{0,8},{4,12},{8,0},{12,4},{16,24},{20,28},{24,16},{28,20},{1,9},{5... | collective-permute-start | bytes 294920 | tf_op jit(solution)/shard_map/ppermute | solution.py:455
  5.4 7.8 %collective-permute-start.3 = (bf16[6,16,512]{2,1,0:T(8,128)(2,1)S(1)}, bf16[6,16,512]{2,1,0:T(8,128)(2,1)S(1)}, u32[]{:S(2)}, u32[]{:S(2)}) collective-permute-start(bf16[6,16,512]{2,1,0:T(8,128)(2,1)S(1)} %get-tuple-element.62), channel_id=1, source_target_pairs={{0,12},{4,8},{8,4},{12,0},{16,28},{20,24},{24,20},{28,16},{1,13},{... | collective-permute-start | bytes 294920 | tf_op jit(solution)/shard_map/ppermute | solution.py:455
  6.9 6.3 %collective-permute-start.4 = (bf16[6,16,512]{2,1,0:T(8,128)(2,1)S(1)}, bf16[6,16,512]{2,1,0:T(8,128)(2,1)S(1)}, u32[]{:S(2)}, u32[]{:S(2)}) collective-permute-start(bf16[6,16,512]{2,1,0:T(8,128)(2,1)S(1)} %get-tuple-element.63), channel_id=1, source_target_pairs={{0,16},{4,20},{8,24},{12,28},{16,0},{20,4},{24,8},{28,12},{1,17},{... | collective-permute-start | bytes 294920 | tf_op jit(solution)/shard_map/ppermute | solution.py:455
  7.4 7.6 %collective-permute-start.5 = (bf16[6,16,512]{2,1,0:T(8,128)(2,1)S(1)}, bf16[6,16,512]{2,1,0:T(8,128)(2,1)S(1)}, u32[]{:S(2)}, u32[]{:S(2)}) collective-permute-start(bf16[6,16,512]{2,1,0:T(8,128)(2,1)S(1)} %get-tuple-element.64), channel_id=1, source_target_pairs={{0,20},{4,16},{8,28},{12,24},{16,4},{20,0},{24,12},{28,8},{1,21},{... | collective-permute-start | bytes 294920 | tf_op jit(solution)/shard_map/ppermute | solution.py:455
  8.4 6.7 %collective-permute-start.6 = (bf16[6,16,512]{2,1,0:T(8,128)(2,1)S(1)}, bf16[6,16,512]{2,1,0:T(8,128)(2,1)S(1)}, u32[]{:S(2)}, u32[]{:S(2)}) collective-permute-start(bf16[6,16,512]{2,1,0:T(8,128)(2,1)S(1)} %get-tuple-element.65), channel_id=1, source_target_pairs={{0,24},{4,28},{8,16},{12,20},{16,8},{20,12},{24,0},{28,4},{1,25},{... | collective-permute-start | bytes 294920 | tf_op jit(solution)/shard_map/ppermute | solution.py:455
  11.5 3.5 %collective-permute-start.1 = (bf16[6,16,512]{2,1,0:T(8,128)(2,1)S(1)}, bf16[6,16,512]{2,1,0:T(8,128)(2,1)S(1)}, u32[]{:S(2)}, u32[]{:S(2)}) collective-permute-start(bf16[6,16,512]{2,1,0:T(8,128)(2,1)S(1)} %get-tuple-element.60), channel_id=1, source_target_pairs={{0,4},{4,0},{8,12},{12,8},{16,20},{20,16},{24,28},{28,24},{1,5},{5... | collective-permute-start | bytes 294920 | tf_op jit(solution)/shard_map/ppermute | solution.py:455
  15.1 33.8 %copy-start = (bf16[512,2048]{1,0:T(8,128)(2,1)S(1)}, bf16[512,2048]{1,0:T(8,128)(2,1)}, u32[]{:S(2)}) copy-start(bf16[512,2048]{1,0:T(8,128)(2,1)} %refs_8_.5) | copy-start | bytes 6291460
  15.1 33.8 %copy-start.1 = (bf16[2048,512]{1,0:T(8,128)(2,1)S(1)}, bf16[2048,512]{1,0:T(8,128)(2,1)}, u32[]{:S(2)}) copy-start(bf16[2048,512]{1,0:T(8,128)(2,1)} %refs_9_.5) | copy-start | bytes 6291460
  15.1 33.8 %copy-start.6 = (bf16[512,512]{1,0:T(8,128)(2,1)S(1)}, bf16[512,512]{1,0:T(8,128)(2,1)}, u32[]{:S(2)}) copy-start(bf16[512,512]{1,0:T(8,128)(2,1)} %refs_4_.3) | copy-start | bytes 1572868
  15.1 33.8 %copy-start.7 = (bf16[512,512]{1,0:T(8,128)(2,1)S(1)}, bf16[512,512]{1,0:T(8,128)(2,1)}, u32[]{:S(2)}) copy-start(bf16[512,512]{1,0:T(8,128)(2,1)} %refs_5_.3) | copy-start | bytes 1572868
  15.1 33.8 %copy-start.8 = (bf16[512,512]{1,0:T(8,128)(2,1)S(1)}, bf16[512,512]{1,0:T(8,128)(2,1)}, u32[]{:S(2)}) copy-start(bf16[512,512]{1,0:T(8,128)(2,1)} %refs_6_.3) | copy-start | bytes 1572868
  21.2 5.6 %collective-permute-start.7 = (bf16[6,16,512]{2,1,0:T(8,128)(2,1)S(1)}, bf16[6,16,512]{2,1,0:T(8,128)(2,1)S(1)}, u32[]{:S(2)}, u32[]{:S(2)}) collective-permute-start(bf16[6,16,512]{2,1,0:T(8,128)(2,1)S(1)} %get-tuple-element.77), channel_id=1, source_target_pairs={{0,28},{4,24},{8,20},{12,16},{16,12},{20,8},{24,4},{28,0},{1,29},{... | collective-permute-start | bytes 294920 | tf_op jit(solution)/shard_map/ppermute | solution.py:455
  23.3 6.7 %collective-permute-start.9 = (bf16[6,16,512]{2,1,0:T(8,128)(2,1)S(1)}, bf16[6,16,512]{2,1,0:T(8,128)(2,1)S(1)}, u32[]{:S(2)}, u32[]{:S(2)}) collective-permute-start(bf16[6,16,512]{2,1,0:T(8,128)(2,1)S(1)} %get-tuple-element.79), channel_id=1, source_target_pairs={{0,8},{4,12},{8,0},{12,4},{16,24},{20,28},{24,16},{28,20},{1,9},{5... | collective-permute-start | bytes 294920 | tf_op jit(solution)/shard_map/ppermute | solution.py:455
  23.9 7.9 %collective-permute-start.10 = (bf16[6,16,512]{2,1,0:T(8,128)(2,1)S(1)}, bf16[6,16,512]{2,1,0:T(8,128)(2,1)S(1)}, u32[]{:S(2)}, u32[]{:S(2)}) collective-permute-start(bf16[6,16,512]{2,1,0:T(8,128)(2,1)S(1)} %get-tuple-element.80), channel_id=1, source_target_pairs={{0,12},{4,8},{8,4},{12,0},{16,28},{20,24},{24,20},{28,16},{1,13},{... | collective-permute-start | bytes 294920 | tf_op jit(solution)/shard_map/ppermute | solution.py:455
  25.4 6.3 %collective-permute-start.11 = (bf16[6,16,512]{2,1,0:T(8,128)(2,1)S(1)}, bf16[6,16,512]{2,1,0:T(8,128)(2,1)S(1)}, u32[]{:S(2)}, u32[]{:S(2)}) collective-permute-start(bf16[6,16,512]{2,1,0:T(8,128)(2,1)S(1)} %get-tuple-element.81), channel_id=1, source_target_pairs={{0,16},{4,20},{8,24},{12,28},{16,0},{20,4},{24,8},{28,12},{1,17},{... | collective-permute-start | bytes 294920 | tf_op jit(solution)/shard_map/ppermute | solution.py:455
  25.9 5.8 %collective-permute-start.12 = (bf16[6,16,512]{2,1,0:T(8,128)(2,1)S(1)}, bf16[6,16,512]{2,1,0:T(8,128)(2,1)S(1)}, u32[]{:S(2)}, u32[]{:S(2)}) collective-permute-start(bf16[6,16,512]{2,1,0:T(8,128)(2,1)S(1)} %get-tuple-element.82), channel_id=1, source_target_pairs={{0,20},{4,16},{8,28},{12,24},{16,4},{20,0},{24,12},{28,8},{1,21},{... | collective-permute-start | bytes 294920 | tf_op jit(solution)/shard_map/ppermute | solution.py:455
  26.8 6.9 %collective-permute-start.13 = (bf16[6,16,512]{2,1,0:T(8,128)(2,1)S(1)}, bf16[6,16,512]{2,1,0:T(8,128)(2,1)S(1)}, u32[]{:S(2)}, u32[]{:S(2)}) collective-permute-start(bf16[6,16,512]{2,1,0:T(8,128)(2,1)S(1)} %get-tuple-element.83), channel_id=1, source_target_pairs={{0,24},{4,28},{8,16},{12,20},{16,8},{20,12},{24,0},{28,4},{1,25},{... | collective-permute-start | bytes 294920 | tf_op jit(solution)/shard_map/ppermute | solution.py:455
  30.0 3.7 %collective-permute-start.8 = (bf16[6,16,512]{2,1,0:T(8,128)(2,1)S(1)}, bf16[6,16,512]{2,1,0:T(8,128)(2,1)S(1)}, u32[]{:S(2)}, u32[]{:S(2)}) collective-permute-start(bf16[6,16,512]{2,1,0:T(8,128)(2,1)S(1)} %get-tuple-element.78), channel_id=1, source_target_pairs={{0,4},{4,0},{8,12},{12,8},{16,20},{20,16},{24,28},{28,24},{1,5},{5... | collective-permute-start | bytes 294920 | tf_op jit(solution)/shard_map/ppermute | solution.py:455
  33.8 10.3 %collective-permute-start.14 = (bf16[128,512]{1,0:T(8,128)(2,1)S(1)}, bf16[128,512]{1,0:T(8,128)(2,1)S(1)}, u32[]{:S(2)}, u32[]{:S(2)}) collective-permute-start(bf16[128,512]{1,0:T(8,128)(2,1)S(1)} %get-tuple-element.93), channel_id=1, source_target_pairs={{0,2},{1,3},{2,0},{3,1},{4,6},{5,7},{6,4},{7,5},{8,10},{9,11},{10,... | collective-permute-start | bytes 393224 | tf_op jit(solution)/shard_map/ppermute | solution.py:455
  36.8 12.1 %collective-permute-start.18 = (bf16[128,512]{1,0:T(8,128)(2,1)S(1)}, bf16[128,512]{1,0:T(8,128)(2,1)S(1)}, u32[]{:S(2)}, u32[]{:S(2)}) collective-permute-start(bf16[128,512]{1,0:T(8,128)(2,1)S(1)} %get-tuple-element.99), channel_id=1, source_target_pairs={{0,1},{1,0},{2,3},{3,2},{4,5},{5,4},{6,7},{7,6},{8,9},{9,8},{10,11... | collective-permute-start | bytes 393224 | tf_op jit(solution)/shard_map/ppermute | solution.py:455
  38.3 10.5 %collective-permute-start.19 = (bf16[128,512]{1,0:T(8,128)(2,1)S(1)}, bf16[128,512]{1,0:T(8,128)(2,1)S(1)}, u32[]{:S(2)}, u32[]{:S(2)}) collective-permute-start(bf16[128,512]{1,0:T(8,128)(2,1)S(1)} %get-tuple-element.100), channel_id=1, source_target_pairs={{0,3},{1,2},{2,1},{3,0},{4,7},{5,6},{6,5},{7,4},{8,11},{9,10},{10,... | collective-permute-start | bytes 393224 | tf_op jit(solution)/shard_map/ppermute | solution.py:455
  44.1 15.6 %collective-permute-start.15 = (bf16[128,512]{1,0:T(8,128)(2,1)S(1)}, bf16[128,512]{1,0:T(8,128)(2,1)S(1)}, u32[]{:S(2)}, u32[]{:S(2)}) collective-permute-start(bf16[128,512]{1,0:T(8,128)(2,1)S(1)} %get-tuple-element.95), channel_id=1, source_target_pairs={{0,1},{3,2},{4,5},{7,6},{8,9},{11,10},{12,13},{15,14},{16,17},{19,... | collective-permute-start | bytes 393224 | tf_op jit(solution)/shard_map/ppermute | solution.py:455
  46.7 14.3 %collective-permute-start.16 = (bf16[128,512]{1,0:T(8,128)(2,1)S(1)}, bf16[128,512]{1,0:T(8,128)(2,1)S(1)}, u32[]{:S(2)}, u32[]{:S(2)}) collective-permute-start(bf16[128,512]{1,0:T(8,128)(2,1)S(1)} %get-tuple-element.96), channel_id=1, source_target_pairs={{0,2},{3,1},{4,6},{7,5},{8,10},{11,9},{12,14},{15,13},{16,18},{19,... | collective-permute-start | bytes 393224 | tf_op jit(solution)/shard_map/ppermute | solution.py:455
  48.0 13.0 %collective-permute-start.17 = (bf16[128,512]{1,0:T(8,128)(2,1)S(1)}, bf16[128,512]{1,0:T(8,128)(2,1)S(1)}, u32[]{:S(2)}, u32[]{:S(2)}) collective-permute-start(bf16[128,512]{1,0:T(8,128)(2,1)S(1)} %get-tuple-element.97), channel_id=1, source_target_pairs={{1,2},{2,1},{5,6},{6,5},{9,10},{10,9},{13,14},{14,13},{17,18},{18,... | collective-permute-start | bytes 393224 | tf_op jit(solution)/shard_map/ppermute | solution.py:455
  56.1 7.8 %collective-permute-start.23 = (bf16[128,512]{1,0:T(8,128)(2,1)S(1)}, bf16[128,512]{1,0:T(8,128)(2,1)S(1)}, u32[]{:S(2)}, u32[]{:S(2)}) collective-permute-start(bf16[128,512]{1,0:T(8,128)(2,1)S(1)} %get-tuple-element.106), channel_id=1, source_target_pairs={{0,1},{1,0},{2,3},{3,2},{4,5},{5,4},{6,7},{7,6},{8,9},{9,8},{10,11... | collective-permute-start | bytes 393224 | tf_op jit(solution)/shard_map/ppermute | solution.py:455
  57.3 7.3 %collective-permute-start.24 = (bf16[128,512]{1,0:T(8,128)(2,1)S(1)}, bf16[128,512]{1,0:T(8,128)(2,1)S(1)}, u32[]{:S(2)}, u32[]{:S(2)}) collective-permute-start(bf16[128,512]{1,0:T(8,128)(2,1)S(1)} %get-tuple-element.107), channel_id=1, source_target_pairs={{0,2},{1,3},{2,0},{3,1},{4,6},{5,7},{6,4},{7,5},{8,10},{9,11},{10,... | collective-permute-start | bytes 393224 | tf_op jit(solution)/shard_map/ppermute | solution.py:455
  59.6 10.3 %collective-permute-start.25 = (bf16[128,512]{1,0:T(8,128)(2,1)S(1)}, bf16[128,512]{1,0:T(8,128)(2,1)S(1)}, u32[]{:S(2)}, u32[]{:S(2)}) collective-permute-start(bf16[128,512]{1,0:T(8,128)(2,1)S(1)} %get-tuple-element.108), channel_id=1, source_target_pairs={{0,3},{1,2},{2,1},{3,0},{4,7},{5,6},{6,5},{7,4},{8,11},{9,10},{10,... | collective-permute-start | bytes 393224 | tf_op jit(solution)/shard_map/ppermute | solution.py:455
  61.0 14.2 %collective-permute-start.20 = (bf16[128,512]{1,0:T(8,128)(2,1)S(1)}, bf16[128,512]{1,0:T(8,128)(2,1)S(1)}, u32[]{:S(2)}, u32[]{:S(2)}) collective-permute-start(bf16[128,512]{1,0:T(8,128)(2,1)S(1)} %get-tuple-element.103), channel_id=1, source_target_pairs={{1,0},{2,3},{5,4},{6,7},{9,8},{10,11},{13,12},{14,15},{17,16},{18,... | collective-permute-start | bytes 393224 | tf_op jit(solution)/shard_map/ppermute | solution.py:523
  62.3 14.5 %collective-permute-start.21 = (bf16[128,512]{1,0:T(8,128)(2,1)S(1)}, bf16[128,512]{1,0:T(8,128)(2,1)S(1)}, u32[]{:S(2)}, u32[]{:S(2)}) collective-permute-start(bf16[128,512]{1,0:T(8,128)(2,1)S(1)} %get-tuple-element.104), channel_id=1, source_target_pairs={{1,3},{2,0},{5,7},{6,4},{9,11},{10,8},{13,15},{14,12},{17,19},{18,... | collective-permute-start | bytes 393224 | tf_op jit(solution)/shard_map/ppermute | solution.py:523
  63.9 12.9 %collective-permute-start.22 = (bf16[128,512]{1,0:T(8,128)(2,1)S(1)}, bf16[128,512]{1,0:T(8,128)(2,1)S(1)}, u32[]{:S(2)}, u32[]{:S(2)}) collective-permute-start(bf16[128,512]{1,0:T(8,128)(2,1)S(1)} %get-tuple-element.105), channel_id=1, source_target_pairs={{1,2},{2,1},{5,6},{6,5},{9,10},{10,9},{13,14},{14,13},{17,18},{18,... | collective-permute-start | bytes 393224 | tf_op jit(solution)/shard_map/ppermute | solution.py:523

commit v5 on v4

--- a/solution.py
+++ b/solution.py
@@ -194,7 +194,7 @@
 def time_kernel(size, *refs):
     pieces, weights = refs[:size], refs[size : size + 4]
     outs = refs[size + 4 : 2 * size + 4]
-    wide, normed, query, key_e, key_o, value_e, value_o, mixed = refs[2 * size + 4 : 2 * size + 12]
+    wide, normed, query, keys, values, mixed = refs[2 * size + 4 :]
     w_query, w_key, w_value, w_out = weights
     steps, agents, features = pieces[0].shape
     rows = steps * agents
@@ -210,33 +210,48 @@
         at = pl.ds(agent, total_steps, stride=agents)
         own = jnp.concatenate([wide[c, at, :] for c in range(len(lanes_of))], axis=1)
         normed[pl.ds(agent * total_steps, total_steps), :] = norm_of(own)
+    group = 2 * total_steps
+    span = -(-group // 128) * 128
+    head_size = features // HEADS
+    factor = math.log2(math.e) * head_size**-0.5
     query[...] = project(normed[...], w_query[...])
-    split_heads(project(normed[...], w_key[...]), key_e, key_o)
-    split_heads(project(normed[...], w_value[...]), value_e, value_o, True)
-
-    group = 2 * total_steps
-    row = lax.broadcasted_iota(jnp.int32, (group, group), 0)
-    column = lax.broadcasted_iota(jnp.int32, (group, group), 1)
+    key = project(normed[...], w_key[...])
+    value = project(normed[...], w_value[...])
+    even = lax.broadcasted_iota(jnp.int32, (group, features), 1) % (2 * head_size) < head_size
+    zero = jnp.zeros((group, features), jnp.bfloat16)
+    spare = jnp.zeros((span - group, features), jnp.bfloat16)
+    for g in range(agents // 2):
+        rows_in = slice(g * group, (g + 1) * group)
+        for h, mine in enumerate((even, jnp.logical_not(even))):
+            at = (2 * g + h) * span
+            keys[at : at + group, :] = jnp.where(mine, key[rows_in], zero)
+            values[at : at + group, :] = jnp.where(mine, value[rows_in], zero)
+            for target in (keys, values):
+                target[at + group : at + span, :] = spare
+    row = lax.broadcasted_iota(jnp.int32, (group, span), 0)
+    column = lax.broadcasted_iota(jnp.int32, (group, span), 1)
     same = (row >= total_steps) == (column >= total_steps)
     bias = jnp.where(jnp.logical_and(same, column <= row), 0.0, negative_floor)
-    head_size = features // HEADS
-    factor = math.log2(math.e) * head_size**-0.5
-
-    def one_group(g, carry):
-        at = pl.ds(pl.multiple_of(g * group, group), group)
+    second_rows = lax.broadcasted_iota(jnp.int32, (2 * span, 2 * head_size), 0) >= span
+    second_lanes = lax.broadcasted_iota(jnp.int32, (2 * span, 2 * head_size), 1) >= head_size
+    counts = (second_rows == second_lanes).astype(jnp.bfloat16)
+    for g in range(agents // 2):
+        at, both = pl.ds(g * group, group), pl.ds(2 * g * span, 2 * span)
         for pair in range(HEADS // 2):
             lanes = pl.ds(pair * 2 * head_size, 2 * head_size)
-            double = pl.ds(pair * 4 * head_size, 4 * head_size)
-            mixed[at, lanes] = pair_attention(
-                query[at, lanes],
-                (key_e[at, lanes], key_o[at, lanes]),
-                (value_e[at, double], value_o[at, double]),
-                factor,
-                bias,
+            scores = lax.dot_general(
+                query[at, lanes], keys[both, lanes], NT, preferred_element_type=jnp.float32
             )
-        return carry
-
-    lax.fori_loop(0, agents // 2, one_group, 0, unroll=True)
+            weights = []
+            for h in range(2):
+                mine = scores[:, h * span : (h + 1) * span] + bias
+                largest = jnp.max(mine, axis=-1, keepdims=True)
+                weights.append(jnp.exp2((mine - largest) * factor).astype(jnp.bfloat16))
+            weights = jnp.concatenate(weights, axis=1)
+            value = jnp.concatenate([values[both, lanes], counts], axis=1)
+            sums = jnp.dot(weights, value, preferred_element_type=jnp.float32)
+            wide_lanes = 2 * head_size
+            mixed[at, lanes] = (sums[:, :wide_lanes] / sums[:, wide_lanes:]).astype(jnp.bfloat16)
     added = jnp.dot(mixed[...], w_out[...], preferred_element_type=jnp.float32)
     for agent in range(agents):
         at = pl.ds(agent, total_steps, stride=agents)
@@ -262,8 +277,8 @@
         in_specs=[spec(VMEM)] * (size + 4),
         out_specs=[spec(VMEM)] * size,
         scratch_shapes=[VMEM((features // 128, rows, 128), jnp.float32)]
-        + [VMEM((rows, features), kind)] * 4
-        + [VMEM((rows, 2 * features), kind)] * 2
+        + [VMEM((rows, features), kind)] * 2
+        + [VMEM((agents * (-(-2 * steps * size // 128) * 128), features), kind)] * 2
         + [VMEM((rows, features), kind)],
         compiler_params=pltpu.CompilerParams(vmem_limit_bytes=24 * 2**20),
         cost_estimate=pl.CostEstimate(
@@ -385,7 +400,7 @@
 
 
 def place_kernel(*refs):
-    sources, out, sems = refs[:4], refs[4], refs[5]
+    sources, out, sems = [refs[k] for k in (0, 1, 2, 3)], refs[4], refs[5]
     plane = lax.axis_index("agent")
     copies = [
         pltpu.make_async_copy(source, out.at[jnp.bitwise_xor(plane, k)], sems.at[k])
@@ -398,7 +413,7 @@
 
 
 def place_extra_kernel(*refs):
-    sources, out, sems = refs[:4], refs[5], refs[6]
+    sources, out, sems = [refs[k] for k in (0, 1, 2, 3)], refs[5], refs[6]
     plane = lax.axis_index("agent")
     middle = jnp.logical_or(plane == 1, plane == 2)
     low = plane // 2
@@ -428,7 +443,7 @@
         scratch_shapes=[pltpu.SemaphoreType.DMA((4,))],
         compiler_params=pltpu.CompilerParams(vmem_limit_bytes=4 * 2**20),
         name="place_steps",
-    )(*whole)
+    )(*[whole[k] for k in (0, 1, 2, 3)])
     return pl.pallas_call(
         place_extra_kernel,
         out_shape=shape,
@@ -438,7 +453,7 @@
         scratch_shapes=[pltpu.SemaphoreType.DMA((2,))],
         compiler_params=pltpu.CompilerParams(vmem_limit_bytes=4 * 2**20),
         name="place_extra",
-    )(*extra, begun)
+    )(*[extra[k] for k in (0, 1, 2, 3)], begun)
 
 
 def xor_pairs(size, k, targets=None):
@@ -457,7 +472,7 @@
 
 
 def together(parts):
-    return lax.optimization_barrier(tuple(parts))
+    return lax.optimization_barrier(tuple(parts[::-1]))[::-1]
 
 
 def picked(plane, values):

time: 77.9 us -> 76.6 us (0.983)
  starting transfers between devices: 36.3 us -> 32.6 us
  waiting for transfers between devices: 24.6 us -> 28.2 us
  Pallas kernels: 16.3 us -> 15.2 us
    ppermute x23, starting transfers between devices: 33 us -> 29.3 us  [exchange(): moved[k] = lax.ppermute(part, axis, xor_pairs(size, k, targets))]
    ppermute x23, waiting for transfers between devices: 18.6 us -> 22 us  [exchange(): moved[k] = lax.ppermute(part, axis, xor_pairs(size, k, targets))]
    pallas_call x1, Pallas kernels: 6.04 us -> 4.9 us  [time_stage(): pl.pallas_call(functools.partial(time_kernel, size), out_shape=[jax.Shape...]
  transfers between devices with their start and end apart: 26 -> 26, of which waited for: 9 -> 13; matrix products, arithmetic and copies ran while one was open for 0% -> 0% of each run, Pallas kernels for 10% -> 11%
where the time goes in v5:
time: 76.6 us; the launch traced here: 76.4 us
  starting transfers between devices  32.6 us (43%)
  waiting for transfers between devices  28.2 us (37%)
  Pallas kernels  15.2 us (20%)
    ppermute x23, starting transfers between devices, exchange(): moved[k] = lax.ppermute(part, axis, xor_pairs(size, k, targets))  29.3 us
    ppermute x23, waiting for transfers between devices, exchange(): moved[k] = lax.ppermute(part, axis, xor_pairs(size, k, targets))  22 us
    pallas_call x2, Pallas kernels, agent_stage(): pl.pallas_call(functools.partial(agent_kernel, count, middle_only), out_s...  7.19 us
    ppermute x3, waiting for transfers between devices, local(): lax.ppermute(result_b[k], 'agent', [(j, j ^ k) for j in (1, 2)])  6.12 us
    pallas_call x1, Pallas kernels, time_stage(): pl.pallas_call(functools.partial(time_kernel, size), out_shape=[jax.Shape...  4.9 us
    ppermute x3, starting transfers between devices, local(): lax.ppermute(result_b[k], 'agent', [(j, j ^ k) for j in (1, 2)])  3.24 us
  transfers between devices with their start and end apart: 26, of which 13 were waited for; matrix products, arithmetic and copies ran while one was open for 0% of the time, Pallas kernels for 11%

profile of v5, /device:TPU:0, one launch (start us, length us, event | category | flops | bytes accessed | tf_op | source)
XLA Modules:
  0.0 76.4 jit_solution(9110285008115626355)
XLA Ops:
  0.0 1.4 %cut_shares.1 = (bf16[6,16,512]{2,1,0:T(8,128)(2,1)S(1)}, bf16[6,16,512]{2,1,0:T(8,128)(2,1)S(1)}, bf16[6,16,512]{2,1,0:T(8,128)(2,1)S(1)}, bf16[6,16,512]{2,1,0...) custom-call(bf16[6,128,512]{2,1,0:T(8,128)(2,1)} %refs_0_.1), custom_call_target="tpu_custom_call" | custom-call | flops 20000000000 | bytes 10000000 | tf_op jit(solution)/shard_map/cut_shares/pallas_call | solution.py:182
  1.4 3.4 %collective-permute-start = (bf16[6,16,512]{2,1,0:T(8,128)(2,1)S(1)}, bf16[6,16,512]{2,1,0:T(8,128)(2,1)S(1)}, u32[]{:S(2)}, u32[]{:S(2)}) collective-permute-start(bf16[6,16,512]{2,1,0:T(8,128)(2,1)S(1)} %get-tuple-element.58), channel_id=1, source_target_pairs={{0,28},{4,24},{8,20},{12,16},{16,12},{20,8},{24,4},{28,0},{1,29},{... | collective-permute-start | bytes 294920 | tf_op jit(solution)/shard_map/ppermute | solution.py:470
  4.9 0.6 collective-permute-start.1
  5.5 1.4 %collective-permute-start.2 = (bf16[6,16,512]{2,1,0:T(8,128)(2,1)S(1)}, bf16[6,16,512]{2,1,0:T(8,128)(2,1)S(1)}, u32[]{:S(2)}, u32[]{:S(2)}) collective-permute-start(bf16[6,16,512]{2,1,0:T(8,128)(2,1)S(1)} %get-tuple-element.61), channel_id=1, source_target_pairs={{0,20},{4,16},{8,28},{12,24},{16,4},{20,0},{24,12},{28,8},{1,21},{... | collective-permute-start | bytes 294920 | tf_op jit(solution)/shard_map/ppermute | solution.py:470
  6.9 0.3 collective-permute-start.3
  7.2 1.1 %collective-permute-start.4 = (bf16[6,16,512]{2,1,0:T(8,128)(2,1)S(1)}, bf16[6,16,512]{2,1,0:T(8,128)(2,1)S(1)}, u32[]{:S(2)}, u32[]{:S(2)}) collective-permute-start(bf16[6,16,512]{2,1,0:T(8,128)(2,1)S(1)} %get-tuple-element.63), channel_id=1, source_target_pairs={{0,12},{4,8},{8,4},{12,0},{16,28},{20,24},{24,20},{28,16},{1,13},{... | collective-permute-start | bytes 294920 | tf_op jit(solution)/shard_map/ppermute | solution.py:470
  8.3 2.2 %collective-permute-start.5 = (bf16[6,16,512]{2,1,0:T(8,128)(2,1)S(1)}, bf16[6,16,512]{2,1,0:T(8,128)(2,1)S(1)}, u32[]{:S(2)}, u32[]{:S(2)}) collective-permute-start(bf16[6,16,512]{2,1,0:T(8,128)(2,1)S(1)} %get-tuple-element.64), channel_id=1, source_target_pairs={{0,8},{4,12},{8,0},{12,4},{16,24},{20,28},{24,16},{28,20},{1,9},{5... | collective-permute-start | bytes 294920 | tf_op jit(solution)/shard_map/ppermute | solution.py:470
  10.5 0.7 collective-permute-done.1.refs_6_
  11.2 1.2 %collective-permute-done.2.refs_5_ = bf16[6,16,512]{2,1,0:T(8,128)(2,1)S(1)} collective-permute-done((bf16[6,16,512]{2,1,0:T(8,128)(2,1)S(1)}, bf16[6,16,512]{2,1,0:T(8,128)(2,1)S(1)}, u32[]{:S(2)}, u32[]{:S(2)}) %collective-permute-start.2) | collective-permute-done | bytes 98336 | tf_op jit(solution)/shard_map/ppermute | solution.py:470
  12.5 2.3 %collective-permute-done.3.refs_4_ = bf16[6,16,512]{2,1,0:T(8,128)(2,1)S(1)} collective-permute-done((bf16[6,16,512]{2,1,0:T(8,128)(2,1)S(1)}, bf16[6,16,512]{2,1,0:T(8,128)(2,1)S(1)}, u32[]{:S(2)}, u32[]{:S(2)}) %collective-permute-start.3) | collective-permute-done | bytes 98336 | tf_op jit(solution)/shard_map/ppermute | solution.py:470
  14.8 0.6 collective-permute-done.5.refs_2_
  15.4 0.0 copy-start
  15.4 0.0 copy-start.1
  15.4 0.0 copy-start.6
  15.5 0.0 copy-start.7
  15.5 4.9 %time_attention.1 = (bf16[6,16,512]{2,1,0:T(8,128)(2,1)S(1)}, bf16[6,16,512]{2,1,0:T(8,128)(2,1)S(1)}, bf16[6,16,512]{2,1,0:T(8,128)(2,1)S(1)}, bf16[6,16,512]{2...) custom-call(bf16[6,16,512]{2,1,0:T(8,128)(2,1)S(1)} %get-tuple-eleme, ...), custom_call_target="tpu_custom_call" | custom-call | flops 1610612736 | bytes 3670016 | tf_op jit(solution)/shard_map/time_attention/pallas_call | solution.py:274
  20.4 2.1 %collective-permute-start.7 = (bf16[6,16,512]{2,1,0:T(8,128)(2,1)S(1)}, bf16[6,16,512]{2,1,0:T(8,128)(2,1)S(1)}, u32[]{:S(2)}, u32[]{:S(2)}) collective-permute-start(bf16[6,16,512]{2,1,0:T(8,128)(2,1)S(1)} %get-tuple-element.76), channel_id=1, source_target_pairs={{0,28},{4,24},{8,20},{12,16},{16,12},{20,8},{24,4},{28,0},{1,29},{... | collective-permute-start | bytes 294920 | tf_op jit(solution)/shard_map/ppermute | solution.py:470
  22.5 0.6 collective-permute-start.8
  23.1 1.2 %collective-permute-start.9 = (bf16[6,16,512]{2,1,0:T(8,128)(2,1)S(1)}, bf16[6,16,512]{2,1,0:T(8,128)(2,1)S(1)}, u32[]{:S(2)}, u32[]{:S(2)}) collective-permute-start(bf16[6,16,512]{2,1,0:T(8,128)(2,1)S(1)} %get-tuple-element.79), channel_id=1, source_target_pairs={{0,20},{4,16},{8,28},{12,24},{16,4},{20,0},{24,12},{28,8},{1,21},{... | collective-permute-start | bytes 294920 | tf_op jit(solution)/shard_map/ppermute | solution.py:470
  24.3 0.6 collective-permute-start.10
  24.9 1.1 %collective-permute-start.11 = (bf16[6,16,512]{2,1,0:T(8,128)(2,1)S(1)}, bf16[6,16,512]{2,1,0:T(8,128)(2,1)S(1)}, u32[]{:S(2)}, u32[]{:S(2)}) collective-permute-start(bf16[6,16,512]{2,1,0:T(8,128)(2,1)S(1)} %get-tuple-element.81), channel_id=1, source_target_pairs={{0,12},{4,8},{8,4},{12,0},{16,28},{20,24},{24,20},{28,16},{1,13},{... | collective-permute-start | bytes 294920 | tf_op jit(solution)/shard_map/ppermute | solution.py:470
  26.0 0.1 collective-permute-done.7.refs_7_
  26.2 1.5 %collective-permute-start.12 = (bf16[6,16,512]{2,1,0:T(8,128)(2,1)S(1)}, bf16[6,16,512]{2,1,0:T(8,128)(2,1)S(1)}, u32[]{:S(2)}, u32[]{:S(2)}) collective-permute-start(bf16[6,16,512]{2,1,0:T(8,128)(2,1)S(1)} %get-tuple-element.82), channel_id=1, source_target_pairs={{0,8},{4,12},{8,0},{12,4},{16,24},{20,28},{24,16},{28,20},{1,9},{5... | collective-permute-start | bytes 294920 | tf_op jit(solution)/shard_map/ppermute | solution.py:470
  27.7 1.0 %collective-permute-done.8.refs_6_ = bf16[6,16,512]{2,1,0:T(8,128)(2,1)S(1)} collective-permute-done((bf16[6,16,512]{2,1,0:T(8,128)(2,1)S(1)}, bf16[6,16,512]{2,1,0:T(8,128)(2,1)S(1)}, u32[]{:S(2)}, u32[]{:S(2)}) %collective-permute-start.8) | collective-permute-done | bytes 98336 | tf_op jit(solution)/shard_map/ppermute | solution.py:470
  28.7 2.0 %collective-permute-done.9.refs_5_ = bf16[6,16,512]{2,1,0:T(8,128)(2,1)S(1)} collective-permute-done((bf16[6,16,512]{2,1,0:T(8,128)(2,1)S(1)}, bf16[6,16,512]{2,1,0:T(8,128)(2,1)S(1)}, u32[]{:S(2)}, u32[]{:S(2)}) %collective-permute-start.9) | collective-permute-done | bytes 98336 | tf_op jit(solution)/shard_map/ppermute | solution.py:470
  30.6 2.1 %collective-permute-done.10.refs_4_ = bf16[6,16,512]{2,1,0:T(8,128)(2,1)S(1)} collective-permute-done((bf16[6,16,512]{2,1,0:T(8,128)(2,1)S(1)}, bf16[6,16,512]{2,1,0:T(8,128)(2,1)S(1)}, u32[]{:S(2)}, u32[]{:S(2)}) %collective-permute-start.10) | collective-permute-done | bytes 98336 | tf_op jit(solution)/shard_map/ppermute | solution.py:470
  32.8 0.0 collective-permute-done.12.refs_2_
  32.8 0.1 pack_steps.2
  32.9 2.6 %collective-permute-start.14 = (bf16[128,512]{1,0:T(8,128)(2,1)S(1)}, bf16[128,512]{1,0:T(8,128)(2,1)S(1)}, u32[]{:S(2)}, u32[]{:S(2)}) collective-permute-start(bf16[128,512]{1,0:T(8,128)(2,1)S(1)} %get-tuple-element.93), channel_id=1, source_target_pairs={{0,2},{1,3},{2,0},{3,1},{4,6},{5,7},{6,4},{7,5},{8,10},{9,11},{10,... | collective-permute-start | bytes 393224 | tf_op jit(solution)/shard_map/ppermute | solution.py:470
  35.5 1.6 %collective-permute-start.18 = (bf16[128,512]{1,0:T(8,128)(2,1)S(1)}, bf16[128,512]{1,0:T(8,128)(2,1)S(1)}, u32[]{:S(2)}, u32[]{:S(2)}) collective-permute-start(bf16[128,512]{1,0:T(8,128)(2,1)S(1)} %get-tuple-element.99), channel_id=1, source_target_pairs={{0,1},{1,0},{2,3},{3,2},{4,5},{5,4},{6,7},{7,6},{8,9},{9,8},{10,11... | collective-permute-start | bytes 393224 | tf_op jit(solution)/shard_map/ppermute | solution.py:470
  37.1 0.2 collective-permute-start.19
  37.3 6.3 %collective-permute-done.14.refs_8_.refs_2_ = bf16[128,512]{1,0:T(8,128)(2,1)S(1)} collective-permute-done((bf16[128,512]{1,0:T(8,128)(2,1)S(1)}, bf16[128,512]{1,0:T(8,128)(2,1)S(1)}, u32[]{:S(2)}, u32[]{:S(2)}) %collective-permute-start.14) | collective-permute-done | bytes 131104 | tf_op jit(solution)/shard_map/ppermute | solution.py:470
  43.7 1.7 %collective-permute-start.15 = (bf16[128,512]{1,0:T(8,128)(2,1)S(1)}, bf16[128,512]{1,0:T(8,128)(2,1)S(1)}, u32[]{:S(2)}, u32[]{:S(2)}) collective-permute-start(bf16[128,512]{1,0:T(8,128)(2,1)S(1)} %get-tuple-element.95), channel_id=1, source_target_pairs={{0,1},{3,2},{4,5},{7,6},{8,9},{11,10},{12,13},{15,14},{16,17},{19,... | collective-permute-start | bytes 393224 | tf_op jit(solution)/shard_map/ppermute | solution.py:470
  45.4 1.3 %collective-permute-start.16 = (bf16[128,512]{1,0:T(8,128)(2,1)S(1)}, bf16[128,512]{1,0:T(8,128)(2,1)S(1)}, u32[]{:S(2)}, u32[]{:S(2)}) collective-permute-start(bf16[128,512]{1,0:T(8,128)(2,1)S(1)} %get-tuple-element.96), channel_id=1, source_target_pairs={{0,2},{3,1},{4,6},{7,5},{8,10},{11,9},{12,14},{15,13},{16,18},{19,... | collective-permute-start | bytes 393224 | tf_op jit(solution)/shard_map/ppermute | solution.py:470
  46.8 0.8 %collective-permute-start.17 = (bf16[128,512]{1,0:T(8,128)(2,1)S(1)}, bf16[128,512]{1,0:T(8,128)(2,1)S(1)}, u32[]{:S(2)}, u32[]{:S(2)}) collective-permute-start(bf16[128,512]{1,0:T(8,128)(2,1)S(1)} %get-tuple-element.97), channel_id=1, source_target_pairs={{1,2},{2,1},{5,6},{6,5},{9,10},{10,9},{13,14},{14,13},{17,18},{18,... | collective-permute-start | bytes 393224 | tf_op jit(solution)/shard_map/ppermute | solution.py:470
  47.7 7.2 %agent_step.2 = (bf16[128,512]{1,0:T(8,128)(2,1)S(1)}, bf16[128,512]{1,0:T(8,128)(2,1)S(1)}, bf16[128,512]{1,0:T(8,128)(2,1)S(1)}, bf16[128,512]{1,0:T(8,128)(2,1)S(1)}) custom-call(bf16[128,512]{1,0:T(8,128)(2,1)S(1)} %get-tuple-element.98.refs_0_, bf16[128,512]{1,0:T(8,128)(2,1)S(1)} %collective-permute-done.18.refs_1_, ...), custom_call_target="tpu_custom_call" | custom-call | flops 3758096384 | bytes 4194304 | tf_op jit(solution)/shard_map/agent_step/pallas_call | solution.py:379
  54.9 1.1 %collective-permute-start.23 = (bf16[128,512]{1,0:T(8,128)(2,1)S(1)}, bf16[128,512]{1,0:T(8,128)(2,1)S(1)}, u32[]{:S(2)}, u32[]{:S(2)}) collective-permute-start(bf16[128,512]{1,0:T(8,128)(2,1)S(1)} %get-tuple-element.106), channel_id=1, source_target_pairs={{0,1},{1,0},{2,3},{3,2},{4,5},{5,4},{6,7},{7,6},{8,9},{9,8},{10,11... | collective-permute-start | bytes 393224 | tf_op jit(solution)/shard_map/ppermute | solution.py:470
  56.0 2.3 %collective-permute-start.24 = (bf16[128,512]{1,0:T(8,128)(2,1)S(1)}, bf16[128,512]{1,0:T(8,128)(2,1)S(1)}, u32[]{:S(2)}, u32[]{:S(2)}) collective-permute-start(bf16[128,512]{1,0:T(8,128)(2,1)S(1)} %get-tuple-element.107), channel_id=1, source_target_pairs={{0,2},{1,3},{2,0},{3,1},{4,6},{5,7},{6,4},{7,5},{8,10},{9,11},{10,... | collective-permute-start | bytes 393224 | tf_op jit(solution)/shard_map/ppermute | solution.py:470
  58.3 1.4 %collective-permute-start.25 = (bf16[128,512]{1,0:T(8,128)(2,1)S(1)}, bf16[128,512]{1,0:T(8,128)(2,1)S(1)}, u32[]{:S(2)}, u32[]{:S(2)}) collective-permute-start(bf16[128,512]{1,0:T(8,128)(2,1)S(1)} %get-tuple-element.108), channel_id=1, source_target_pairs={{0,3},{1,2},{2,1},{3,0},{4,7},{5,6},{6,5},{7,4},{8,11},{9,10},{10,... | collective-permute-start | bytes 393224 | tf_op jit(solution)/shard_map/ppermute | solution.py:470
  59.7 1.3 %collective-permute-start.20 = (bf16[128,512]{1,0:T(8,128)(2,1)S(1)}, bf16[128,512]{1,0:T(8,128)(2,1)S(1)}, u32[]{:S(2)}, u32[]{:S(2)}) collective-permute-start(bf16[128,512]{1,0:T(8,128)(2,1)S(1)} %get-tuple-element.103), channel_id=1, source_target_pairs={{1,0},{2,3},{5,4},{6,7},{9,8},{10,11},{13,12},{14,15},{17,16},{18,... | collective-permute-start | bytes 393224 | tf_op jit(solution)/shard_map/ppermute | solution.py:538
  61.0 1.3 %collective-permute-start.21 = (bf16[128,512]{1,0:T(8,128)(2,1)S(1)}, bf16[128,512]{1,0:T(8,128)(2,1)S(1)}, u32[]{:S(2)}, u32[]{:S(2)}) collective-permute-start(bf16[128,512]{1,0:T(8,128)(2,1)S(1)} %get-tuple-element.104), channel_id=1, source_target_pairs={{1,3},{2,0},{5,7},{6,4},{9,11},{10,8},{13,15},{14,12},{17,19},{18,... | collective-permute-start | bytes 393224 | tf_op jit(solution)/shard_map/ppermute | solution.py:538
  62.3 0.4 collective-permute-done.23.refs_1_
  62.7 0.7 collective-permute-start.22
  63.3 5.2 %collective-permute-done.25.refs_3_ = bf16[128,512]{1,0:T(8,128)(2,1)S(1)} collective-permute-done((bf16[128,512]{1,0:T(8,128)(2,1)S(1)}, bf16[128,512]{1,0:T(8,128)(2,1)S(1)}, u32[]{:S(2)}, u32[]{:S(2)}) %collective-permute-start.25) | collective-permute-done | bytes 131104 | tf_op jit(solution)/shard_map/ppermute | solution.py:470
  68.6 0.8 %place_steps.1.refs_4_ = bf16[6,128,512]{2,1,0:T(8,128)(2,1)} custom-call(bf16[128,512]{1,0:T(8,128)(2,1)S(1)} %get-tuple-element.101.refs_10_.refs_0_, bf16[128,512]{1,0:T(8,128)(2,1)S(1)} %collective-permute-done.23.refs_1_, bf16[128,512]{1,0:T(8,128)(2,1)S(1)} %collective-permute-done.24.refs_2_, bf16[128,512]{1,0:T(8,128)(2,1)S(1)} %collective-permute-done.25.refs_3_), custom_call_target="tpu_custom_call" | custom-call | tf_op jit(solution)/shard_map/place_steps/pallas_call | solution.py:438
  69.4 4.6 %collective-permute-done.20.refs_1_ = bf16[128,512]{1,0:T(8,128)(2,1)S(1)} collective-permute-done((bf16[128,512]{1,0:T(8,128)(2,1)S(1)}, bf16[128,512]{1,0:T(8,128)(2,1)S(1)}, u32[]{:S(2)}, u32[]{:S(2)}) %collective-permute-start.20) | collective-permute-done | bytes 131104 | tf_op jit(solution)/shard_map/ppermute | solution.py:538
  73.9 1.6 %collective-permute-done.21.refs_2_ = bf16[128,512]{1,0:T(8,128)(2,1)S(1)} collective-permute-done((bf16[128,512]{1,0:T(8,128)(2,1)S(1)}, bf16[128,512]{1,0:T(8,128)(2,1)S(1)}, u32[]{:S(2)}, u32[]{:S(2)}) %collective-permute-start.21) | collective-permute-done | bytes 131104 | tf_op jit(solution)/shard_map/ppermute | solution.py:538
  75.5 0.7 place_extra.1
  (30 shorter events, 0.1 us)
Async XLA Ops:
  0.0 15.4 %copy-start.5 = (bf16[512,512]{1,0:T(8,128)(2,1)S(1)}, bf16[512,512]{1,0:T(8,128)(2,1)}, u32[]{:S(2)}) copy-start(bf16[512,512]{1,0:T(8,128)(2,1)} %refs_11_.1) | copy-start | bytes 1572868
  0.0 15.4 %copy-start.4 = (bf16[512,512]{1,0:T(8,128)(2,1)S(1)}, bf16[512,512]{1,0:T(8,128)(2,1)}, u32[]{:S(2)}) copy-start(bf16[512,512]{1,0:T(8,128)(2,1)} %refs_10_.1) | copy-start | bytes 1572868
  0.0 15.4 %copy-start.3 = (bf16[512,512]{1,0:T(8,128)(2,1)S(1)}, bf16[512,512]{1,0:T(8,128)(2,1)}, u32[]{:S(2)}) copy-start(bf16[512,512]{1,0:T(8,128)(2,1)} %refs_9_.3) | copy-start | bytes 1572868
  0.0 15.4 %copy-start.2 = (bf16[512,512]{1,0:T(8,128)(2,1)S(1)}, bf16[512,512]{1,0:T(8,128)(2,1)}, u32[]{:S(2)}) copy-start(bf16[512,512]{1,0:T(8,128)(2,1)} %refs_8_.3) | copy-start | bytes 1572868
  1.4 6.9 %collective-permute-start = (bf16[6,16,512]{2,1,0:T(8,128)(2,1)S(1)}, bf16[6,16,512]{2,1,0:T(8,128)(2,1)S(1)}, u32[]{:S(2)}, u32[]{:S(2)}) collective-permute-start(bf16[6,16,512]{2,1,0:T(8,128)(2,1)S(1)} %get-tuple-element.58), channel_id=1, source_target_pairs={{0,28},{4,24},{8,20},{12,16},{16,12},{20,8},{24,4},{28,0},{1,29},{... | collective-permute-start | bytes 294920 | tf_op jit(solution)/shard_map/ppermute | solution.py:470
  4.9 6.4 %collective-permute-start.1 = (bf16[6,16,512]{2,1,0:T(8,128)(2,1)S(1)}, bf16[6,16,512]{2,1,0:T(8,128)(2,1)S(1)}, u32[]{:S(2)}, u32[]{:S(2)}) collective-permute-start(bf16[6,16,512]{2,1,0:T(8,128)(2,1)S(1)} %get-tuple-element.60), channel_id=1, source_target_pairs={{0,24},{4,28},{8,16},{12,20},{16,8},{20,12},{24,0},{28,4},{1,25},{... | collective-permute-start | bytes 294920 | tf_op jit(solution)/shard_map/ppermute | solution.py:470
  5.5 7.0 %collective-permute-start.2 = (bf16[6,16,512]{2,1,0:T(8,128)(2,1)S(1)}, bf16[6,16,512]{2,1,0:T(8,128)(2,1)S(1)}, u32[]{:S(2)}, u32[]{:S(2)}) collective-permute-start(bf16[6,16,512]{2,1,0:T(8,128)(2,1)S(1)} %get-tuple-element.61), channel_id=1, source_target_pairs={{0,20},{4,16},{8,28},{12,24},{16,4},{20,0},{24,12},{28,8},{1,21},{... | collective-permute-start | bytes 294920 | tf_op jit(solution)/shard_map/ppermute | solution.py:470
  6.9 7.9 %collective-permute-start.3 = (bf16[6,16,512]{2,1,0:T(8,128)(2,1)S(1)}, bf16[6,16,512]{2,1,0:T(8,128)(2,1)S(1)}, u32[]{:S(2)}, u32[]{:S(2)}) collective-permute-start(bf16[6,16,512]{2,1,0:T(8,128)(2,1)S(1)} %get-tuple-element.62), channel_id=1, source_target_pairs={{0,16},{4,20},{8,24},{12,28},{16,0},{20,4},{24,8},{28,12},{1,17},{... | collective-permute-start | bytes 294920 | tf_op jit(solution)/shard_map/ppermute | solution.py:470
  7.2 7.6 %collective-permute-start.4 = (bf16[6,16,512]{2,1,0:T(8,128)(2,1)S(1)}, bf16[6,16,512]{2,1,0:T(8,128)(2,1)S(1)}, u32[]{:S(2)}, u32[]{:S(2)}) collective-permute-start(bf16[6,16,512]{2,1,0:T(8,128)(2,1)S(1)} %get-tuple-element.63), channel_id=1, source_target_pairs={{0,12},{4,8},{8,4},{12,0},{16,28},{20,24},{24,20},{28,16},{1,13},{... | collective-permute-start | bytes 294920 | tf_op jit(solution)/shard_map/ppermute | solution.py:470
  8.3 7.1 %collective-permute-start.5 = (bf16[6,16,512]{2,1,0:T(8,128)(2,1)S(1)}, bf16[6,16,512]{2,1,0:T(8,128)(2,1)S(1)}, u32[]{:S(2)}, u32[]{:S(2)}) collective-permute-start(bf16[6,16,512]{2,1,0:T(8,128)(2,1)S(1)} %get-tuple-element.64), channel_id=1, source_target_pairs={{0,8},{4,12},{8,0},{12,4},{16,24},{20,28},{24,16},{28,20},{1,9},{5... | collective-permute-start | bytes 294920 | tf_op jit(solution)/shard_map/ppermute | solution.py:470
  11.2 4.1 %collective-permute-start.6 = (bf16[6,16,512]{2,1,0:T(8,128)(2,1)S(1)}, bf16[6,16,512]{2,1,0:T(8,128)(2,1)S(1)}, u32[]{:S(2)}, u32[]{:S(2)}) collective-permute-start(bf16[6,16,512]{2,1,0:T(8,128)(2,1)S(1)} %get-tuple-element.65), channel_id=1, source_target_pairs={{0,4},{4,0},{8,12},{12,8},{16,20},{20,16},{24,28},{28,24},{1,5},{5... | collective-permute-start | bytes 294920 | tf_op jit(solution)/shard_map/ppermute | solution.py:470
  15.4 32.2 %copy-start = (bf16[512,2048]{1,0:T(8,128)(2,1)S(1)}, bf16[512,2048]{1,0:T(8,128)(2,1)}, u32[]{:S(2)}) copy-start(bf16[512,2048]{1,0:T(8,128)(2,1)} %refs_8_.5) | copy-start | bytes 6291460
  15.4 32.2 %copy-start.1 = (bf16[2048,512]{1,0:T(8,128)(2,1)S(1)}, bf16[2048,512]{1,0:T(8,128)(2,1)}, u32[]{:S(2)}) copy-start(bf16[2048,512]{1,0:T(8,128)(2,1)} %refs_9_.5) | copy-start | bytes 6291460
  15.4 32.2 %copy-start.6 = (bf16[512,512]{1,0:T(8,128)(2,1)S(1)}, bf16[512,512]{1,0:T(8,128)(2,1)}, u32[]{:S(2)}) copy-start(bf16[512,512]{1,0:T(8,128)(2,1)} %refs_4_.3) | copy-start | bytes 1572868
  15.5 32.2 %copy-start.7 = (bf16[512,512]{1,0:T(8,128)(2,1)S(1)}, bf16[512,512]{1,0:T(8,128)(2,1)}, u32[]{:S(2)}) copy-start(bf16[512,512]{1,0:T(8,128)(2,1)} %refs_5_.3) | copy-start | bytes 1572868
  15.5 32.2 %copy-start.8 = (bf16[512,512]{1,0:T(8,128)(2,1)S(1)}, bf16[512,512]{1,0:T(8,128)(2,1)}, u32[]{:S(2)}) copy-start(bf16[512,512]{1,0:T(8,128)(2,1)} %refs_6_.3) | copy-start | bytes 1572868
  20.4 5.8 %collective-permute-start.7 = (bf16[6,16,512]{2,1,0:T(8,128)(2,1)S(1)}, bf16[6,16,512]{2,1,0:T(8,128)(2,1)S(1)}, u32[]{:S(2)}, u32[]{:S(2)}) collective-permute-start(bf16[6,16,512]{2,1,0:T(8,128)(2,1)S(1)} %get-tuple-element.76), channel_id=1, source_target_pairs={{0,28},{4,24},{8,20},{12,16},{16,12},{20,8},{24,4},{28,0},{1,29},{... | collective-permute-start | bytes 294920 | tf_op jit(solution)/shard_map/ppermute | solution.py:470
  22.5 6.2 %collective-permute-start.8 = (bf16[6,16,512]{2,1,0:T(8,128)(2,1)S(1)}, bf16[6,16,512]{2,1,0:T(8,128)(2,1)S(1)}, u32[]{:S(2)}, u32[]{:S(2)}) collective-permute-start(bf16[6,16,512]{2,1,0:T(8,128)(2,1)S(1)} %get-tuple-element.78), channel_id=1, source_target_pairs={{0,24},{4,28},{8,16},{12,20},{16,8},{20,12},{24,0},{28,4},{1,25},{... | collective-permute-start | bytes 294920 | tf_op jit(solution)/shard_map/ppermute | solution.py:470
  23.1 7.6 %collective-permute-start.9 = (bf16[6,16,512]{2,1,0:T(8,128)(2,1)S(1)}, bf16[6,16,512]{2,1,0:T(8,128)(2,1)S(1)}, u32[]{:S(2)}, u32[]{:S(2)}) collective-permute-start(bf16[6,16,512]{2,1,0:T(8,128)(2,1)S(1)} %get-tuple-element.79), channel_id=1, source_target_pairs={{0,20},{4,16},{8,28},{12,24},{16,4},{20,0},{24,12},{28,8},{1,21},{... | collective-permute-start | bytes 294920 | tf_op jit(solution)/shard_map/ppermute | solution.py:470
  24.3 8.5 %collective-permute-start.10 = (bf16[6,16,512]{2,1,0:T(8,128)(2,1)S(1)}, bf16[6,16,512]{2,1,0:T(8,128)(2,1)S(1)}, u32[]{:S(2)}, u32[]{:S(2)}) collective-permute-start(bf16[6,16,512]{2,1,0:T(8,128)(2,1)S(1)} %get-tuple-element.80), channel_id=1, source_target_pairs={{0,16},{4,20},{8,24},{12,28},{16,0},{20,4},{24,8},{28,12},{1,17},{... | collective-permute-start | bytes 294920 | tf_op jit(solution)/shard_map/ppermute | solution.py:470
  24.9 7.9 %collective-permute-start.11 = (bf16[6,16,512]{2,1,0:T(8,128)(2,1)S(1)}, bf16[6,16,512]{2,1,0:T(8,128)(2,1)S(1)}, u32[]{:S(2)}, u32[]{:S(2)}) collective-permute-start(bf16[6,16,512]{2,1,0:T(8,128)(2,1)S(1)} %get-tuple-element.81), channel_id=1, source_target_pairs={{0,12},{4,8},{8,4},{12,0},{16,28},{20,24},{24,20},{28,16},{1,13},{... | collective-permute-start | bytes 294920 | tf_op jit(solution)/shard_map/ppermute | solution.py:470
  26.2 6.6 %collective-permute-start.12 = (bf16[6,16,512]{2,1,0:T(8,128)(2,1)S(1)}, bf16[6,16,512]{2,1,0:T(8,128)(2,1)S(1)}, u32[]{:S(2)}, u32[]{:S(2)}) collective-permute-start(bf16[6,16,512]{2,1,0:T(8,128)(2,1)S(1)} %get-tuple-element.82), channel_id=1, source_target_pairs={{0,8},{4,12},{8,0},{12,4},{16,24},{20,28},{24,16},{28,20},{1,9},{5... | collective-permute-start | bytes 294920 | tf_op jit(solution)/shard_map/ppermute | solution.py:470
  28.7 4.1 %collective-permute-start.13 = (bf16[6,16,512]{2,1,0:T(8,128)(2,1)S(1)}, bf16[6,16,512]{2,1,0:T(8,128)(2,1)S(1)}, u32[]{:S(2)}, u32[]{:S(2)}) collective-permute-start(bf16[6,16,512]{2,1,0:T(8,128)(2,1)S(1)} %get-tuple-element.83), channel_id=1, source_target_pairs={{0,4},{4,0},{8,12},{12,8},{16,20},{20,16},{24,28},{28,24},{1,5},{5... | collective-permute-start | bytes 294920 | tf_op jit(solution)/shard_map/ppermute | solution.py:470
  32.9 10.8 %collective-permute-start.14 = (bf16[128,512]{1,0:T(8,128)(2,1)S(1)}, bf16[128,512]{1,0:T(8,128)(2,1)S(1)}, u32[]{:S(2)}, u32[]{:S(2)}) collective-permute-start(bf16[128,512]{1,0:T(8,128)(2,1)S(1)} %get-tuple-element.93), channel_id=1, source_target_pairs={{0,2},{1,3},{2,0},{3,1},{4,6},{5,7},{6,4},{7,5},{8,10},{9,11},{10,... | collective-permute-start | bytes 393224 | tf_op jit(solution)/shard_map/ppermute | solution.py:470
  35.5 12.1 %collective-permute-start.18 = (bf16[128,512]{1,0:T(8,128)(2,1)S(1)}, bf16[128,512]{1,0:T(8,128)(2,1)S(1)}, u32[]{:S(2)}, u32[]{:S(2)}) collective-permute-start(bf16[128,512]{1,0:T(8,128)(2,1)S(1)} %get-tuple-element.99), channel_id=1, source_target_pairs={{0,1},{1,0},{2,3},{3,2},{4,5},{5,4},{6,7},{7,6},{8,9},{9,8},{10,11... | collective-permute-start | bytes 393224 | tf_op jit(solution)/shard_map/ppermute | solution.py:470
  37.1 10.5 %collective-permute-start.19 = (bf16[128,512]{1,0:T(8,128)(2,1)S(1)}, bf16[128,512]{1,0:T(8,128)(2,1)S(1)}, u32[]{:S(2)}, u32[]{:S(2)}) collective-permute-start(bf16[128,512]{1,0:T(8,128)(2,1)S(1)} %get-tuple-element.100), channel_id=1, source_target_pairs={{0,3},{1,2},{2,1},{3,0},{4,7},{5,6},{6,5},{7,4},{8,11},{9,10},{10,... | collective-permute-start | bytes 393224 | tf_op jit(solution)/shard_map/ppermute | solution.py:470
  43.7 14.6 %collective-permute-start.15 = (bf16[128,512]{1,0:T(8,128)(2,1)S(1)}, bf16[128,512]{1,0:T(8,128)(2,1)S(1)}, u32[]{:S(2)}, u32[]{:S(2)}) collective-permute-start(bf16[128,512]{1,0:T(8,128)(2,1)S(1)} %get-tuple-element.95), channel_id=1, source_target_pairs={{0,1},{3,2},{4,5},{7,6},{8,9},{11,10},{12,13},{15,14},{16,17},{19,... | collective-permute-start | bytes 393224 | tf_op jit(solution)/shard_map/ppermute | solution.py:470
  45.4 14.2 %collective-permute-start.16 = (bf16[128,512]{1,0:T(8,128)(2,1)S(1)}, bf16[128,512]{1,0:T(8,128)(2,1)S(1)}, u32[]{:S(2)}, u32[]{:S(2)}) collective-permute-start(bf16[128,512]{1,0:T(8,128)(2,1)S(1)} %get-tuple-element.96), channel_id=1, source_target_pairs={{0,2},{3,1},{4,6},{7,5},{8,10},{11,9},{12,14},{15,13},{16,18},{19,... | collective-permute-start | bytes 393224 | tf_op jit(solution)/shard_map/ppermute | solution.py:470
  46.8 12.9 %collective-permute-start.17 = (bf16[128,512]{1,0:T(8,128)(2,1)S(1)}, bf16[128,512]{1,0:T(8,128)(2,1)S(1)}, u32[]{:S(2)}, u32[]{:S(2)}) collective-permute-start(bf16[128,512]{1,0:T(8,128)(2,1)S(1)} %get-tuple-element.97), channel_id=1, source_target_pairs={{1,2},{2,1},{5,6},{6,5},{9,10},{10,9},{13,14},{14,13},{17,18},{18,... | collective-permute-start | bytes 393224 | tf_op jit(solution)/shard_map/ppermute | solution.py:470
  54.9 7.8 %collective-permute-start.23 = (bf16[128,512]{1,0:T(8,128)(2,1)S(1)}, bf16[128,512]{1,0:T(8,128)(2,1)S(1)}, u32[]{:S(2)}, u32[]{:S(2)}) collective-permute-start(bf16[128,512]{1,0:T(8,128)(2,1)S(1)} %get-tuple-element.106), channel_id=1, source_target_pairs={{0,1},{1,0},{2,3},{3,2},{4,5},{5,4},{6,7},{7,6},{8,9},{9,8},{10,11... | collective-permute-start | bytes 393224 | tf_op jit(solution)/shard_map/ppermute | solution.py:470
  56.0 7.4 %collective-permute-start.24 = (bf16[128,512]{1,0:T(8,128)(2,1)S(1)}, bf16[128,512]{1,0:T(8,128)(2,1)S(1)}, u32[]{:S(2)}, u32[]{:S(2)}) collective-permute-start(bf16[128,512]{1,0:T(8,128)(2,1)S(1)} %get-tuple-element.107), channel_id=1, source_target_pairs={{0,2},{1,3},{2,0},{3,1},{4,6},{5,7},{6,4},{7,5},{8,10},{9,11},{10,... | collective-permute-start | bytes 393224 | tf_op jit(solution)/shard_map/ppermute | solution.py:470
  58.3 10.3 %collective-permute-start.25 = (bf16[128,512]{1,0:T(8,128)(2,1)S(1)}, bf16[128,512]{1,0:T(8,128)(2,1)S(1)}, u32[]{:S(2)}, u32[]{:S(2)}) collective-permute-start(bf16[128,512]{1,0:T(8,128)(2,1)S(1)} %get-tuple-element.108), channel_id=1, source_target_pairs={{0,3},{1,2},{2,1},{3,0},{4,7},{5,6},{6,5},{7,4},{8,11},{9,10},{10,... | collective-permute-start | bytes 393224 | tf_op jit(solution)/shard_map/ppermute | solution.py:470
  59.7 14.2 %collective-permute-start.20 = (bf16[128,512]{1,0:T(8,128)(2,1)S(1)}, bf16[128,512]{1,0:T(8,128)(2,1)S(1)}, u32[]{:S(2)}, u32[]{:S(2)}) collective-permute-start(bf16[128,512]{1,0:T(8,128)(2,1)S(1)} %get-tuple-element.103), channel_id=1, source_target_pairs={{1,0},{2,3},{5,4},{6,7},{9,8},{10,11},{13,12},{14,15},{17,16},{18,... | collective-permute-start | bytes 393224 | tf_op jit(solution)/shard_map/ppermute | solution.py:538
  61.0 14.5 %collective-permute-start.21 = (bf16[128,512]{1,0:T(8,128)(2,1)S(1)}, bf16[128,512]{1,0:T(8,128)(2,1)S(1)}, u32[]{:S(2)}, u32[]{:S(2)}) collective-permute-start(bf16[128,512]{1,0:T(8,128)(2,1)S(1)} %get-tuple-element.104), channel_id=1, source_target_pairs={{1,3},{2,0},{5,7},{6,4},{9,11},{10,8},{13,15},{14,12},{17,19},{18,... | collective-permute-start | bytes 393224 | tf_op jit(solution)/shard_map/ppermute | solution.py:538
  62.7 12.8 %collective-permute-start.22 = (bf16[128,512]{1,0:T(8,128)(2,1)S(1)}, bf16[128,512]{1,0:T(8,128)(2,1)S(1)}, u32[]{:S(2)}, u32[]{:S(2)}) collective-permute-start(bf16[128,512]{1,0:T(8,128)(2,1)S(1)} %get-tuple-element.105), channel_id=1, source_target_pairs={{1,2},{2,1},{5,6},{6,5},{9,10},{10,9},{13,14},{14,13},{17,18},{18,... | collective-permute-start | bytes 393224 | tf_op jit(solution)/shard_map/ppermute | solution.py:538

commit v6 on v5

--- a/solution.py
+++ b/solution.py
@@ -126,40 +126,6 @@
     for copy in copies:
         copy.start()
     return copies
-
-
-def split_heads(values, even, odd, ones=False):
-    width = values.shape[1]
-    for pair in range(HEADS // 2):
-        wide = width // (HEADS // 2)
-        own = values[:, pair * wide : (pair + 1) * wide]
-        first = lax.broadcasted_iota(jnp.int32, own.shape, 1) < wide // 2
-        zero = jnp.zeros_like(own)
-        if ones:
-            one = jnp.ones_like(own)
-            at = 2 * pair * wide
-            even[:, at : at + wide] = jnp.where(first, own, zero)
-            odd[:, at : at + wide] = jnp.where(first, zero, own)
-            even[:, at + wide : at + 2 * wide] = jnp.where(first, one, zero)
-            odd[:, at + wide : at + 2 * wide] = jnp.where(first, zero, one)
-        else:
-            at = pair * wide
-            even[:, at : at + wide] = jnp.where(first, own, zero)
-            odd[:, at : at + wide] = jnp.where(first, zero, own)
-
-
-def pair_attention(query, keys, values, factor, bias=None):
-    sums = None
-    for key, value in zip(keys, values):
-        scores = lax.dot_general(query, key, NT, preferred_element_type=jnp.float32)
-        if bias is not None:
-            scores = scores + bias
-        largest = jnp.max(scores, axis=-1, keepdims=True)
-        weights = jnp.exp2((scores - largest) * factor).astype(jnp.bfloat16)
-        part = jnp.dot(weights, value, preferred_element_type=jnp.float32)
-        sums = part if sums is None else sums + part
-    wide = query.shape[1]
-    return (sums[:, :wide] / sums[:, wide:]).astype(jnp.bfloat16)
 
 
 def share_kernel(size, *refs):
@@ -315,7 +281,7 @@
 
 
 def agent_body(count, blocks, weights, outs, scratch):
-    normed, query, key_e, key_o, value_e, value_o, mixed, after, inner, w_out, sems = scratch
+    normed, query, keys, values, mixed, after, inner, w_out, sems = scratch
     w_query, w_key, w_value, far_out, w_in, w_mlp_out = weights
     copies = fetch((far_out,), (w_out,), sems)
     agents, features = blocks[0].shape
@@ -324,22 +290,38 @@
     for b in range(count):
         normed[pl.ds(b * agents, agents), :] = norm_of(blocks[b][...].astype(jnp.float32))
     query[...] = project(normed[...], w_query[...])
-    split_heads(project(normed[...], w_key[...]), key_e, key_o)
-    split_heads(project(normed[...], w_value[...]), value_e, value_o, True)
-    for pair in range(HEADS // 2):
-        lanes = pl.ds(pair * 2 * head_size, 2 * head_size)
-        double = pl.ds(pair * 4 * head_size, 4 * head_size)
-        mixed[:, lanes] = pair_attention(
-            query[:, lanes],
-            (key_e[:, lanes], key_o[:, lanes]),
-            (value_e[:, double], value_o[:, double]),
-            factor,
+    rows, wide_lanes = count * agents, 2 * head_size
+    for weight, target in ((w_key, keys), (w_value, values)):
+        found = project(normed[...], weight[...])
+        even = lax.broadcasted_iota(jnp.int32, found.shape, 1) % wide_lanes < head_size
+        zero = jnp.zeros_like(found)
+        target[:rows, :] = jnp.where(even, found, zero)
+        target[rows:, :] = jnp.where(even, zero, found)
+    second_rows = lax.broadcasted_iota(jnp.int32, (2 * rows, wide_lanes), 0) >= rows
+    second_lanes = lax.broadcasted_iota(jnp.int32, (2 * rows, wide_lanes), 1) >= head_size
+    counts = (second_rows == second_lanes).astype(jnp.bfloat16)
+    for pair, part in [(p, r) for p in range(HEADS // 2) for r in range(2)]:
+        lanes = pl.ds(pair * wide_lanes, wide_lanes)
+        at = pl.ds(part * (rows // 2), rows // 2)
+        weights_of = []
+        both = lax.dot_general(query[at, lanes], keys[:, lanes], NT, preferred_element_type=jnp.float32)
+        for h in range(2):
+            scores = both[:, h * rows : (h + 1) * rows]
+            largest = jnp.max(scores, axis=-1, keepdims=True)
+            weights_of.append(jnp.exp2((scores - largest) * factor).astype(jnp.bfloat16))
+        sums = jnp.dot(
+            jnp.concatenate(weights_of, axis=1),
+            jnp.concatenate([values[:, lanes], counts], axis=1),
+            preferred_element_type=jnp.float32,
         )
+        mixed[at, lanes] = (sums[:, :wide_lanes] / sums[:, wide_lanes:]).astype(jnp.bfloat16)
     copies[0].wait()
-    added = jnp.dot(mixed[...], w_out[...], preferred_element_type=jnp.float32)
     for b in range(count):
         at = pl.ds(b * agents, agents)
-        own = blocks[b][...].astype(jnp.float32) + added[b * agents : (b + 1) * agents]
+        if b % 2 == 0:
+            two = pl.ds(b * agents, 2 * agents)
+            added = jnp.dot(mixed[two, :], w_out[...], preferred_element_type=jnp.float32)
+        own = blocks[b][...].astype(jnp.float32) + added[b % 2 * agents : (b % 2 + 1) * agents]
         after[at, :] = own.astype(jnp.bfloat16)
         normed[at, :] = norm_of(after[at, :].astype(jnp.float32))
     hidden = w_in.shape[1]
@@ -358,7 +340,7 @@
 
 def agent_kernel(count, middle_only, *refs):
     blocks, weights = refs[:count], refs[count : count + 6]
-    outs, scratch = refs[-11 - count : -11], refs[-11:]
+    outs, scratch = refs[-9 - count : -9], refs[-9:]
 
     def run():
         agent_body(count, blocks, weights, outs, scratch)
@@ -384,8 +366,8 @@
         + [spec(VMEM)] * 2
         + [spec(pl.ANY)] * len(after),
         out_specs=[spec(VMEM)] * count,
-        scratch_shapes=[VMEM((rows, features), kind)] * 4
-        + [VMEM((rows, 2 * features), kind)] * 2
+        scratch_shapes=[VMEM((rows, features), kind)] * 2
+        + [VMEM((2 * rows, features), kind)] * 2
         + [VMEM((rows, features), kind)] * 2
         + [VMEM((rows, hidden), kind)]
         + [VMEM(weights[3].shape, kind), pltpu.SemaphoreType.DMA((1,))],

time: 76.6 us -> 75.6 us (0.987)
  transfers between devices with their start and end apart: 26 -> 26, of which waited for: 13 -> 13; matrix products, arithmetic and copies ran while one was open for 0% -> 0% of each run, Pallas kernels for 11% -> 10%
where the time goes in v6:
time: 75.6 us; the launch traced here: 75.4 us
  starting transfers between devices  32.6 us (43%)
  waiting for transfers between devices  27.6 us (37%)
  Pallas kernels  14.7 us (19%)
    ppermute x23, starting transfers between devices, exchange(): moved[k] = lax.ppermute(part, axis, xor_pairs(size, k, targets))  29.3 us
    ppermute x23, waiting for transfers between devices, exchange(): moved[k] = lax.ppermute(part, axis, xor_pairs(size, k, targets))  22.1 us
    pallas_call x2, Pallas kernels, agent_stage(): pl.pallas_call(functools.partial(agent_kernel, count, middle_only), out_s...  6.69 us
    ppermute x3, waiting for transfers between devices, local(): lax.ppermute(result_b[k], 'agent', [(j, j ^ k) for j in (1, 2)])  5.58 us
    pallas_call x1, Pallas kernels, time_stage(): pl.pallas_call(functools.partial(time_kernel, size), out_shape=[jax.Shape...  4.9 us
    ppermute x3, starting transfers between devices, local(): lax.ppermute(result_b[k], 'agent', [(j, j ^ k) for j in (1, 2)])  3.24 us
  transfers between devices with their start and end apart: 26, of which 13 were waited for; matrix products, arithmetic and copies ran while one was open for 0% of the time, Pallas kernels for 10%

profile of v6, /device:TPU:0, one launch (start us, length us, event | category | flops | bytes accessed | tf_op | source)
XLA Modules:
  0.0 75.4 jit_solution(3730706846387943590)
XLA Ops:
  0.0 1.4 %cut_shares.1 = (bf16[6,16,512]{2,1,0:T(8,128)(2,1)S(1)}, bf16[6,16,512]{2,1,0:T(8,128)(2,1)S(1)}, bf16[6,16,512]{2,1,0:T(8,128)(2,1)S(1)}, bf16[6,16,512]{2,1,0...) custom-call(bf16[6,128,512]{2,1,0:T(8,128)(2,1)} %refs_0_.1), custom_call_target="tpu_custom_call" | custom-call | flops 20000000000 | bytes 10000000 | tf_op jit(solution)/shard_map/cut_shares/pallas_call | solution.py:148
  1.4 3.4 %collective-permute-start = (bf16[6,16,512]{2,1,0:T(8,128)(2,1)S(1)}, bf16[6,16,512]{2,1,0:T(8,128)(2,1)S(1)}, u32[]{:S(2)}, u32[]{:S(2)}) collective-permute-start(bf16[6,16,512]{2,1,0:T(8,128)(2,1)S(1)} %get-tuple-element.58), channel_id=1, source_target_pairs={{0,28},{4,24},{8,20},{12,16},{16,12},{20,8},{24,4},{28,0},{1,29},{... | collective-permute-start | bytes 294920 | tf_op jit(solution)/shard_map/ppermute | solution.py:452
  4.9 0.6 collective-permute-start.1
  5.5 1.4 %collective-permute-start.2 = (bf16[6,16,512]{2,1,0:T(8,128)(2,1)S(1)}, bf16[6,16,512]{2,1,0:T(8,128)(2,1)S(1)}, u32[]{:S(2)}, u32[]{:S(2)}) collective-permute-start(bf16[6,16,512]{2,1,0:T(8,128)(2,1)S(1)} %get-tuple-element.61), channel_id=1, source_target_pairs={{0,20},{4,16},{8,28},{12,24},{16,4},{20,0},{24,12},{28,8},{1,21},{... | collective-permute-start | bytes 294920 | tf_op jit(solution)/shard_map/ppermute | solution.py:452
  6.9 0.3 collective-permute-start.3
  7.2 1.1 %collective-permute-start.4 = (bf16[6,16,512]{2,1,0:T(8,128)(2,1)S(1)}, bf16[6,16,512]{2,1,0:T(8,128)(2,1)S(1)}, u32[]{:S(2)}, u32[]{:S(2)}) collective-permute-start(bf16[6,16,512]{2,1,0:T(8,128)(2,1)S(1)} %get-tuple-element.63), channel_id=1, source_target_pairs={{0,12},{4,8},{8,4},{12,0},{16,28},{20,24},{24,20},{28,16},{1,13},{... | collective-permute-start | bytes 294920 | tf_op jit(solution)/shard_map/ppermute | solution.py:452
  8.3 2.2 %collective-permute-start.5 = (bf16[6,16,512]{2,1,0:T(8,128)(2,1)S(1)}, bf16[6,16,512]{2,1,0:T(8,128)(2,1)S(1)}, u32[]{:S(2)}, u32[]{:S(2)}) collective-permute-start(bf16[6,16,512]{2,1,0:T(8,128)(2,1)S(1)} %get-tuple-element.64), channel_id=1, source_target_pairs={{0,8},{4,12},{8,0},{12,4},{16,24},{20,28},{24,16},{28,20},{1,9},{5... | collective-permute-start | bytes 294920 | tf_op jit(solution)/shard_map/ppermute | solution.py:452
  10.5 0.7 collective-permute-done.1.refs_6_
  11.2 1.2 %collective-permute-done.2.refs_5_ = bf16[6,16,512]{2,1,0:T(8,128)(2,1)S(1)} collective-permute-done((bf16[6,16,512]{2,1,0:T(8,128)(2,1)S(1)}, bf16[6,16,512]{2,1,0:T(8,128)(2,1)S(1)}, u32[]{:S(2)}, u32[]{:S(2)}) %collective-permute-start.2) | collective-permute-done | bytes 98336 | tf_op jit(solution)/shard_map/ppermute | solution.py:452
  12.5 2.3 %collective-permute-done.3.refs_4_ = bf16[6,16,512]{2,1,0:T(8,128)(2,1)S(1)} collective-permute-done((bf16[6,16,512]{2,1,0:T(8,128)(2,1)S(1)}, bf16[6,16,512]{2,1,0:T(8,128)(2,1)S(1)}, u32[]{:S(2)}, u32[]{:S(2)}) %collective-permute-start.3) | collective-permute-done | bytes 98336 | tf_op jit(solution)/shard_map/ppermute | solution.py:452
  14.8 0.6 collective-permute-done.5.refs_2_
  15.4 0.0 copy-start
  15.4 0.0 copy-start.1
  15.5 0.0 copy-start.7
  15.5 0.0 copy-start.8
  15.5 4.9 %time_attention.1 = (bf16[6,16,512]{2,1,0:T(8,128)(2,1)S(1)}, bf16[6,16,512]{2,1,0:T(8,128)(2,1)S(1)}, bf16[6,16,512]{2,1,0:T(8,128)(2,1)S(1)}, bf16[6,16,512]{2...) custom-call(bf16[6,16,512]{2,1,0:T(8,128)(2,1)S(1)} %get-tuple-eleme, ...), custom_call_target="tpu_custom_call" | custom-call | flops 1610612736 | bytes 3670016 | tf_op jit(solution)/shard_map/time_attention/pallas_call | solution.py:240
  20.4 2.1 %collective-permute-start.7 = (bf16[6,16,512]{2,1,0:T(8,128)(2,1)S(1)}, bf16[6,16,512]{2,1,0:T(8,128)(2,1)S(1)}, u32[]{:S(2)}, u32[]{:S(2)}) collective-permute-start(bf16[6,16,512]{2,1,0:T(8,128)(2,1)S(1)} %get-tuple-element.76), channel_id=1, source_target_pairs={{0,28},{4,24},{8,20},{12,16},{16,12},{20,8},{24,4},{28,0},{1,29},{... | collective-permute-start | bytes 294920 | tf_op jit(solution)/shard_map/ppermute | solution.py:452
  22.5 0.6 collective-permute-start.8
  23.1 1.2 %collective-permute-start.9 = (bf16[6,16,512]{2,1,0:T(8,128)(2,1)S(1)}, bf16[6,16,512]{2,1,0:T(8,128)(2,1)S(1)}, u32[]{:S(2)}, u32[]{:S(2)}) collective-permute-start(bf16[6,16,512]{2,1,0:T(8,128)(2,1)S(1)} %get-tuple-element.79), channel_id=1, source_target_pairs={{0,20},{4,16},{8,28},{12,24},{16,4},{20,0},{24,12},{28,8},{1,21},{... | collective-permute-start | bytes 294920 | tf_op jit(solution)/shard_map/ppermute | solution.py:452
  24.3 0.6 collective-permute-start.10
  24.9 1.1 %collective-permute-start.11 = (bf16[6,16,512]{2,1,0:T(8,128)(2,1)S(1)}, bf16[6,16,512]{2,1,0:T(8,128)(2,1)S(1)}, u32[]{:S(2)}, u32[]{:S(2)}) collective-permute-start(bf16[6,16,512]{2,1,0:T(8,128)(2,1)S(1)} %get-tuple-element.81), channel_id=1, source_target_pairs={{0,12},{4,8},{8,4},{12,0},{16,28},{20,24},{24,20},{28,16},{1,13},{... | collective-permute-start | bytes 294920 | tf_op jit(solution)/shard_map/ppermute | solution.py:452
  26.0 0.1 collective-permute-done.7.refs_7_
  26.2 1.5 %collective-permute-start.12 = (bf16[6,16,512]{2,1,0:T(8,128)(2,1)S(1)}, bf16[6,16,512]{2,1,0:T(8,128)(2,1)S(1)}, u32[]{:S(2)}, u32[]{:S(2)}) collective-permute-start(bf16[6,16,512]{2,1,0:T(8,128)(2,1)S(1)} %get-tuple-element.82), channel_id=1, source_target_pairs={{0,8},{4,12},{8,0},{12,4},{16,24},{20,28},{24,16},{28,20},{1,9},{5... | collective-permute-start | bytes 294920 | tf_op jit(solution)/shard_map/ppermute | solution.py:452
  27.7 1.0 %collective-permute-done.8.refs_6_ = bf16[6,16,512]{2,1,0:T(8,128)(2,1)S(1)} collective-permute-done((bf16[6,16,512]{2,1,0:T(8,128)(2,1)S(1)}, bf16[6,16,512]{2,1,0:T(8,128)(2,1)S(1)}, u32[]{:S(2)}, u32[]{:S(2)}) %collective-permute-start.8) | collective-permute-done | bytes 98336 | tf_op jit(solution)/shard_map/ppermute | solution.py:452
  28.7 2.0 %collective-permute-done.9.refs_5_ = bf16[6,16,512]{2,1,0:T(8,128)(2,1)S(1)} collective-permute-done((bf16[6,16,512]{2,1,0:T(8,128)(2,1)S(1)}, bf16[6,16,512]{2,1,0:T(8,128)(2,1)S(1)}, u32[]{:S(2)}, u32[]{:S(2)}) %collective-permute-start.9) | collective-permute-done | bytes 98336 | tf_op jit(solution)/shard_map/ppermute | solution.py:452
  30.6 2.1 %collective-permute-done.10.refs_4_ = bf16[6,16,512]{2,1,0:T(8,128)(2,1)S(1)} collective-permute-done((bf16[6,16,512]{2,1,0:T(8,128)(2,1)S(1)}, bf16[6,16,512]{2,1,0:T(8,128)(2,1)S(1)}, u32[]{:S(2)}, u32[]{:S(2)}) %collective-permute-start.10) | collective-permute-done | bytes 98336 | tf_op jit(solution)/shard_map/ppermute | solution.py:452
  32.8 0.0 collective-permute-done.12.refs_2_
  32.8 0.1 pack_steps.2
  32.9 2.6 %collective-permute-start.14 = (bf16[128,512]{1,0:T(8,128)(2,1)S(1)}, bf16[128,512]{1,0:T(8,128)(2,1)S(1)}, u32[]{:S(2)}, u32[]{:S(2)}) collective-permute-start(bf16[128,512]{1,0:T(8,128)(2,1)S(1)} %get-tuple-element.93), channel_id=1, source_target_pairs={{0,2},{1,3},{2,0},{3,1},{4,6},{5,7},{6,4},{7,5},{8,10},{9,11},{10,... | collective-permute-start | bytes 393224 | tf_op jit(solution)/shard_map/ppermute | solution.py:452
  35.5 1.6 %collective-permute-start.18 = (bf16[128,512]{1,0:T(8,128)(2,1)S(1)}, bf16[128,512]{1,0:T(8,128)(2,1)S(1)}, u32[]{:S(2)}, u32[]{:S(2)}) collective-permute-start(bf16[128,512]{1,0:T(8,128)(2,1)S(1)} %get-tuple-element.99), channel_id=1, source_target_pairs={{0,1},{1,0},{2,3},{3,2},{4,5},{5,4},{6,7},{7,6},{8,9},{9,8},{10,11... | collective-permute-start | bytes 393224 | tf_op jit(solution)/shard_map/ppermute | solution.py:452
  37.1 0.2 collective-permute-start.19
  37.3 6.3 %collective-permute-done.14.refs_8_.refs_2_ = bf16[128,512]{1,0:T(8,128)(2,1)S(1)} collective-permute-done((bf16[128,512]{1,0:T(8,128)(2,1)S(1)}, bf16[128,512]{1,0:T(8,128)(2,1)S(1)}, u32[]{:S(2)}, u32[]{:S(2)}) %collective-permute-start.14) | collective-permute-done | bytes 131104 | tf_op jit(solution)/shard_map/ppermute | solution.py:452
  43.7 1.7 %collective-permute-start.15 = (bf16[128,512]{1,0:T(8,128)(2,1)S(1)}, bf16[128,512]{1,0:T(8,128)(2,1)S(1)}, u32[]{:S(2)}, u32[]{:S(2)}) collective-permute-start(bf16[128,512]{1,0:T(8,128)(2,1)S(1)} %get-tuple-element.95), channel_id=1, source_target_pairs={{0,1},{3,2},{4,5},{7,6},{8,9},{11,10},{12,13},{15,14},{16,17},{19,... | collective-permute-start | bytes 393224 | tf_op jit(solution)/shard_map/ppermute | solution.py:452
  45.4 1.3 %collective-permute-start.16 = (bf16[128,512]{1,0:T(8,128)(2,1)S(1)}, bf16[128,512]{1,0:T(8,128)(2,1)S(1)}, u32[]{:S(2)}, u32[]{:S(2)}) collective-permute-start(bf16[128,512]{1,0:T(8,128)(2,1)S(1)} %get-tuple-element.96), channel_id=1, source_target_pairs={{0,2},{3,1},{4,6},{7,5},{8,10},{11,9},{12,14},{15,13},{16,18},{19,... | collective-permute-start | bytes 393224 | tf_op jit(solution)/shard_map/ppermute | solution.py:452
  46.8 0.8 %collective-permute-start.17 = (bf16[128,512]{1,0:T(8,128)(2,1)S(1)}, bf16[128,512]{1,0:T(8,128)(2,1)S(1)}, u32[]{:S(2)}, u32[]{:S(2)}) collective-permute-start(bf16[128,512]{1,0:T(8,128)(2,1)S(1)} %get-tuple-element.97), channel_id=1, source_target_pairs={{1,2},{2,1},{5,6},{6,5},{9,10},{10,9},{13,14},{14,13},{17,18},{18,... | collective-permute-start | bytes 393224 | tf_op jit(solution)/shard_map/ppermute | solution.py:452
  47.7 6.7 %agent_step.2 = (bf16[128,512]{1,0:T(8,128)(2,1)S(1)}, bf16[128,512]{1,0:T(8,128)(2,1)S(1)}, bf16[128,512]{1,0:T(8,128)(2,1)S(1)}, bf16[128,512]{1,0:T(8,128)(2,1)S(1)}) custom-call(bf16[128,512]{1,0:T(8,128)(2,1)S(1)} %get-tuple-element.98.refs_0_, bf16[128,512]{1,0:T(8,128)(2,1)S(1)} %collective-permute-done.18.refs_1_, ...), custom_call_target="tpu_custom_call" | custom-call | flops 3758096384 | bytes 4194304 | tf_op jit(solution)/shard_map/agent_step/pallas_call | solution.py:361
  54.4 1.1 %collective-permute-start.23 = (bf16[128,512]{1,0:T(8,128)(2,1)S(1)}, bf16[128,512]{1,0:T(8,128)(2,1)S(1)}, u32[]{:S(2)}, u32[]{:S(2)}) collective-permute-start(bf16[128,512]{1,0:T(8,128)(2,1)S(1)} %get-tuple-element.106), channel_id=1, source_target_pairs={{0,1},{1,0},{2,3},{3,2},{4,5},{5,4},{6,7},{7,6},{8,9},{9,8},{10,11... | collective-permute-start | bytes 393224 | tf_op jit(solution)/shard_map/ppermute | solution.py:452
  55.5 2.3 %collective-permute-start.24 = (bf16[128,512]{1,0:T(8,128)(2,1)S(1)}, bf16[128,512]{1,0:T(8,128)(2,1)S(1)}, u32[]{:S(2)}, u32[]{:S(2)}) collective-permute-start(bf16[128,512]{1,0:T(8,128)(2,1)S(1)} %get-tuple-element.107), channel_id=1, source_target_pairs={{0,2},{1,3},{2,0},{3,1},{4,6},{5,7},{6,4},{7,5},{8,10},{9,11},{10,... | collective-permute-start | bytes 393224 | tf_op jit(solution)/shard_map/ppermute | solution.py:452
  57.8 1.4 %collective-permute-start.25 = (bf16[128,512]{1,0:T(8,128)(2,1)S(1)}, bf16[128,512]{1,0:T(8,128)(2,1)S(1)}, u32[]{:S(2)}, u32[]{:S(2)}) collective-permute-start(bf16[128,512]{1,0:T(8,128)(2,1)S(1)} %get-tuple-element.108), channel_id=1, source_target_pairs={{0,3},{1,2},{2,1},{3,0},{4,7},{5,6},{6,5},{7,4},{8,11},{9,10},{10,... | collective-permute-start | bytes 393224 | tf_op jit(solution)/shard_map/ppermute | solution.py:452
  59.2 1.3 %collective-permute-start.20 = (bf16[128,512]{1,0:T(8,128)(2,1)S(1)}, bf16[128,512]{1,0:T(8,128)(2,1)S(1)}, u32[]{:S(2)}, u32[]{:S(2)}) collective-permute-start(bf16[128,512]{1,0:T(8,128)(2,1)S(1)} %get-tuple-element.103), channel_id=1, source_target_pairs={{1,0},{2,3},{5,4},{6,7},{9,8},{10,11},{13,12},{14,15},{17,16},{18,... | collective-permute-start | bytes 393224 | tf_op jit(solution)/shard_map/ppermute | solution.py:520
  60.5 1.3 %collective-permute-start.21 = (bf16[128,512]{1,0:T(8,128)(2,1)S(1)}, bf16[128,512]{1,0:T(8,128)(2,1)S(1)}, u32[]{:S(2)}, u32[]{:S(2)}) collective-permute-start(bf16[128,512]{1,0:T(8,128)(2,1)S(1)} %get-tuple-element.104), channel_id=1, source_target_pairs={{1,3},{2,0},{5,7},{6,4},{9,11},{10,8},{13,15},{14,12},{17,19},{18,... | collective-permute-start | bytes 393224 | tf_op jit(solution)/shard_map/ppermute | solution.py:520
  61.8 0.4 collective-permute-done.23.refs_1_
  62.2 0.7 collective-permute-start.22
  62.9 5.2 %collective-permute-done.25.refs_3_ = bf16[128,512]{1,0:T(8,128)(2,1)S(1)} collective-permute-done((bf16[128,512]{1,0:T(8,128)(2,1)S(1)}, bf16[128,512]{1,0:T(8,128)(2,1)S(1)}, u32[]{:S(2)}, u32[]{:S(2)}) %collective-permute-start.25) | collective-permute-done | bytes 131104 | tf_op jit(solution)/shard_map/ppermute | solution.py:452
  68.1 0.8 %place_steps.1.refs_4_ = bf16[6,128,512]{2,1,0:T(8,128)(2,1)} custom-call(bf16[128,512]{1,0:T(8,128)(2,1)S(1)} %get-tuple-element.101.refs_10_.refs_0_, bf16[128,512]{1,0:T(8,128)(2,1)S(1)} %collective-permute-done.23.refs_1_, bf16[128,512]{1,0:T(8,128)(2,1)S(1)} %collective-permute-done.24.refs_2_, bf16[128,512]{1,0:T(8,128)(2,1)S(1)} %collective-permute-done.25.refs_3_), custom_call_target="tpu_custom_call" | custom-call | tf_op jit(solution)/shard_map/place_steps/pallas_call | solution.py:420
  68.9 4.0 %collective-permute-done.20.refs_1_ = bf16[128,512]{1,0:T(8,128)(2,1)S(1)} collective-permute-done((bf16[128,512]{1,0:T(8,128)(2,1)S(1)}, bf16[128,512]{1,0:T(8,128)(2,1)S(1)}, u32[]{:S(2)}, u32[]{:S(2)}) %collective-permute-start.20) | collective-permute-done | bytes 131104 | tf_op jit(solution)/shard_map/ppermute | solution.py:520
  72.9 1.5 %collective-permute-done.21.refs_2_ = bf16[128,512]{1,0:T(8,128)(2,1)S(1)} collective-permute-done((bf16[128,512]{1,0:T(8,128)(2,1)S(1)}, bf16[128,512]{1,0:T(8,128)(2,1)S(1)}, u32[]{:S(2)}, u32[]{:S(2)}) %collective-permute-start.21) | collective-permute-done | bytes 131104 | tf_op jit(solution)/shard_map/ppermute | solution.py:520
  74.5 0.7 place_extra.1
  (30 shorter events, 0.1 us)
Async XLA Ops:
  0.0 15.4 %copy-start.5 = (bf16[512,512]{1,0:T(8,128)(2,1)S(1)}, bf16[512,512]{1,0:T(8,128)(2,1)}, u32[]{:S(2)}) copy-start(bf16[512,512]{1,0:T(8,128)(2,1)} %refs_11_.1) | copy-start | bytes 1572868
  0.0 15.4 %copy-start.4 = (bf16[512,512]{1,0:T(8,128)(2,1)S(1)}, bf16[512,512]{1,0:T(8,128)(2,1)}, u32[]{:S(2)}) copy-start(bf16[512,512]{1,0:T(8,128)(2,1)} %refs_10_.1) | copy-start | bytes 1572868
  0.0 15.4 %copy-start.3 = (bf16[512,512]{1,0:T(8,128)(2,1)S(1)}, bf16[512,512]{1,0:T(8,128)(2,1)}, u32[]{:S(2)}) copy-start(bf16[512,512]{1,0:T(8,128)(2,1)} %refs_9_.3) | copy-start | bytes 1572868
  0.0 15.4 %copy-start.2 = (bf16[512,512]{1,0:T(8,128)(2,1)S(1)}, bf16[512,512]{1,0:T(8,128)(2,1)}, u32[]{:S(2)}) copy-start(bf16[512,512]{1,0:T(8,128)(2,1)} %refs_8_.3) | copy-start | bytes 1572868
  1.4 6.9 %collective-permute-start = (bf16[6,16,512]{2,1,0:T(8,128)(2,1)S(1)}, bf16[6,16,512]{2,1,0:T(8,128)(2,1)S(1)}, u32[]{:S(2)}, u32[]{:S(2)}) collective-permute-start(bf16[6,16,512]{2,1,0:T(8,128)(2,1)S(1)} %get-tuple-element.58), channel_id=1, source_target_pairs={{0,28},{4,24},{8,20},{12,16},{16,12},{20,8},{24,4},{28,0},{1,29},{... | collective-permute-start | bytes 294920 | tf_op jit(solution)/shard_map/ppermute | solution.py:452
  4.9 6.4 %collective-permute-start.1 = (bf16[6,16,512]{2,1,0:T(8,128)(2,1)S(1)}, bf16[6,16,512]{2,1,0:T(8,128)(2,1)S(1)}, u32[]{:S(2)}, u32[]{:S(2)}) collective-permute-start(bf16[6,16,512]{2,1,0:T(8,128)(2,1)S(1)} %get-tuple-element.60), channel_id=1, source_target_pairs={{0,24},{4,28},{8,16},{12,20},{16,8},{20,12},{24,0},{28,4},{1,25},{... | collective-permute-start | bytes 294920 | tf_op jit(solution)/shard_map/ppermute | solution.py:452
  5.5 7.0 %collective-permute-start.2 = (bf16[6,16,512]{2,1,0:T(8,128)(2,1)S(1)}, bf16[6,16,512]{2,1,0:T(8,128)(2,1)S(1)}, u32[]{:S(2)}, u32[]{:S(2)}) collective-permute-start(bf16[6,16,512]{2,1,0:T(8,128)(2,1)S(1)} %get-tuple-element.61), channel_id=1, source_target_pairs={{0,20},{4,16},{8,28},{12,24},{16,4},{20,0},{24,12},{28,8},{1,21},{... | collective-permute-start | bytes 294920 | tf_op jit(solution)/shard_map/ppermute | solution.py:452
  6.9 7.9 %collective-permute-start.3 = (bf16[6,16,512]{2,1,0:T(8,128)(2,1)S(1)}, bf16[6,16,512]{2,1,0:T(8,128)(2,1)S(1)}, u32[]{:S(2)}, u32[]{:S(2)}) collective-permute-start(bf16[6,16,512]{2,1,0:T(8,128)(2,1)S(1)} %get-tuple-element.62), channel_id=1, source_target_pairs={{0,16},{4,20},{8,24},{12,28},{16,0},{20,4},{24,8},{28,12},{1,17},{... | collective-permute-start | bytes 294920 | tf_op jit(solution)/shard_map/ppermute | solution.py:452
  7.2 7.6 %collective-permute-start.4 = (bf16[6,16,512]{2,1,0:T(8,128)(2,1)S(1)}, bf16[6,16,512]{2,1,0:T(8,128)(2,1)S(1)}, u32[]{:S(2)}, u32[]{:S(2)}) collective-permute-start(bf16[6,16,512]{2,1,0:T(8,128)(2,1)S(1)} %get-tuple-element.63), channel_id=1, source_target_pairs={{0,12},{4,8},{8,4},{12,0},{16,28},{20,24},{24,20},{28,16},{1,13},{... | collective-permute-start | bytes 294920 | tf_op jit(solution)/shard_map/ppermute | solution.py:452
  8.3 7.1 %collective-permute-start.5 = (bf16[6,16,512]{2,1,0:T(8,128)(2,1)S(1)}, bf16[6,16,512]{2,1,0:T(8,128)(2,1)S(1)}, u32[]{:S(2)}, u32[]{:S(2)}) collective-permute-start(bf16[6,16,512]{2,1,0:T(8,128)(2,1)S(1)} %get-tuple-element.64), channel_id=1, source_target_pairs={{0,8},{4,12},{8,0},{12,4},{16,24},{20,28},{24,16},{28,20},{1,9},{5... | collective-permute-start | bytes 294920 | tf_op jit(solution)/shard_map/ppermute | solution.py:452
  11.2 4.1 %collective-permute-start.6 = (bf16[6,16,512]{2,1,0:T(8,128)(2,1)S(1)}, bf16[6,16,512]{2,1,0:T(8,128)(2,1)S(1)}, u32[]{:S(2)}, u32[]{:S(2)}) collective-permute-start(bf16[6,16,512]{2,1,0:T(8,128)(2,1)S(1)} %get-tuple-element.65), channel_id=1, source_target_pairs={{0,4},{4,0},{8,12},{12,8},{16,20},{20,16},{24,28},{28,24},{1,5},{5... | collective-permute-start | bytes 294920 | tf_op jit(solution)/shard_map/ppermute | solution.py:452
  15.4 32.2 %copy-start = (bf16[512,2048]{1,0:T(8,128)(2,1)S(1)}, bf16[512,2048]{1,0:T(8,128)(2,1)}, u32[]{:S(2)}) copy-start(bf16[512,2048]{1,0:T(8,128)(2,1)} %refs_8_.5) | copy-start | bytes 6291460
  15.4 32.2 %copy-start.1 = (bf16[2048,512]{1,0:T(8,128)(2,1)S(1)}, bf16[2048,512]{1,0:T(8,128)(2,1)}, u32[]{:S(2)}) copy-start(bf16[2048,512]{1,0:T(8,128)(2,1)} %refs_9_.5) | copy-start | bytes 6291460
  15.4 32.2 %copy-start.6 = (bf16[512,512]{1,0:T(8,128)(2,1)S(1)}, bf16[512,512]{1,0:T(8,128)(2,1)}, u32[]{:S(2)}) copy-start(bf16[512,512]{1,0:T(8,128)(2,1)} %refs_4_.3) | copy-start | bytes 1572868
  15.5 32.2 %copy-start.7 = (bf16[512,512]{1,0:T(8,128)(2,1)S(1)}, bf16[512,512]{1,0:T(8,128)(2,1)}, u32[]{:S(2)}) copy-start(bf16[512,512]{1,0:T(8,128)(2,1)} %refs_5_.3) | copy-start | bytes 1572868
  15.5 32.2 %copy-start.8 = (bf16[512,512]{1,0:T(8,128)(2,1)S(1)}, bf16[512,512]{1,0:T(8,128)(2,1)}, u32[]{:S(2)}) copy-start(bf16[512,512]{1,0:T(8,128)(2,1)} %refs_6_.3) | copy-start | bytes 1572868
  20.4 5.8 %collective-permute-start.7 = (bf16[6,16,512]{2,1,0:T(8,128)(2,1)S(1)}, bf16[6,16,512]{2,1,0:T(8,128)(2,1)S(1)}, u32[]{:S(2)}, u32[]{:S(2)}) collective-permute-start(bf16[6,16,512]{2,1,0:T(8,128)(2,1)S(1)} %get-tuple-element.76), channel_id=1, source_target_pairs={{0,28},{4,24},{8,20},{12,16},{16,12},{20,8},{24,4},{28,0},{1,29},{... | collective-permute-start | bytes 294920 | tf_op jit(solution)/shard_map/ppermute | solution.py:452
  22.5 6.2 %collective-permute-start.8 = (bf16[6,16,512]{2,1,0:T(8,128)(2,1)S(1)}, bf16[6,16,512]{2,1,0:T(8,128)(2,1)S(1)}, u32[]{:S(2)}, u32[]{:S(2)}) collective-permute-start(bf16[6,16,512]{2,1,0:T(8,128)(2,1)S(1)} %get-tuple-element.78), channel_id=1, source_target_pairs={{0,24},{4,28},{8,16},{12,20},{16,8},{20,12},{24,0},{28,4},{1,25},{... | collective-permute-start | bytes 294920 | tf_op jit(solution)/shard_map/ppermute | solution.py:452
  23.1 7.6 %collective-permute-start.9 = (bf16[6,16,512]{2,1,0:T(8,128)(2,1)S(1)}, bf16[6,16,512]{2,1,0:T(8,128)(2,1)S(1)}, u32[]{:S(2)}, u32[]{:S(2)}) collective-permute-start(bf16[6,16,512]{2,1,0:T(8,128)(2,1)S(1)} %get-tuple-element.79), channel_id=1, source_target_pairs={{0,20},{4,16},{8,28},{12,24},{16,4},{20,0},{24,12},{28,8},{1,21},{... | collective-permute-start | bytes 294920 | tf_op jit(solution)/shard_map/ppermute | solution.py:452
  24.3 8.5 %collective-permute-start.10 = (bf16[6,16,512]{2,1,0:T(8,128)(2,1)S(1)}, bf16[6,16,512]{2,1,0:T(8,128)(2,1)S(1)}, u32[]{:S(2)}, u32[]{:S(2)}) collective-permute-start(bf16[6,16,512]{2,1,0:T(8,128)(2,1)S(1)} %get-tuple-element.80), channel_id=1, source_target_pairs={{0,16},{4,20},{8,24},{12,28},{16,0},{20,4},{24,8},{28,12},{1,17},{... | collective-permute-start | bytes 294920 | tf_op jit(solution)/shard_map/ppermute | solution.py:452
  24.9 7.9 %collective-permute-start.11 = (bf16[6,16,512]{2,1,0:T(8,128)(2,1)S(1)}, bf16[6,16,512]{2,1,0:T(8,128)(2,1)S(1)}, u32[]{:S(2)}, u32[]{:S(2)}) collective-permute-start(bf16[6,16,512]{2,1,0:T(8,128)(2,1)S(1)} %get-tuple-element.81), channel_id=1, source_target_pairs={{0,12},{4,8},{8,4},{12,0},{16,28},{20,24},{24,20},{28,16},{1,13},{... | collective-permute-start | bytes 294920 | tf_op jit(solution)/shard_map/ppermute | solution.py:452
  26.2 6.6 %collective-permute-start.12 = (bf16[6,16,512]{2,1,0:T(8,128)(2,1)S(1)}, bf16[6,16,512]{2,1,0:T(8,128)(2,1)S(1)}, u32[]{:S(2)}, u32[]{:S(2)}) collective-permute-start(bf16[6,16,512]{2,1,0:T(8,128)(2,1)S(1)} %get-tuple-element.82), channel_id=1, source_target_pairs={{0,8},{4,12},{8,0},{12,4},{16,24},{20,28},{24,16},{28,20},{1,9},{5... | collective-permute-start | bytes 294920 | tf_op jit(solution)/shard_map/ppermute | solution.py:452
  28.7 4.1 %collective-permute-start.13 = (bf16[6,16,512]{2,1,0:T(8,128)(2,1)S(1)}, bf16[6,16,512]{2,1,0:T(8,128)(2,1)S(1)}, u32[]{:S(2)}, u32[]{:S(2)}) collective-permute-start(bf16[6,16,512]{2,1,0:T(8,128)(2,1)S(1)} %get-tuple-element.83), channel_id=1, source_target_pairs={{0,4},{4,0},{8,12},{12,8},{16,20},{20,16},{24,28},{28,24},{1,5},{5... | collective-permute-start | bytes 294920 | tf_op jit(solution)/shard_map/ppermute | solution.py:452
  32.9 10.8 %collective-permute-start.14 = (bf16[128,512]{1,0:T(8,128)(2,1)S(1)}, bf16[128,512]{1,0:T(8,128)(2,1)S(1)}, u32[]{:S(2)}, u32[]{:S(2)}) collective-permute-start(bf16[128,512]{1,0:T(8,128)(2,1)S(1)} %get-tuple-element.93), channel_id=1, source_target_pairs={{0,2},{1,3},{2,0},{3,1},{4,6},{5,7},{6,4},{7,5},{8,10},{9,11},{10,... | collective-permute-start | bytes 393224 | tf_op jit(solution)/shard_map/ppermute | solution.py:452
  35.5 12.1 %collective-permute-start.18 = (bf16[128,512]{1,0:T(8,128)(2,1)S(1)}, bf16[128,512]{1,0:T(8,128)(2,1)S(1)}, u32[]{:S(2)}, u32[]{:S(2)}) collective-permute-start(bf16[128,512]{1,0:T(8,128)(2,1)S(1)} %get-tuple-element.99), channel_id=1, source_target_pairs={{0,1},{1,0},{2,3},{3,2},{4,5},{5,4},{6,7},{7,6},{8,9},{9,8},{10,11... | collective-permute-start | bytes 393224 | tf_op jit(solution)/shard_map/ppermute | solution.py:452
  37.1 10.5 %collective-permute-start.19 = (bf16[128,512]{1,0:T(8,128)(2,1)S(1)}, bf16[128,512]{1,0:T(8,128)(2,1)S(1)}, u32[]{:S(2)}, u32[]{:S(2)}) collective-permute-start(bf16[128,512]{1,0:T(8,128)(2,1)S(1)} %get-tuple-element.100), channel_id=1, source_target_pairs={{0,3},{1,2},{2,1},{3,0},{4,7},{5,6},{6,5},{7,4},{8,11},{9,10},{10,... | collective-permute-start | bytes 393224 | tf_op jit(solution)/shard_map/ppermute | solution.py:452
  43.7 14.1 %collective-permute-start.15 = (bf16[128,512]{1,0:T(8,128)(2,1)S(1)}, bf16[128,512]{1,0:T(8,128)(2,1)S(1)}, u32[]{:S(2)}, u32[]{:S(2)}) collective-permute-start(bf16[128,512]{1,0:T(8,128)(2,1)S(1)} %get-tuple-element.95), channel_id=1, source_target_pairs={{0,1},{3,2},{4,5},{7,6},{8,9},{11,10},{12,13},{15,14},{16,17},{19,... | collective-permute-start | bytes 393224 | tf_op jit(solution)/shard_map/ppermute | solution.py:452
  45.4 13.8 %collective-permute-start.16 = (bf16[128,512]{1,0:T(8,128)(2,1)S(1)}, bf16[128,512]{1,0:T(8,128)(2,1)S(1)}, u32[]{:S(2)}, u32[]{:S(2)}) collective-permute-start(bf16[128,512]{1,0:T(8,128)(2,1)S(1)} %get-tuple-element.96), channel_id=1, source_target_pairs={{0,2},{3,1},{4,6},{7,5},{8,10},{11,9},{12,14},{15,13},{16,18},{19,... | collective-permute-start | bytes 393224 | tf_op jit(solution)/shard_map/ppermute | solution.py:452
  46.8 12.5 %collective-permute-start.17 = (bf16[128,512]{1,0:T(8,128)(2,1)S(1)}, bf16[128,512]{1,0:T(8,128)(2,1)S(1)}, u32[]{:S(2)}, u32[]{:S(2)}) collective-permute-start(bf16[128,512]{1,0:T(8,128)(2,1)S(1)} %get-tuple-element.97), channel_id=1, source_target_pairs={{1,2},{2,1},{5,6},{6,5},{9,10},{10,9},{13,14},{14,13},{17,18},{18,... | collective-permute-start | bytes 393224 | tf_op jit(solution)/shard_map/ppermute | solution.py:452
  54.4 7.8 %collective-permute-start.23 = (bf16[128,512]{1,0:T(8,128)(2,1)S(1)}, bf16[128,512]{1,0:T(8,128)(2,1)S(1)}, u32[]{:S(2)}, u32[]{:S(2)}) collective-permute-start(bf16[128,512]{1,0:T(8,128)(2,1)S(1)} %get-tuple-element.106), channel_id=1, source_target_pairs={{0,1},{1,0},{2,3},{3,2},{4,5},{5,4},{6,7},{7,6},{8,9},{9,8},{10,11... | collective-permute-start | bytes 393224 | tf_op jit(solution)/shard_map/ppermute | solution.py:452
  55.5 7.4 %collective-permute-start.24 = (bf16[128,512]{1,0:T(8,128)(2,1)S(1)}, bf16[128,512]{1,0:T(8,128)(2,1)S(1)}, u32[]{:S(2)}, u32[]{:S(2)}) collective-permute-start(bf16[128,512]{1,0:T(8,128)(2,1)S(1)} %get-tuple-element.107), channel_id=1, source_target_pairs={{0,2},{1,3},{2,0},{3,1},{4,6},{5,7},{6,4},{7,5},{8,10},{9,11},{10,... | collective-permute-start | bytes 393224 | tf_op jit(solution)/shard_map/ppermute | solution.py:452
  57.8 10.3 %collective-permute-start.25 = (bf16[128,512]{1,0:T(8,128)(2,1)S(1)}, bf16[128,512]{1,0:T(8,128)(2,1)S(1)}, u32[]{:S(2)}, u32[]{:S(2)}) collective-permute-start(bf16[128,512]{1,0:T(8,128)(2,1)S(1)} %get-tuple-element.108), channel_id=1, source_target_pairs={{0,3},{1,2},{2,1},{3,0},{4,7},{5,6},{6,5},{7,4},{8,11},{9,10},{10,... | collective-permute-start | bytes 393224 | tf_op jit(solution)/shard_map/ppermute | solution.py:452
  59.2 13.7 %collective-permute-start.20 = (bf16[128,512]{1,0:T(8,128)(2,1)S(1)}, bf16[128,512]{1,0:T(8,128)(2,1)S(1)}, u32[]{:S(2)}, u32[]{:S(2)}) collective-permute-start(bf16[128,512]{1,0:T(8,128)(2,1)S(1)} %get-tuple-element.103), channel_id=1, source_target_pairs={{1,0},{2,3},{5,4},{6,7},{9,8},{10,11},{13,12},{14,15},{17,16},{18,... | collective-permute-start | bytes 393224 | tf_op jit(solution)/shard_map/ppermute | solution.py:520
  60.5 14.0 %collective-permute-start.21 = (bf16[128,512]{1,0:T(8,128)(2,1)S(1)}, bf16[128,512]{1,0:T(8,128)(2,1)S(1)}, u32[]{:S(2)}, u32[]{:S(2)}) collective-permute-start(bf16[128,512]{1,0:T(8,128)(2,1)S(1)} %get-tuple-element.104), channel_id=1, source_target_pairs={{1,3},{2,0},{5,7},{6,4},{9,11},{10,8},{13,15},{14,12},{17,19},{18,... | collective-permute-start | bytes 393224 | tf_op jit(solution)/shard_map/ppermute | solution.py:520
  62.2 12.3 %collective-permute-start.22 = (bf16[128,512]{1,0:T(8,128)(2,1)S(1)}, bf16[128,512]{1,0:T(8,128)(2,1)S(1)}, u32[]{:S(2)}, u32[]{:S(2)}) collective-permute-start(bf16[128,512]{1,0:T(8,128)(2,1)S(1)} %get-tuple-element.105), channel_id=1, source_target_pairs={{1,2},{2,1},{5,6},{6,5},{9,10},{10,9},{13,14},{14,13},{17,18},{18,... | collective-permute-start | bytes 393224 | tf_op jit(solution)/shard_map/ppermute | solution.py:520

commit v7 on v6

--- a/solution.py
+++ b/solution.py
@@ -169,13 +169,13 @@
     lanes_of = [slice(c * 128, (c + 1) * 128) for c in range(features // 128)]
     for k in range(size):
         start = pl.multiple_of(jnp.bitwise_xor(me, k) * rows, rows)
-        piece = pieces[k][...].reshape(rows, features).astype(jnp.float32)
+        piece = norm_of(pieces[k][...].reshape(rows, features).astype(jnp.float32)).astype(jnp.float32)
         for c, lanes in enumerate(lanes_of):
             wide[c, pl.ds(start, rows), :] = piece[:, lanes]
     for agent in range(agents):
         at = pl.ds(agent, total_steps, stride=agents)
         own = jnp.concatenate([wide[c, at, :] for c in range(len(lanes_of))], axis=1)
-        normed[pl.ds(agent * total_steps, total_steps), :] = norm_of(own)
+        normed[pl.ds(agent * total_steps, total_steps), :] = own.astype(jnp.bfloat16)
     group = 2 * total_steps
     span = -(-group // 128) * 128
     head_size = features // HEADS
@@ -223,12 +223,13 @@
         at = pl.ds(agent, total_steps, stride=agents)
         mine = added[agent * total_steps : (agent + 1) * total_steps]
         for c, lanes in enumerate(lanes_of):
-            wide[c, at, :] = wide[c, at, :] + mine[:, lanes]
+            wide[c, at, :] = mine[:, lanes]
     for k in range(size):
         start = pl.multiple_of(jnp.bitwise_xor(me, k) * rows, rows)
         piece = jnp.concatenate(
             [wide[c, pl.ds(start, rows), :] for c in range(len(lanes_of))], axis=1
         )
+        piece = piece + pieces[k][...].reshape(rows, features).astype(jnp.float32)
         outs[k][...] = piece.astype(jnp.bfloat16).reshape(pieces[0].shape)
 
 
@@ -401,10 +402,14 @@
     low = plane // 2
 
     def place(one, other):
-        copies = [
-            pltpu.make_async_copy(one, out.at[4 + low], sems.at[0]),
-            pltpu.make_async_copy(other, out.at[5 - low], sems.at[1]),
-        ]
+        rows = one.shape[0] // 4
+        copies = []
+        for n, (source, step) in enumerate(((one, 4 + low), (other, 5 - low))):
+            for part in range(4):
+                at = pl.ds(part * rows, rows)
+                copies.append(
+                    pltpu.make_async_copy(source.at[at], out.at[step, at], sems.at[n, part])
+                )
         for copy in copies:
             copy.start()
         for copy in copies:
@@ -432,7 +437,7 @@
         in_specs=[spec(VMEM)] * 4 + [spec(HBM)],
         out_specs=spec(HBM),
         input_output_aliases={4: 0},
-        scratch_shapes=[pltpu.SemaphoreType.DMA((2,))],
+        scratch_shapes=[pltpu.SemaphoreType.DMA((2, 4))],
         compiler_params=pltpu.CompilerParams(vmem_limit_bytes=4 * 2**20),
         name="place_extra",
     )(*[extra[k] for k in (0, 1, 2, 3)], begun)

time: 75.6 us -> 75.3 us (level)
  no operation moved by 1% of the time
where the time goes in v7:
time: 75.3 us; the launch traced here: 75 us
  starting transfers between devices  32.6 us (43%)
  waiting for transfers between devices  27.6 us (37%)
  Pallas kernels  14.3 us (19%)
    ppermute x23, starting transfers between devices, exchange(): moved[k] = lax.ppermute(part, axis, xor_pairs(size, k, targets))  29.3 us
    ppermute x23, waiting for transfers between devices, exchange(): moved[k] = lax.ppermute(part, axis, xor_pairs(size, k, targets))  22.1 us
    pallas_call x2, Pallas kernels, agent_stage(): pl.pallas_call(functools.partial(agent_kernel, count, middle_only), out_s...  6.69 us
    ppermute x3, waiting for transfers between devices, local(): lax.ppermute(result_b[k], 'agent', [(j, j ^ k) for j in (1, 2)])  5.58 us
    pallas_call x1, Pallas kernels, time_stage(): pl.pallas_call(functools.partial(time_kernel, size), out_shape=[jax.Shape...  4.5 us
    ppermute x3, starting transfers between devices, local(): lax.ppermute(result_b[k], 'agent', [(j, j ^ k) for j in (1, 2)])  3.24 us
  transfers between devices with their start and end apart: 26, of which 13 were waited for; matrix products, arithmetic and copies ran while one was open for 0% of the time, Pallas kernels for 10%

profile of v7, /device:TPU:0, one launch (start us, length us, event | category | flops | bytes accessed | tf_op | source)
XLA Modules:
  0.0 75.0 jit_solution(13768625678647413381)
XLA Ops:
  0.0 1.4 %cut_shares.1 = (bf16[6,16,512]{2,1,0:T(8,128)(2,1)S(1)}, bf16[6,16,512]{2,1,0:T(8,128)(2,1)S(1)}, bf16[6,16,512]{2,1,0:T(8,128)(2,1)S(1)}, bf16[6,16,512]{2,1,0...) custom-call(bf16[6,128,512]{2,1,0:T(8,128)(2,1)} %refs_0_.1), custom_call_target="tpu_custom_call" | custom-call | flops 20000000000 | bytes 10000000 | tf_op jit(solution)/shard_map/cut_shares/pallas_call | solution.py:148
  1.4 3.4 %collective-permute-start = (bf16[6,16,512]{2,1,0:T(8,128)(2,1)S(1)}, bf16[6,16,512]{2,1,0:T(8,128)(2,1)S(1)}, u32[]{:S(2)}, u32[]{:S(2)}) collective-permute-start(bf16[6,16,512]{2,1,0:T(8,128)(2,1)S(1)} %get-tuple-element.58), channel_id=1, source_target_pairs={{0,28},{4,24},{8,20},{12,16},{16,12},{20,8},{24,4},{28,0},{1,29},{... | collective-permute-start | bytes 294920 | tf_op jit(solution)/shard_map/ppermute | solution.py:457
  4.9 0.6 collective-permute-start.1
  5.5 1.4 %collective-permute-start.2 = (bf16[6,16,512]{2,1,0:T(8,128)(2,1)S(1)}, bf16[6,16,512]{2,1,0:T(8,128)(2,1)S(1)}, u32[]{:S(2)}, u32[]{:S(2)}) collective-permute-start(bf16[6,16,512]{2,1,0:T(8,128)(2,1)S(1)} %get-tuple-element.61), channel_id=1, source_target_pairs={{0,20},{4,16},{8,28},{12,24},{16,4},{20,0},{24,12},{28,8},{1,21},{... | collective-permute-start | bytes 294920 | tf_op jit(solution)/shard_map/ppermute | solution.py:457
  6.9 0.3 collective-permute-start.3
  7.2 1.1 %collective-permute-start.4 = (bf16[6,16,512]{2,1,0:T(8,128)(2,1)S(1)}, bf16[6,16,512]{2,1,0:T(8,128)(2,1)S(1)}, u32[]{:S(2)}, u32[]{:S(2)}) collective-permute-start(bf16[6,16,512]{2,1,0:T(8,128)(2,1)S(1)} %get-tuple-element.63), channel_id=1, source_target_pairs={{0,12},{4,8},{8,4},{12,0},{16,28},{20,24},{24,20},{28,16},{1,13},{... | collective-permute-start | bytes 294920 | tf_op jit(solution)/shard_map/ppermute | solution.py:457
  8.3 2.2 %collective-permute-start.5 = (bf16[6,16,512]{2,1,0:T(8,128)(2,1)S(1)}, bf16[6,16,512]{2,1,0:T(8,128)(2,1)S(1)}, u32[]{:S(2)}, u32[]{:S(2)}) collective-permute-start(bf16[6,16,512]{2,1,0:T(8,128)(2,1)S(1)} %get-tuple-element.64), channel_id=1, source_target_pairs={{0,8},{4,12},{8,0},{12,4},{16,24},{20,28},{24,16},{28,20},{1,9},{5... | collective-permute-start | bytes 294920 | tf_op jit(solution)/shard_map/ppermute | solution.py:457
  10.5 0.7 collective-permute-done.1.refs_6_
  11.2 1.2 %collective-permute-done.2.refs_5_ = bf16[6,16,512]{2,1,0:T(8,128)(2,1)S(1)} collective-permute-done((bf16[6,16,512]{2,1,0:T(8,128)(2,1)S(1)}, bf16[6,16,512]{2,1,0:T(8,128)(2,1)S(1)}, u32[]{:S(2)}, u32[]{:S(2)}) %collective-permute-start.2) | collective-permute-done | bytes 98336 | tf_op jit(solution)/shard_map/ppermute | solution.py:457
  12.5 2.3 %collective-permute-done.3.refs_4_ = bf16[6,16,512]{2,1,0:T(8,128)(2,1)S(1)} collective-permute-done((bf16[6,16,512]{2,1,0:T(8,128)(2,1)S(1)}, bf16[6,16,512]{2,1,0:T(8,128)(2,1)S(1)}, u32[]{:S(2)}, u32[]{:S(2)}) %collective-permute-start.3) | collective-permute-done | bytes 98336 | tf_op jit(solution)/shard_map/ppermute | solution.py:457
  14.8 0.6 collective-permute-done.5.refs_2_
  15.4 0.0 copy-start
  15.4 0.0 copy-start.1
  15.4 0.0 copy-start.6
  15.5 0.0 copy-start.7
  15.5 4.5 %time_attention.1 = (bf16[6,16,512]{2,1,0:T(8,128)(2,1)S(1)}, bf16[6,16,512]{2,1,0:T(8,128)(2,1)S(1)}, bf16[6,16,512]{2,1,0:T(8,128)(2,1)S(1)}, bf16[6,16,512]{2...) custom-call(bf16[6,16,512]{2,1,0:T(8,128)(2,1)S(1)} %get-tuple-eleme, ...), custom_call_target="tpu_custom_call" | custom-call | flops 1610612736 | bytes 3670016 | tf_op jit(solution)/shard_map/time_attention/pallas_call | solution.py:241
  20.0 2.1 %collective-permute-start.7 = (bf16[6,16,512]{2,1,0:T(8,128)(2,1)S(1)}, bf16[6,16,512]{2,1,0:T(8,128)(2,1)S(1)}, u32[]{:S(2)}, u32[]{:S(2)}) collective-permute-start(bf16[6,16,512]{2,1,0:T(8,128)(2,1)S(1)} %get-tuple-element.76), channel_id=1, source_target_pairs={{0,28},{4,24},{8,20},{12,16},{16,12},{20,8},{24,4},{28,0},{1,29},{... | collective-permute-start | bytes 294920 | tf_op jit(solution)/shard_map/ppermute | solution.py:457
  22.1 0.6 collective-permute-start.8
  22.7 1.2 %collective-permute-start.9 = (bf16[6,16,512]{2,1,0:T(8,128)(2,1)S(1)}, bf16[6,16,512]{2,1,0:T(8,128)(2,1)S(1)}, u32[]{:S(2)}, u32[]{:S(2)}) collective-permute-start(bf16[6,16,512]{2,1,0:T(8,128)(2,1)S(1)} %get-tuple-element.79), channel_id=1, source_target_pairs={{0,20},{4,16},{8,28},{12,24},{16,4},{20,0},{24,12},{28,8},{1,21},{... | collective-permute-start | bytes 294920 | tf_op jit(solution)/shard_map/ppermute | solution.py:457
  23.9 0.6 collective-permute-start.10
  24.5 1.1 %collective-permute-start.11 = (bf16[6,16,512]{2,1,0:T(8,128)(2,1)S(1)}, bf16[6,16,512]{2,1,0:T(8,128)(2,1)S(1)}, u32[]{:S(2)}, u32[]{:S(2)}) collective-permute-start(bf16[6,16,512]{2,1,0:T(8,128)(2,1)S(1)} %get-tuple-element.81), channel_id=1, source_target_pairs={{0,12},{4,8},{8,4},{12,0},{16,28},{20,24},{24,20},{28,16},{1,13},{... | collective-permute-start | bytes 294920 | tf_op jit(solution)/shard_map/ppermute | solution.py:457
  25.6 0.1 collective-permute-done.7.refs_7_
  25.8 1.5 %collective-permute-start.12 = (bf16[6,16,512]{2,1,0:T(8,128)(2,1)S(1)}, bf16[6,16,512]{2,1,0:T(8,128)(2,1)S(1)}, u32[]{:S(2)}, u32[]{:S(2)}) collective-permute-start(bf16[6,16,512]{2,1,0:T(8,128)(2,1)S(1)} %get-tuple-element.82), channel_id=1, source_target_pairs={{0,8},{4,12},{8,0},{12,4},{16,24},{20,28},{24,16},{28,20},{1,9},{5... | collective-permute-start | bytes 294920 | tf_op jit(solution)/shard_map/ppermute | solution.py:457
  27.3 1.0 %collective-permute-done.8.refs_6_ = bf16[6,16,512]{2,1,0:T(8,128)(2,1)S(1)} collective-permute-done((bf16[6,16,512]{2,1,0:T(8,128)(2,1)S(1)}, bf16[6,16,512]{2,1,0:T(8,128)(2,1)S(1)}, u32[]{:S(2)}, u32[]{:S(2)}) %collective-permute-start.8) | collective-permute-done | bytes 98336 | tf_op jit(solution)/shard_map/ppermute | solution.py:457
  28.3 2.0 %collective-permute-done.9.refs_5_ = bf16[6,16,512]{2,1,0:T(8,128)(2,1)S(1)} collective-permute-done((bf16[6,16,512]{2,1,0:T(8,128)(2,1)S(1)}, bf16[6,16,512]{2,1,0:T(8,128)(2,1)S(1)}, u32[]{:S(2)}, u32[]{:S(2)}) %collective-permute-start.9) | collective-permute-done | bytes 98336 | tf_op jit(solution)/shard_map/ppermute | solution.py:457
  30.2 2.1 %collective-permute-done.10.refs_4_ = bf16[6,16,512]{2,1,0:T(8,128)(2,1)S(1)} collective-permute-done((bf16[6,16,512]{2,1,0:T(8,128)(2,1)S(1)}, bf16[6,16,512]{2,1,0:T(8,128)(2,1)S(1)}, u32[]{:S(2)}, u32[]{:S(2)}) %collective-permute-start.10) | collective-permute-done | bytes 98336 | tf_op jit(solution)/shard_map/ppermute | solution.py:457
  32.4 0.0 collective-permute-done.12.refs_2_
  32.4 0.1 pack_steps.2
  32.5 2.6 %collective-permute-start.14 = (bf16[128,512]{1,0:T(8,128)(2,1)S(1)}, bf16[128,512]{1,0:T(8,128)(2,1)S(1)}, u32[]{:S(2)}, u32[]{:S(2)}) collective-permute-start(bf16[128,512]{1,0:T(8,128)(2,1)S(1)} %get-tuple-element.93), channel_id=1, source_target_pairs={{0,2},{1,3},{2,0},{3,1},{4,6},{5,7},{6,4},{7,5},{8,10},{9,11},{10,... | collective-permute-start | bytes 393224 | tf_op jit(solution)/shard_map/ppermute | solution.py:457
  35.1 1.6 %collective-permute-start.18 = (bf16[128,512]{1,0:T(8,128)(2,1)S(1)}, bf16[128,512]{1,0:T(8,128)(2,1)S(1)}, u32[]{:S(2)}, u32[]{:S(2)}) collective-permute-start(bf16[128,512]{1,0:T(8,128)(2,1)S(1)} %get-tuple-element.99), channel_id=1, source_target_pairs={{0,1},{1,0},{2,3},{3,2},{4,5},{5,4},{6,7},{7,6},{8,9},{9,8},{10,11... | collective-permute-start | bytes 393224 | tf_op jit(solution)/shard_map/ppermute | solution.py:457
  36.7 0.2 collective-permute-start.19
  36.9 6.3 %collective-permute-done.14.refs_8_.refs_2_ = bf16[128,512]{1,0:T(8,128)(2,1)S(1)} collective-permute-done((bf16[128,512]{1,0:T(8,128)(2,1)S(1)}, bf16[128,512]{1,0:T(8,128)(2,1)S(1)}, u32[]{:S(2)}, u32[]{:S(2)}) %collective-permute-start.14) | collective-permute-done | bytes 131104 | tf_op jit(solution)/shard_map/ppermute | solution.py:457
  43.3 1.7 %collective-permute-start.15 = (bf16[128,512]{1,0:T(8,128)(2,1)S(1)}, bf16[128,512]{1,0:T(8,128)(2,1)S(1)}, u32[]{:S(2)}, u32[]{:S(2)}) collective-permute-start(bf16[128,512]{1,0:T(8,128)(2,1)S(1)} %get-tuple-element.95), channel_id=1, source_target_pairs={{0,1},{3,2},{4,5},{7,6},{8,9},{11,10},{12,13},{15,14},{16,17},{19,... | collective-permute-start | bytes 393224 | tf_op jit(solution)/shard_map/ppermute | solution.py:457
  45.0 1.3 %collective-permute-start.16 = (bf16[128,512]{1,0:T(8,128)(2,1)S(1)}, bf16[128,512]{1,0:T(8,128)(2,1)S(1)}, u32[]{:S(2)}, u32[]{:S(2)}) collective-permute-start(bf16[128,512]{1,0:T(8,128)(2,1)S(1)} %get-tuple-element.96), channel_id=1, source_target_pairs={{0,2},{3,1},{4,6},{7,5},{8,10},{11,9},{12,14},{15,13},{16,18},{19,... | collective-permute-start | bytes 393224 | tf_op jit(solution)/shard_map/ppermute | solution.py:457
  46.3 0.8 %collective-permute-start.17 = (bf16[128,512]{1,0:T(8,128)(2,1)S(1)}, bf16[128,512]{1,0:T(8,128)(2,1)S(1)}, u32[]{:S(2)}, u32[]{:S(2)}) collective-permute-start(bf16[128,512]{1,0:T(8,128)(2,1)S(1)} %get-tuple-element.97), channel_id=1, source_target_pairs={{1,2},{2,1},{5,6},{6,5},{9,10},{10,9},{13,14},{14,13},{17,18},{18,... | collective-permute-start | bytes 393224 | tf_op jit(solution)/shard_map/ppermute | solution.py:457
  47.3 6.7 %agent_step.2 = (bf16[128,512]{1,0:T(8,128)(2,1)S(1)}, bf16[128,512]{1,0:T(8,128)(2,1)S(1)}, bf16[128,512]{1,0:T(8,128)(2,1)S(1)}, bf16[128,512]{1,0:T(8,128)(2,1)S(1)}) custom-call(bf16[128,512]{1,0:T(8,128)(2,1)S(1)} %get-tuple-element.98.refs_0_, bf16[128,512]{1,0:T(8,128)(2,1)S(1)} %collective-permute-done.18.refs_1_, ...), custom_call_target="tpu_custom_call" | custom-call | flops 3758096384 | bytes 4194304 | tf_op jit(solution)/shard_map/agent_step/pallas_call | solution.py:362
  54.0 1.1 %collective-permute-start.23 = (bf16[128,512]{1,0:T(8,128)(2,1)S(1)}, bf16[128,512]{1,0:T(8,128)(2,1)S(1)}, u32[]{:S(2)}, u32[]{:S(2)}) collective-permute-start(bf16[128,512]{1,0:T(8,128)(2,1)S(1)} %get-tuple-element.106), channel_id=1, source_target_pairs={{0,1},{1,0},{2,3},{3,2},{4,5},{5,4},{6,7},{7,6},{8,9},{9,8},{10,11... | collective-permute-start | bytes 393224 | tf_op jit(solution)/shard_map/ppermute | solution.py:457
  55.1 2.3 %collective-permute-start.24 = (bf16[128,512]{1,0:T(8,128)(2,1)S(1)}, bf16[128,512]{1,0:T(8,128)(2,1)S(1)}, u32[]{:S(2)}, u32[]{:S(2)}) collective-permute-start(bf16[128,512]{1,0:T(8,128)(2,1)S(1)} %get-tuple-element.107), channel_id=1, source_target_pairs={{0,2},{1,3},{2,0},{3,1},{4,6},{5,7},{6,4},{7,5},{8,10},{9,11},{10,... | collective-permute-start | bytes 393224 | tf_op jit(solution)/shard_map/ppermute | solution.py:457
  57.4 1.4 %collective-permute-start.25 = (bf16[128,512]{1,0:T(8,128)(2,1)S(1)}, bf16[128,512]{1,0:T(8,128)(2,1)S(1)}, u32[]{:S(2)}, u32[]{:S(2)}) collective-permute-start(bf16[128,512]{1,0:T(8,128)(2,1)S(1)} %get-tuple-element.108), channel_id=1, source_target_pairs={{0,3},{1,2},{2,1},{3,0},{4,7},{5,6},{6,5},{7,4},{8,11},{9,10},{10,... | collective-permute-start | bytes 393224 | tf_op jit(solution)/shard_map/ppermute | solution.py:457
  58.8 1.3 %collective-permute-start.20 = (bf16[128,512]{1,0:T(8,128)(2,1)S(1)}, bf16[128,512]{1,0:T(8,128)(2,1)S(1)}, u32[]{:S(2)}, u32[]{:S(2)}) collective-permute-start(bf16[128,512]{1,0:T(8,128)(2,1)S(1)} %get-tuple-element.103), channel_id=1, source_target_pairs={{1,0},{2,3},{5,4},{6,7},{9,8},{10,11},{13,12},{14,15},{17,16},{18,... | collective-permute-start | bytes 393224 | tf_op jit(solution)/shard_map/ppermute | solution.py:525
  60.1 1.3 %collective-permute-start.21 = (bf16[128,512]{1,0:T(8,128)(2,1)S(1)}, bf16[128,512]{1,0:T(8,128)(2,1)S(1)}, u32[]{:S(2)}, u32[]{:S(2)}) collective-permute-start(bf16[128,512]{1,0:T(8,128)(2,1)S(1)} %get-tuple-element.104), channel_id=1, source_target_pairs={{1,3},{2,0},{5,7},{6,4},{9,11},{10,8},{13,15},{14,12},{17,19},{18,... | collective-permute-start | bytes 393224 | tf_op jit(solution)/shard_map/ppermute | solution.py:525
  61.4 0.4 collective-permute-done.23.refs_1_
  61.8 0.7 collective-permute-start.22
  62.5 5.2 %collective-permute-done.25.refs_3_ = bf16[128,512]{1,0:T(8,128)(2,1)S(1)} collective-permute-done((bf16[128,512]{1,0:T(8,128)(2,1)S(1)}, bf16[128,512]{1,0:T(8,128)(2,1)S(1)}, u32[]{:S(2)}, u32[]{:S(2)}) %collective-permute-start.25) | collective-permute-done | bytes 131104 | tf_op jit(solution)/shard_map/ppermute | solution.py:457
  67.7 0.8 %place_steps.1.refs_4_ = bf16[6,128,512]{2,1,0:T(8,128)(2,1)} custom-call(bf16[128,512]{1,0:T(8,128)(2,1)S(1)} %get-tuple-element.101.refs_10_.refs_0_, bf16[128,512]{1,0:T(8,128)(2,1)S(1)} %collective-permute-done.23.refs_1_, bf16[128,512]{1,0:T(8,128)(2,1)S(1)} %collective-permute-done.24.refs_2_, bf16[128,512]{1,0:T(8,128)(2,1)S(1)} %collective-permute-done.25.refs_3_), custom_call_target="tpu_custom_call" | custom-call | tf_op jit(solution)/shard_map/place_steps/pallas_call | solution.py:425
  68.5 4.0 %collective-permute-done.20.refs_1_ = bf16[128,512]{1,0:T(8,128)(2,1)S(1)} collective-permute-done((bf16[128,512]{1,0:T(8,128)(2,1)S(1)}, bf16[128,512]{1,0:T(8,128)(2,1)S(1)}, u32[]{:S(2)}, u32[]{:S(2)}) %collective-permute-start.20) | collective-permute-done | bytes 131104 | tf_op jit(solution)/shard_map/ppermute | solution.py:525
  72.5 1.5 %collective-permute-done.21.refs_2_ = bf16[128,512]{1,0:T(8,128)(2,1)S(1)} collective-permute-done((bf16[128,512]{1,0:T(8,128)(2,1)S(1)}, bf16[128,512]{1,0:T(8,128)(2,1)S(1)}, u32[]{:S(2)}, u32[]{:S(2)}) %collective-permute-start.21) | collective-permute-done | bytes 131104 | tf_op jit(solution)/shard_map/ppermute | solution.py:525
  74.1 0.8 %place_extra.1 = bf16[6,128,512]{2,1,0:T(8,128)(2,1)} custom-call(bf16[128,512]{1,0:T(8,128)(2,1)S(1)} %get-tuple-element.102.refs_0_, bf16[128,512]{1,0:T(8,128)(2,1)S(1)} %collective-permute-done.20.refs_1_, bf16[128,512]{1,0:T(8,128)(2,1)S(1)} %collective-permute-done.21.refs_2_, ...), custom_call_target="tpu_custom_call", output_to_operand_aliasing={{}: (4, {})} | custom-call | tf_op jit(solution)/shard_map/place_extra/pallas_call | solution.py:434
  (30 shorter events, 0.1 us)
Async XLA Ops:
  0.0 15.4 %copy-start.5 = (bf16[512,512]{1,0:T(8,128)(2,1)S(1)}, bf16[512,512]{1,0:T(8,128)(2,1)}, u32[]{:S(2)}) copy-start(bf16[512,512]{1,0:T(8,128)(2,1)} %refs_11_.1) | copy-start | bytes 1572868
  0.0 15.4 %copy-start.4 = (bf16[512,512]{1,0:T(8,128)(2,1)S(1)}, bf16[512,512]{1,0:T(8,128)(2,1)}, u32[]{:S(2)}) copy-start(bf16[512,512]{1,0:T(8,128)(2,1)} %refs_10_.1) | copy-start | bytes 1572868
  0.0 15.4 %copy-start.3 = (bf16[512,512]{1,0:T(8,128)(2,1)S(1)}, bf16[512,512]{1,0:T(8,128)(2,1)}, u32[]{:S(2)}) copy-start(bf16[512,512]{1,0:T(8,128)(2,1)} %refs_9_.3) | copy-start | bytes 1572868
  0.0 15.4 %copy-start.2 = (bf16[512,512]{1,0:T(8,128)(2,1)S(1)}, bf16[512,512]{1,0:T(8,128)(2,1)}, u32[]{:S(2)}) copy-start(bf16[512,512]{1,0:T(8,128)(2,1)} %refs_8_.3) | copy-start | bytes 1572868
  1.4 6.9 %collective-permute-start = (bf16[6,16,512]{2,1,0:T(8,128)(2,1)S(1)}, bf16[6,16,512]{2,1,0:T(8,128)(2,1)S(1)}, u32[]{:S(2)}, u32[]{:S(2)}) collective-permute-start(bf16[6,16,512]{2,1,0:T(8,128)(2,1)S(1)} %get-tuple-element.58), channel_id=1, source_target_pairs={{0,28},{4,24},{8,20},{12,16},{16,12},{20,8},{24,4},{28,0},{1,29},{... | collective-permute-start | bytes 294920 | tf_op jit(solution)/shard_map/ppermute | solution.py:457
  4.9 6.4 %collective-permute-start.1 = (bf16[6,16,512]{2,1,0:T(8,128)(2,1)S(1)}, bf16[6,16,512]{2,1,0:T(8,128)(2,1)S(1)}, u32[]{:S(2)}, u32[]{:S(2)}) collective-permute-start(bf16[6,16,512]{2,1,0:T(8,128)(2,1)S(1)} %get-tuple-element.60), channel_id=1, source_target_pairs={{0,24},{4,28},{8,16},{12,20},{16,8},{20,12},{24,0},{28,4},{1,25},{... | collective-permute-start | bytes 294920 | tf_op jit(solution)/shard_map/ppermute | solution.py:457
  5.5 7.0 %collective-permute-start.2 = (bf16[6,16,512]{2,1,0:T(8,128)(2,1)S(1)}, bf16[6,16,512]{2,1,0:T(8,128)(2,1)S(1)}, u32[]{:S(2)}, u32[]{:S(2)}) collective-permute-start(bf16[6,16,512]{2,1,0:T(8,128)(2,1)S(1)} %get-tuple-element.61), channel_id=1, source_target_pairs={{0,20},{4,16},{8,28},{12,24},{16,4},{20,0},{24,12},{28,8},{1,21},{... | collective-permute-start | bytes 294920 | tf_op jit(solution)/shard_map/ppermute | solution.py:457
  6.9 7.9 %collective-permute-start.3 = (bf16[6,16,512]{2,1,0:T(8,128)(2,1)S(1)}, bf16[6,16,512]{2,1,0:T(8,128)(2,1)S(1)}, u32[]{:S(2)}, u32[]{:S(2)}) collective-permute-start(bf16[6,16,512]{2,1,0:T(8,128)(2,1)S(1)} %get-tuple-element.62), channel_id=1, source_target_pairs={{0,16},{4,20},{8,24},{12,28},{16,0},{20,4},{24,8},{28,12},{1,17},{... | collective-permute-start | bytes 294920 | tf_op jit(solution)/shard_map/ppermute | solution.py:457
  7.2 7.6 %collective-permute-start.4 = (bf16[6,16,512]{2,1,0:T(8,128)(2,1)S(1)}, bf16[6,16,512]{2,1,0:T(8,128)(2,1)S(1)}, u32[]{:S(2)}, u32[]{:S(2)}) collective-permute-start(bf16[6,16,512]{2,1,0:T(8,128)(2,1)S(1)} %get-tuple-element.63), channel_id=1, source_target_pairs={{0,12},{4,8},{8,4},{12,0},{16,28},{20,24},{24,20},{28,16},{1,13},{... | collective-permute-start | bytes 294920 | tf_op jit(solution)/shard_map/ppermute | solution.py:457
  8.3 7.1 %collective-permute-start.5 = (bf16[6,16,512]{2,1,0:T(8,128)(2,1)S(1)}, bf16[6,16,512]{2,1,0:T(8,128)(2,1)S(1)}, u32[]{:S(2)}, u32[]{:S(2)}) collective-permute-start(bf16[6,16,512]{2,1,0:T(8,128)(2,1)S(1)} %get-tuple-element.64), channel_id=1, source_target_pairs={{0,8},{4,12},{8,0},{12,4},{16,24},{20,28},{24,16},{28,20},{1,9},{5... | collective-permute-start | bytes 294920 | tf_op jit(solution)/shard_map/ppermute | solution.py:457
  11.2 4.1 %collective-permute-start.6 = (bf16[6,16,512]{2,1,0:T(8,128)(2,1)S(1)}, bf16[6,16,512]{2,1,0:T(8,128)(2,1)S(1)}, u32[]{:S(2)}, u32[]{:S(2)}) collective-permute-start(bf16[6,16,512]{2,1,0:T(8,128)(2,1)S(1)} %get-tuple-element.65), channel_id=1, source_target_pairs={{0,4},{4,0},{8,12},{12,8},{16,20},{20,16},{24,28},{28,24},{1,5},{5... | collective-permute-start | bytes 294920 | tf_op jit(solution)/shard_map/ppermute | solution.py:457
  15.4 31.8 %copy-start = (bf16[512,2048]{1,0:T(8,128)(2,1)S(1)}, bf16[512,2048]{1,0:T(8,128)(2,1)}, u32[]{:S(2)}) copy-start(bf16[512,2048]{1,0:T(8,128)(2,1)} %refs_8_.5) | copy-start | bytes 6291460
  15.4 31.8 %copy-start.1 = (bf16[2048,512]{1,0:T(8,128)(2,1)S(1)}, bf16[2048,512]{1,0:T(8,128)(2,1)}, u32[]{:S(2)}) copy-start(bf16[2048,512]{1,0:T(8,128)(2,1)} %refs_9_.5) | copy-start | bytes 6291460
  15.4 31.8 %copy-start.6 = (bf16[512,512]{1,0:T(8,128)(2,1)S(1)}, bf16[512,512]{1,0:T(8,128)(2,1)}, u32[]{:S(2)}) copy-start(bf16[512,512]{1,0:T(8,128)(2,1)} %refs_4_.3) | copy-start | bytes 1572868
  15.5 31.8 %copy-start.7 = (bf16[512,512]{1,0:T(8,128)(2,1)S(1)}, bf16[512,512]{1,0:T(8,128)(2,1)}, u32[]{:S(2)}) copy-start(bf16[512,512]{1,0:T(8,128)(2,1)} %refs_5_.3) | copy-start | bytes 1572868
  15.5 31.8 %copy-start.8 = (bf16[512,512]{1,0:T(8,128)(2,1)S(1)}, bf16[512,512]{1,0:T(8,128)(2,1)}, u32[]{:S(2)}) copy-start(bf16[512,512]{1,0:T(8,128)(2,1)} %refs_6_.3) | copy-start | bytes 1572868
  20.0 5.8 %collective-permute-start.7 = (bf16[6,16,512]{2,1,0:T(8,128)(2,1)S(1)}, bf16[6,16,512]{2,1,0:T(8,128)(2,1)S(1)}, u32[]{:S(2)}, u32[]{:S(2)}) collective-permute-start(bf16[6,16,512]{2,1,0:T(8,128)(2,1)S(1)} %get-tuple-element.76), channel_id=1, source_target_pairs={{0,28},{4,24},{8,20},{12,16},{16,12},{20,8},{24,4},{28,0},{1,29},{... | collective-permute-start | bytes 294920 | tf_op jit(solution)/shard_map/ppermute | solution.py:457
  22.1 6.2 %collective-permute-start.8 = (bf16[6,16,512]{2,1,0:T(8,128)(2,1)S(1)}, bf16[6,16,512]{2,1,0:T(8,128)(2,1)S(1)}, u32[]{:S(2)}, u32[]{:S(2)}) collective-permute-start(bf16[6,16,512]{2,1,0:T(8,128)(2,1)S(1)} %get-tuple-element.78), channel_id=1, source_target_pairs={{0,24},{4,28},{8,16},{12,20},{16,8},{20,12},{24,0},{28,4},{1,25},{... | collective-permute-start | bytes 294920 | tf_op jit(solution)/shard_map/ppermute | solution.py:457
  22.7 7.5 %collective-permute-start.9 = (bf16[6,16,512]{2,1,0:T(8,128)(2,1)S(1)}, bf16[6,16,512]{2,1,0:T(8,128)(2,1)S(1)}, u32[]{:S(2)}, u32[]{:S(2)}) collective-permute-start(bf16[6,16,512]{2,1,0:T(8,128)(2,1)S(1)} %get-tuple-element.79), channel_id=1, source_target_pairs={{0,20},{4,16},{8,28},{12,24},{16,4},{20,0},{24,12},{28,8},{1,21},{... | collective-permute-start | bytes 294920 | tf_op jit(solution)/shard_map/ppermute | solution.py:457
  23.9 8.5 %collective-permute-start.10 = (bf16[6,16,512]{2,1,0:T(8,128)(2,1)S(1)}, bf16[6,16,512]{2,1,0:T(8,128)(2,1)S(1)}, u32[]{:S(2)}, u32[]{:S(2)}) collective-permute-start(bf16[6,16,512]{2,1,0:T(8,128)(2,1)S(1)} %get-tuple-element.80), channel_id=1, source_target_pairs={{0,16},{4,20},{8,24},{12,28},{16,0},{20,4},{24,8},{28,12},{1,17},{... | collective-permute-start | bytes 294920 | tf_op jit(solution)/shard_map/ppermute | solution.py:457
  24.5 7.9 %collective-permute-start.11 = (bf16[6,16,512]{2,1,0:T(8,128)(2,1)S(1)}, bf16[6,16,512]{2,1,0:T(8,128)(2,1)S(1)}, u32[]{:S(2)}, u32[]{:S(2)}) collective-permute-start(bf16[6,16,512]{2,1,0:T(8,128)(2,1)S(1)} %get-tuple-element.81), channel_id=1, source_target_pairs={{0,12},{4,8},{8,4},{12,0},{16,28},{20,24},{24,20},{28,16},{1,13},{... | collective-permute-start | bytes 294920 | tf_op jit(solution)/shard_map/ppermute | solution.py:457
  25.8 6.6 %collective-permute-start.12 = (bf16[6,16,512]{2,1,0:T(8,128)(2,1)S(1)}, bf16[6,16,512]{2,1,0:T(8,128)(2,1)S(1)}, u32[]{:S(2)}, u32[]{:S(2)}) collective-permute-start(bf16[6,16,512]{2,1,0:T(8,128)(2,1)S(1)} %get-tuple-element.82), channel_id=1, source_target_pairs={{0,8},{4,12},{8,0},{12,4},{16,24},{20,28},{24,16},{28,20},{1,9},{5... | collective-permute-start | bytes 294920 | tf_op jit(solution)/shard_map/ppermute | solution.py:457
  28.3 4.1 %collective-permute-start.13 = (bf16[6,16,512]{2,1,0:T(8,128)(2,1)S(1)}, bf16[6,16,512]{2,1,0:T(8,128)(2,1)S(1)}, u32[]{:S(2)}, u32[]{:S(2)}) collective-permute-start(bf16[6,16,512]{2,1,0:T(8,128)(2,1)S(1)} %get-tuple-element.83), channel_id=1, source_target_pairs={{0,4},{4,0},{8,12},{12,8},{16,20},{20,16},{24,28},{28,24},{1,5},{5... | collective-permute-start | bytes 294920 | tf_op jit(solution)/shard_map/ppermute | solution.py:457
  32.5 10.8 %collective-permute-start.14 = (bf16[128,512]{1,0:T(8,128)(2,1)S(1)}, bf16[128,512]{1,0:T(8,128)(2,1)S(1)}, u32[]{:S(2)}, u32[]{:S(2)}) collective-permute-start(bf16[128,512]{1,0:T(8,128)(2,1)S(1)} %get-tuple-element.93), channel_id=1, source_target_pairs={{0,2},{1,3},{2,0},{3,1},{4,6},{5,7},{6,4},{7,5},{8,10},{9,11},{10,... | collective-permute-start | bytes 393224 | tf_op jit(solution)/shard_map/ppermute | solution.py:457
  35.1 12.1 %collective-permute-start.18 = (bf16[128,512]{1,0:T(8,128)(2,1)S(1)}, bf16[128,512]{1,0:T(8,128)(2,1)S(1)}, u32[]{:S(2)}, u32[]{:S(2)}) collective-permute-start(bf16[128,512]{1,0:T(8,128)(2,1)S(1)} %get-tuple-element.99), channel_id=1, source_target_pairs={{0,1},{1,0},{2,3},{3,2},{4,5},{5,4},{6,7},{7,6},{8,9},{9,8},{10,11... | collective-permute-start | bytes 393224 | tf_op jit(solution)/shard_map/ppermute | solution.py:457
  36.7 10.5 %collective-permute-start.19 = (bf16[128,512]{1,0:T(8,128)(2,1)S(1)}, bf16[128,512]{1,0:T(8,128)(2,1)S(1)}, u32[]{:S(2)}, u32[]{:S(2)}) collective-permute-start(bf16[128,512]{1,0:T(8,128)(2,1)S(1)} %get-tuple-element.100), channel_id=1, source_target_pairs={{0,3},{1,2},{2,1},{3,0},{4,7},{5,6},{6,5},{7,4},{8,11},{9,10},{10,... | collective-permute-start | bytes 393224 | tf_op jit(solution)/shard_map/ppermute | solution.py:457
  43.3 14.1 %collective-permute-start.15 = (bf16[128,512]{1,0:T(8,128)(2,1)S(1)}, bf16[128,512]{1,0:T(8,128)(2,1)S(1)}, u32[]{:S(2)}, u32[]{:S(2)}) collective-permute-start(bf16[128,512]{1,0:T(8,128)(2,1)S(1)} %get-tuple-element.95), channel_id=1, source_target_pairs={{0,1},{3,2},{4,5},{7,6},{8,9},{11,10},{12,13},{15,14},{16,17},{19,... | collective-permute-start | bytes 393224 | tf_op jit(solution)/shard_map/ppermute | solution.py:457
  45.0 13.8 %collective-permute-start.16 = (bf16[128,512]{1,0:T(8,128)(2,1)S(1)}, bf16[128,512]{1,0:T(8,128)(2,1)S(1)}, u32[]{:S(2)}, u32[]{:S(2)}) collective-permute-start(bf16[128,512]{1,0:T(8,128)(2,1)S(1)} %get-tuple-element.96), channel_id=1, source_target_pairs={{0,2},{3,1},{4,6},{7,5},{8,10},{11,9},{12,14},{15,13},{16,18},{19,... | collective-permute-start | bytes 393224 | tf_op jit(solution)/shard_map/ppermute | solution.py:457
  46.3 12.5 %collective-permute-start.17 = (bf16[128,512]{1,0:T(8,128)(2,1)S(1)}, bf16[128,512]{1,0:T(8,128)(2,1)S(1)}, u32[]{:S(2)}, u32[]{:S(2)}) collective-permute-start(bf16[128,512]{1,0:T(8,128)(2,1)S(1)} %get-tuple-element.97), channel_id=1, source_target_pairs={{1,2},{2,1},{5,6},{6,5},{9,10},{10,9},{13,14},{14,13},{17,18},{18,... | collective-permute-start | bytes 393224 | tf_op jit(solution)/shard_map/ppermute | solution.py:457
  54.0 7.8 %collective-permute-start.23 = (bf16[128,512]{1,0:T(8,128)(2,1)S(1)}, bf16[128,512]{1,0:T(8,128)(2,1)S(1)}, u32[]{:S(2)}, u32[]{:S(2)}) collective-permute-start(bf16[128,512]{1,0:T(8,128)(2,1)S(1)} %get-tuple-element.106), channel_id=1, source_target_pairs={{0,1},{1,0},{2,3},{3,2},{4,5},{5,4},{6,7},{7,6},{8,9},{9,8},{10,11... | collective-permute-start | bytes 393224 | tf_op jit(solution)/shard_map/ppermute | solution.py:457
  55.1 7.4 %collective-permute-start.24 = (bf16[128,512]{1,0:T(8,128)(2,1)S(1)}, bf16[128,512]{1,0:T(8,128)(2,1)S(1)}, u32[]{:S(2)}, u32[]{:S(2)}) collective-permute-start(bf16[128,512]{1,0:T(8,128)(2,1)S(1)} %get-tuple-element.107), channel_id=1, source_target_pairs={{0,2},{1,3},{2,0},{3,1},{4,6},{5,7},{6,4},{7,5},{8,10},{9,11},{10,... | collective-permute-start | bytes 393224 | tf_op jit(solution)/shard_map/ppermute | solution.py:457
  57.4 10.3 %collective-permute-start.25 = (bf16[128,512]{1,0:T(8,128)(2,1)S(1)}, bf16[128,512]{1,0:T(8,128)(2,1)S(1)}, u32[]{:S(2)}, u32[]{:S(2)}) collective-permute-start(bf16[128,512]{1,0:T(8,128)(2,1)S(1)} %get-tuple-element.108), channel_id=1, source_target_pairs={{0,3},{1,2},{2,1},{3,0},{4,7},{5,6},{6,5},{7,4},{8,11},{9,10},{10,... | collective-permute-start | bytes 393224 | tf_op jit(solution)/shard_map/ppermute | solution.py:457
  58.8 13.7 %collective-permute-start.20 = (bf16[128,512]{1,0:T(8,128)(2,1)S(1)}, bf16[128,512]{1,0:T(8,128)(2,1)S(1)}, u32[]{:S(2)}, u32[]{:S(2)}) collective-permute-start(bf16[128,512]{1,0:T(8,128)(2,1)S(1)} %get-tuple-element.103), channel_id=1, source_target_pairs={{1,0},{2,3},{5,4},{6,7},{9,8},{10,11},{13,12},{14,15},{17,16},{18,... | collective-permute-start | bytes 393224 | tf_op jit(solution)/shard_map/ppermute | solution.py:525
  60.1 14.0 %collective-permute-start.21 = (bf16[128,512]{1,0:T(8,128)(2,1)S(1)}, bf16[128,512]{1,0:T(8,128)(2,1)S(1)}, u32[]{:S(2)}, u32[]{:S(2)}) collective-permute-start(bf16[128,512]{1,0:T(8,128)(2,1)S(1)} %get-tuple-element.104), channel_id=1, source_target_pairs={{1,3},{2,0},{5,7},{6,4},{9,11},{10,8},{13,15},{14,12},{17,19},{18,... | collective-permute-start | bytes 393224 | tf_op jit(solution)/shard_map/ppermute | solution.py:525
  61.8 12.3 %collective-permute-start.22 = (bf16[128,512]{1,0:T(8,128)(2,1)S(1)}, bf16[128,512]{1,0:T(8,128)(2,1)S(1)}, u32[]{:S(2)}, u32[]{:S(2)}) collective-permute-start(bf16[128,512]{1,0:T(8,128)(2,1)S(1)} %get-tuple-element.105), channel_id=1, source_target_pairs={{1,2},{2,1},{5,6},{6,5},{9,10},{10,9},{13,14},{14,13},{17,18},{18,... | collective-permute-start | bytes 393224 | tf_op jit(solution)/shard_map/ppermute | solution.py:525

commit v8 on v7

--- a/solution.py
+++ b/solution.py
@@ -281,23 +281,56 @@
     )(*pieces, *after)
 
 
-def agent_body(count, blocks, weights, outs, scratch):
+def near_kernel(count, *refs):
+    blocks, weights = refs[:count], refs[count : count + 3]
+    outs, normed = refs[count + 3 : count + 6], refs[-1]
+    agents = blocks[0].shape[0]
+    for b, block in enumerate(blocks):
+        normed[pl.ds(b * agents, agents), :] = norm_of(block[...].astype(jnp.float32))
+    for weight, out in zip(weights, outs):
+        out[...] = project(normed[...], weight[...])
+
+
+def near_stage(blocks, weights):
+    count = len(blocks)
+    agents, features = blocks[0].shape
+    shape = (count * agents, features)
+    return pl.pallas_call(
+        functools.partial(near_kernel, count),
+        out_shape=[jax.ShapeDtypeStruct(shape, jnp.bfloat16)] * 3,
+        in_specs=[spec(VMEM)] * (count + 3),
+        out_specs=[spec(VMEM)] * 3,
+        scratch_shapes=[VMEM(shape, jnp.bfloat16)],
+        compiler_params=pltpu.CompilerParams(vmem_limit_bytes=8 * 2**20),
+        name="near_blocks",
+    )(*blocks, *weights)
+
+
+def agent_body(count, blocks, weights, given, outs, scratch):
     normed, query, keys, values, mixed, after, inner, w_out, sems = scratch
     w_query, w_key, w_value, far_out, w_in, w_mlp_out = weights
     copies = fetch((far_out,), (w_out,), sems)
     agents, features = blocks[0].shape
     head_size = features // HEADS
     factor = math.log2(math.e) * head_size**-0.5
-    for b in range(count):
+    rows, wide_lanes = count * agents, 2 * head_size
+    ready = given[0].shape[0] if given else 0
+    rest = pl.ds(ready, rows - ready)
+    for b in range(ready // agents, count):
         normed[pl.ds(b * agents, agents), :] = norm_of(blocks[b][...].astype(jnp.float32))
-    query[...] = project(normed[...], w_query[...])
-    rows, wide_lanes = count * agents, 2 * head_size
-    for weight, target in ((w_key, keys), (w_value, values)):
-        found = project(normed[...], weight[...])
-        even = lax.broadcasted_iota(jnp.int32, found.shape, 1) % wide_lanes < head_size
-        zero = jnp.zeros_like(found)
-        target[:rows, :] = jnp.where(even, found, zero)
-        target[rows:, :] = jnp.where(even, zero, found)
+    query[rest, :] = project(normed[rest, :], w_query[...])
+    if given:
+        query[:ready, :] = given[0][...]
+    for n, (weight, target) in enumerate(((w_key, keys), (w_value, values))):
+        parts = [(ready, project(normed[rest, :], weight[...]))]
+        if given:
+            parts.append((0, given[n + 1][...]))
+        for start, found in parts:
+            even = lax.broadcasted_iota(jnp.int32, found.shape, 1) % wide_lanes < head_size
+            zero = jnp.zeros_like(found)
+            length = found.shape[0]
+            target[start : start + length, :] = jnp.where(even, found, zero)
+            target[rows + start : rows + start + length, :] = jnp.where(even, zero, found)
     second_rows = lax.broadcasted_iota(jnp.int32, (2 * rows, wide_lanes), 0) >= rows
     second_lanes = lax.broadcasted_iota(jnp.int32, (2 * rows, wide_lanes), 1) >= head_size
     counts = (second_rows == second_lanes).astype(jnp.bfloat16)
@@ -339,12 +372,13 @@
         outs[b][...] = final[b * agents : (b + 1) * agents].astype(jnp.bfloat16)
 
 
-def agent_kernel(count, middle_only, *refs):
+def agent_kernel(count, ready, middle_only, *refs):
     blocks, weights = refs[:count], refs[count : count + 6]
+    given = refs[count + 6 : count + 6 + ready]
     outs, scratch = refs[-9 - count : -9], refs[-9:]
 
     def run():
-        agent_body(count, blocks, weights, outs, scratch)
+        agent_body(count, blocks, weights, given, outs, scratch)
 
     if middle_only:
         plane = lax.axis_index("agent")
@@ -353,18 +387,18 @@
         run()
 
 
-def agent_stage(blocks, weights, middle_only, after=()):
+def agent_stage(blocks, weights, middle_only, after=(), given=()):
     count = len(blocks)
     agents, features = blocks[0].shape
     hidden = weights[4].shape[1]
     rows = count * agents
     kind = jnp.bfloat16
     return pl.pallas_call(
-        functools.partial(agent_kernel, count, middle_only),
+        functools.partial(agent_kernel, count, len(given), middle_only),
         out_shape=[jax.ShapeDtypeStruct((agents, features), kind)] * count,
         in_specs=[spec(VMEM)] * (count + 3)
         + [spec(HBM)]
-        + [spec(VMEM)] * 2
+        + [spec(VMEM)] * (2 + len(given))
         + [spec(pl.ANY)] * len(after),
         out_specs=[spec(VMEM)] * count,
         scratch_shapes=[VMEM((rows, features), kind)] * 2
@@ -379,7 +413,7 @@
             transcendentals=rows * (HEADS * rows + hidden),
         ),
         name="agent_step",
-    )(*blocks, *weights[:3], *in_hbm(weights[3:4]), *weights[4:], *after)
+    )(*blocks, *weights[:3], *in_hbm(weights[3:4]), *weights[4:], *given, *after)
 
 
 def place_kernel(*refs):
@@ -518,7 +552,8 @@
     blocks_a = exchange(pack_stage(pieces, whole_steps), "agent")
     blocks_b = exchange(pack_stage(pieces, extra_steps, blocks_a[2:3]), "agent", (1, 2))
 
-    result_a = agent_stage(blocks_a, agent_weights, False)
+    near = near_stage(blocks_a[:3], agent_weights[:3])
+    result_a = agent_stage(blocks_a, agent_weights, False, (), near)
     done_a = exchange(result_a, "agent")
     result_b = agent_stage(blocks_b, agent_weights, True, result_a[:1])
     done_b = [result_b[0]] + [

time: 75.3 us -> 74.8 us (level)
    pallas_call x2 -> x3, Pallas kernels: 6.69 us -> 7.07 us  [the longest x2 6.23 us: agent_stage(): pl.pallas_call(functools.partial(agent_kernel, count, len(given), middle_...]
  transfers between devices with their start and end apart: 26 -> 26, of which waited for: 13 -> 13; matrix products, arithmetic and copies ran while one was open for 0% -> 0% of each run, Pallas kernels for 10% -> 11%
where the time goes in v8:
time: 74.8 us; the launch traced here: 74.5 us
  starting transfers between devices  32.3 us (43%)
  waiting for transfers between devices  27.1 us (36%)
  Pallas kernels  14.7 us (20%)
    ppermute x23, starting transfers between devices, exchange(): moved[k] = lax.ppermute(part, axis, xor_pairs(size, k, targets))  29.1 us
    ppermute x23, waiting for transfers between devices, exchange(): moved[k] = lax.ppermute(part, axis, xor_pairs(size, k, targets))  21.7 us
    pallas_call x2, Pallas kernels, agent_stage(): pl.pallas_call(functools.partial(agent_kernel, count, len(given), middle_...  6.23 us
    ppermute x3, waiting for transfers between devices, local(): lax.ppermute(result_b[k], 'agent', [(j, j ^ k) for j in (1, 2)])  5.35 us
    pallas_call x1, Pallas kernels, time_stage(): pl.pallas_call(functools.partial(time_kernel, size), out_shape=[jax.Shape...  4.48 us
    ppermute x3, starting transfers between devices, local(): lax.ppermute(result_b[k], 'agent', [(j, j ^ k) for j in (1, 2)])  3.24 us
  transfers between devices with their start and end apart: 26, of which 13 were waited for; matrix products, arithmetic and copies ran while one was open for 0% of the time, Pallas kernels for 11%

profile of v8, /device:TPU:0, one launch (start us, length us, event | category | flops | bytes accessed | tf_op | source)
XLA Modules:
  0.0 74.5 jit_solution(9137794955609761762)
XLA Ops:
  0.0 1.4 %cut_shares.1 = (bf16[6,16,512]{2,1,0:T(8,128)(2,1)S(1)}, bf16[6,16,512]{2,1,0:T(8,128)(2,1)S(1)}, bf16[6,16,512]{2,1,0:T(8,128)(2,1)S(1)}, bf16[6,16,512]{2,1,0...) custom-call(bf16[6,128,512]{2,1,0:T(8,128)(2,1)} %refs_0_.1), custom_call_target="tpu_custom_call" | custom-call | flops 20000000000 | bytes 10000000 | tf_op jit(solution)/shard_map/cut_shares/pallas_call | solution.py:148
  1.4 3.4 %collective-permute-start = (bf16[6,16,512]{2,1,0:T(8,128)(2,1)S(1)}, bf16[6,16,512]{2,1,0:T(8,128)(2,1)S(1)}, u32[]{:S(2)}, u32[]{:S(2)}) collective-permute-start(bf16[6,16,512]{2,1,0:T(8,128)(2,1)S(1)} %get-tuple-element.61), channel_id=1, source_target_pairs={{0,28},{4,24},{8,20},{12,16},{16,12},{20,8},{24,4},{28,0},{1,29},{... | collective-permute-start | bytes 294920 | tf_op jit(solution)/shard_map/ppermute | solution.py:491
  4.9 0.6 collective-permute-start.1
  5.5 1.4 %collective-permute-start.2 = (bf16[6,16,512]{2,1,0:T(8,128)(2,1)S(1)}, bf16[6,16,512]{2,1,0:T(8,128)(2,1)S(1)}, u32[]{:S(2)}, u32[]{:S(2)}) collective-permute-start(bf16[6,16,512]{2,1,0:T(8,128)(2,1)S(1)} %get-tuple-element.64), channel_id=1, source_target_pairs={{0,20},{4,16},{8,28},{12,24},{16,4},{20,0},{24,12},{28,8},{1,21},{... | collective-permute-start | bytes 294920 | tf_op jit(solution)/shard_map/ppermute | solution.py:491
  6.9 0.3 collective-permute-start.3
  7.2 1.1 %collective-permute-start.4 = (bf16[6,16,512]{2,1,0:T(8,128)(2,1)S(1)}, bf16[6,16,512]{2,1,0:T(8,128)(2,1)S(1)}, u32[]{:S(2)}, u32[]{:S(2)}) collective-permute-start(bf16[6,16,512]{2,1,0:T(8,128)(2,1)S(1)} %get-tuple-element.66), channel_id=1, source_target_pairs={{0,12},{4,8},{8,4},{12,0},{16,28},{20,24},{24,20},{28,16},{1,13},{... | collective-permute-start | bytes 294920 | tf_op jit(solution)/shard_map/ppermute | solution.py:491
  8.3 2.2 %collective-permute-start.5 = (bf16[6,16,512]{2,1,0:T(8,128)(2,1)S(1)}, bf16[6,16,512]{2,1,0:T(8,128)(2,1)S(1)}, u32[]{:S(2)}, u32[]{:S(2)}) collective-permute-start(bf16[6,16,512]{2,1,0:T(8,128)(2,1)S(1)} %get-tuple-element.67), channel_id=1, source_target_pairs={{0,8},{4,12},{8,0},{12,4},{16,24},{20,28},{24,16},{28,20},{1,9},{5... | collective-permute-start | bytes 294920 | tf_op jit(solution)/shard_map/ppermute | solution.py:491
  10.5 0.7 collective-permute-done.1.refs_6_
  11.2 1.2 %collective-permute-done.2.refs_5_ = bf16[6,16,512]{2,1,0:T(8,128)(2,1)S(1)} collective-permute-done((bf16[6,16,512]{2,1,0:T(8,128)(2,1)S(1)}, bf16[6,16,512]{2,1,0:T(8,128)(2,1)S(1)}, u32[]{:S(2)}, u32[]{:S(2)}) %collective-permute-start.2) | collective-permute-done | bytes 98336 | tf_op jit(solution)/shard_map/ppermute | solution.py:491
  12.5 2.3 %collective-permute-done.3.refs_4_ = bf16[6,16,512]{2,1,0:T(8,128)(2,1)S(1)} collective-permute-done((bf16[6,16,512]{2,1,0:T(8,128)(2,1)S(1)}, bf16[6,16,512]{2,1,0:T(8,128)(2,1)S(1)}, u32[]{:S(2)}, u32[]{:S(2)}) %collective-permute-start.3) | collective-permute-done | bytes 98336 | tf_op jit(solution)/shard_map/ppermute | solution.py:491
  14.8 0.6 collective-permute-done.5.refs_2_
  15.4 0.0 copy-start
  15.5 0.0 copy-start.4
  15.5 4.5 %time_attention.1 = (bf16[6,16,512]{2,1,0:T(8,128)(2,1)S(1)}, bf16[6,16,512]{2,1,0:T(8,128)(2,1)S(1)}, bf16[6,16,512]{2,1,0:T(8,128)(2,1)S(1)}, bf16[6,16,512]{2...) custom-call(bf16[6,16,512]{2,1,0:T(8,128)(2,1)S(1)} %get-tuple-eleme, ...), custom_call_target="tpu_custom_call" | custom-call | flops 1610612736 | bytes 3670016 | tf_op jit(solution)/shard_map/time_attention/pallas_call | solution.py:241
  20.0 0.0 copy-start.3
  20.0 2.1 %collective-permute-start.7 = (bf16[6,16,512]{2,1,0:T(8,128)(2,1)S(1)}, bf16[6,16,512]{2,1,0:T(8,128)(2,1)S(1)}, u32[]{:S(2)}, u32[]{:S(2)}) collective-permute-start(bf16[6,16,512]{2,1,0:T(8,128)(2,1)S(1)} %get-tuple-element.79), channel_id=1, source_target_pairs={{0,28},{4,24},{8,20},{12,16},{16,12},{20,8},{24,4},{28,0},{1,29},{... | collective-permute-start | bytes 294920 | tf_op jit(solution)/shard_map/ppermute | solution.py:491
  22.1 0.6 collective-permute-start.8
  22.7 1.1 %collective-permute-start.9 = (bf16[6,16,512]{2,1,0:T(8,128)(2,1)S(1)}, bf16[6,16,512]{2,1,0:T(8,128)(2,1)S(1)}, u32[]{:S(2)}, u32[]{:S(2)}) collective-permute-start(bf16[6,16,512]{2,1,0:T(8,128)(2,1)S(1)} %get-tuple-element.82), channel_id=1, source_target_pairs={{0,20},{4,16},{8,28},{12,24},{16,4},{20,0},{24,12},{28,8},{1,21},{... | collective-permute-start | bytes 294920 | tf_op jit(solution)/shard_map/ppermute | solution.py:491
  23.9 0.6 collective-permute-start.10
  24.4 1.2 %collective-permute-start.11 = (bf16[6,16,512]{2,1,0:T(8,128)(2,1)S(1)}, bf16[6,16,512]{2,1,0:T(8,128)(2,1)S(1)}, u32[]{:S(2)}, u32[]{:S(2)}) collective-permute-start(bf16[6,16,512]{2,1,0:T(8,128)(2,1)S(1)} %get-tuple-element.84), channel_id=1, source_target_pairs={{0,12},{4,8},{8,4},{12,0},{16,28},{20,24},{24,20},{28,16},{1,13},{... | collective-permute-start | bytes 294920 | tf_op jit(solution)/shard_map/ppermute | solution.py:491
  25.6 0.1 collective-permute-done.7.refs_7_
  25.7 1.6 %collective-permute-start.12 = (bf16[6,16,512]{2,1,0:T(8,128)(2,1)S(1)}, bf16[6,16,512]{2,1,0:T(8,128)(2,1)S(1)}, u32[]{:S(2)}, u32[]{:S(2)}) collective-permute-start(bf16[6,16,512]{2,1,0:T(8,128)(2,1)S(1)} %get-tuple-element.85), channel_id=1, source_target_pairs={{0,8},{4,12},{8,0},{12,4},{16,24},{20,28},{24,16},{28,20},{1,9},{5... | collective-permute-start | bytes 294920 | tf_op jit(solution)/shard_map/ppermute | solution.py:491
  27.3 1.0 %collective-permute-done.8.refs_6_ = bf16[6,16,512]{2,1,0:T(8,128)(2,1)S(1)} collective-permute-done((bf16[6,16,512]{2,1,0:T(8,128)(2,1)S(1)}, bf16[6,16,512]{2,1,0:T(8,128)(2,1)S(1)}, u32[]{:S(2)}, u32[]{:S(2)}) %collective-permute-start.8) | collective-permute-done | bytes 98336 | tf_op jit(solution)/shard_map/ppermute | solution.py:491
  28.2 2.0 %collective-permute-done.9.refs_5_ = bf16[6,16,512]{2,1,0:T(8,128)(2,1)S(1)} collective-permute-done((bf16[6,16,512]{2,1,0:T(8,128)(2,1)S(1)}, bf16[6,16,512]{2,1,0:T(8,128)(2,1)S(1)}, u32[]{:S(2)}, u32[]{:S(2)}) %collective-permute-start.9) | collective-permute-done | bytes 98336 | tf_op jit(solution)/shard_map/ppermute | solution.py:491
  30.2 2.1 %collective-permute-done.10.refs_4_ = bf16[6,16,512]{2,1,0:T(8,128)(2,1)S(1)} collective-permute-done((bf16[6,16,512]{2,1,0:T(8,128)(2,1)S(1)}, bf16[6,16,512]{2,1,0:T(8,128)(2,1)S(1)}, u32[]{:S(2)}, u32[]{:S(2)}) %collective-permute-start.10) | collective-permute-done | bytes 98336 | tf_op jit(solution)/shard_map/ppermute | solution.py:491
  32.4 0.0 collective-permute-done.12.refs_2_
  32.4 0.1 pack_steps.2
  32.5 2.7 %collective-permute-start.14 = (bf16[128,512]{1,0:T(8,128)(2,1)S(1)}, bf16[128,512]{1,0:T(8,128)(2,1)S(1)}, u32[]{:S(2)}, u32[]{:S(2)}) collective-permute-start(bf16[128,512]{1,0:T(8,128)(2,1)S(1)} %get-tuple-element.96), channel_id=1, source_target_pairs={{0,2},{1,3},{2,0},{3,1},{4,6},{5,7},{6,4},{7,5},{8,10},{9,11},{10,... | collective-permute-start | bytes 393224 | tf_op jit(solution)/shard_map/ppermute | solution.py:491
  35.1 1.6 %collective-permute-start.18 = (bf16[128,512]{1,0:T(8,128)(2,1)S(1)}, bf16[128,512]{1,0:T(8,128)(2,1)S(1)}, u32[]{:S(2)}, u32[]{:S(2)}) collective-permute-start(bf16[128,512]{1,0:T(8,128)(2,1)S(1)} %get-tuple-element.102), channel_id=1, source_target_pairs={{0,1},{1,0},{2,3},{3,2},{4,5},{5,4},{6,7},{7,6},{8,9},{9,8},{10,11... | collective-permute-start | bytes 393224 | tf_op jit(solution)/shard_map/ppermute | solution.py:491
  36.7 0.2 collective-permute-start.19
  36.9 6.3 %collective-permute-done.14.refs_8_.refs_2_ = bf16[128,512]{1,0:T(8,128)(2,1)S(1)} collective-permute-done((bf16[128,512]{1,0:T(8,128)(2,1)S(1)}, bf16[128,512]{1,0:T(8,128)(2,1)S(1)}, u32[]{:S(2)}, u32[]{:S(2)}) %collective-permute-start.14) | collective-permute-done | bytes 131104 | tf_op jit(solution)/shard_map/ppermute | solution.py:491
  43.3 1.7 %collective-permute-start.15 = (bf16[128,512]{1,0:T(8,128)(2,1)S(1)}, bf16[128,512]{1,0:T(8,128)(2,1)S(1)}, u32[]{:S(2)}, u32[]{:S(2)}) collective-permute-start(bf16[128,512]{1,0:T(8,128)(2,1)S(1)} %get-tuple-element.98), channel_id=1, source_target_pairs={{0,1},{3,2},{4,5},{7,6},{8,9},{11,10},{12,13},{15,14},{16,17},{19,... | collective-permute-start | bytes 393224 | tf_op jit(solution)/shard_map/ppermute | solution.py:491
  45.1 1.3 %collective-permute-start.16 = (bf16[128,512]{1,0:T(8,128)(2,1)S(1)}, bf16[128,512]{1,0:T(8,128)(2,1)S(1)}, u32[]{:S(2)}, u32[]{:S(2)}) collective-permute-start(bf16[128,512]{1,0:T(8,128)(2,1)S(1)} %get-tuple-element.99), channel_id=1, source_target_pairs={{0,2},{3,1},{4,6},{7,5},{8,10},{11,9},{12,14},{15,13},{16,18},{19,... | collective-permute-start | bytes 393224 | tf_op jit(solution)/shard_map/ppermute | solution.py:491
  46.4 0.8 %collective-permute-start.17 = (bf16[128,512]{1,0:T(8,128)(2,1)S(1)}, bf16[128,512]{1,0:T(8,128)(2,1)S(1)}, u32[]{:S(2)}, u32[]{:S(2)}) collective-permute-start(bf16[128,512]{1,0:T(8,128)(2,1)S(1)} %get-tuple-element.100), channel_id=1, source_target_pairs={{1,2},{2,1},{5,6},{6,5},{9,10},{10,9},{13,14},{14,13},{17,18},{18,... | collective-permute-start | bytes 393224 | tf_op jit(solution)/shard_map/ppermute | solution.py:491
  47.3 0.8 %near_blocks.1 = (bf16[384,512]{1,0:T(8,128)(2,1)S(1)}, bf16[384,512]{1,0:T(8,128)(2,1)S(1)}, bf16[384,512]{1,0:T(8,128)(2,1)S(1)}) custom-call(bf16[128,512]{1,0:T(8,128)(2,1)S(1)} %get-tuple-element.101.refs_0_, bf16[128,512]{1,0:T(8,128)(2,1)S(1)} %collective-permute-done.18.refs_1_, bf16[128,512]{1,0:T(8,128)(2,1)S(1)} %collective-permute-done.14.refs_8_.refs_2_, ...), custom_call_target="tpu_custom_call" | custom-call | tf_op jit(solution)/shard_map/near_blocks/pallas_call | solution.py:298
  48.1 6.2 %agent_step.2 = (bf16[128,512]{1,0:T(8,128)(2,1)S(1)}, bf16[128,512]{1,0:T(8,128)(2,1)S(1)}, bf16[128,512]{1,0:T(8,128)(2,1)S(1)}, bf16[128,512]{1,0:T(8,128)(2,1)S(1)}) custom-call(bf16[128,512]{1,0:T(8,128)(2,1)S(1)} %get-tuple-element.101.refs_0_, bf16[128,512]{1,0:T(8,128)(2,1)S(1)} %collective-permute-done.18.refs_1_, ...), custom_call_target="tpu_custom_call" | custom-call | flops 3758096384 | bytes 4194304 | tf_op jit(solution)/shard_map/agent_step/pallas_call | solution.py:396
  54.4 0.7 collective-permute-start.23
  55.1 2.4 %collective-permute-start.24 = (bf16[128,512]{1,0:T(8,128)(2,1)S(1)}, bf16[128,512]{1,0:T(8,128)(2,1)S(1)}, u32[]{:S(2)}, u32[]{:S(2)}) collective-permute-start(bf16[128,512]{1,0:T(8,128)(2,1)S(1)} %get-tuple-element.113), channel_id=1, source_target_pairs={{0,2},{1,3},{2,0},{3,1},{4,6},{5,7},{6,4},{7,5},{8,10},{9,11},{10,... | collective-permute-start | bytes 393224 | tf_op jit(solution)/shard_map/ppermute | solution.py:491
  57.5 1.3 %collective-permute-start.25 = (bf16[128,512]{1,0:T(8,128)(2,1)S(1)}, bf16[128,512]{1,0:T(8,128)(2,1)S(1)}, u32[]{:S(2)}, u32[]{:S(2)}) collective-permute-start(bf16[128,512]{1,0:T(8,128)(2,1)S(1)} %get-tuple-element.114), channel_id=1, source_target_pairs={{0,3},{1,2},{2,1},{3,0},{4,7},{5,6},{6,5},{7,4},{8,11},{9,10},{10,... | collective-permute-start | bytes 393224 | tf_op jit(solution)/shard_map/ppermute | solution.py:491
  58.8 1.3 %collective-permute-start.20 = (bf16[128,512]{1,0:T(8,128)(2,1)S(1)}, bf16[128,512]{1,0:T(8,128)(2,1)S(1)}, u32[]{:S(2)}, u32[]{:S(2)}) collective-permute-start(bf16[128,512]{1,0:T(8,128)(2,1)S(1)} %get-tuple-element.109), channel_id=1, source_target_pairs={{1,0},{2,3},{5,4},{6,7},{9,8},{10,11},{13,12},{14,15},{17,16},{18,... | collective-permute-start | bytes 393224 | tf_op jit(solution)/shard_map/ppermute | solution.py:560
  60.1 1.3 %collective-permute-start.21 = (bf16[128,512]{1,0:T(8,128)(2,1)S(1)}, bf16[128,512]{1,0:T(8,128)(2,1)S(1)}, u32[]{:S(2)}, u32[]{:S(2)}) collective-permute-start(bf16[128,512]{1,0:T(8,128)(2,1)S(1)} %get-tuple-element.110), channel_id=1, source_target_pairs={{1,3},{2,0},{5,7},{6,4},{9,11},{10,8},{13,15},{14,12},{17,19},{18,... | collective-permute-start | bytes 393224 | tf_op jit(solution)/shard_map/ppermute | solution.py:560
  61.4 0.2 collective-permute-done.23.refs_1_
  61.6 0.7 collective-permute-start.22
  62.3 5.1 %collective-permute-done.24.refs_2_ = bf16[128,512]{1,0:T(8,128)(2,1)S(1)} collective-permute-done((bf16[128,512]{1,0:T(8,128)(2,1)S(1)}, bf16[128,512]{1,0:T(8,128)(2,1)S(1)}, u32[]{:S(2)}, u32[]{:S(2)}) %collective-permute-start.24) | collective-permute-done | bytes 131104 | tf_op jit(solution)/shard_map/ppermute | solution.py:491
  67.4 0.8 %place_steps.1.refs_4_ = bf16[6,128,512]{2,1,0:T(8,128)(2,1)} custom-call(bf16[128,512]{1,0:T(8,128)(2,1)S(1)} %get-tuple-element.107.refs_10_.refs_0_, bf16[128,512]{1,0:T(8,128)(2,1)S(1)} %collective-permute-done.23.refs_1_, bf16[128,512]{1,0:T(8,128)(2,1)S(1)} %collective-permute-done.24.refs_2_, bf16[128,512]{1,0:T(8,128)(2,1)S(1)} %collective-permute-done.25.refs_3_), custom_call_target="tpu_custom_call" | custom-call | tf_op jit(solution)/shard_map/place_steps/pallas_call | solution.py:459
  68.2 4.0 %collective-permute-done.20.refs_1_ = bf16[128,512]{1,0:T(8,128)(2,1)S(1)} collective-permute-done((bf16[128,512]{1,0:T(8,128)(2,1)S(1)}, bf16[128,512]{1,0:T(8,128)(2,1)S(1)}, u32[]{:S(2)}, u32[]{:S(2)}) %collective-permute-start.20) | collective-permute-done | bytes 131104 | tf_op jit(solution)/shard_map/ppermute | solution.py:560
  72.2 1.4 %collective-permute-done.21.refs_2_ = bf16[128,512]{1,0:T(8,128)(2,1)S(1)} collective-permute-done((bf16[128,512]{1,0:T(8,128)(2,1)S(1)}, bf16[128,512]{1,0:T(8,128)(2,1)S(1)}, u32[]{:S(2)}, u32[]{:S(2)}) %collective-permute-start.21) | collective-permute-done | bytes 131104 | tf_op jit(solution)/shard_map/ppermute | solution.py:560
  73.6 0.8 %place_extra.1 = bf16[6,128,512]{2,1,0:T(8,128)(2,1)} custom-call(bf16[128,512]{1,0:T(8,128)(2,1)S(1)} %get-tuple-element.108.refs_0_, bf16[128,512]{1,0:T(8,128)(2,1)S(1)} %collective-permute-done.20.refs_1_, bf16[128,512]{1,0:T(8,128)(2,1)S(1)} %collective-permute-done.21.refs_2_, ...), custom_call_target="tpu_custom_call", output_to_operand_aliasing={{}: (4, {})} | custom-call | tf_op jit(solution)/shard_map/place_extra/pallas_call | solution.py:468
  (31 shorter events, 0.1 us)
Async XLA Ops:
  0.0 15.4 %copy-start.8 = (bf16[512,512]{1,0:T(8,128)(2,1)S(1)}, bf16[512,512]{1,0:T(8,128)(2,1)}, u32[]{:S(2)}) copy-start(bf16[512,512]{1,0:T(8,128)(2,1)} %refs_11_.1) | copy-start | bytes 1572868
  0.0 15.4 %copy-start.7 = (bf16[512,512]{1,0:T(8,128)(2,1)S(1)}, bf16[512,512]{1,0:T(8,128)(2,1)}, u32[]{:S(2)}) copy-start(bf16[512,512]{1,0:T(8,128)(2,1)} %refs_10_.1) | copy-start | bytes 1572868
  0.0 15.4 %copy-start.6 = (bf16[512,512]{1,0:T(8,128)(2,1)S(1)}, bf16[512,512]{1,0:T(8,128)(2,1)}, u32[]{:S(2)}) copy-start(bf16[512,512]{1,0:T(8,128)(2,1)} %refs_9_.3) | copy-start | bytes 1572868
  0.0 15.4 %copy-start.5 = (bf16[512,512]{1,0:T(8,128)(2,1)S(1)}, bf16[512,512]{1,0:T(8,128)(2,1)}, u32[]{:S(2)}) copy-start(bf16[512,512]{1,0:T(8,128)(2,1)} %refs_8_.3) | copy-start | bytes 1572868
  1.4 6.9 %collective-permute-start = (bf16[6,16,512]{2,1,0:T(8,128)(2,1)S(1)}, bf16[6,16,512]{2,1,0:T(8,128)(2,1)S(1)}, u32[]{:S(2)}, u32[]{:S(2)}) collective-permute-start(bf16[6,16,512]{2,1,0:T(8,128)(2,1)S(1)} %get-tuple-element.61), channel_id=1, source_target_pairs={{0,28},{4,24},{8,20},{12,16},{16,12},{20,8},{24,4},{28,0},{1,29},{... | collective-permute-start | bytes 294920 | tf_op jit(solution)/shard_map/ppermute | solution.py:491
  4.9 6.4 %collective-permute-start.1 = (bf16[6,16,512]{2,1,0:T(8,128)(2,1)S(1)}, bf16[6,16,512]{2,1,0:T(8,128)(2,1)S(1)}, u32[]{:S(2)}, u32[]{:S(2)}) collective-permute-start(bf16[6,16,512]{2,1,0:T(8,128)(2,1)S(1)} %get-tuple-element.63), channel_id=1, source_target_pairs={{0,24},{4,28},{8,16},{12,20},{16,8},{20,12},{24,0},{28,4},{1,25},{... | collective-permute-start | bytes 294920 | tf_op jit(solution)/shard_map/ppermute | solution.py:491
  5.5 7.0 %collective-permute-start.2 = (bf16[6,16,512]{2,1,0:T(8,128)(2,1)S(1)}, bf16[6,16,512]{2,1,0:T(8,128)(2,1)S(1)}, u32[]{:S(2)}, u32[]{:S(2)}) collective-permute-start(bf16[6,16,512]{2,1,0:T(8,128)(2,1)S(1)} %get-tuple-element.64), channel_id=1, source_target_pairs={{0,20},{4,16},{8,28},{12,24},{16,4},{20,0},{24,12},{28,8},{1,21},{... | collective-permute-start | bytes 294920 | tf_op jit(solution)/shard_map/ppermute | solution.py:491
  6.9 7.9 %collective-permute-start.3 = (bf16[6,16,512]{2,1,0:T(8,128)(2,1)S(1)}, bf16[6,16,512]{2,1,0:T(8,128)(2,1)S(1)}, u32[]{:S(2)}, u32[]{:S(2)}) collective-permute-start(bf16[6,16,512]{2,1,0:T(8,128)(2,1)S(1)} %get-tuple-element.65), channel_id=1, source_target_pairs={{0,16},{4,20},{8,24},{12,28},{16,0},{20,4},{24,8},{28,12},{1,17},{... | collective-permute-start | bytes 294920 | tf_op jit(solution)/shard_map/ppermute | solution.py:491
  7.2 7.6 %collective-permute-start.4 = (bf16[6,16,512]{2,1,0:T(8,128)(2,1)S(1)}, bf16[6,16,512]{2,1,0:T(8,128)(2,1)S(1)}, u32[]{:S(2)}, u32[]{:S(2)}) collective-permute-start(bf16[6,16,512]{2,1,0:T(8,128)(2,1)S(1)} %get-tuple-element.66), channel_id=1, source_target_pairs={{0,12},{4,8},{8,4},{12,0},{16,28},{20,24},{24,20},{28,16},{1,13},{... | collective-permute-start | bytes 294920 | tf_op jit(solution)/shard_map/ppermute | solution.py:491
  8.3 7.1 %collective-permute-start.5 = (bf16[6,16,512]{2,1,0:T(8,128)(2,1)S(1)}, bf16[6,16,512]{2,1,0:T(8,128)(2,1)S(1)}, u32[]{:S(2)}, u32[]{:S(2)}) collective-permute-start(bf16[6,16,512]{2,1,0:T(8,128)(2,1)S(1)} %get-tuple-element.67), channel_id=1, source_target_pairs={{0,8},{4,12},{8,0},{12,4},{16,24},{20,28},{24,16},{28,20},{1,9},{5... | collective-permute-start | bytes 294920 | tf_op jit(solution)/shard_map/ppermute | solution.py:491
  11.2 4.1 %collective-permute-start.6 = (bf16[6,16,512]{2,1,0:T(8,128)(2,1)S(1)}, bf16[6,16,512]{2,1,0:T(8,128)(2,1)S(1)}, u32[]{:S(2)}, u32[]{:S(2)}) collective-permute-start(bf16[6,16,512]{2,1,0:T(8,128)(2,1)S(1)} %get-tuple-element.68), channel_id=1, source_target_pairs={{0,4},{4,0},{8,12},{12,8},{16,20},{20,16},{24,28},{28,24},{1,5},{5... | collective-permute-start | bytes 294920 | tf_op jit(solution)/shard_map/ppermute | solution.py:491
  15.4 31.8 %copy-start = (bf16[512,512]{1,0:T(8,128)(2,1)S(1)}, bf16[512,512]{1,0:T(8,128)(2,1)}, u32[]{:S(2)}) copy-start(bf16[512,512]{1,0:T(8,128)(2,1)} %refs_4_.5) | copy-start | bytes 1572868
  15.4 31.8 %copy-start.1 = (bf16[512,512]{1,0:T(8,128)(2,1)S(1)}, bf16[512,512]{1,0:T(8,128)(2,1)}, u32[]{:S(2)}) copy-start(bf16[512,512]{1,0:T(8,128)(2,1)} %refs_5_.5) | copy-start | bytes 1572868
  15.4 31.8 %copy-start.2 = (bf16[512,512]{1,0:T(8,128)(2,1)S(1)}, bf16[512,512]{1,0:T(8,128)(2,1)}, u32[]{:S(2)}) copy-start(bf16[512,512]{1,0:T(8,128)(2,1)} %refs_6_.3) | copy-start | bytes 1572868
  15.5 32.7 %copy-start.4 = (bf16[2048,512]{1,0:T(8,128)(2,1)S(1)}, bf16[2048,512]{1,0:T(8,128)(2,1)}, u32[]{:S(2)}) copy-start(bf16[2048,512]{1,0:T(8,128)(2,1)} %refs_9_.5) | copy-start | bytes 6291460
  20.0 28.2 %copy-start.3 = (bf16[512,2048]{1,0:T(8,128)(2,1)S(1)}, bf16[512,2048]{1,0:T(8,128)(2,1)}, u32[]{:S(2)}) copy-start(bf16[512,2048]{1,0:T(8,128)(2,1)} %refs_8_.5) | copy-start | bytes 6291460
  20.0 5.7 %collective-permute-start.7 = (bf16[6,16,512]{2,1,0:T(8,128)(2,1)S(1)}, bf16[6,16,512]{2,1,0:T(8,128)(2,1)S(1)}, u32[]{:S(2)}, u32[]{:S(2)}) collective-permute-start(bf16[6,16,512]{2,1,0:T(8,128)(2,1)S(1)} %get-tuple-element.79), channel_id=1, source_target_pairs={{0,28},{4,24},{8,20},{12,16},{16,12},{20,8},{24,4},{28,0},{1,29},{... | collective-permute-start | bytes 294920 | tf_op jit(solution)/shard_map/ppermute | solution.py:491
  22.1 6.2 %collective-permute-start.8 = (bf16[6,16,512]{2,1,0:T(8,128)(2,1)S(1)}, bf16[6,16,512]{2,1,0:T(8,128)(2,1)S(1)}, u32[]{:S(2)}, u32[]{:S(2)}) collective-permute-start(bf16[6,16,512]{2,1,0:T(8,128)(2,1)S(1)} %get-tuple-element.81), channel_id=1, source_target_pairs={{0,24},{4,28},{8,16},{12,20},{16,8},{20,12},{24,0},{28,4},{1,25},{... | collective-permute-start | bytes 294920 | tf_op jit(solution)/shard_map/ppermute | solution.py:491
  22.7 7.5 %collective-permute-start.9 = (bf16[6,16,512]{2,1,0:T(8,128)(2,1)S(1)}, bf16[6,16,512]{2,1,0:T(8,128)(2,1)S(1)}, u32[]{:S(2)}, u32[]{:S(2)}) collective-permute-start(bf16[6,16,512]{2,1,0:T(8,128)(2,1)S(1)} %get-tuple-element.82), channel_id=1, source_target_pairs={{0,20},{4,16},{8,28},{12,24},{16,4},{20,0},{24,12},{28,8},{1,21},{... | collective-permute-start | bytes 294920 | tf_op jit(solution)/shard_map/ppermute | solution.py:491
  23.9 8.5 %collective-permute-start.10 = (bf16[6,16,512]{2,1,0:T(8,128)(2,1)S(1)}, bf16[6,16,512]{2,1,0:T(8,128)(2,1)S(1)}, u32[]{:S(2)}, u32[]{:S(2)}) collective-permute-start(bf16[6,16,512]{2,1,0:T(8,128)(2,1)S(1)} %get-tuple-element.83), channel_id=1, source_target_pairs={{0,16},{4,20},{8,24},{12,28},{16,0},{20,4},{24,8},{28,12},{1,17},{... | collective-permute-start | bytes 294920 | tf_op jit(solution)/shard_map/ppermute | solution.py:491
  24.4 7.9 %collective-permute-start.11 = (bf16[6,16,512]{2,1,0:T(8,128)(2,1)S(1)}, bf16[6,16,512]{2,1,0:T(8,128)(2,1)S(1)}, u32[]{:S(2)}, u32[]{:S(2)}) collective-permute-start(bf16[6,16,512]{2,1,0:T(8,128)(2,1)S(1)} %get-tuple-element.84), channel_id=1, source_target_pairs={{0,12},{4,8},{8,4},{12,0},{16,28},{20,24},{24,20},{28,16},{1,13},{... | collective-permute-start | bytes 294920 | tf_op jit(solution)/shard_map/ppermute | solution.py:491
  25.7 6.7 %collective-permute-start.12 = (bf16[6,16,512]{2,1,0:T(8,128)(2,1)S(1)}, bf16[6,16,512]{2,1,0:T(8,128)(2,1)S(1)}, u32[]{:S(2)}, u32[]{:S(2)}) collective-permute-start(bf16[6,16,512]{2,1,0:T(8,128)(2,1)S(1)} %get-tuple-element.85), channel_id=1, source_target_pairs={{0,8},{4,12},{8,0},{12,4},{16,24},{20,28},{24,16},{28,20},{1,9},{5... | collective-permute-start | bytes 294920 | tf_op jit(solution)/shard_map/ppermute | solution.py:491
  28.2 4.2 %collective-permute-start.13 = (bf16[6,16,512]{2,1,0:T(8,128)(2,1)S(1)}, bf16[6,16,512]{2,1,0:T(8,128)(2,1)S(1)}, u32[]{:S(2)}, u32[]{:S(2)}) collective-permute-start(bf16[6,16,512]{2,1,0:T(8,128)(2,1)S(1)} %get-tuple-element.86), channel_id=1, source_target_pairs={{0,4},{4,0},{8,12},{12,8},{16,20},{20,16},{24,28},{28,24},{1,5},{5... | collective-permute-start | bytes 294920 | tf_op jit(solution)/shard_map/ppermute | solution.py:491
  32.5 10.8 %collective-permute-start.14 = (bf16[128,512]{1,0:T(8,128)(2,1)S(1)}, bf16[128,512]{1,0:T(8,128)(2,1)S(1)}, u32[]{:S(2)}, u32[]{:S(2)}) collective-permute-start(bf16[128,512]{1,0:T(8,128)(2,1)S(1)} %get-tuple-element.96), channel_id=1, source_target_pairs={{0,2},{1,3},{2,0},{3,1},{4,6},{5,7},{6,4},{7,5},{8,10},{9,11},{10,... | collective-permute-start | bytes 393224 | tf_op jit(solution)/shard_map/ppermute | solution.py:491
  35.1 12.1 %collective-permute-start.18 = (bf16[128,512]{1,0:T(8,128)(2,1)S(1)}, bf16[128,512]{1,0:T(8,128)(2,1)S(1)}, u32[]{:S(2)}, u32[]{:S(2)}) collective-permute-start(bf16[128,512]{1,0:T(8,128)(2,1)S(1)} %get-tuple-element.102), channel_id=1, source_target_pairs={{0,1},{1,0},{2,3},{3,2},{4,5},{5,4},{6,7},{7,6},{8,9},{9,8},{10,11... | collective-permute-start | bytes 393224 | tf_op jit(solution)/shard_map/ppermute | solution.py:491
  36.7 11.4 %collective-permute-start.19 = (bf16[128,512]{1,0:T(8,128)(2,1)S(1)}, bf16[128,512]{1,0:T(8,128)(2,1)S(1)}, u32[]{:S(2)}, u32[]{:S(2)}) collective-permute-start(bf16[128,512]{1,0:T(8,128)(2,1)S(1)} %get-tuple-element.103), channel_id=1, source_target_pairs={{0,3},{1,2},{2,1},{3,0},{4,7},{5,6},{6,5},{7,4},{8,11},{9,10},{10,... | collective-permute-start | bytes 393224 | tf_op jit(solution)/shard_map/ppermute | solution.py:491
  43.3 14.2 %collective-permute-start.15 = (bf16[128,512]{1,0:T(8,128)(2,1)S(1)}, bf16[128,512]{1,0:T(8,128)(2,1)S(1)}, u32[]{:S(2)}, u32[]{:S(2)}) collective-permute-start(bf16[128,512]{1,0:T(8,128)(2,1)S(1)} %get-tuple-element.98), channel_id=1, source_target_pairs={{0,1},{3,2},{4,5},{7,6},{8,9},{11,10},{12,13},{15,14},{16,17},{19,... | collective-permute-start | bytes 393224 | tf_op jit(solution)/shard_map/ppermute | solution.py:491
  45.1 13.8 %collective-permute-start.16 = (bf16[128,512]{1,0:T(8,128)(2,1)S(1)}, bf16[128,512]{1,0:T(8,128)(2,1)S(1)}, u32[]{:S(2)}, u32[]{:S(2)}) collective-permute-start(bf16[128,512]{1,0:T(8,128)(2,1)S(1)} %get-tuple-element.99), channel_id=1, source_target_pairs={{0,2},{3,1},{4,6},{7,5},{8,10},{11,9},{12,14},{15,13},{16,18},{19,... | collective-permute-start | bytes 393224 | tf_op jit(solution)/shard_map/ppermute | solution.py:491
  46.4 12.5 %collective-permute-start.17 = (bf16[128,512]{1,0:T(8,128)(2,1)S(1)}, bf16[128,512]{1,0:T(8,128)(2,1)S(1)}, u32[]{:S(2)}, u32[]{:S(2)}) collective-permute-start(bf16[128,512]{1,0:T(8,128)(2,1)S(1)} %get-tuple-element.100), channel_id=1, source_target_pairs={{1,2},{2,1},{5,6},{6,5},{9,10},{10,9},{13,14},{14,13},{17,18},{18,... | collective-permute-start | bytes 393224 | tf_op jit(solution)/shard_map/ppermute | solution.py:491
  54.4 7.3 %collective-permute-start.23 = (bf16[128,512]{1,0:T(8,128)(2,1)S(1)}, bf16[128,512]{1,0:T(8,128)(2,1)S(1)}, u32[]{:S(2)}, u32[]{:S(2)}) collective-permute-start(bf16[128,512]{1,0:T(8,128)(2,1)S(1)} %get-tuple-element.112), channel_id=1, source_target_pairs={{0,1},{1,0},{2,3},{3,2},{4,5},{5,4},{6,7},{7,6},{8,9},{9,8},{10,11... | collective-permute-start | bytes 393224 | tf_op jit(solution)/shard_map/ppermute | solution.py:491
  55.1 12.4 %collective-permute-start.24 = (bf16[128,512]{1,0:T(8,128)(2,1)S(1)}, bf16[128,512]{1,0:T(8,128)(2,1)S(1)}, u32[]{:S(2)}, u32[]{:S(2)}) collective-permute-start(bf16[128,512]{1,0:T(8,128)(2,1)S(1)} %get-tuple-element.113), channel_id=1, source_target_pairs={{0,2},{1,3},{2,0},{3,1},{4,6},{5,7},{6,4},{7,5},{8,10},{9,11},{10,... | collective-permute-start | bytes 393224 | tf_op jit(solution)/shard_map/ppermute | solution.py:491
  57.5 10.0 %collective-permute-start.25 = (bf16[128,512]{1,0:T(8,128)(2,1)S(1)}, bf16[128,512]{1,0:T(8,128)(2,1)S(1)}, u32[]{:S(2)}, u32[]{:S(2)}) collective-permute-start(bf16[128,512]{1,0:T(8,128)(2,1)S(1)} %get-tuple-element.114), channel_id=1, source_target_pairs={{0,3},{1,2},{2,1},{3,0},{4,7},{5,6},{6,5},{7,4},{8,11},{9,10},{10,... | collective-permute-start | bytes 393224 | tf_op jit(solution)/shard_map/ppermute | solution.py:491
  58.8 13.4 %collective-permute-start.20 = (bf16[128,512]{1,0:T(8,128)(2,1)S(1)}, bf16[128,512]{1,0:T(8,128)(2,1)S(1)}, u32[]{:S(2)}, u32[]{:S(2)}) collective-permute-start(bf16[128,512]{1,0:T(8,128)(2,1)S(1)} %get-tuple-element.109), channel_id=1, source_target_pairs={{1,0},{2,3},{5,4},{6,7},{9,8},{10,11},{13,12},{14,15},{17,16},{18,... | collective-permute-start | bytes 393224 | tf_op jit(solution)/shard_map/ppermute | solution.py:560
  60.1 13.5 %collective-permute-start.21 = (bf16[128,512]{1,0:T(8,128)(2,1)S(1)}, bf16[128,512]{1,0:T(8,128)(2,1)S(1)}, u32[]{:S(2)}, u32[]{:S(2)}) collective-permute-start(bf16[128,512]{1,0:T(8,128)(2,1)S(1)} %get-tuple-element.110), channel_id=1, source_target_pairs={{1,3},{2,0},{5,7},{6,4},{9,11},{10,8},{13,15},{14,12},{17,19},{18,... | collective-permute-start | bytes 393224 | tf_op jit(solution)/shard_map/ppermute | solution.py:560
  61.6 12.0 %collective-permute-start.22 = (bf16[128,512]{1,0:T(8,128)(2,1)S(1)}, bf16[128,512]{1,0:T(8,128)(2,1)S(1)}, u32[]{:S(2)}, u32[]{:S(2)}) collective-permute-start(bf16[128,512]{1,0:T(8,128)(2,1)S(1)} %get-tuple-element.111), channel_id=1, source_target_pairs={{1,2},{2,1},{5,6},{6,5},{9,10},{10,9},{13,14},{14,13},{17,18},{18,... | collective-permute-start | bytes 393224 | tf_op jit(solution)/shard_map/ppermute | solution.py:560

commit v9 on v8

--- a/solution.py
+++ b/solution.py
@@ -243,7 +243,7 @@
         out_shape=[jax.ShapeDtypeStruct((steps, agents, features), kind)] * size,
         in_specs=[spec(VMEM)] * (size + 4),
         out_specs=[spec(VMEM)] * size,
-        scratch_shapes=[VMEM((features // 128, rows, 128), jnp.float32)]
+        scratch_shapes=[VMEM((features // 128, rows + agents, 128), jnp.float32)]
         + [VMEM((rows, features), kind)] * 2
         + [VMEM((agents * (-(-2 * steps * size // 128) * 128), features), kind)] * 2
         + [VMEM((rows, features), kind)],

time: 74.8 us -> 74.8 us (level)
  no operation moved by 1% of the time
where the time goes in v9:
time: 74.8 us; the launch traced here: 74.6 us
  starting transfers between devices  32.3 us (43%)
  waiting for transfers between devices  27.2 us (36%)
  Pallas kernels  14.7 us (20%)
    ppermute x23, starting transfers between devices, exchange(): moved[k] = lax.ppermute(part, axis, xor_pairs(size, k, targets))  29 us
    ppermute x23, waiting for transfers between devices, exchange(): moved[k] = lax.ppermute(part, axis, xor_pairs(size, k, targets))  21.8 us
    pallas_call x2, Pallas kernels, agent_stage(): pl.pallas_call(functools.partial(agent_kernel, count, len(given), middle_...  6.24 us
    ppermute x3, waiting for transfers between devices, local(): lax.ppermute(result_b[k], 'agent', [(j, j ^ k) for j in (1, 2)])  5.39 us
    pallas_call x1, Pallas kernels, time_stage(): pl.pallas_call(functools.partial(time_kernel, size), out_shape=[jax.Shape...  4.48 us
    ppermute x3, starting transfers between devices, local(): lax.ppermute(result_b[k], 'agent', [(j, j ^ k) for j in (1, 2)])  3.24 us
  transfers between devices with their start and end apart: 26, of which 13 were waited for; matrix products, arithmetic and copies ran while one was open for 0% of the time, Pallas kernels for 11%

profile of v9, /device:TPU:0, one launch (start us, length us, event | category | flops | bytes accessed | tf_op | source)
XLA Modules:
  0.0 74.6 jit_solution(17941803618561856994)
XLA Ops:
  0.0 1.4 %cut_shares.1 = (bf16[6,16,512]{2,1,0:T(8,128)(2,1)S(1)}, bf16[6,16,512]{2,1,0:T(8,128)(2,1)S(1)}, bf16[6,16,512]{2,1,0:T(8,128)(2,1)S(1)}, bf16[6,16,512]{2,1,0...) custom-call(bf16[6,128,512]{2,1,0:T(8,128)(2,1)} %refs_0_.1), custom_call_target="tpu_custom_call" | custom-call | flops 20000000000 | bytes 10000000 | tf_op jit(solution)/shard_map/cut_shares/pallas_call | solution.py:148
  1.4 3.4 %collective-permute-start = (bf16[6,16,512]{2,1,0:T(8,128)(2,1)S(1)}, bf16[6,16,512]{2,1,0:T(8,128)(2,1)S(1)}, u32[]{:S(2)}, u32[]{:S(2)}) collective-permute-start(bf16[6,16,512]{2,1,0:T(8,128)(2,1)S(1)} %get-tuple-element.61), channel_id=1, source_target_pairs={{0,28},{4,24},{8,20},{12,16},{16,12},{20,8},{24,4},{28,0},{1,29},{... | collective-permute-start | bytes 294920 | tf_op jit(solution)/shard_map/ppermute | solution.py:491
  4.9 0.6 collective-permute-start.1
  5.5 1.4 %collective-permute-start.2 = (bf16[6,16,512]{2,1,0:T(8,128)(2,1)S(1)}, bf16[6,16,512]{2,1,0:T(8,128)(2,1)S(1)}, u32[]{:S(2)}, u32[]{:S(2)}) collective-permute-start(bf16[6,16,512]{2,1,0:T(8,128)(2,1)S(1)} %get-tuple-element.64), channel_id=1, source_target_pairs={{0,20},{4,16},{8,28},{12,24},{16,4},{20,0},{24,12},{28,8},{1,21},{... | collective-permute-start | bytes 294920 | tf_op jit(solution)/shard_map/ppermute | solution.py:491
  6.9 0.3 collective-permute-start.3
  7.2 1.1 %collective-permute-start.4 = (bf16[6,16,512]{2,1,0:T(8,128)(2,1)S(1)}, bf16[6,16,512]{2,1,0:T(8,128)(2,1)S(1)}, u32[]{:S(2)}, u32[]{:S(2)}) collective-permute-start(bf16[6,16,512]{2,1,0:T(8,128)(2,1)S(1)} %get-tuple-element.66), channel_id=1, source_target_pairs={{0,12},{4,8},{8,4},{12,0},{16,28},{20,24},{24,20},{28,16},{1,13},{... | collective-permute-start | bytes 294920 | tf_op jit(solution)/shard_map/ppermute | solution.py:491
  8.3 2.2 %collective-permute-start.5 = (bf16[6,16,512]{2,1,0:T(8,128)(2,1)S(1)}, bf16[6,16,512]{2,1,0:T(8,128)(2,1)S(1)}, u32[]{:S(2)}, u32[]{:S(2)}) collective-permute-start(bf16[6,16,512]{2,1,0:T(8,128)(2,1)S(1)} %get-tuple-element.67), channel_id=1, source_target_pairs={{0,8},{4,12},{8,0},{12,4},{16,24},{20,28},{24,16},{28,20},{1,9},{5... | collective-permute-start | bytes 294920 | tf_op jit(solution)/shard_map/ppermute | solution.py:491
  10.5 0.7 collective-permute-done.1.refs_6_
  11.2 1.2 %collective-permute-done.2.refs_5_ = bf16[6,16,512]{2,1,0:T(8,128)(2,1)S(1)} collective-permute-done((bf16[6,16,512]{2,1,0:T(8,128)(2,1)S(1)}, bf16[6,16,512]{2,1,0:T(8,128)(2,1)S(1)}, u32[]{:S(2)}, u32[]{:S(2)}) %collective-permute-start.2) | collective-permute-done | bytes 98336 | tf_op jit(solution)/shard_map/ppermute | solution.py:491
  12.5 2.3 %collective-permute-done.3.refs_4_ = bf16[6,16,512]{2,1,0:T(8,128)(2,1)S(1)} collective-permute-done((bf16[6,16,512]{2,1,0:T(8,128)(2,1)S(1)}, bf16[6,16,512]{2,1,0:T(8,128)(2,1)S(1)}, u32[]{:S(2)}, u32[]{:S(2)}) %collective-permute-start.3) | collective-permute-done | bytes 98336 | tf_op jit(solution)/shard_map/ppermute | solution.py:491
  14.8 0.6 collective-permute-done.5.refs_2_
  15.4 0.0 copy-start
  15.4 0.0 copy-start.2
  15.5 0.0 copy-start.4
  15.5 4.5 %time_attention.1 = (bf16[6,16,512]{2,1,0:T(8,128)(2,1)S(1)}, bf16[6,16,512]{2,1,0:T(8,128)(2,1)S(1)}, bf16[6,16,512]{2,1,0:T(8,128)(2,1)S(1)}, bf16[6,16,512]{2...) custom-call(bf16[6,16,512]{2,1,0:T(8,128)(2,1)S(1)} %get-tuple-eleme, ...), custom_call_target="tpu_custom_call" | custom-call | flops 1610612736 | bytes 3670016 | tf_op jit(solution)/shard_map/time_attention/pallas_call | solution.py:241
  20.0 2.1 %collective-permute-start.7 = (bf16[6,16,512]{2,1,0:T(8,128)(2,1)S(1)}, bf16[6,16,512]{2,1,0:T(8,128)(2,1)S(1)}, u32[]{:S(2)}, u32[]{:S(2)}) collective-permute-start(bf16[6,16,512]{2,1,0:T(8,128)(2,1)S(1)} %get-tuple-element.79), channel_id=1, source_target_pairs={{0,28},{4,24},{8,20},{12,16},{16,12},{20,8},{24,4},{28,0},{1,29},{... | collective-permute-start | bytes 294920 | tf_op jit(solution)/shard_map/ppermute | solution.py:491
  22.1 0.6 collective-permute-start.8
  22.7 1.2 %collective-permute-start.9 = (bf16[6,16,512]{2,1,0:T(8,128)(2,1)S(1)}, bf16[6,16,512]{2,1,0:T(8,128)(2,1)S(1)}, u32[]{:S(2)}, u32[]{:S(2)}) collective-permute-start(bf16[6,16,512]{2,1,0:T(8,128)(2,1)S(1)} %get-tuple-element.82), channel_id=1, source_target_pairs={{0,20},{4,16},{8,28},{12,24},{16,4},{20,0},{24,12},{28,8},{1,21},{... | collective-permute-start | bytes 294920 | tf_op jit(solution)/shard_map/ppermute | solution.py:491
  23.9 0.6 collective-permute-start.10
  24.5 1.2 %collective-permute-start.11 = (bf16[6,16,512]{2,1,0:T(8,128)(2,1)S(1)}, bf16[6,16,512]{2,1,0:T(8,128)(2,1)S(1)}, u32[]{:S(2)}, u32[]{:S(2)}) collective-permute-start(bf16[6,16,512]{2,1,0:T(8,128)(2,1)S(1)} %get-tuple-element.84), channel_id=1, source_target_pairs={{0,12},{4,8},{8,4},{12,0},{16,28},{20,24},{24,20},{28,16},{1,13},{... | collective-permute-start | bytes 294920 | tf_op jit(solution)/shard_map/ppermute | solution.py:491
  25.6 0.1 collective-permute-done.7.refs_7_
  25.8 1.5 %collective-permute-start.12 = (bf16[6,16,512]{2,1,0:T(8,128)(2,1)S(1)}, bf16[6,16,512]{2,1,0:T(8,128)(2,1)S(1)}, u32[]{:S(2)}, u32[]{:S(2)}) collective-permute-start(bf16[6,16,512]{2,1,0:T(8,128)(2,1)S(1)} %get-tuple-element.85), channel_id=1, source_target_pairs={{0,8},{4,12},{8,0},{12,4},{16,24},{20,28},{24,16},{28,20},{1,9},{5... | collective-permute-start | bytes 294920 | tf_op jit(solution)/shard_map/ppermute | solution.py:491
  27.2 1.0 %collective-permute-done.8.refs_6_ = bf16[6,16,512]{2,1,0:T(8,128)(2,1)S(1)} collective-permute-done((bf16[6,16,512]{2,1,0:T(8,128)(2,1)S(1)}, bf16[6,16,512]{2,1,0:T(8,128)(2,1)S(1)}, u32[]{:S(2)}, u32[]{:S(2)}) %collective-permute-start.8) | collective-permute-done | bytes 98336 | tf_op jit(solution)/shard_map/ppermute | solution.py:491
  28.2 2.0 %collective-permute-done.9.refs_5_ = bf16[6,16,512]{2,1,0:T(8,128)(2,1)S(1)} collective-permute-done((bf16[6,16,512]{2,1,0:T(8,128)(2,1)S(1)}, bf16[6,16,512]{2,1,0:T(8,128)(2,1)S(1)}, u32[]{:S(2)}, u32[]{:S(2)}) %collective-permute-start.9) | collective-permute-done | bytes 98336 | tf_op jit(solution)/shard_map/ppermute | solution.py:491
  30.2 2.1 %collective-permute-done.10.refs_4_ = bf16[6,16,512]{2,1,0:T(8,128)(2,1)S(1)} collective-permute-done((bf16[6,16,512]{2,1,0:T(8,128)(2,1)S(1)}, bf16[6,16,512]{2,1,0:T(8,128)(2,1)S(1)}, u32[]{:S(2)}, u32[]{:S(2)}) %collective-permute-start.10) | collective-permute-done | bytes 98336 | tf_op jit(solution)/shard_map/ppermute | solution.py:491
  32.4 0.0 collective-permute-done.12.refs_2_
  32.4 0.1 pack_steps.2
  32.5 2.7 %collective-permute-start.14 = (bf16[128,512]{1,0:T(8,128)(2,1)S(1)}, bf16[128,512]{1,0:T(8,128)(2,1)S(1)}, u32[]{:S(2)}, u32[]{:S(2)}) collective-permute-start(bf16[128,512]{1,0:T(8,128)(2,1)S(1)} %get-tuple-element.96), channel_id=1, source_target_pairs={{0,2},{1,3},{2,0},{3,1},{4,6},{5,7},{6,4},{7,5},{8,10},{9,11},{10,... | collective-permute-start | bytes 393224 | tf_op jit(solution)/shard_map/ppermute | solution.py:491
  35.1 1.6 %collective-permute-start.18 = (bf16[128,512]{1,0:T(8,128)(2,1)S(1)}, bf16[128,512]{1,0:T(8,128)(2,1)S(1)}, u32[]{:S(2)}, u32[]{:S(2)}) collective-permute-start(bf16[128,512]{1,0:T(8,128)(2,1)S(1)} %get-tuple-element.102), channel_id=1, source_target_pairs={{0,1},{1,0},{2,3},{3,2},{4,5},{5,4},{6,7},{7,6},{8,9},{9,8},{10,11... | collective-permute-start | bytes 393224 | tf_op jit(solution)/shard_map/ppermute | solution.py:491
  36.7 0.2 collective-permute-start.19
  36.9 6.3 %collective-permute-done.14.refs_8_.refs_2_ = bf16[128,512]{1,0:T(8,128)(2,1)S(1)} collective-permute-done((bf16[128,512]{1,0:T(8,128)(2,1)S(1)}, bf16[128,512]{1,0:T(8,128)(2,1)S(1)}, u32[]{:S(2)}, u32[]{:S(2)}) %collective-permute-start.14) | collective-permute-done | bytes 131104 | tf_op jit(solution)/shard_map/ppermute | solution.py:491
  43.3 1.7 %collective-permute-start.15 = (bf16[128,512]{1,0:T(8,128)(2,1)S(1)}, bf16[128,512]{1,0:T(8,128)(2,1)S(1)}, u32[]{:S(2)}, u32[]{:S(2)}) collective-permute-start(bf16[128,512]{1,0:T(8,128)(2,1)S(1)} %get-tuple-element.98), channel_id=1, source_target_pairs={{0,1},{3,2},{4,5},{7,6},{8,9},{11,10},{12,13},{15,14},{16,17},{19,... | collective-permute-start | bytes 393224 | tf_op jit(solution)/shard_map/ppermute | solution.py:491
  45.1 1.3 %collective-permute-start.16 = (bf16[128,512]{1,0:T(8,128)(2,1)S(1)}, bf16[128,512]{1,0:T(8,128)(2,1)S(1)}, u32[]{:S(2)}, u32[]{:S(2)}) collective-permute-start(bf16[128,512]{1,0:T(8,128)(2,1)S(1)} %get-tuple-element.99), channel_id=1, source_target_pairs={{0,2},{3,1},{4,6},{7,5},{8,10},{11,9},{12,14},{15,13},{16,18},{19,... | collective-permute-start | bytes 393224 | tf_op jit(solution)/shard_map/ppermute | solution.py:491
  46.4 0.8 %collective-permute-start.17 = (bf16[128,512]{1,0:T(8,128)(2,1)S(1)}, bf16[128,512]{1,0:T(8,128)(2,1)S(1)}, u32[]{:S(2)}, u32[]{:S(2)}) collective-permute-start(bf16[128,512]{1,0:T(8,128)(2,1)S(1)} %get-tuple-element.100), channel_id=1, source_target_pairs={{1,2},{2,1},{5,6},{6,5},{9,10},{10,9},{13,14},{14,13},{17,18},{18,... | collective-permute-start | bytes 393224 | tf_op jit(solution)/shard_map/ppermute | solution.py:491
  47.3 0.8 %near_blocks.1 = (bf16[384,512]{1,0:T(8,128)(2,1)S(1)}, bf16[384,512]{1,0:T(8,128)(2,1)S(1)}, bf16[384,512]{1,0:T(8,128)(2,1)S(1)}) custom-call(bf16[128,512]{1,0:T(8,128)(2,1)S(1)} %get-tuple-element.101.refs_0_, bf16[128,512]{1,0:T(8,128)(2,1)S(1)} %collective-permute-done.18.refs_1_, bf16[128,512]{1,0:T(8,128)(2,1)S(1)} %collective-permute-done.14.refs_8_.refs_2_, ...), custom_call_target="tpu_custom_call" | custom-call | tf_op jit(solution)/shard_map/near_blocks/pallas_call | solution.py:298
  48.1 6.2 %agent_step.2 = (bf16[128,512]{1,0:T(8,128)(2,1)S(1)}, bf16[128,512]{1,0:T(8,128)(2,1)S(1)}, bf16[128,512]{1,0:T(8,128)(2,1)S(1)}, bf16[128,512]{1,0:T(8,128)(2,1)S(1)}) custom-call(bf16[128,512]{1,0:T(8,128)(2,1)S(1)} %get-tuple-element.101.refs_0_, bf16[128,512]{1,0:T(8,128)(2,1)S(1)} %collective-permute-done.18.refs_1_, ...), custom_call_target="tpu_custom_call" | custom-call | flops 3758096384 | bytes 4194304 | tf_op jit(solution)/shard_map/agent_step/pallas_call | solution.py:396
  54.4 0.7 collective-permute-start.23
  55.1 2.4 %collective-permute-start.24 = (bf16[128,512]{1,0:T(8,128)(2,1)S(1)}, bf16[128,512]{1,0:T(8,128)(2,1)S(1)}, u32[]{:S(2)}, u32[]{:S(2)}) collective-permute-start(bf16[128,512]{1,0:T(8,128)(2,1)S(1)} %get-tuple-element.113), channel_id=1, source_target_pairs={{0,2},{1,3},{2,0},{3,1},{4,6},{5,7},{6,4},{7,5},{8,10},{9,11},{10,... | collective-permute-start | bytes 393224 | tf_op jit(solution)/shard_map/ppermute | solution.py:491
  57.5 1.3 %collective-permute-start.25 = (bf16[128,512]{1,0:T(8,128)(2,1)S(1)}, bf16[128,512]{1,0:T(8,128)(2,1)S(1)}, u32[]{:S(2)}, u32[]{:S(2)}) collective-permute-start(bf16[128,512]{1,0:T(8,128)(2,1)S(1)} %get-tuple-element.114), channel_id=1, source_target_pairs={{0,3},{1,2},{2,1},{3,0},{4,7},{5,6},{6,5},{7,4},{8,11},{9,10},{10,... | collective-permute-start | bytes 393224 | tf_op jit(solution)/shard_map/ppermute | solution.py:491
  58.8 1.3 %collective-permute-start.20 = (bf16[128,512]{1,0:T(8,128)(2,1)S(1)}, bf16[128,512]{1,0:T(8,128)(2,1)S(1)}, u32[]{:S(2)}, u32[]{:S(2)}) collective-permute-start(bf16[128,512]{1,0:T(8,128)(2,1)S(1)} %get-tuple-element.109), channel_id=1, source_target_pairs={{1,0},{2,3},{5,4},{6,7},{9,8},{10,11},{13,12},{14,15},{17,16},{18,... | collective-permute-start | bytes 393224 | tf_op jit(solution)/shard_map/ppermute | solution.py:560
  60.1 1.3 %collective-permute-start.21 = (bf16[128,512]{1,0:T(8,128)(2,1)S(1)}, bf16[128,512]{1,0:T(8,128)(2,1)S(1)}, u32[]{:S(2)}, u32[]{:S(2)}) collective-permute-start(bf16[128,512]{1,0:T(8,128)(2,1)S(1)} %get-tuple-element.110), channel_id=1, source_target_pairs={{1,3},{2,0},{5,7},{6,4},{9,11},{10,8},{13,15},{14,12},{17,19},{18,... | collective-permute-start | bytes 393224 | tf_op jit(solution)/shard_map/ppermute | solution.py:560
  61.4 0.2 collective-permute-done.23.refs_1_
  61.7 0.7 collective-permute-start.22
  62.3 5.1 %collective-permute-done.24.refs_2_ = bf16[128,512]{1,0:T(8,128)(2,1)S(1)} collective-permute-done((bf16[128,512]{1,0:T(8,128)(2,1)S(1)}, bf16[128,512]{1,0:T(8,128)(2,1)S(1)}, u32[]{:S(2)}, u32[]{:S(2)}) %collective-permute-start.24) | collective-permute-done | bytes 131104 | tf_op jit(solution)/shard_map/ppermute | solution.py:491
  67.4 0.8 %place_steps.1.refs_4_ = bf16[6,128,512]{2,1,0:T(8,128)(2,1)} custom-call(bf16[128,512]{1,0:T(8,128)(2,1)S(1)} %get-tuple-element.107.refs_10_.refs_0_, bf16[128,512]{1,0:T(8,128)(2,1)S(1)} %collective-permute-done.23.refs_1_, bf16[128,512]{1,0:T(8,128)(2,1)S(1)} %collective-permute-done.24.refs_2_, bf16[128,512]{1,0:T(8,128)(2,1)S(1)} %collective-permute-done.25.refs_3_), custom_call_target="tpu_custom_call" | custom-call | tf_op jit(solution)/shard_map/place_steps/pallas_call | solution.py:459
  68.2 4.0 %collective-permute-done.20.refs_1_ = bf16[128,512]{1,0:T(8,128)(2,1)S(1)} collective-permute-done((bf16[128,512]{1,0:T(8,128)(2,1)S(1)}, bf16[128,512]{1,0:T(8,128)(2,1)S(1)}, u32[]{:S(2)}, u32[]{:S(2)}) %collective-permute-start.20) | collective-permute-done | bytes 131104 | tf_op jit(solution)/shard_map/ppermute | solution.py:560
  72.2 1.4 %collective-permute-done.21.refs_2_ = bf16[128,512]{1,0:T(8,128)(2,1)S(1)} collective-permute-done((bf16[128,512]{1,0:T(8,128)(2,1)S(1)}, bf16[128,512]{1,0:T(8,128)(2,1)S(1)}, u32[]{:S(2)}, u32[]{:S(2)}) %collective-permute-start.21) | collective-permute-done | bytes 131104 | tf_op jit(solution)/shard_map/ppermute | solution.py:560
  73.6 0.8 %place_extra.1 = bf16[6,128,512]{2,1,0:T(8,128)(2,1)} custom-call(bf16[128,512]{1,0:T(8,128)(2,1)S(1)} %get-tuple-element.108.refs_0_, bf16[128,512]{1,0:T(8,128)(2,1)S(1)} %collective-permute-done.20.refs_1_, bf16[128,512]{1,0:T(8,128)(2,1)S(1)} %collective-permute-done.21.refs_2_, ...), custom_call_target="tpu_custom_call", output_to_operand_aliasing={{}: (4, {})} | custom-call | tf_op jit(solution)/shard_map/place_extra/pallas_call | solution.py:468
  (31 shorter events, 0.1 us)
Async XLA Ops:
  0.0 15.4 %copy-start.8 = (bf16[512,512]{1,0:T(8,128)(2,1)S(1)}, bf16[512,512]{1,0:T(8,128)(2,1)}, u32[]{:S(2)}) copy-start(bf16[512,512]{1,0:T(8,128)(2,1)} %refs_11_.1) | copy-start | bytes 1572868
  0.0 15.4 %copy-start.7 = (bf16[512,512]{1,0:T(8,128)(2,1)S(1)}, bf16[512,512]{1,0:T(8,128)(2,1)}, u32[]{:S(2)}) copy-start(bf16[512,512]{1,0:T(8,128)(2,1)} %refs_10_.1) | copy-start | bytes 1572868
  0.0 15.4 %copy-start.6 = (bf16[512,512]{1,0:T(8,128)(2,1)S(1)}, bf16[512,512]{1,0:T(8,128)(2,1)}, u32[]{:S(2)}) copy-start(bf16[512,512]{1,0:T(8,128)(2,1)} %refs_9_.3) | copy-start | bytes 1572868
  0.0 15.4 %copy-start.5 = (bf16[512,512]{1,0:T(8,128)(2,1)S(1)}, bf16[512,512]{1,0:T(8,128)(2,1)}, u32[]{:S(2)}) copy-start(bf16[512,512]{1,0:T(8,128)(2,1)} %refs_8_.3) | copy-start | bytes 1572868
  1.4 6.9 %collective-permute-start = (bf16[6,16,512]{2,1,0:T(8,128)(2,1)S(1)}, bf16[6,16,512]{2,1,0:T(8,128)(2,1)S(1)}, u32[]{:S(2)}, u32[]{:S(2)}) collective-permute-start(bf16[6,16,512]{2,1,0:T(8,128)(2,1)S(1)} %get-tuple-element.61), channel_id=1, source_target_pairs={{0,28},{4,24},{8,20},{12,16},{16,12},{20,8},{24,4},{28,0},{1,29},{... | collective-permute-start | bytes 294920 | tf_op jit(solution)/shard_map/ppermute | solution.py:491
  4.9 6.4 %collective-permute-start.1 = (bf16[6,16,512]{2,1,0:T(8,128)(2,1)S(1)}, bf16[6,16,512]{2,1,0:T(8,128)(2,1)S(1)}, u32[]{:S(2)}, u32[]{:S(2)}) collective-permute-start(bf16[6,16,512]{2,1,0:T(8,128)(2,1)S(1)} %get-tuple-element.63), channel_id=1, source_target_pairs={{0,24},{4,28},{8,16},{12,20},{16,8},{20,12},{24,0},{28,4},{1,25},{... | collective-permute-start | bytes 294920 | tf_op jit(solution)/shard_map/ppermute | solution.py:491
  5.5 7.0 %collective-permute-start.2 = (bf16[6,16,512]{2,1,0:T(8,128)(2,1)S(1)}, bf16[6,16,512]{2,1,0:T(8,128)(2,1)S(1)}, u32[]{:S(2)}, u32[]{:S(2)}) collective-permute-start(bf16[6,16,512]{2,1,0:T(8,128)(2,1)S(1)} %get-tuple-element.64), channel_id=1, source_target_pairs={{0,20},{4,16},{8,28},{12,24},{16,4},{20,0},{24,12},{28,8},{1,21},{... | collective-permute-start | bytes 294920 | tf_op jit(solution)/shard_map/ppermute | solution.py:491
  6.9 7.9 %collective-permute-start.3 = (bf16[6,16,512]{2,1,0:T(8,128)(2,1)S(1)}, bf16[6,16,512]{2,1,0:T(8,128)(2,1)S(1)}, u32[]{:S(2)}, u32[]{:S(2)}) collective-permute-start(bf16[6,16,512]{2,1,0:T(8,128)(2,1)S(1)} %get-tuple-element.65), channel_id=1, source_target_pairs={{0,16},{4,20},{8,24},{12,28},{16,0},{20,4},{24,8},{28,12},{1,17},{... | collective-permute-start | bytes 294920 | tf_op jit(solution)/shard_map/ppermute | solution.py:491
  7.2 7.6 %collective-permute-start.4 = (bf16[6,16,512]{2,1,0:T(8,128)(2,1)S(1)}, bf16[6,16,512]{2,1,0:T(8,128)(2,1)S(1)}, u32[]{:S(2)}, u32[]{:S(2)}) collective-permute-start(bf16[6,16,512]{2,1,0:T(8,128)(2,1)S(1)} %get-tuple-element.66), channel_id=1, source_target_pairs={{0,12},{4,8},{8,4},{12,0},{16,28},{20,24},{24,20},{28,16},{1,13},{... | collective-permute-start | bytes 294920 | tf_op jit(solution)/shard_map/ppermute | solution.py:491
  8.3 7.1 %collective-permute-start.5 = (bf16[6,16,512]{2,1,0:T(8,128)(2,1)S(1)}, bf16[6,16,512]{2,1,0:T(8,128)(2,1)S(1)}, u32[]{:S(2)}, u32[]{:S(2)}) collective-permute-start(bf16[6,16,512]{2,1,0:T(8,128)(2,1)S(1)} %get-tuple-element.67), channel_id=1, source_target_pairs={{0,8},{4,12},{8,0},{12,4},{16,24},{20,28},{24,16},{28,20},{1,9},{5... | collective-permute-start | bytes 294920 | tf_op jit(solution)/shard_map/ppermute | solution.py:491
  11.2 4.1 %collective-permute-start.6 = (bf16[6,16,512]{2,1,0:T(8,128)(2,1)S(1)}, bf16[6,16,512]{2,1,0:T(8,128)(2,1)S(1)}, u32[]{:S(2)}, u32[]{:S(2)}) collective-permute-start(bf16[6,16,512]{2,1,0:T(8,128)(2,1)S(1)} %get-tuple-element.68), channel_id=1, source_target_pairs={{0,4},{4,0},{8,12},{12,8},{16,20},{20,16},{24,28},{28,24},{1,5},{5... | collective-permute-start | bytes 294920 | tf_op jit(solution)/shard_map/ppermute | solution.py:491
  15.4 31.8 %copy-start = (bf16[512,512]{1,0:T(8,128)(2,1)S(1)}, bf16[512,512]{1,0:T(8,128)(2,1)}, u32[]{:S(2)}) copy-start(bf16[512,512]{1,0:T(8,128)(2,1)} %refs_4_.5) | copy-start | bytes 1572868
  15.4 31.8 %copy-start.1 = (bf16[512,512]{1,0:T(8,128)(2,1)S(1)}, bf16[512,512]{1,0:T(8,128)(2,1)}, u32[]{:S(2)}) copy-start(bf16[512,512]{1,0:T(8,128)(2,1)} %refs_5_.5) | copy-start | bytes 1572868
  15.4 31.8 %copy-start.2 = (bf16[512,512]{1,0:T(8,128)(2,1)S(1)}, bf16[512,512]{1,0:T(8,128)(2,1)}, u32[]{:S(2)}) copy-start(bf16[512,512]{1,0:T(8,128)(2,1)} %refs_6_.3) | copy-start | bytes 1572868
  15.5 32.7 %copy-start.4 = (bf16[2048,512]{1,0:T(8,128)(2,1)S(1)}, bf16[2048,512]{1,0:T(8,128)(2,1)}, u32[]{:S(2)}) copy-start(bf16[2048,512]{1,0:T(8,128)(2,1)} %refs_9_.5) | copy-start | bytes 6291460
  20.0 28.2 %copy-start.3 = (bf16[512,2048]{1,0:T(8,128)(2,1)S(1)}, bf16[512,2048]{1,0:T(8,128)(2,1)}, u32[]{:S(2)}) copy-start(bf16[512,2048]{1,0:T(8,128)(2,1)} %refs_8_.5) | copy-start | bytes 6291460
  20.0 5.8 %collective-permute-start.7 = (bf16[6,16,512]{2,1,0:T(8,128)(2,1)S(1)}, bf16[6,16,512]{2,1,0:T(8,128)(2,1)S(1)}, u32[]{:S(2)}, u32[]{:S(2)}) collective-permute-start(bf16[6,16,512]{2,1,0:T(8,128)(2,1)S(1)} %get-tuple-element.79), channel_id=1, source_target_pairs={{0,28},{4,24},{8,20},{12,16},{16,12},{20,8},{24,4},{28,0},{1,29},{... | collective-permute-start | bytes 294920 | tf_op jit(solution)/shard_map/ppermute | solution.py:491
  22.1 6.2 %collective-permute-start.8 = (bf16[6,16,512]{2,1,0:T(8,128)(2,1)S(1)}, bf16[6,16,512]{2,1,0:T(8,128)(2,1)S(1)}, u32[]{:S(2)}, u32[]{:S(2)}) collective-permute-start(bf16[6,16,512]{2,1,0:T(8,128)(2,1)S(1)} %get-tuple-element.81), channel_id=1, source_target_pairs={{0,24},{4,28},{8,16},{12,20},{16,8},{20,12},{24,0},{28,4},{1,25},{... | collective-permute-start | bytes 294920 | tf_op jit(solution)/shard_map/ppermute | solution.py:491
  22.7 7.5 %collective-permute-start.9 = (bf16[6,16,512]{2,1,0:T(8,128)(2,1)S(1)}, bf16[6,16,512]{2,1,0:T(8,128)(2,1)S(1)}, u32[]{:S(2)}, u32[]{:S(2)}) collective-permute-start(bf16[6,16,512]{2,1,0:T(8,128)(2,1)S(1)} %get-tuple-element.82), channel_id=1, source_target_pairs={{0,20},{4,16},{8,28},{12,24},{16,4},{20,0},{24,12},{28,8},{1,21},{... | collective-permute-start | bytes 294920 | tf_op jit(solution)/shard_map/ppermute | solution.py:491
  23.9 8.5 %collective-permute-start.10 = (bf16[6,16,512]{2,1,0:T(8,128)(2,1)S(1)}, bf16[6,16,512]{2,1,0:T(8,128)(2,1)S(1)}, u32[]{:S(2)}, u32[]{:S(2)}) collective-permute-start(bf16[6,16,512]{2,1,0:T(8,128)(2,1)S(1)} %get-tuple-element.83), channel_id=1, source_target_pairs={{0,16},{4,20},{8,24},{12,28},{16,0},{20,4},{24,8},{28,12},{1,17},{... | collective-permute-start | bytes 294920 | tf_op jit(solution)/shard_map/ppermute | solution.py:491
  24.5 7.9 %collective-permute-start.11 = (bf16[6,16,512]{2,1,0:T(8,128)(2,1)S(1)}, bf16[6,16,512]{2,1,0:T(8,128)(2,1)S(1)}, u32[]{:S(2)}, u32[]{:S(2)}) collective-permute-start(bf16[6,16,512]{2,1,0:T(8,128)(2,1)S(1)} %get-tuple-element.84), channel_id=1, source_target_pairs={{0,12},{4,8},{8,4},{12,0},{16,28},{20,24},{24,20},{28,16},{1,13},{... | collective-permute-start | bytes 294920 | tf_op jit(solution)/shard_map/ppermute | solution.py:491
  25.8 6.6 %collective-permute-start.12 = (bf16[6,16,512]{2,1,0:T(8,128)(2,1)S(1)}, bf16[6,16,512]{2,1,0:T(8,128)(2,1)S(1)}, u32[]{:S(2)}, u32[]{:S(2)}) collective-permute-start(bf16[6,16,512]{2,1,0:T(8,128)(2,1)S(1)} %get-tuple-element.85), channel_id=1, source_target_pairs={{0,8},{4,12},{8,0},{12,4},{16,24},{20,28},{24,16},{28,20},{1,9},{5... | collective-permute-start | bytes 294920 | tf_op jit(solution)/shard_map/ppermute | solution.py:491
  28.2 4.2 %collective-permute-start.13 = (bf16[6,16,512]{2,1,0:T(8,128)(2,1)S(1)}, bf16[6,16,512]{2,1,0:T(8,128)(2,1)S(1)}, u32[]{:S(2)}, u32[]{:S(2)}) collective-permute-start(bf16[6,16,512]{2,1,0:T(8,128)(2,1)S(1)} %get-tuple-element.86), channel_id=1, source_target_pairs={{0,4},{4,0},{8,12},{12,8},{16,20},{20,16},{24,28},{28,24},{1,5},{5... | collective-permute-start | bytes 294920 | tf_op jit(solution)/shard_map/ppermute | solution.py:491
  32.5 10.8 %collective-permute-start.14 = (bf16[128,512]{1,0:T(8,128)(2,1)S(1)}, bf16[128,512]{1,0:T(8,128)(2,1)S(1)}, u32[]{:S(2)}, u32[]{:S(2)}) collective-permute-start(bf16[128,512]{1,0:T(8,128)(2,1)S(1)} %get-tuple-element.96), channel_id=1, source_target_pairs={{0,2},{1,3},{2,0},{3,1},{4,6},{5,7},{6,4},{7,5},{8,10},{9,11},{10,... | collective-permute-start | bytes 393224 | tf_op jit(solution)/shard_map/ppermute | solution.py:491
  35.1 12.1 %collective-permute-start.18 = (bf16[128,512]{1,0:T(8,128)(2,1)S(1)}, bf16[128,512]{1,0:T(8,128)(2,1)S(1)}, u32[]{:S(2)}, u32[]{:S(2)}) collective-permute-start(bf16[128,512]{1,0:T(8,128)(2,1)S(1)} %get-tuple-element.102), channel_id=1, source_target_pairs={{0,1},{1,0},{2,3},{3,2},{4,5},{5,4},{6,7},{7,6},{8,9},{9,8},{10,11... | collective-permute-start | bytes 393224 | tf_op jit(solution)/shard_map/ppermute | solution.py:491
  36.7 11.4 %collective-permute-start.19 = (bf16[128,512]{1,0:T(8,128)(2,1)S(1)}, bf16[128,512]{1,0:T(8,128)(2,1)S(1)}, u32[]{:S(2)}, u32[]{:S(2)}) collective-permute-start(bf16[128,512]{1,0:T(8,128)(2,1)S(1)} %get-tuple-element.103), channel_id=1, source_target_pairs={{0,3},{1,2},{2,1},{3,0},{4,7},{5,6},{6,5},{7,4},{8,11},{9,10},{10,... | collective-permute-start | bytes 393224 | tf_op jit(solution)/shard_map/ppermute | solution.py:491
  43.3 14.2 %collective-permute-start.15 = (bf16[128,512]{1,0:T(8,128)(2,1)S(1)}, bf16[128,512]{1,0:T(8,128)(2,1)S(1)}, u32[]{:S(2)}, u32[]{:S(2)}) collective-permute-start(bf16[128,512]{1,0:T(8,128)(2,1)S(1)} %get-tuple-element.98), channel_id=1, source_target_pairs={{0,1},{3,2},{4,5},{7,6},{8,9},{11,10},{12,13},{15,14},{16,17},{19,... | collective-permute-start | bytes 393224 | tf_op jit(solution)/shard_map/ppermute | solution.py:491
  45.1 13.8 %collective-permute-start.16 = (bf16[128,512]{1,0:T(8,128)(2,1)S(1)}, bf16[128,512]{1,0:T(8,128)(2,1)S(1)}, u32[]{:S(2)}, u32[]{:S(2)}) collective-permute-start(bf16[128,512]{1,0:T(8,128)(2,1)S(1)} %get-tuple-element.99), channel_id=1, source_target_pairs={{0,2},{3,1},{4,6},{7,5},{8,10},{11,9},{12,14},{15,13},{16,18},{19,... | collective-permute-start | bytes 393224 | tf_op jit(solution)/shard_map/ppermute | solution.py:491
  46.4 12.5 %collective-permute-start.17 = (bf16[128,512]{1,0:T(8,128)(2,1)S(1)}, bf16[128,512]{1,0:T(8,128)(2,1)S(1)}, u32[]{:S(2)}, u32[]{:S(2)}) collective-permute-start(bf16[128,512]{1,0:T(8,128)(2,1)S(1)} %get-tuple-element.100), channel_id=1, source_target_pairs={{1,2},{2,1},{5,6},{6,5},{9,10},{10,9},{13,14},{14,13},{17,18},{18,... | collective-permute-start | bytes 393224 | tf_op jit(solution)/shard_map/ppermute | solution.py:491
  54.4 7.3 %collective-permute-start.23 = (bf16[128,512]{1,0:T(8,128)(2,1)S(1)}, bf16[128,512]{1,0:T(8,128)(2,1)S(1)}, u32[]{:S(2)}, u32[]{:S(2)}) collective-permute-start(bf16[128,512]{1,0:T(8,128)(2,1)S(1)} %get-tuple-element.112), channel_id=1, source_target_pairs={{0,1},{1,0},{2,3},{3,2},{4,5},{5,4},{6,7},{7,6},{8,9},{9,8},{10,11... | collective-permute-start | bytes 393224 | tf_op jit(solution)/shard_map/ppermute | solution.py:491
  55.1 12.3 %collective-permute-start.24 = (bf16[128,512]{1,0:T(8,128)(2,1)S(1)}, bf16[128,512]{1,0:T(8,128)(2,1)S(1)}, u32[]{:S(2)}, u32[]{:S(2)}) collective-permute-start(bf16[128,512]{1,0:T(8,128)(2,1)S(1)} %get-tuple-element.113), channel_id=1, source_target_pairs={{0,2},{1,3},{2,0},{3,1},{4,6},{5,7},{6,4},{7,5},{8,10},{9,11},{10,... | collective-permute-start | bytes 393224 | tf_op jit(solution)/shard_map/ppermute | solution.py:491
  57.5 9.9 %collective-permute-start.25 = (bf16[128,512]{1,0:T(8,128)(2,1)S(1)}, bf16[128,512]{1,0:T(8,128)(2,1)S(1)}, u32[]{:S(2)}, u32[]{:S(2)}) collective-permute-start(bf16[128,512]{1,0:T(8,128)(2,1)S(1)} %get-tuple-element.114), channel_id=1, source_target_pairs={{0,3},{1,2},{2,1},{3,0},{4,7},{5,6},{6,5},{7,4},{8,11},{9,10},{10,... | collective-permute-start | bytes 393224 | tf_op jit(solution)/shard_map/ppermute | solution.py:491
  58.8 13.3 %collective-permute-start.20 = (bf16[128,512]{1,0:T(8,128)(2,1)S(1)}, bf16[128,512]{1,0:T(8,128)(2,1)S(1)}, u32[]{:S(2)}, u32[]{:S(2)}) collective-permute-start(bf16[128,512]{1,0:T(8,128)(2,1)S(1)} %get-tuple-element.109), channel_id=1, source_target_pairs={{1,0},{2,3},{5,4},{6,7},{9,8},{10,11},{13,12},{14,15},{17,16},{18,... | collective-permute-start | bytes 393224 | tf_op jit(solution)/shard_map/ppermute | solution.py:560
  60.1 13.5 %collective-permute-start.21 = (bf16[128,512]{1,0:T(8,128)(2,1)S(1)}, bf16[128,512]{1,0:T(8,128)(2,1)S(1)}, u32[]{:S(2)}, u32[]{:S(2)}) collective-permute-start(bf16[128,512]{1,0:T(8,128)(2,1)S(1)} %get-tuple-element.110), channel_id=1, source_target_pairs={{1,3},{2,0},{5,7},{6,4},{9,11},{10,8},{13,15},{14,12},{17,19},{18,... | collective-permute-start | bytes 393224 | tf_op jit(solution)/shard_map/ppermute | solution.py:560
  61.7 12.0 %collective-permute-start.22 = (bf16[128,512]{1,0:T(8,128)(2,1)S(1)}, bf16[128,512]{1,0:T(8,128)(2,1)S(1)}, u32[]{:S(2)}, u32[]{:S(2)}) collective-permute-start(bf16[128,512]{1,0:T(8,128)(2,1)S(1)} %get-tuple-element.111), channel_id=1, source_target_pairs={{1,2},{2,1},{5,6},{6,5},{9,10},{10,9},{13,14},{14,13},{17,18},{18,... | collective-permute-start | bytes 393224 | tf_op jit(solution)/shard_map/ppermute | solution.py:560
